TPU v7x, 32 devices: a whole 2x2x4 slice. The times are simulated.
32 devices in a mesh: src: 4 (over y, x), tgt: 8 (over z, core).
Axes of the slice: x: 2, y: 2, z: 4, core: 2. Of those that a mesh axis runs over, the one named last changes fastest.
Arguments:
- box_weights: bfloat16 [128, 1024, 128], P('src', 'tgt'), may hold values from -6 to 6
- slowness: float32 [1024], P('tgt'), may hold values from 0 to 3
- dip_field: float32 [128], P('src'), may hold values from 0 to 3
Outputs:
- interpolants: bfloat16 [128, 1024, 128], P('src', 'tgt')
All inputs are finite; a program needn't handle non-finite values.
Results may differ from a plain program's by a relative error of at most 0.038.
Values may be sent and summed in bfloat16 or wider, within the bound.
No kernel may reach another device: no remote copies, remote signals or barrier semaphores. Data moves between devices by JAX's collectives and lax.ppermute only.
A program may use at most 64 MiB of HBM per device.

v0:
```python
import functools
import math

import jax
import jax.numpy as jnp
import ml_dtypes
import numpy as np
from jax import lax
from jax.experimental import pallas as pl
from jax.experimental.pallas import tpu as pltpu
from jax.sharding import PartitionSpec as P

HALF = 64
WIDE = 128


def nodes():
    points = np.cos((2.0 * np.arange(8) + 1.0) * (math.pi / 16.0))
    return np.repeat(points, 8), np.tile(points, 8)


def node_weights():
    first, second = nodes()
    return (first * first + second * second).astype(np.float32)


def level_matrix(number):
    first, second = nodes()
    frequency = 9.0 + 3.0 * (number % 5)
    shifts = np.array([-0.5, 0.5])
    out_first = first[None, :] + shifts[:, None]
    in_second = second[None, :] + shifts[:, None]
    inner = (
        out_first[:, None, :, None] * first[None, None, None, :]
        + second[None, None, :, None] * in_second[None, :, None, :]
    )
    out_norm = np.sqrt(out_first**2 + second[None, :] ** 2)
    in_norm = np.sqrt(first[None, :] ** 2 + in_second**2)
    phases = frequency * (inner + 0.5 * out_norm[:, None, :, None] * in_norm[None, :, None, :])
    factor = 1.0 / math.sqrt(128.0)
    real = np.transpose(factor * np.cos(phases), (1, 3, 0, 2))
    imag = np.transpose(factor * np.sin(phases), (1, 3, 0, 2))
    upper = np.concatenate([real, imag], axis=3)
    lower = np.concatenate([-imag, real], axis=3)
    full = np.concatenate([upper, lower], axis=1)
    return full.reshape(2 * WIDE, 2 * WIDE).astype(ml_dtypes.bfloat16)


def tables(scales):
    weights = np.tile(node_weights(), 2)
    angles = scales[..., None] * weights
    signs = np.repeat(np.array([-1.0, 1.0], np.float32), HALF)
    return jnp.cos(angles), jnp.sin(angles) * signs


def butterfly(source, target, apart, matrix, phase_of, group):
    count = source.shape[0]
    lows = [i for i in range(count) if not i & apart]
    for start in range(0, len(lows), group):
        picked = lows[start : start + group]
        left = jnp.concatenate([source[i] for i in picked], axis=0)
        right = jnp.concatenate([source[i + apart] for i in picked], axis=0)
        both = jnp.dot(
            jnp.concatenate([left, right], axis=1), matrix, preferred_element_type=jnp.float32
        )
        rows = source.shape[1]
        for place, low in enumerate(picked):
            for child in range(2):
                value = both[
                    place * rows : (place + 1) * rows, child * WIDE : (child + 1) * WIDE
                ]
                index = low + child * apart
                cosine, sine = phase_of(index)
                value = value * cosine + pltpu.roll(value, HALF, 1) * sine
                target[index] = value.astype(target.dtype)


def local_kernel(aparts, group, x_ref, m_ref, c_ref, s_ref, o_ref):
    source = x_ref
    for step, apart in enumerate(aparts):
        butterfly(
            source, o_ref, apart, m_ref[step], lambda index: (c_ref[...], s_ref[...]), group
        )
        source = o_ref


def local_levels(x, matrices, cosine, sine, aparts):
    rows = x.shape[1]
    return pl.pallas_call(
        functools.partial(local_kernel, aparts, max(1, 512 // rows)),
        out_shape=jax.ShapeDtypeStruct(x.shape, x.dtype),
        in_specs=[pl.BlockSpec(memory_space=pltpu.VMEM)] * 4,
        out_specs=pl.BlockSpec(memory_space=pltpu.VMEM),
        compiler_params=pltpu.CompilerParams(vmem_limit_bytes=32 << 20),
    )(x, matrices, cosine, sine)


def swapped_kernel(levels, group, tgt_count, x_ref, m_ref, cs_ref, ss_ref, ct_ref, st_ref, o_ref):
    source = x_ref
    for step, (apart, by_source) in enumerate(levels):

        def phase_of(index):
            if by_source:
                at = index % tgt_count
                return cs_ref[at], ss_ref[at]
            at = index // tgt_count
            return ct_ref[at], st_ref[at]

        butterfly(source, o_ref, apart, m_ref[step], phase_of, group)
        source = o_ref


def swapped_levels(x, matrices, src_tables, tgt_tables, levels, tgt_count):
    rows = x.shape[1]
    return pl.pallas_call(
        functools.partial(swapped_kernel, levels, max(1, 512 // rows), tgt_count),
        out_shape=jax.ShapeDtypeStruct(x.shape, x.dtype),
        in_specs=[pl.BlockSpec(memory_space=pltpu.VMEM)] * 6,
        out_specs=pl.BlockSpec(memory_space=pltpu.VMEM),
        compiler_params=pltpu.CompilerParams(vmem_limit_bytes=32 << 20),
    )(x, matrices, *src_tables, *tgt_tables)


def local(box_weights, slowness, dip_field):
    rows, cols, _ = box_weights.shape
    src_count = lax.axis_size("src")
    tgt_count = lax.axis_size("tgt")
    devices = src_count * tgt_count
    row_bits, col_bits = rows.bit_length() - 1, cols.bit_length() - 1
    src_bits, tgt_bits = src_count.bit_length() - 1, tgt_count.bit_length() - 1
    first_target = row_bits + src_bits
    total = first_target + tgt_bits + col_bits
    matrices = [level_matrix(number) for number in range(total)]

    def matrices_of(low, high):
        return jnp.asarray(np.stack(matrices[low:high]))

    row_parts = min(rows, devices)
    col_parts = devices // row_parts
    row_each, col_each = rows // row_parts, cols // col_parts
    place = lax.axis_index("src") * tgt_count + lax.axis_index("tgt")
    row_at, col_at = place // col_parts, place % col_parts

    all_slowness = lax.all_gather(slowness, "tgt")
    all_dip = lax.all_gather(dip_field, "src")

    cosine, sine = tables(slowness)
    state = local_levels(
        box_weights,
        matrices_of(0, row_bits),
        cosine,
        sine,
        [1 << bit for bit in range(row_bits)],
    )

    state = state.reshape(row_parts, row_each, col_parts, col_each, WIDE)
    state = jnp.swapaxes(state, 1, 2).reshape(devices, row_each * col_each, WIDE)
    state = lax.all_to_all(state, ("src", "tgt"), 0, 0, tiled=True)

    part_slowness = lax.dynamic_slice_in_dim(all_slowness, col_at * col_each, col_each, 1)
    part_slowness = jnp.broadcast_to(
        part_slowness[:, None, :], (tgt_count, row_each, col_each)
    ).reshape(tgt_count, row_each * col_each)
    part_dip = lax.dynamic_slice_in_dim(all_dip, row_at * row_each, row_each, 1)
    part_dip = jnp.broadcast_to(
        part_dip[:, :, None], (src_count, row_each, col_each)
    ).reshape(src_count, row_each * col_each)
    levels = [(tgt_count << bit, True) for bit in range(src_bits)]
    levels += [(1 << bit, False) for bit in reversed(range(tgt_bits))]
    state = swapped_levels(
        state,
        matrices_of(row_bits, first_target + tgt_bits),
        tables(part_slowness),
        tables(part_dip),
        levels,
        tgt_count,
    )

    state = lax.all_to_all(state, ("src", "tgt"), 0, 0, tiled=True)
    state = state.reshape(row_parts, col_parts, row_each, col_each, WIDE)
    state = jnp.transpose(state, (1, 3, 0, 2, 4)).reshape(cols, rows, WIDE)

    cosine, sine = tables(dip_field)
    state = local_levels(
        state,
        matrices_of(first_target + tgt_bits, total),
        cosine,
        sine,
        [1 << bit for bit in reversed(range(col_bits))],
    )
    return jnp.swapaxes(state, 0, 1)


def solution(mesh):
    in_specs = (P("src", "tgt", None), P("tgt"), P("src"))
    out_specs = P("src", "tgt", None)
    return jax.shard_map(local, mesh=mesh, in_specs=in_specs, out_specs=out_specs, check_vma=False)
```

profile of v0, /device:TPU:0, one launch (start us, length us, event | category | flops | bytes accessed | tf_op | source)
XLA Modules:
  0.0 88.6 jit_solution(14937997317356048750)
XLA Ops:
  0.0 0.7 copy-done.4
  0.7 0.0 copy-done.5
  0.7 1.0 %fusion.2 = (f32[128,128]{1,0:T(8,128)S(1)}, f32[128,128]{1,0:T(8,128)S(1)}) fusion(f32[128]{0:T(128)S(1)} %copy-done.5, f32[128]{0:T(128)S(1)} %copy-done.4, f32[128]{0:T(128)} %param.15), kind=kLoop, calls=%fused_computation.9 | loop fusion | flops 32768 | bytes 132608 | tf_op jit(solution)/shard_map/mul | solution.py:53
  1.6 0.0 copy-start
  1.7 1.1 %copy-done = bf16[5,256,256]{2,1,0:T(8,128)(2,1)S(1)} copy-done((bf16[5,256,256]{2,1,0:T(8,128)(2,1)S(1)}, bf16[5,256,256]{2,1,0:T(8,128)(2,1)}, u32[]{:S(2)}) %copy-start) | copy-done | bytes 655384
  2.7 1.2 %copy-done.2 = bf16[32,128,128]{2,1,0:T(8,128)(2,1)S(1)} copy-done((bf16[32,128,128]{2,1,0:T(8,128)(2,1)S(1)}, bf16[32,128,128]{2,1,0:T(8,128)(2,1)}, u32[]{:S(2)}) %copy-start.2) | copy-done | bytes 1048600
  4.0 4.1 %shard_map.136 = bf16[32,128,128]{2,1,0:T(8,128)(2,1)} custom-call(bf16[32,128,128]{2,1,0:T(8,128)(2,1)S(1)} %copy-done.2, bf16[5,256,256]{2,1,0:T(8,128)(2,1)S(1)} %copy-done, f32[128,128]{1,0:T(8,128)S(1)} %get-tuple-element.12.c_ref, f32[128,128]{1,0:T(8,128)S(1)} %get-tuple-element.11.s_ref), custom_call_target="tpu_custom_call" | custom-call | tf_op jit(solution)/shard_map/pallas_call | solution.py:89
  8.1 7.3 %all-to-all-start = ((bf16[32,128,128]{2,1,0:T(8,128)(2,1)}), bf16[32,128,128]{2,1,0:T(8,128)(2,1)S(1)}, u32[]{:S(2)}, u32[]{:S(2)}) async-start(bf16[32,128,128]{2,1,0:T(8,128)(2,1)} %shard_map.136), calls=%async_computation | async-start | bytes 2097152 | tf_op jit(solution)/shard_map/all_to_all | solution.py:158
  15.4 0.0 copy-start.8
  15.4 0.6 copy-done.8
  16.1 0.6 dynamic-slice
  17.3 0.0 copy-start.7
  17.4 0.6 copy-done.7
  18.0 0.2 dynamic-update-slice
  18.2 0.1 reshape.23
  18.3 10.3 %all-reduce.1 = f32[4,32]{1,0:T(4,128)S(1)} all-reduce(f32[4,32]{1,0:T(4,128)S(1)} %reshape.23), channel_id=3, replica_groups=mesh['src'=4,'tgt'=8] {'src'}, use_global_device_ids=true, to_apply=%add | all-reduce | flops 128 | bytes 1024
  28.5 0.2 dynamic-slice_reduce_fusion
  28.7 0.7 copy-done.6
  29.4 11.8 %all-gather.2 = f32[8,1,128]{2,1,0:T(1,128)S(1)} all-gather(f32[1,1,128]{2,1,0:T(1,128)S(1)} %bitcast.14), channel_id=2, replica_groups=mesh['src'=4,'tgt'=8] {'tgt'}, dimensions={0}, use_global_device_ids=true | all-gather | bytes 4608 | tf_op jit(solution)/shard_map/all_gather | solution.py:144
  41.2 0.1 fusion.1
  41.3 0.0 copy-start.1
  41.3 1.9 %fusion = (f32[8,128,128]{2,1,0:T(8,128)S(1)}, f32[8,128,128]{2,1,0:T(8,128)S(1)}) fusion(f32[128]{0:T(128)S(1)} %copy-done.5, f32[128]{0:T(128)S(1)} %copy-done.4, f32[8,128]{1,0:T(8,128)S(1)} %bitcast.13), kind=kLoop, calls=%fused_computation.3 | loop fusion | flops 262144 | bytes 1053696 | tf_op jit(solution)/shard_map/mul | solution.py:53
  43.2 0.0 all-to-all-done.x_ref
  43.3 0.0 copy-done.1
  43.3 4.1 %shard_map.137 = bf16[32,128,128]{2,1,0:T(8,128)(2,1)} custom-call(bf16[32,128,128]{2,1,0:T(8,128)(2,1)S(1)} %all-to-all-done.x_ref, bf16[5,256,256]{2,1,0:T(8,128)(2,1)S(1)} %copy-done.1, f32[8,128,128]{2,1,0:T(8,128)S(1)} %get-tuple-element.6.cs_ref, f32[8,128,128]{2,1,0:T(8,128)S(1)} %get-tuple-element.5.ss_ref, ...), custom_call_target="tpu_custom_call" | custom-call | tf_op jit(solution)/shard_map/pallas_call | solution.py:115
  47.4 7.2 %all-to-all-start.1 = ((bf16[32,128,128]{2,1,0:T(8,128)(2,1)}), bf16[32,128,128]{2,1,0:T(8,128)(2,1)S(1)}, u32[]{:S(2)}, u32[]{:S(2)}) async-start(bf16[32,128,128]{2,1,0:T(8,128)(2,1)} %shard_map.137), calls=%async_computation.1 | async-start | bytes 2097152 | tf_op jit(solution)/shard_map/all_to_all | solution.py:179
  54.6 0.1 fusion.3
  54.7 0.0 copy-start.3
  54.7 27.2 %all-to-all-done.1 = bf16[32,128,128]{2,1,0:T(8,128)(2,1)S(1)} async-done(((bf16[32,128,128]{2,1,0:T(8,128)(2,1)}), bf16[32,128,128]{2,1,0:T(8,128)(2,1)S(1)}, u32[]{:S(2)}, u32[]{:S(2)}) %all-to-all-start.1) | async-done | bytes 1048608 | tf_op jit(solution)/shard_map/all_to_all | solution.py:179
  82.0 0.7 copy.22
  82.7 4.5 %shard_map.138 = bf16[128,32,128]{2,1,0:T(8,128)(2,1)S(1)} custom-call(bf16[128,32,128]{2,1,0:T(8,128)(2,1)S(1)} %bitcast.11, bf16[7,256,256]{2,1,0:T(8,128)(2,1)S(1)} %copy-done.3, f32[32,128]{1,0:T(8,128)S(1)} %get-tuple-element.8.c_ref, f32[32,128]{1,0:T(8,128)S(1)} %get-tuple-element.7.s_ref), custom_call_target="tpu_custom_call" | custom-call | tf_op jit(solution)/shard_map/pallas_call | solution.py:89
  87.2 1.4 %copy.20 = bf16[32,128,128]{2,1,0:T(8,128)(2,1)} copy(bf16[32,128,128]{2,0,1:T(8,128)(2,1)S(1)} %bitcast.12) | data formatting | bytes 2097152 | tf_op jit(solution)/shard_map/transpose | solution.py:191
  (6 shorter events, 0.0 us)
Async XLA Ops:
  0.0 0.7 copy-start.4
  0.0 0.7 copy-start.5
  1.6 1.1 %copy-start = (bf16[5,256,256]{2,1,0:T(8,128)(2,1)S(1)}, bf16[5,256,256]{2,1,0:T(8,128)(2,1)}, u32[]{:S(2)}) copy-start(bf16[5,256,256]{2,1,0:T(8,128)(2,1)} %constant.43.clone.m_ref) | copy-start | bytes 1966084
  2.7 1.2 %copy-start.2 = (bf16[32,128,128]{2,1,0:T(8,128)(2,1)S(1)}, bf16[32,128,128]{2,1,0:T(8,128)(2,1)}, u32[]{:S(2)}) copy-start(bf16[32,128,128]{2,1,0:T(8,128)(2,1)} %x_ref.1) | copy-start | bytes 3145732
  8.1 35.2 %all-to-all-start = ((bf16[32,128,128]{2,1,0:T(8,128)(2,1)}), bf16[32,128,128]{2,1,0:T(8,128)(2,1)S(1)}, u32[]{:S(2)}, u32[]{:S(2)}) async-start(bf16[32,128,128]{2,1,0:T(8,128)(2,1)} %shard_map.136), calls=%async_computation | async-start | bytes 2097152 | tf_op jit(solution)/shard_map/all_to_all | solution.py:158
  15.4 0.7 copy-start.8
  17.3 0.7 copy-start.7
  28.7 0.7 copy-start.6
  41.3 1.9 %copy-start.1 = (bf16[5,256,256]{2,1,0:T(8,128)(2,1)S(1)}, bf16[5,256,256]{2,1,0:T(8,128)(2,1)}, u32[]{:S(2)}) copy-start(bf16[5,256,256]{2,1,0:T(8,128)(2,1)} %constant.43.clone.m_ref) | copy-start | bytes 1966084
  47.4 34.6 %all-to-all-start.1 = ((bf16[32,128,128]{2,1,0:T(8,128)(2,1)}), bf16[32,128,128]{2,1,0:T(8,128)(2,1)S(1)}, u32[]{:S(2)}, u32[]{:S(2)}) async-start(bf16[32,128,128]{2,1,0:T(8,128)(2,1)} %shard_map.137), calls=%async_computation.1 | async-start | bytes 2097152 | tf_op jit(solution)/shard_map/all_to_all | solution.py:179
  54.7 27.9 %copy-start.3 = (bf16[7,256,256]{2,1,0:T(8,128)(2,1)S(1)}, bf16[7,256,256]{2,1,0:T(8,128)(2,1)}, u32[]{:S(2)}) copy-start(bf16[7,256,256]{2,1,0:T(8,128)(2,1)} %constant.44.clone.m_ref) | copy-start | bytes 2752516
where the time goes:
time: 89 us; the launch traced here: 88.6 us
  waiting for transfers between devices  27.3 us (31%)
  blocking collectives  22.1 us (25%)
  starting transfers between devices  14.5 us (16%)
  Pallas kernels  12.8 us (14%)
  local copies, waits for them, and re-layouts  8.09 us (9%)
  other arithmetic  3.15 us (4%)
    all_to_all x2, waiting for transfers between devices, local(): state = lax.all_to_all(state, ('src', 'tgt'), 0, 0, tiled=True)  27.3 us
    all_to_all x2, starting transfers between devices, local(): state = lax.all_to_all(state, ('src', 'tgt'), 0, 0, tiled=True)  14.5 us
    all_gather x1, blocking collectives, local(): all_slowness = lax.all_gather(slowness, 'tgt')  11.8 us
    unnamed x1, blocking collectives  10.3 us
    pallas_call x2, Pallas kernels, local_levels(): pl.pallas_call(functools.partial(local_kernel, aparts, max(1, 512 // rows...  8.66 us
    unnamed x21, local copies, waits for them, and re-layouts  5.77 us
    pallas_call x1, Pallas kernels, swapped_levels(): pl.pallas_call(functools.partial(swapped_kernel, levels, max(1, 512 // ro...  4.09 us
    mul x4, other arithmetic, tables(): return (jnp.cos(angles), jnp.sin(angles) * signs)  3.15 us
  transfers between devices with their start and end apart: 2, of which 1 were waited for; matrix products, arithmetic and copies ran while one was open for 4% of the time, Pallas kernels for 0%

commit v1 on v0

v1 whole, which is shorter than its diff:
```python
import functools
import math

import jax
import jax.numpy as jnp
import ml_dtypes
import numpy as np
from jax import lax
from jax.experimental import pallas as pl
from jax.experimental.pallas import tpu as pltpu
from jax.sharding import PartitionSpec as P

HALF = 64
WIDE = 128


def nodes():
    points = np.cos((2.0 * np.arange(8) + 1.0) * (math.pi / 16.0))
    return np.repeat(points, 8), np.tile(points, 8)


def node_weights():
    first, second = nodes()
    return (first * first + second * second).astype(np.float32)


def level_matrix(number):
    first, second = nodes()
    frequency = 9.0 + 3.0 * (number % 5)
    shifts = np.array([-0.5, 0.5])
    out_first = first[None, :] + shifts[:, None]
    in_second = second[None, :] + shifts[:, None]
    inner = (
        out_first[:, None, :, None] * first[None, None, None, :]
        + second[None, None, :, None] * in_second[None, :, None, :]
    )
    out_norm = np.sqrt(out_first**2 + second[None, :] ** 2)
    in_norm = np.sqrt(first[None, :] ** 2 + in_second**2)
    phases = frequency * (inner + 0.5 * out_norm[:, None, :, None] * in_norm[None, :, None, :])
    factor = 1.0 / math.sqrt(128.0)
    real = np.transpose(factor * np.cos(phases), (1, 3, 0, 2))
    imag = np.transpose(factor * np.sin(phases), (1, 3, 0, 2))
    upper = np.concatenate([real, imag], axis=3)
    lower = np.concatenate([-imag, real], axis=3)
    full = np.concatenate([upper, lower], axis=1)
    return full.reshape(2 * WIDE, 2 * WIDE).astype(ml_dtypes.bfloat16)


def tables(scales):
    weights = np.tile(node_weights(), 2)
    angles = scales[..., None] * weights
    signs = np.repeat(np.array([-1.0, 1.0], np.float32), HALF)
    return jnp.cos(angles), jnp.sin(angles) * signs


def rotated(value, cosine, sine):
    return value * cosine + pltpu.roll(value, HALF, 1) * sine


def butterfly(load, store, count, apart, matrix, phase_of, group):
    lows = [i for i in range(count) if not i & apart]
    for start in range(0, len(lows), group):
        picked = lows[start : start + group]
        left = jnp.concatenate([load(i) for i in picked], axis=0)
        right = jnp.concatenate([load(i + apart) for i in picked], axis=0)
        rows = left.shape[0] // len(picked)
        both = jnp.dot(
            jnp.concatenate([left, right], axis=1), matrix, preferred_element_type=jnp.float32
        )
        for place, low in enumerate(picked):
            for child in range(2):
                index = low + child * apart
                value = both[
                    place * rows : (place + 1) * rows, child * WIDE : (child + 1) * WIDE
                ]
                store(index, rotated(value, *phase_of(index)))


def source_kernel(parts, x_ref, m_ref, c_ref, s_ref, *rest):
    out_refs, state_ref, wide_ref = rest[:parts], rest[parts], rest[parts + 1]
    rows, cols, _ = x_ref.shape
    levels = m_ref.shape[0]
    cosine, sine = c_ref[...], s_ref[...]
    for level in range(levels):
        source = x_ref if level == 0 else state_ref

        def store(index, value):
            if level < levels - 1:
                state_ref[index] = value.astype(jnp.bfloat16)
            else:
                wide_ref[pl.ds(index * cols, cols), :] = value

        butterfly(
            lambda index: source[index],
            store,
            rows,
            1 << level,
            m_ref[level],
            lambda index: (cosine, sine),
            max(1, 512 // cols),
        )
    each = rows // parts
    for part in range(parts):
        for col in range(cols):
            picked = wide_ref[pl.ds(part * each * cols + col, each, stride=cols), :]
            out_refs[part][col] = picked.astype(jnp.bfloat16)


def source_levels(x, matrices, cosine, sine, parts):
    rows, cols, _ = x.shape
    block = min(cols, 32)
    each = rows // parts
    table = pl.BlockSpec((block, WIDE), lambda i: (i, 0))
    return pl.pallas_call(
        functools.partial(source_kernel, parts),
        out_shape=[jax.ShapeDtypeStruct((cols, each, WIDE), x.dtype)] * parts,
        grid=(cols // block,),
        in_specs=[
            pl.BlockSpec((rows, block, WIDE), lambda i: (0, i, 0)),
            pl.BlockSpec(matrices.shape, lambda i: (0, 0, 0)),
            table,
            table,
        ],
        out_specs=[pl.BlockSpec((block, each, WIDE), lambda i: (i, 0, 0))] * parts,
        scratch_shapes=[
            pltpu.VMEM((rows, block, WIDE), x.dtype),
            pltpu.VMEM((rows * block, WIDE), jnp.float32),
        ],
        compiler_params=pltpu.CompilerParams(vmem_limit_bytes=32 << 20),
    )(x, matrices, cosine, sine)


def swapped_kernel(levels, tgt_count, x_ref, m_ref, cs_ref, ss_ref, ct_ref, st_ref, o_ref):
    count, rows, _ = x_ref.shape
    cols, each = cs_ref.shape[1], ct_ref.shape[1]

    def spread(ref, at):
        return jnp.concatenate(
            [jnp.broadcast_to(ref[at, col : col + 1, :], (each, WIDE)) for col in range(cols)],
            axis=0,
        )

    def tiled(ref, at):
        return jnp.concatenate([ref[at]] * cols, axis=0)

    for step, (apart, by_source) in enumerate(levels):
        source = x_ref if step == 0 else o_ref

        def phase_of(index):
            if by_source:
                at = index % tgt_count
                return spread(cs_ref, at), spread(ss_ref, at)
            at = index // tgt_count
            return tiled(ct_ref, at), tiled(st_ref, at)

        def store(index, value):
            o_ref[index] = value.astype(jnp.bfloat16)

        butterfly(
            lambda index: source[index],
            store,
            count,
            apart,
            m_ref[step],
            phase_of,
            max(1, 512 // rows),
        )


def swapped_levels(x, matrices, src_tables, tgt_tables, levels, tgt_count):
    return pl.pallas_call(
        functools.partial(swapped_kernel, levels, tgt_count),
        out_shape=jax.ShapeDtypeStruct(x.shape, x.dtype),
        in_specs=[pl.BlockSpec(memory_space=pltpu.VMEM)] * 6,
        out_specs=pl.BlockSpec(memory_space=pltpu.VMEM),
        compiler_params=pltpu.CompilerParams(vmem_limit_bytes=32 << 20),
    )(x, matrices, *src_tables, *tgt_tables)


def target_kernel(x_ref, m_ref, c_ref, s_ref, *rest):
    o_ref, state_ref, wide_ref = rest[-3:]
    cols, each, _ = x_ref.shape
    levels = m_ref.shape[0]
    cosine, sine = c_ref[...], s_ref[...]
    for level in range(levels):
        source = x_ref if level == 0 else state_ref

        def store(index, value):
            if level < levels - 1:
                state_ref[index] = value.astype(jnp.bfloat16)
            else:
                wide_ref[pl.ds(index * each, each), :] = value

        butterfly(
            lambda index: source[index],
            store,
            cols,
            1 << (levels - 1 - level),
            m_ref[level],
            lambda index: (cosine, sine),
            max(1, 512 // each),
        )
    for row in range(each):
        for col in range(0, cols, 16):
            picked = wide_ref[pl.ds(col * each + row, 16, stride=each), :]
            o_ref[row, pl.ds(col, 16), :] = picked.astype(jnp.bfloat16)


def target_levels(x, matrices, cosine, sine, part, parts, earlier):
    cols, each, _ = x.shape
    whole = pl.BlockSpec(memory_space=pltpu.VMEM)
    operands = [x, matrices, cosine, sine]
    in_specs = [
        pl.BlockSpec(x.shape, lambda i: (0, 0, 0)),
        pl.BlockSpec(matrices.shape, lambda i: (0, 0, 0)),
        pl.BlockSpec(cosine.shape, lambda i: (0, 0)),
        pl.BlockSpec(sine.shape, lambda i: (0, 0)),
    ]
    if earlier is not None:
        operands.append(earlier)
        in_specs.append(pl.BlockSpec(memory_space=pl.ANY))
    return pl.pallas_call(
        target_kernel,
        out_shape=jax.ShapeDtypeStruct((each * parts, cols, WIDE), x.dtype),
        grid=(1,),
        in_specs=in_specs,
        out_specs=pl.BlockSpec((each, cols, WIDE), lambda i: (part, 0, 0)),
        scratch_shapes=[
            pltpu.VMEM((cols, each, WIDE), x.dtype),
            pltpu.VMEM((cols * each, WIDE), jnp.float32),
        ],
        input_output_aliases={} if earlier is None else {4: 0},
        compiler_params=pltpu.CompilerParams(vmem_limit_bytes=32 << 20),
    )(*operands)


def local(box_weights, slowness, dip_field):
    rows, cols, _ = box_weights.shape
    src_count = lax.axis_size("src")
    tgt_count = lax.axis_size("tgt")
    devices = src_count * tgt_count
    row_bits, col_bits = rows.bit_length() - 1, cols.bit_length() - 1
    src_bits, tgt_bits = src_count.bit_length() - 1, tgt_count.bit_length() - 1
    first_target = row_bits + src_bits
    total = first_target + tgt_bits + col_bits
    matrices = [level_matrix(number) for number in range(total)]

    def matrices_of(low, high):
        return jnp.asarray(np.stack(matrices[low:high]))

    parts = max(1, rows // 16)
    each = rows // parts
    run = cols // devices
    place = lax.axis_index("src") * tgt_count + lax.axis_index("tgt")

    both = lax.all_gather(jnp.concatenate([slowness, dip_field]), ("src", "tgt"))
    both = both.reshape(src_count, tgt_count, cols + rows)
    all_slowness = lax.dynamic_slice_in_dim(both[0, :, :cols], place * run, run, 1)
    all_dip = both[:, 0, cols:]

    states = source_levels(
        box_weights, matrices_of(0, row_bits), *tables(slowness), parts
    )

    states = [
        lax.all_to_all(
            state.reshape(devices, run * each, WIDE), ("src", "tgt"), 0, 0, tiled=True
        )
        for state in states
    ]
    levels = [(tgt_count << bit, True) for bit in range(src_bits)]
    levels += [(1 << bit, False) for bit in reversed(range(tgt_bits))]
    src_tables = tables(all_slowness)
    tgt_tables = tables(all_dip)
    middle = matrices_of(row_bits, first_target + tgt_bits)
    backs = []
    for part, state in enumerate(states):
        picked = [table[:, part * each : (part + 1) * each] for table in tgt_tables]
        state = swapped_levels(state, middle, src_tables, picked, levels, tgt_count)
        backs.append(lax.all_to_all(state, ("src", "tgt"), 0, 0, tiled=True))

    last = matrices_of(first_target + tgt_bits, total)
    cosine, sine = tables(dip_field)
    result = None
    for part, state in enumerate(backs):
        own = slice(part * each, (part + 1) * each)
        result = target_levels(
            state.reshape(cols, each, WIDE), last, cosine[own], sine[own], part, parts, result
        )
    return result


def solution(mesh):
    in_specs = (P("src", "tgt", None), P("tgt"), P("src"))
    out_specs = P("src", "tgt", None)
    return jax.shard_map(local, mesh=mesh, in_specs=in_specs, out_specs=out_specs, check_vma=False)
```

time: 89 us -> 128 us (1.44)
  blocking collectives: 22.1 us -> 64.4 us
  Pallas kernels: 12.8 us -> 20.8 us
  starting transfers between devices: 14.5 us -> 10.2 us
  local copies, waits for them, and re-layouts: 8.09 us -> 3.8 us
  other arithmetic: 3.15 us -> 1.7 us
  waiting for transfers between devices: 27.3 us -> 26 us
    unnamed x1, blocking collectives: 10.3 us -> 41 us
    all_to_all x0 -> x1, blocking collectives: none -> 23.4 us  [local(): lax.all_to_all(state.reshape(devices, run * each, WIDE), ('src', 'tgt'),...]
    all_gather x1 -> x0, blocking collectives: 11.8 us -> none  [local(): all_slowness = lax.all_gather(slowness, 'tgt')]
    pallas_call x3 -> x5, Pallas kernels: 12.8 us -> 20.8 us  [the longest x1 8.18 us: source_levels(): pl.pallas_call(functools.partial(source_kernel, parts), out_shape=[jax.Sh...]
    all_to_all x2 -> x3, starting transfers between devices: 14.5 us -> 10.2 us  [the longest x2 7.51 us: local(): backs.append(lax.all_to_all(state, ('src', 'tgt'), 0, 0, tiled=True))]
    unnamed x21 -> x17, local copies, waits for them, and re-layouts: 5.77 us -> 3.63 us
    mul x4, other arithmetic: 3.15 us -> 1.61 us  [tables(): return (jnp.cos(angles), jnp.sin(angles) * signs)]
    transpose x1 -> x0, local copies, waits for them, and re-layouts: 1.38 us -> none  [local(): return jnp.swapaxes(state, 0, 1)]
  transfers between devices with their start and end apart: 2 -> 3, of which waited for: 1 -> 2; matrix products, arithmetic and copies ran while one was open for 4% -> 1% of each run, Pallas kernels for 0% -> 7%
where the time goes in v1:
time: 128 us; the launch traced here: 127 us
  blocking collectives  64.4 us (50%)
  waiting for transfers between devices  26 us (20%)
  Pallas kernels  20.8 us (16%)
  starting transfers between devices  10.2 us (8%)
  local copies, waits for them, and re-layouts  3.8 us (3%)
  other arithmetic  1.7 us (1%)
    unnamed x1, blocking collectives  41 us
    all_to_all x2, waiting for transfers between devices, local(): backs.append(lax.all_to_all(state, ('src', 'tgt'), 0, 0, tiled=True))  26 us
    all_to_all x1, blocking collectives, local(): lax.all_to_all(state.reshape(devices, run * each, WIDE), ('src', 'tgt'),...  23.4 us
    pallas_call x1, Pallas kernels, source_levels(): pl.pallas_call(functools.partial(source_kernel, parts), out_shape=[jax.Sh...  8.18 us
    all_to_all x2, starting transfers between devices, local(): backs.append(lax.all_to_all(state, ('src', 'tgt'), 0, 0, tiled=True))  7.51 us
    pallas_call x2, Pallas kernels, target_levels(): pl.pallas_call(target_kernel, out_shape=jax.ShapeDtypeStruct((each * part...  7.21 us
    pallas_call x2, Pallas kernels, swapped_levels(): pl.pallas_call(functools.partial(swapped_kernel, levels, tgt_count), out_...  5.41 us
    unnamed x17, local copies, waits for them, and re-layouts  3.63 us
  transfers between devices with their start and end apart: 3, of which 2 were waited for; matrix products, arithmetic and copies ran while one was open for 1% of the time, Pallas kernels for 7%

profile of v1, /device:TPU:0, one launch (start us, length us, event | category | flops | bytes accessed | tf_op | source)
XLA Modules:
  0.0 127.2 jit_solution(11424755704056206889)
XLA Ops:
  0.0 0.0 copy-start.4
  0.0 0.7 copy-done.4
  0.7 0.0 copy-done.5
  0.7 1.0 fusion
  1.6 0.0 copy-start
  1.7 1.1 copy-done
  2.7 1.2 copy-done.3
  4.0 8.2 %shard_map.136 = (bf16[128,16,128]{2,1,0:T(8,128)(2,1)S(1)}, bf16[128,16,128]{2,1,0:T(8,128)(2,1)}) custom-call(bf16[32,128,128]{2,1,0:T(8,128)(2,1)S(1)} %copy-done.3, bf16[5,256,256]{2,1,0:T(8,128)(2,1)S(1)} %copy-done, f32[128,128]{1,0:T(8,128)S(1)} %get-tuple-element.24.c_ref, f32[128,128]{1,0:T(8,128)S(1)} %get-tuple-element.23.s_ref), custom_call_target="tpu_custom_call" | custom-call | tf_op jit(solution)/shard_map/pallas_call | solution.py:114
  12.1 23.4 %all_to_all.20.x_ref = bf16[32,64,128]{2,1,0:T(8,128)(2,1)S(1)} all-to-all(bf16[32,64,128]{2,1,0:T(8,128)(2,1)S(1)} %bitcast.9), channel_id=1, replica_groups=mesh['src'=4,'tgt'=8] {'src','tgt'}, dimensions={0} | all-to-all | bytes 1048576 | tf_op jit(solution)/shard_map/all_to_all | solution.py:266
  35.6 2.7 %all-to-all-start = ((bf16[32,64,128]{2,1,0:T(8,128)(2,1)}), bf16[32,64,128]{2,1,0:T(8,128)(2,1)S(1)}, u32[]{:S(2)}, u32[]{:S(2)}) async-start(bf16[32,64,128]{2,1,0:T(8,128)(2,1)} %bitcast), calls=%async_computation | async-start | bytes 1048576 | tf_op jit(solution)/shard_map/all_to_all | solution.py:266
  38.3 0.0 copy-start.6
  38.4 0.0 copy-start.7
  38.4 0.6 copy-done.6
  39.0 0.0 copy-done.7
  39.0 0.1 maximum_dynamic-update-slice_fusion
  39.1 41.0 %all-reduce = f32[5120]{0:T(1024)S(1)} all-reduce(f32[5120]{0:T(1024)S(1)} %maximum_dynamic-update-slice_fusion), channel_id=2, replica_groups=mesh['src'=4,'tgt'=8] {'src','tgt'}, use_global_device_ids=true, to_apply=%add | all-reduce | flops 5120 | bytes 40960
  80.1 0.1 reshape.30
  80.2 0.1 dynamic-slice_bitcast_fusion
  80.2 0.2 fusion.2
  80.4 0.3 fusion.1
  80.8 0.0 copy-done.1
  80.8 2.7 %shard_map.138 = bf16[32,64,128]{2,1,0:T(8,128)(2,1)} custom-call(bf16[32,64,128]{2,1,0:T(8,128)(2,1)S(1)} %all_to_all.20.x_ref, bf16[5,256,256]{2,1,0:T(8,128)(2,1)S(1)} %copy-done.1, f32[8,4,128]{2,1,0:T(4,128)S(1)} %get-tuple-element.18.cs_ref, f32[8,4,128]{2,1,0:T(4,128)S(1)} %get-tuple-element.17.ss_ref, f32[4,16,128]{2,1,0:T(8,128)S(1)} %get-tuple-element.26.ct_ref, ...), custom_call_target="tpu_custom_call" | custom-call | tf_op jit(solution)/shard_map/pallas_call | solution.py:171
  83.5 0.0 all-to-all-done.x_ref
  83.5 4.7 %all-to-all-start.3 = ((bf16[32,64,128]{2,1,0:T(8,128)(2,1)}), bf16[32,64,128]{2,1,0:T(8,128)(2,1)S(1)}, u32[]{:S(2)}, u32[]{:S(2)}) async-start(bf16[32,64,128]{2,1,0:T(8,128)(2,1)} %shard_map.138), calls=%async_computation.3 | async-start | bytes 1048576 | tf_op jit(solution)/shard_map/all_to_all | solution.py:280
  88.2 2.7 %shard_map.137 = bf16[32,64,128]{2,1,0:T(8,128)(2,1)} custom-call(bf16[32,64,128]{2,1,0:T(8,128)(2,1)S(1)} %all-to-all-done.x_ref, bf16[5,256,256]{2,1,0:T(8,128)(2,1)S(1)} %copy-done.1, f32[8,4,128]{2,1,0:T(4,128)S(1)} %get-tuple-element.18.cs_ref, f32[8,4,128]{2,1,0:T(4,128)S(1)} %get-tuple-element.17.ss_ref, f32[4,16,128]{2,1,0:T(8,128)S(1)} %get-tuple-element.25.ct_ref, ...), custom_call_target="tpu_custom_call" | custom-call | tf_op jit(solution)/shard_map/pallas_call | solution.py:171
  90.9 13.6 %all-to-all-done.3 = bf16[32,64,128]{2,1,0:T(8,128)(2,1)S(1)} async-done(((bf16[32,64,128]{2,1,0:T(8,128)(2,1)}), bf16[32,64,128]{2,1,0:T(8,128)(2,1)S(1)}, u32[]{:S(2)}, u32[]{:S(2)}) %all-to-all-start.3) | async-done | bytes 524320 | tf_op jit(solution)/shard_map/all_to_all | solution.py:280
  104.6 2.8 %all-to-all-start.1 = ((bf16[32,64,128]{2,1,0:T(8,128)(2,1)}), bf16[32,64,128]{2,1,0:T(8,128)(2,1)S(1)}, u32[]{:S(2)}, u32[]{:S(2)}) async-start(bf16[32,64,128]{2,1,0:T(8,128)(2,1)} %shard_map.137), calls=%async_computation.1 | async-start | bytes 1048576 | tf_op jit(solution)/shard_map/all_to_all | solution.py:280
  107.4 0.1 fusion.3
  107.5 0.0 copy-done.2
  107.5 3.6 %shard_map.139.rest_0_ = bf16[32,128,128]{2,1,0:T(8,128)(2,1)} custom-call(bf16[128,16,128]{2,1,0:T(8,128)(2,1)S(1)} %bitcast.7, bf16[7,256,256]{2,1,0:T(8,128)(2,1)S(1)} %copy-done.2, f32[16,128]{1,0:T(8,128)S(1)} %get-tuple-element.28.c_ref, f32[16,128]{1,0:T(8,128)S(1)} %get-tuple-element.13.s_ref), custom_call_target="tpu_custom_call" | custom-call | tf_op jit(solution)/shard_map/pallas_call | solution.py:222
  111.2 12.4 %all-to-all-done.1 = bf16[32,64,128]{2,1,0:T(8,128)(2,1)S(1)} async-done(((bf16[32,64,128]{2,1,0:T(8,128)(2,1)}), bf16[32,64,128]{2,1,0:T(8,128)(2,1)S(1)}, u32[]{:S(2)}, u32[]{:S(2)}) %all-to-all-start.1) | async-done | bytes 524320 | tf_op jit(solution)/shard_map/all_to_all | solution.py:280
  123.6 3.6 %shard_map.140 = bf16[32,128,128]{2,1,0:T(8,128)(2,1)} custom-call(bf16[128,16,128]{2,1,0:T(8,128)(2,1)S(1)} %bitcast.8, bf16[7,256,256]{2,1,0:T(8,128)(2,1)S(1)} %copy-done.2, f32[16,128]{1,0:T(8,128)S(1)} %get-tuple-element.27.c_ref, f32[16,128]{1,0:T(8,128)S(1)} %get-tuple-element.14.s_ref, ...), custom_call_target="tpu_custom_call", output_to_operand_aliasing={{}: (4, {})} | custom-call | tf_op jit(solution)/shard_map/pallas_call | solution.py:222
  (9 shorter events, 0.0 us)
Async XLA Ops:
  0.0 0.7 copy-start.4
  0.0 0.7 copy-start.5
  1.6 1.1 copy-start
  2.7 1.2 copy-start.3
  35.6 45.2 %copy-start.1 = (bf16[5,256,256]{2,1,0:T(8,128)(2,1)S(1)}, bf16[5,256,256]{2,1,0:T(8,128)(2,1)}, u32[]{:S(2)}) copy-start(bf16[5,256,256]{2,1,0:T(8,128)(2,1)} %constant.25.clone.m_ref) | copy-start | bytes 1966084
  35.6 47.9 %all-to-all-start = ((bf16[32,64,128]{2,1,0:T(8,128)(2,1)}), bf16[32,64,128]{2,1,0:T(8,128)(2,1)S(1)}, u32[]{:S(2)}, u32[]{:S(2)}) async-start(bf16[32,64,128]{2,1,0:T(8,128)(2,1)} %bitcast), calls=%async_computation | async-start | bytes 1048576 | tf_op jit(solution)/shard_map/all_to_all | solution.py:266
  38.3 0.7 copy-start.6
  38.4 0.7 copy-start.7
  83.5 21.1 %all-to-all-start.3 = ((bf16[32,64,128]{2,1,0:T(8,128)(2,1)}), bf16[32,64,128]{2,1,0:T(8,128)(2,1)S(1)}, u32[]{:S(2)}, u32[]{:S(2)}) async-start(bf16[32,64,128]{2,1,0:T(8,128)(2,1)} %shard_map.138), calls=%async_computation.3 | async-start | bytes 1048576 | tf_op jit(solution)/shard_map/all_to_all | solution.py:280
  90.9 16.6 %copy-start.2 = (bf16[7,256,256]{2,1,0:T(8,128)(2,1)S(1)}, bf16[7,256,256]{2,1,0:T(8,128)(2,1)}, u32[]{:S(2)}) copy-start(bf16[7,256,256]{2,1,0:T(8,128)(2,1)} %constant.28.clone.m_ref) | copy-start | bytes 2752516
  104.6 19.0 %all-to-all-start.1 = ((bf16[32,64,128]{2,1,0:T(8,128)(2,1)}), bf16[32,64,128]{2,1,0:T(8,128)(2,1)S(1)}, u32[]{:S(2)}, u32[]{:S(2)}) async-start(bf16[32,64,128]{2,1,0:T(8,128)(2,1)} %shard_map.137), calls=%async_computation.1 | async-start | bytes 1048576 | tf_op jit(solution)/shard_map/all_to_all | solution.py:280

commit v2 on v1

v2 whole, which is shorter than its diff:
```python
import functools
import math

import jax
import jax.numpy as jnp
import ml_dtypes
import numpy as np
from jax import lax
from jax.experimental import pallas as pl
from jax.experimental.pallas import tpu as pltpu
from jax.sharding import PartitionSpec as P

HALF = 64
WIDE = 128


def nodes():
    points = np.cos((2.0 * np.arange(8) + 1.0) * (math.pi / 16.0))
    return np.repeat(points, 8), np.tile(points, 8)


def node_weights():
    first, second = nodes()
    return (first * first + second * second).astype(np.float32)


def level_matrix(number):
    first, second = nodes()
    frequency = 9.0 + 3.0 * (number % 5)
    shifts = np.array([-0.5, 0.5])
    out_first = first[None, :] + shifts[:, None]
    in_second = second[None, :] + shifts[:, None]
    inner = (
        out_first[:, None, :, None] * first[None, None, None, :]
        + second[None, None, :, None] * in_second[None, :, None, :]
    )
    out_norm = np.sqrt(out_first**2 + second[None, :] ** 2)
    in_norm = np.sqrt(first[None, :] ** 2 + in_second**2)
    phases = frequency * (inner + 0.5 * out_norm[:, None, :, None] * in_norm[None, :, None, :])
    factor = 1.0 / math.sqrt(128.0)
    real = np.transpose(factor * np.cos(phases), (1, 3, 0, 2))
    imag = np.transpose(factor * np.sin(phases), (1, 3, 0, 2))
    upper = np.concatenate([real, imag], axis=3)
    lower = np.concatenate([-imag, real], axis=3)
    full = np.concatenate([upper, lower], axis=1)
    return full.reshape(2 * WIDE, 2 * WIDE).astype(ml_dtypes.bfloat16)


def tables(scales):
    weights = np.tile(node_weights(), 2)
    angles = scales[..., None] * weights
    signs = np.repeat(np.array([-1.0, 1.0], np.float32), HALF)
    return jnp.cos(angles), jnp.sin(angles) * signs


def flipped(matrix):
    return np.roll(matrix, (WIDE, WIDE), (0, 1))


def shuffles(run, each):
    groups = 16 // run
    found = np.zeros((groups, 16 * each, 16 * each), np.float32)
    for own in range(groups):
        for chip in range(groups):
            for col in range(run):
                for row in range(each):
                    at = (chip * run + col) * each + row
                    found[own, at, row * 16 + (chip ^ own) * run + col] = 1.0
    return found.astype(ml_dtypes.bfloat16)


def rotated(value, cosine, sine):
    return value * cosine + pltpu.roll(value, HALF, 1) * sine


def butterfly(load, store, count, apart, matrix, phase_of, group):
    lows = [i for i in range(count) if not i & apart]
    for start in range(0, len(lows), group):
        picked = lows[start : start + group]
        left = jnp.concatenate([load(i) for i in picked], axis=0)
        right = jnp.concatenate([load(i + apart) for i in picked], axis=0)
        rows = left.shape[0] // len(picked)
        both = jnp.dot(
            jnp.concatenate([left, right], axis=1), matrix, preferred_element_type=jnp.float32
        )
        for place, low in enumerate(picked):
            for child in range(2):
                index = low + child * apart
                value = both[
                    place * rows : (place + 1) * rows, child * WIDE : (child + 1) * WIDE
                ]
                store(index, rotated(value, *phase_of(index)).astype(jnp.bfloat16))


def source_kernel(parts, own_ref, x_ref, m_ref, c_ref, s_ref, p_ref, *rest):
    out_refs, state_ref = rest[:-1], rest[-1]
    rows, cols, _ = x_ref.shape
    chips = len(out_refs) // parts
    run, each = cols // chips, rows // parts
    for level in range(m_ref.shape[0]):
        source = x_ref if level == 0 else state_ref

        def store(index, value):
            state_ref[index] = value

        butterfly(
            lambda index: source[index],
            store,
            rows,
            1 << level,
            m_ref[level],
            lambda index: (c_ref[...], s_ref[...]),
            max(1, 512 // cols),
        )
    groups = 16 // run
    own = own_ref[0]
    shuffle = p_ref[lax.rem(own, groups)]
    own_high = lax.div(own, groups)
    for part in range(parts):
        for high in range(0, cols // 16, 2):
            sides = []
            for at in (high, high + 1):
                begin = pl.multiple_of(lax.bitwise_xor(own_high, at) * 16, 16)
                side = state_ref[part * each : (part + 1) * each, pl.ds(begin, 16), :]
                sides.append(side.reshape(each * 16, WIDE))
            moved = jnp.dot(
                shuffle, jnp.concatenate(sides, axis=1), preferred_element_type=jnp.float32
            ).astype(jnp.bfloat16)
            for side in range(2):
                for chip in range(groups):
                    block = moved[
                        chip * run * each : (chip + 1) * run * each,
                        side * WIDE : (side + 1) * WIDE,
                    ]
                    mask = (high + side) * groups + chip
                    out_refs[part * chips + mask][...] = block


def call(kernel, out_shape, operands, scratch, own=None, out_specs=None, aliases=None, whole=()):
    in_specs = []
    if own is not None:
        operands = (own, *operands)
        in_specs.append(pl.BlockSpec(memory_space=pltpu.SMEM))
    while len(in_specs) < len(operands):
        in_specs.append(pl.BlockSpec(memory_space=pltpu.VMEM))
    for at in whole:
        in_specs[at] = pl.BlockSpec(memory_space=pl.ANY)
    if out_specs is None:
        out_specs = jax.tree.map(lambda _: pl.BlockSpec(memory_space=pltpu.VMEM), out_shape)
    return pl.pallas_call(
        kernel,
        out_shape=out_shape,
        in_specs=in_specs,
        out_specs=out_specs,
        scratch_shapes=scratch,
        input_output_aliases=aliases or {},
        compiler_params=pltpu.CompilerParams(vmem_limit_bytes=32 << 20),
    )(*operands)


def middle_kernel(levels, part, each, own_ref, m_ref, cs_ref, ss_ref, ct_ref, st_ref, *rest):
    x_refs, o_ref = rest[:-1], rest[-1]
    count, rows, _ = o_ref.shape
    run = rows // each
    own = own_ref[0]
    rows_of = pl.ds(part * each, each)

    def spread(ref, at):
        return jnp.concatenate(
            [jnp.broadcast_to(ref[at, col : col + 1, :], (each, WIDE)) for col in range(run)],
            axis=0,
        )

    def tiled(ref, at):
        return jnp.concatenate([ref[at, rows_of, :]] * run, axis=0)

    tgt_chips = cs_ref.shape[0]
    for step, (bit, by_source) in enumerate(levels):

        def phase_of(index):
            if by_source:
                at = index % tgt_chips
                return spread(cs_ref, at), spread(ss_ref, at)
            at = index // tgt_chips
            return tiled(ct_ref, at), tiled(st_ref, at)

        def load(index):
            return x_refs[index][...] if step == 0 else o_ref[index]

        def store(index, value):
            o_ref[index] = value

        side = lax.rem(lax.div(own, 1 << bit), 2)
        butterfly(
            load, store, count, 1 << bit, m_ref[2 * step + side], phase_of, max(1, 512 // rows)
        )


def core_kernel(part, each, own_ref, m_ref, ct_ref, st_ref, x_ref, y_ref, *out_refs):
    count, rows, _ = x_ref.shape
    run = rows // each
    matrix = m_ref[own_ref[1]]
    tgt_chips = count // ct_ref.shape[0]
    group = max(1, 512 // rows)
    for start in range(0, count, group):
        picked = range(start, start + group)
        left = jnp.concatenate([x_ref[i] for i in picked], axis=0)
        right = jnp.concatenate([y_ref[i] for i in picked], axis=0)
        both = jnp.dot(
            jnp.concatenate([left, right], axis=1), matrix, preferred_element_type=jnp.float32
        )
        for place, index in enumerate(picked):
            at = index // tgt_chips
            cosine = jnp.concatenate([ct_ref[at, pl.ds(part * each, each), :]] * run, axis=0)
            sine = jnp.concatenate([st_ref[at, pl.ds(part * each, each), :]] * run, axis=0)
            value = both[place * rows : (place + 1) * rows]
            out_refs[index][...] = rotated(value, cosine, sine).astype(jnp.bfloat16)


def target_kernel(chips, part, own_ref, m_ref, c_ref, s_ref, p_ref, *rest):
    x_refs = rest[:chips]
    o_ref, state_ref = rest[-2:]
    cols, each, _ = state_ref.shape
    run = cols // chips
    chip_bits, run_bits = chips.bit_length() - 1, run.bit_length() - 1
    own = own_ref[0]
    rows_of = pl.ds(part * each, each)
    cosine, sine = c_ref[rows_of, :], s_ref[rows_of, :]

    def load_first(index):
        return x_refs[index // run][pl.ds(index % run * each, each), :]

    def store(index, value):
        state_ref[index] = value

    for step in range(chip_bits + run_bits):
        bit = chip_bits + run_bits - 1 - step
        if step < chip_bits:
            side = lax.rem(lax.div(own, 1 << (bit - run_bits)), 2)
            matrix = m_ref[2 * step + side]
        else:
            matrix = m_ref[chip_bits + step]
        butterfly(
            load_first if step == 0 else lambda index: state_ref[index],
            store,
            cols,
            1 << bit,
            matrix,
            lambda index: (cosine, sine),
            max(1, 512 // each),
        )
    groups = 16 // run
    shuffle = p_ref[lax.rem(own, groups)]
    own_high = lax.div(own, groups)
    for high in range(0, cols // 16, 2):
        sides = [state_ref[at * 16 : at * 16 + 16].reshape(16 * each, WIDE) for at in (high, high + 1)]
        moved = jnp.dot(
            shuffle, jnp.concatenate(sides, axis=1), preferred_element_type=jnp.float32
        ).astype(jnp.bfloat16)
        for side in range(2):
            begin = pl.multiple_of(lax.bitwise_xor(own_high, high + side) * 16, 16)
            block = moved[:, side * WIDE : (side + 1) * WIDE].reshape(each, 16, WIDE)
            o_ref[:, pl.ds(begin, 16), :] = block


def target_levels(own, matrices, cosine, sine, shuffle, blocks, part, parts, earlier):
    chips = len(blocks)
    run = blocks[0].shape[0] * parts // cosine.shape[0]
    each, cols = cosine.shape[0] // parts, run * chips
    operands = [matrices, cosine, sine, shuffle, *blocks]
    whole, aliases = (), None
    if earlier is not None:
        operands.append(earlier)
        whole, aliases = (len(operands),), {len(operands): 0}
    in_specs = [pl.BlockSpec(memory_space=pltpu.SMEM)]
    for operand in operands:
        zeros = (0,) * operand.ndim
        in_specs.append(pl.BlockSpec(operand.shape, lambda i, zeros=zeros: zeros))
    for at in whole:
        in_specs[at] = pl.BlockSpec(memory_space=pl.ANY)
    return pl.pallas_call(
        functools.partial(target_kernel, chips, part),
        out_shape=jax.ShapeDtypeStruct((each * parts, cols, WIDE), jnp.bfloat16),
        grid=(1,),
        in_specs=in_specs,
        out_specs=pl.BlockSpec((each, cols, WIDE), lambda i: (part, 0, 0)),
        scratch_shapes=[pltpu.VMEM((cols, each, WIDE), jnp.bfloat16)],
        input_output_aliases=aliases or {},
        compiler_params=pltpu.CompilerParams(vmem_limit_bytes=32 << 20),
    )(own, *operands)


def local(box_weights, slowness, dip_field):
    rows, cols, _ = box_weights.shape
    src_count = lax.axis_size("src")
    tgt_count = lax.axis_size("tgt")
    tgt_chips = tgt_count // 2
    chips = src_count * tgt_chips
    row_bits, col_bits = rows.bit_length() - 1, cols.bit_length() - 1
    src_bits, chip_bits = src_count.bit_length() - 1, tgt_chips.bit_length() - 1
    first_target = row_bits + src_bits
    core_level = first_target + chip_bits
    total = core_level + 1 + col_bits
    matrices = [level_matrix(number) for number in range(total)]
    parts = max(1, rows // 16)
    each = rows // parts
    run = cols // chips
    src_at, tgt_at = lax.axis_index("src"), lax.axis_index("tgt")
    chip = src_at * tgt_chips + tgt_at // 2
    own = jnp.stack([chip, tgt_at % 2]).astype(jnp.int32)

    def traded(block, mask):
        devices = src_count * tgt_count
        return lax.ppermute(block, ("src", "tgt"), [(i, i ^ mask) for i in range(devices)])

    def chip_mask(mask):
        return mask // tgt_chips * tgt_count + mask % tgt_chips * 2

    all_slowness = jnp.stack([slowness] + [traded(slowness, 2 * m) for m in range(1, tgt_chips)])
    all_dip = jnp.stack(
        [dip_field] + [traded(dip_field, tgt_count * m) for m in range(1, src_count)]
    )
    run_slowness = lax.dynamic_slice_in_dim(all_slowness, chip * run, run, 1)

    shuffle = shuffles(run, each)
    block = jax.ShapeDtypeStruct((run * each, WIDE), jnp.bfloat16)
    blocks = call(
        functools.partial(source_kernel, parts),
        [block] * (parts * chips),
        (
            box_weights,
            jnp.asarray(np.stack(matrices[:row_bits])),
            *tables(slowness),
            jnp.asarray(shuffle),
        ),
        [pltpu.VMEM(box_weights.shape, jnp.bfloat16)],
        own,
    )

    levels = [(chip_bits + bit, True) for bit in range(src_bits)]
    levels += [(bit, False) for bit in reversed(range(chip_bits))]
    middle = [
        kind(matrix)
        for matrix in matrices[row_bits:core_level]
        for kind in (lambda m: m, flipped)
    ]
    middle = jnp.asarray(np.stack(middle))
    core = matrices[core_level]
    core = jnp.asarray(np.stack([core[:, :WIDE], flipped(core)[:, :WIDE]]))
    last = [
        kind(matrix)
        for matrix in matrices[core_level + 1 : core_level + 1 + src_bits + chip_bits]
        for kind in (lambda m: m, flipped)
    ]
    last = jnp.asarray(np.stack(last + matrices[core_level + 1 + src_bits + chip_bits :]))
    back_shuffle = jnp.asarray(np.swapaxes(shuffle, 1, 2))
    src_tables, tgt_tables = tables(run_slowness), tables(all_dip)
    own_tables = tables(dip_field)

    result = None
    for part in range(parts):
        mine = blocks[part * chips : (part + 1) * chips]
        here = [mine[0]] + [traded(mine[m], chip_mask(m)) for m in range(1, chips)]
        state = call(
            functools.partial(middle_kernel, levels, part, each),
            jax.ShapeDtypeStruct((chips, run * each, WIDE), jnp.bfloat16),
            (middle, *src_tables, *tgt_tables, *here),
            [],
            own,
        )
        outs = call(
            functools.partial(core_kernel, part, each),
            [block] * chips,
            (core, *tgt_tables, state, traded(state, 1)),
            [],
            own,
        )
        home = [outs[0]] + [traded(outs[m], chip_mask(m)) for m in range(1, chips)]
        result = target_levels(
            own, last, *own_tables, back_shuffle, home, part, parts, result
        )
    return result


def solution(mesh):
    in_specs = (P("src", "tgt", None), P("tgt"), P("src"))
    out_specs = P("src", "tgt", None)
    return jax.shard_map(local, mesh=mesh, in_specs=in_specs, out_specs=out_specs, check_vma=False)
```

time: 128 us -> 146 us (1.14)
  starting transfers between devices: 10.2 us -> 116 us
  blocking collectives: 64.4 us -> 0 us
  waiting for transfers between devices: 26 us -> 4.88 us
    ppermute x0 -> x68, starting transfers between devices: none -> 116 us  [traded(): lax.ppermute(block, ('src', 'tgt'), [(i, i ^ mask) for i in range(devices)])]
    unnamed x1 -> x0, blocking collectives: 41 us -> none
    all_to_all x3 -> x0, waiting for transfers between devices: 26 us -> none  [the longest x2 26 us: local(): backs.append(lax.all_to_all(state, ('src', 'tgt'), 0, 0, tiled=True))]
    all_to_all x1 -> x0, blocking collectives: 23.4 us -> none  [local(): lax.all_to_all(state.reshape(devices, run * each, WIDE), ('src', 'tgt'),...]
    all_to_all x3 -> x0, starting transfers between devices: 10.2 us -> none  [the longest x2 7.51 us: local(): backs.append(lax.all_to_all(state, ('src', 'tgt'), 0, 0, tiled=True))]
    ppermute x0 -> x68, waiting for transfers between devices: none -> 4.88 us  [traded(): lax.ppermute(block, ('src', 'tgt'), [(i, i ^ mask) for i in range(devices)])]
    pallas_call x5 -> x7, Pallas kernels: 20.8 us -> 19.8 us  [the longest x5 10.9 us: call(): pl.pallas_call(kernel, out_shape=out_shape, in_specs=in_specs, out_specs=...]
    unnamed x17 -> x22, local copies, waits for them, and re-layouts: 3.63 us -> 3.3 us
  transfers between devices with their start and end apart: 3 -> 68, of which waited for: 2 -> 2; matrix products, arithmetic and copies ran while one was open for 1% -> 1% of each run, Pallas kernels for 7% -> 11%
where the time goes in v2:
time: 146 us
  starting transfers between devices  116 us (79%)
  Pallas kernels  19.8 us (14%)
  waiting for transfers between devices  4.88 us (3%)
  local copies, waits for them, and re-layouts  3.37 us (2%)
  other arithmetic  1.68 us (1%)
    ppermute x68, starting transfers between devices, traded(): lax.ppermute(block, ('src', 'tgt'), [(i, i ^ mask) for i in range(devices)])  116 us
    pallas_call x5, Pallas kernels, call(): pl.pallas_call(kernel, out_shape=out_shape, in_specs=in_specs, out_specs=...  10.9 us
    pallas_call x2, Pallas kernels, target_levels(): pl.pallas_call(functools.partial(target_kernel, chips, part), out_shape=j...  8.93 us
    ppermute x68, waiting for transfers between devices, traded(): lax.ppermute(block, ('src', 'tgt'), [(i, i ^ mask) for i in range(devices)])  4.88 us
    unnamed x22, local copies, waits for them, and re-layouts  3.3 us
  transfers between devices with their start and end apart: 68, of which 2 were waited for; matrix products, arithmetic and copies ran while one was open for 1% of the time, Pallas kernels for 11%

profile of v2, /device:TPU:0, one launch (start us, length us, event | category | flops | bytes accessed | tf_op | source)
XLA Modules:
  0.0 145.9 jit_solution(7567055033667417278)
XLA Ops:
  0.0 4.0 %collective-permute-start.2 = (f32[32]{0:T(128)}, f32[32]{0:T(128)S(1)}, u32[]{:S(2)}, u32[]{:S(2)}) collective-permute-start(f32[32]{0:T(128)} %param.19), channel_id=1, source_target_pairs={{0,24},{1,25},{2,26},{3,27},{4,28},{5,29},{6,30},{7,31},{8,16},{9,... | collective-permute-start | bytes 392 | tf_op jit(solution)/shard_map/ppermute | solution.py:314
  4.6 4.0 %collective-permute-start.5 = (f32[128]{0:T(128)}, f32[128]{0:T(128)S(1)}, u32[]{:S(2)}, u32[]{:S(2)}) collective-permute-start(f32[128]{0:T(128)} %param.18), channel_id=1, source_target_pairs={{0,6},{1,7},{2,4},{3,5},{4,2},{5,3},{6,0},{7,1},{8,14},{9,15},{10,... | collective-permute-start | bytes 1544 | tf_op jit(solution)/shard_map/ppermute | solution.py:314
  13.0 4.4 %shard_map.163 = (bf16[128,128]{1,0:T(8,128)(2,1)S(1)}, bf16[128,128]{1,0:T(8,128)(2,1)S(1)}, bf16[128,128]{1,0:T(8,128)(2,1)S(1)}, bf16[128,128]{1,0:T(8,128)(2...) custom-call(s32[2]{0:T(128)S(1)} %pad_add_fusion.own_ref, ...), custom_call_target="tpu_custom_call" | custom-call | tf_op jit(solution)/shard_map/pallas_call | solution.py:150
  19.5 2.9 %collective-permute-start.7 = (bf16[128,128]{1,0:T(8,128)(2,1)S(1)}, bf16[128,128]{1,0:T(8,128)(2,1)S(1)}, u32[]{:S(2)}, u32[]{:S(2)}) collective-permute-start(bf16[128,128]{1,0:T(8,128)(2,1)S(1)} %get-tuple-element.71), channel_id=1, source_target_pairs={{0,4},{1,5},{2,6},{3,7},{4,0},{5,1},{6,2},{7,3},{8,12},{9,13},{10,... | collective-permute-start | bytes 98312 | tf_op jit(solution)/shard_map/ppermute | solution.py:314
  22.4 1.7 %collective-permute-start.9 = (bf16[128,128]{1,0:T(8,128)(2,1)S(1)}, bf16[128,128]{1,0:T(8,128)(2,1)S(1)}, u32[]{:S(2)}, u32[]{:S(2)}) collective-permute-start(bf16[128,128]{1,0:T(8,128)(2,1)S(1)} %get-tuple-element.73), channel_id=1, source_target_pairs={{0,8},{1,9},{2,10},{3,11},{4,12},{5,13},{6,14},{7,15},{8,0},{9,1},... | collective-permute-start | bytes 98312 | tf_op jit(solution)/shard_map/ppermute | solution.py:314
  24.5 4.7 %collective-permute-start.11 = (bf16[128,128]{1,0:T(8,128)(2,1)S(1)}, bf16[128,128]{1,0:T(8,128)(2,1)S(1)}, u32[]{:S(2)}, u32[]{:S(2)}) collective-permute-start(bf16[128,128]{1,0:T(8,128)(2,1)S(1)} %get-tuple-element.75), channel_id=1, source_target_pairs={{0,12},{1,13},{2,14},{3,15},{4,8},{5,9},{6,10},{7,11},{8,4},{9,5},... | collective-permute-start | bytes 98312 | tf_op jit(solution)/shard_map/ppermute | solution.py:314
  29.3 1.7 %collective-permute-start.13 = (bf16[128,128]{1,0:T(8,128)(2,1)S(1)}, bf16[128,128]{1,0:T(8,128)(2,1)S(1)}, u32[]{:S(2)}, u32[]{:S(2)}) collective-permute-start(bf16[128,128]{1,0:T(8,128)(2,1)S(1)} %get-tuple-element.77), channel_id=1, source_target_pairs={{0,16},{1,17},{2,18},{3,19},{4,20},{5,21},{6,22},{7,23},{8,24},{9,... | collective-permute-start | bytes 98312 | tf_op jit(solution)/shard_map/ppermute | solution.py:314
  31.3 4.7 %collective-permute-start.15 = (bf16[128,128]{1,0:T(8,128)(2,1)S(1)}, bf16[128,128]{1,0:T(8,128)(2,1)S(1)}, u32[]{:S(2)}, u32[]{:S(2)}) collective-permute-start(bf16[128,128]{1,0:T(8,128)(2,1)S(1)} %get-tuple-element.79), channel_id=1, source_target_pairs={{0,20},{1,21},{2,22},{3,23},{4,16},{5,17},{6,18},{7,19},{8,28},{9,... | collective-permute-start | bytes 98312 | tf_op jit(solution)/shard_map/ppermute | solution.py:314
  36.2 2.6 %collective-permute-start.17 = (bf16[128,128]{1,0:T(8,128)(2,1)S(1)}, bf16[128,128]{1,0:T(8,128)(2,1)S(1)}, u32[]{:S(2)}, u32[]{:S(2)}) collective-permute-start(bf16[128,128]{1,0:T(8,128)(2,1)S(1)} %get-tuple-element.81), channel_id=1, source_target_pairs={{0,24},{1,25},{2,26},{3,27},{4,28},{5,29},{6,30},{7,31},{8,16},{9,... | collective-permute-start | bytes 98312 | tf_op jit(solution)/shard_map/ppermute | solution.py:314
  39.1 5.6 %collective-permute-start.19 = (bf16[128,128]{1,0:T(8,128)(2,1)S(1)}, bf16[128,128]{1,0:T(8,128)(2,1)S(1)}, u32[]{:S(2)}, u32[]{:S(2)}) collective-permute-start(bf16[128,128]{1,0:T(8,128)(2,1)S(1)} %get-tuple-element.83), channel_id=1, source_target_pairs={{0,28},{1,29},{2,30},{3,31},{4,24},{5,25},{6,26},{7,27},{8,20},{9,... | collective-permute-start | bytes 98312 | tf_op jit(solution)/shard_map/ppermute | solution.py:314
  45.7 3.7 %collective-permute-start.38 = (bf16[128,128]{1,0:T(8,128)(2,1)S(1)}, bf16[128,128]{1,0:T(8,128)(2,1)S(1)}, u32[]{:S(2)}, u32[]{:S(2)}) collective-permute-start(bf16[128,128]{1,0:T(8,128)(2,1)S(1)} %get-tuple-element.103), channel_id=1, source_target_pairs={{0,4},{1,5},{2,6},{3,7},{4,0},{5,1},{6,2},{7,3},{8,12},{9,13},{10,... | collective-permute-start | bytes 98312 | tf_op jit(solution)/shard_map/ppermute | solution.py:314
  52.3 4.0 %collective-permute-start.42 = (bf16[128,128]{1,0:T(8,128)(2,1)S(1)}, bf16[128,128]{1,0:T(8,128)(2,1)S(1)}, u32[]{:S(2)}, u32[]{:S(2)}) collective-permute-start(bf16[128,128]{1,0:T(8,128)(2,1)S(1)} %get-tuple-element.107), channel_id=1, source_target_pairs={{0,12},{1,13},{2,14},{3,15},{4,8},{5,9},{6,10},{7,11},{8,4},{9,5},... | collective-permute-start | bytes 98312 | tf_op jit(solution)/shard_map/ppermute | solution.py:314
  58.4 4.7 %collective-permute-start.46 = (bf16[128,128]{1,0:T(8,128)(2,1)S(1)}, bf16[128,128]{1,0:T(8,128)(2,1)S(1)}, u32[]{:S(2)}, u32[]{:S(2)}) collective-permute-start(bf16[128,128]{1,0:T(8,128)(2,1)S(1)} %get-tuple-element.111), channel_id=1, source_target_pairs={{0,20},{1,21},{2,22},{3,23},{4,16},{5,17},{6,18},{7,19},{8,28},{9,... | collective-permute-start | bytes 98312 | tf_op jit(solution)/shard_map/ppermute | solution.py:314
  66.3 5.5 %collective-permute-start.50 = (bf16[128,128]{1,0:T(8,128)(2,1)S(1)}, bf16[128,128]{1,0:T(8,128)(2,1)S(1)}, u32[]{:S(2)}, u32[]{:S(2)}) collective-permute-start(bf16[128,128]{1,0:T(8,128)(2,1)S(1)} %get-tuple-element.115), channel_id=1, source_target_pairs={{0,28},{1,29},{2,30},{3,31},{4,24},{5,25},{6,26},{7,27},{8,20},{9,... | collective-permute-start | bytes 98312 | tf_op jit(solution)/shard_map/ppermute | solution.py:314
  73.4 2.2 %shard_map.164.x_ref = bf16[16,128,128]{2,1,0:T(8,128)(2,1)S(1)} custom-call(s32[2]{0:T(128)S(1)} %pad_add_fusion.own_ref, bf16[8,256,256]{2,1,0:T(8,128)(2,1)S(1)} %copy-done.1, f32[4,8,128]{2,1,0:T(8,128)S(1)} %get-tuple-element.134.cs_ref, f32[4,8,128]{2,1,0:T(8,128)S(1)} %get-tuple-element.133.ss_ref, f32[4,32,128]{2,1,0:T(8,128)S(1)} %get-tuple-element.136.ct_ref, ...), custom_call_target="tpu_custom_call" | custom-call | tf_op jit(solution)/shard_map/pallas_call | solution.py:150
  75.7 3.6 %collective-permute-done.51.rest_15_ = bf16[128,128]{1,0:T(8,128)(2,1)S(1)} collective-permute-done((bf16[128,128]{1,0:T(8,128)(2,1)S(1)}, bf16[128,128]{1,0:T(8,128)(2,1)S(1)}, u32[]{:S(2)}, u32[]{:S(2)}) %collective-permute-start.51) | collective-permute-done | bytes 32800 | tf_op jit(solution)/shard_map/ppermute | solution.py:314
  79.3 2.1 %shard_map.166.x_ref = bf16[16,128,128]{2,1,0:T(8,128)(2,1)S(1)} custom-call(s32[2]{0:T(128)S(1)} %pad_add_fusion.own_ref, bf16[8,256,256]{2,1,0:T(8,128)(2,1)S(1)} %copy-done.1, f32[4,8,128]{2,1,0:T(8,128)S(1)} %get-tuple-element.134.cs_ref, f32[4,8,128]{2,1,0:T(8,128)S(1)} %get-tuple-element.133.ss_ref, f32[4,32,128]{2,1,0:T(8,128)S(1)} %get-tuple-element.136.ct_ref, ...), custom_call_target="tpu_custom_call" | custom-call | tf_op jit(solution)/shard_map/pallas_call | solution.py:150
  83.9 3.1 %collective-permute-start.24 = (bf16[128,128]{1,0:T(8,128)(2,1)S(1)}, bf16[128,128]{1,0:T(8,128)(2,1)S(1)}, u32[]{:S(2)}, u32[]{:S(2)}) collective-permute-start(bf16[128,128]{1,0:T(8,128)(2,1)S(1)} %get-tuple-element.88), channel_id=1, source_target_pairs={{0,6},{1,7},{2,4},{3,5},{4,2},{5,3},{6,0},{7,1},{8,14},{9,15},{10,... | collective-permute-start | bytes 98312 | tf_op jit(solution)/shard_map/ppermute | solution.py:314
  87.7 1.6 %collective-permute-start.27 = (bf16[128,128]{1,0:T(8,128)(2,1)S(1)}, bf16[128,128]{1,0:T(8,128)(2,1)S(1)}, u32[]{:S(2)}, u32[]{:S(2)}) collective-permute-start(bf16[128,128]{1,0:T(8,128)(2,1)S(1)} %get-tuple-element.91), channel_id=1, source_target_pairs={{0,12},{1,13},{2,14},{3,15},{4,8},{5,9},{6,10},{7,11},{8,4},{9,5},... | collective-permute-start | bytes 98312 | tf_op jit(solution)/shard_map/ppermute | solution.py:314
  89.4 4.5 %collective-permute-start.28 = (bf16[128,128]{1,0:T(8,128)(2,1)S(1)}, bf16[128,128]{1,0:T(8,128)(2,1)S(1)}, u32[]{:S(2)}, u32[]{:S(2)}) collective-permute-start(bf16[128,128]{1,0:T(8,128)(2,1)S(1)} %get-tuple-element.92), channel_id=1, source_target_pairs={{0,14},{1,15},{2,12},{3,13},{4,10},{5,11},{6,8},{7,9},{8,6},{9,7},... | collective-permute-start | bytes 98312 | tf_op jit(solution)/shard_map/ppermute | solution.py:314
  94.3 2.8 %collective-permute-start.31 = (bf16[128,128]{1,0:T(8,128)(2,1)S(1)}, bf16[128,128]{1,0:T(8,128)(2,1)S(1)}, u32[]{:S(2)}, u32[]{:S(2)}) collective-permute-start(bf16[128,128]{1,0:T(8,128)(2,1)S(1)} %get-tuple-element.95), channel_id=1, source_target_pairs={{0,20},{1,21},{2,22},{3,23},{4,16},{5,17},{6,18},{7,19},{8,28},{9,... | collective-permute-start | bytes 98312 | tf_op jit(solution)/shard_map/ppermute | solution.py:314
  98.5 2.9 %collective-permute-start.54 = (bf16[128,128]{1,0:T(8,128)(2,1)S(1)}, bf16[128,128]{1,0:T(8,128)(2,1)S(1)}, u32[]{:S(2)}, u32[]{:S(2)}) collective-permute-start(bf16[128,128]{1,0:T(8,128)(2,1)S(1)} %get-tuple-element.119), channel_id=1, source_target_pairs={{0,4},{1,5},{2,6},{3,7},{4,0},{5,1},{6,2},{7,3},{8,12},{9,13},{10,... | collective-permute-start | bytes 98312 | tf_op jit(solution)/shard_map/ppermute | solution.py:314
  103.5 3.7 %collective-permute-start.58 = (bf16[128,128]{1,0:T(8,128)(2,1)S(1)}, bf16[128,128]{1,0:T(8,128)(2,1)S(1)}, u32[]{:S(2)}, u32[]{:S(2)}) collective-permute-start(bf16[128,128]{1,0:T(8,128)(2,1)S(1)} %get-tuple-element.123), channel_id=1, source_target_pairs={{0,12},{1,13},{2,14},{3,15},{4,8},{5,9},{6,10},{7,11},{8,4},{9,5},... | collective-permute-start | bytes 98312 | tf_op jit(solution)/shard_map/ppermute | solution.py:314
  107.2 2.3 %collective-permute-start.59 = (bf16[128,128]{1,0:T(8,128)(2,1)S(1)}, bf16[128,128]{1,0:T(8,128)(2,1)S(1)}, u32[]{:S(2)}, u32[]{:S(2)}) collective-permute-start(bf16[128,128]{1,0:T(8,128)(2,1)S(1)} %get-tuple-element.124), channel_id=1, source_target_pairs={{0,14},{1,15},{2,12},{3,13},{4,10},{5,11},{6,8},{7,9},{8,6},{9,7},... | collective-permute-start | bytes 98312 | tf_op jit(solution)/shard_map/ppermute | solution.py:314
  110.3 4.6 %collective-permute-start.62 = (bf16[128,128]{1,0:T(8,128)(2,1)S(1)}, bf16[128,128]{1,0:T(8,128)(2,1)S(1)}, u32[]{:S(2)}, u32[]{:S(2)}) collective-permute-start(bf16[128,128]{1,0:T(8,128)(2,1)S(1)} %get-tuple-element.127), channel_id=1, source_target_pairs={{0,20},{1,21},{2,22},{3,23},{4,16},{5,17},{6,18},{7,19},{8,28},{9,... | collective-permute-start | bytes 98312 | tf_op jit(solution)/shard_map/ppermute | solution.py:314
  117.9 4.6 %collective-permute-start.66 = (bf16[128,128]{1,0:T(8,128)(2,1)S(1)}, bf16[128,128]{1,0:T(8,128)(2,1)S(1)}, u32[]{:S(2)}, u32[]{:S(2)}) collective-permute-start(bf16[128,128]{1,0:T(8,128)(2,1)S(1)} %get-tuple-element.131), channel_id=1, source_target_pairs={{0,28},{1,29},{2,30},{3,31},{4,24},{5,25},{6,26},{7,27},{8,20},{9,... | collective-permute-start | bytes 98312 | tf_op jit(solution)/shard_map/ppermute | solution.py:314
  122.6 2.2 %collective-permute-start.67 = (bf16[128,128]{1,0:T(8,128)(2,1)S(1)}, bf16[128,128]{1,0:T(8,128)(2,1)S(1)}, u32[]{:S(2)}, u32[]{:S(2)}) collective-permute-start(bf16[128,128]{1,0:T(8,128)(2,1)S(1)} %get-tuple-element.132), channel_id=1, source_target_pairs={{0,30},{1,31},{2,28},{3,29},{4,26},{5,27},{6,24},{7,25},{8,22},{9,... | collective-permute-start | bytes 98312 | tf_op jit(solution)/shard_map/ppermute | solution.py:314
  124.8 3.5 %collective-permute-start.32 = (bf16[128,128]{1,0:T(8,128)(2,1)S(1)}, bf16[128,128]{1,0:T(8,128)(2,1)S(1)}, u32[]{:S(2)}, u32[]{:S(2)}) collective-permute-start(bf16[128,128]{1,0:T(8,128)(2,1)S(1)} %get-tuple-element.96), channel_id=1, source_target_pairs={{0,22},{1,23},{2,20},{3,21},{4,18},{5,19},{6,16},{7,17},{8,30},{9,... | collective-permute-start | bytes 98312 | tf_op jit(solution)/shard_map/ppermute | solution.py:314
  128.7 3.9 %collective-permute-start.35 = (bf16[128,128]{1,0:T(8,128)(2,1)S(1)}, bf16[128,128]{1,0:T(8,128)(2,1)S(1)}, u32[]{:S(2)}, u32[]{:S(2)}) collective-permute-start(bf16[128,128]{1,0:T(8,128)(2,1)S(1)} %get-tuple-element.99), channel_id=1, source_target_pairs={{0,28},{1,29},{2,30},{3,31},{4,24},{5,25},{6,26},{7,27},{8,20},{9,... | collective-permute-start | bytes 98312 | tf_op jit(solution)/shard_map/ppermute | solution.py:314
  132.6 4.1 %collective-permute-start.36 = (bf16[128,128]{1,0:T(8,128)(2,1)S(1)}, bf16[128,128]{1,0:T(8,128)(2,1)S(1)}, u32[]{:S(2)}, u32[]{:S(2)}) collective-permute-start(bf16[128,128]{1,0:T(8,128)(2,1)S(1)} %get-tuple-element.100), channel_id=1, source_target_pairs={{0,30},{1,31},{2,28},{3,29},{4,26},{5,27},{6,24},{7,25},{8,22},{9,... | collective-permute-start | bytes 98312 | tf_op jit(solution)/shard_map/ppermute | solution.py:314
  136.9 4.5 %shard_map.168.rest_16_ = bf16[32,128,128]{2,1,0:T(8,128)(2,1)} custom-call(s32[2]{0:T(128)S(1)} %pad_add_fusion.own_ref, bf16[11,256,256]{2,1,0:T(8,128)(2,1)S(1)} %copy-done, f32[32,128]{1,0:T(8,128)S(1)} %get-tuple-element.140.c_ref, f32[32,128]{1,0:T(8,128)S(1)} %get-tuple-element.139.s_ref, bf16[2,256,256]{2,1,0:T(8,128)(2,1)S(1)} %copy-done.3, ...), custom_call_target="tpu_custom_call" | custom-call | tf_op jit(solution)/shard_map/pallas_call | solution.py:281
  141.4 4.5 %shard_map.169 = bf16[32,128,128]{2,1,0:T(8,128)(2,1)} custom-call(s32[2]{0:T(128)S(1)} %pad_add_fusion.own_ref, bf16[11,256,256]{2,1,0:T(8,128)(2,1)S(1)} %copy-done, f32[32,128]{1,0:T(8,128)S(1)} %get-tuple-element.140.c_ref, f32[32,128]{1,0:T(8,128)S(1)} %get-tuple-element.139.s_ref, ...), custom_call_target="tpu_custom_call", output_to_operand_aliasing={{}: (21, {})} | custom-call | tf_op jit(solution)/shard_map/pallas_call | solution.py:281
  (141 shorter events, 30.8 us)
Async XLA Ops:
  0.0 17.4 %collective-permute-start.2 = (f32[32]{0:T(128)}, f32[32]{0:T(128)S(1)}, u32[]{:S(2)}, u32[]{:S(2)}) collective-permute-start(f32[32]{0:T(128)} %param.19), channel_id=1, source_target_pairs={{0,24},{1,25},{2,26},{3,27},{4,28},{5,29},{6,30},{7,31},{8,16},{9,... | collective-permute-start | bytes 392 | tf_op jit(solution)/shard_map/ppermute | solution.py:314
  4.0 14.1 %collective-permute-start.1 = (f32[32]{0:T(128)}, f32[32]{0:T(128)S(1)}, u32[]{:S(2)}, u32[]{:S(2)}) collective-permute-start(f32[32]{0:T(128)} %param.19), channel_id=1, source_target_pairs={{0,16},{1,17},{2,18},{3,19},{4,20},{5,21},{6,22},{7,23},{8,24},{9,... | collective-permute-start | bytes 392 | tf_op jit(solution)/shard_map/ppermute | solution.py:314
  4.5 15.1 %collective-permute-start = (f32[32]{0:T(128)}, f32[32]{0:T(128)S(1)}, u32[]{:S(2)}, u32[]{:S(2)}) collective-permute-start(f32[32]{0:T(128)} %param.19), channel_id=1, source_target_pairs={{0,8},{1,9},{2,10},{3,11},{4,12},{5,13},{6,14},{7,15},{8,0},{9,1},... | collective-permute-start | bytes 392 | tf_op jit(solution)/shard_map/ppermute | solution.py:314
  4.6 17.8 %collective-permute-start.5 = (f32[128]{0:T(128)}, f32[128]{0:T(128)S(1)}, u32[]{:S(2)}, u32[]{:S(2)}) collective-permute-start(f32[128]{0:T(128)} %param.18), channel_id=1, source_target_pairs={{0,6},{1,7},{2,4},{3,5},{4,2},{5,3},{6,0},{7,1},{8,14},{9,15},{10,... | collective-permute-start | bytes 1544 | tf_op jit(solution)/shard_map/ppermute | solution.py:314
  8.6 13.8 %collective-permute-start.4 = (f32[128]{0:T(128)}, f32[128]{0:T(128)S(1)}, u32[]{:S(2)}, u32[]{:S(2)}) collective-permute-start(f32[128]{0:T(128)} %param.18), channel_id=1, source_target_pairs={{0,4},{1,5},{2,6},{3,7},{4,0},{5,1},{6,2},{7,3},{8,12},{9,13},{10,... | collective-permute-start | bytes 1544 | tf_op jit(solution)/shard_map/ppermute | solution.py:314
  19.5 9.7 %collective-permute-start.7 = (bf16[128,128]{1,0:T(8,128)(2,1)S(1)}, bf16[128,128]{1,0:T(8,128)(2,1)S(1)}, u32[]{:S(2)}, u32[]{:S(2)}) collective-permute-start(bf16[128,128]{1,0:T(8,128)(2,1)S(1)} %get-tuple-element.71), channel_id=1, source_target_pairs={{0,4},{1,5},{2,6},{3,7},{4,0},{5,1},{6,2},{7,3},{8,12},{9,13},{10,... | collective-permute-start | bytes 98312 | tf_op jit(solution)/shard_map/ppermute | solution.py:314
  24.5 11.5 %collective-permute-start.11 = (bf16[128,128]{1,0:T(8,128)(2,1)S(1)}, bf16[128,128]{1,0:T(8,128)(2,1)S(1)}, u32[]{:S(2)}, u32[]{:S(2)}) collective-permute-start(bf16[128,128]{1,0:T(8,128)(2,1)S(1)} %get-tuple-element.75), channel_id=1, source_target_pairs={{0,12},{1,13},{2,14},{3,15},{4,8},{5,9},{6,10},{7,11},{8,4},{9,5},... | collective-permute-start | bytes 98312 | tf_op jit(solution)/shard_map/ppermute | solution.py:314
  29.3 9.5 %collective-permute-start.13 = (bf16[128,128]{1,0:T(8,128)(2,1)S(1)}, bf16[128,128]{1,0:T(8,128)(2,1)S(1)}, u32[]{:S(2)}, u32[]{:S(2)}) collective-permute-start(bf16[128,128]{1,0:T(8,128)(2,1)S(1)} %get-tuple-element.77), channel_id=1, source_target_pairs={{0,16},{1,17},{2,18},{3,19},{4,20},{5,21},{6,22},{7,23},{8,24},{9,... | collective-permute-start | bytes 98312 | tf_op jit(solution)/shard_map/ppermute | solution.py:314
  31.3 13.4 %collective-permute-start.15 = (bf16[128,128]{1,0:T(8,128)(2,1)S(1)}, bf16[128,128]{1,0:T(8,128)(2,1)S(1)}, u32[]{:S(2)}, u32[]{:S(2)}) collective-permute-start(bf16[128,128]{1,0:T(8,128)(2,1)S(1)} %get-tuple-element.79), channel_id=1, source_target_pairs={{0,20},{1,21},{2,22},{3,23},{4,16},{5,17},{6,18},{7,19},{8,28},{9,... | collective-permute-start | bytes 98312 | tf_op jit(solution)/shard_map/ppermute | solution.py:314
  36.2 9.6 %collective-permute-start.17 = (bf16[128,128]{1,0:T(8,128)(2,1)S(1)}, bf16[128,128]{1,0:T(8,128)(2,1)S(1)}, u32[]{:S(2)}, u32[]{:S(2)}) collective-permute-start(bf16[128,128]{1,0:T(8,128)(2,1)S(1)} %get-tuple-element.81), channel_id=1, source_target_pairs={{0,24},{1,25},{2,26},{3,27},{4,28},{5,29},{6,30},{7,31},{8,16},{9,... | collective-permute-start | bytes 98312 | tf_op jit(solution)/shard_map/ppermute | solution.py:314
  38.7 10.7 %collective-permute-start.18 = (bf16[128,128]{1,0:T(8,128)(2,1)S(1)}, bf16[128,128]{1,0:T(8,128)(2,1)S(1)}, u32[]{:S(2)}, u32[]{:S(2)}) collective-permute-start(bf16[128,128]{1,0:T(8,128)(2,1)S(1)} %get-tuple-element.82), channel_id=1, source_target_pairs={{0,26},{1,27},{2,24},{3,25},{4,30},{5,31},{6,28},{7,29},{8,18},{9,... | collective-permute-start | bytes 98312 | tf_op jit(solution)/shard_map/ppermute | solution.py:314
  39.1 10.5 %collective-permute-start.19 = (bf16[128,128]{1,0:T(8,128)(2,1)S(1)}, bf16[128,128]{1,0:T(8,128)(2,1)S(1)}, u32[]{:S(2)}, u32[]{:S(2)}) collective-permute-start(bf16[128,128]{1,0:T(8,128)(2,1)S(1)} %get-tuple-element.83), channel_id=1, source_target_pairs={{0,28},{1,29},{2,30},{3,31},{4,24},{5,25},{6,26},{7,27},{8,20},{9,... | collective-permute-start | bytes 98312 | tf_op jit(solution)/shard_map/ppermute | solution.py:314
  45.7 10.6 %collective-permute-start.38 = (bf16[128,128]{1,0:T(8,128)(2,1)S(1)}, bf16[128,128]{1,0:T(8,128)(2,1)S(1)}, u32[]{:S(2)}, u32[]{:S(2)}) collective-permute-start(bf16[128,128]{1,0:T(8,128)(2,1)S(1)} %get-tuple-element.103), channel_id=1, source_target_pairs={{0,4},{1,5},{2,6},{3,7},{4,0},{5,1},{6,2},{7,3},{8,12},{9,13},{10,... | collective-permute-start | bytes 98312 | tf_op jit(solution)/shard_map/ppermute | solution.py:314
  52.3 10.9 %collective-permute-start.42 = (bf16[128,128]{1,0:T(8,128)(2,1)S(1)}, bf16[128,128]{1,0:T(8,128)(2,1)S(1)}, u32[]{:S(2)}, u32[]{:S(2)}) collective-permute-start(bf16[128,128]{1,0:T(8,128)(2,1)S(1)} %get-tuple-element.107), channel_id=1, source_target_pairs={{0,12},{1,13},{2,14},{3,15},{4,8},{5,9},{6,10},{7,11},{8,4},{9,5},... | collective-permute-start | bytes 98312 | tf_op jit(solution)/shard_map/ppermute | solution.py:314
  58.4 13.3 %collective-permute-start.46 = (bf16[128,128]{1,0:T(8,128)(2,1)S(1)}, bf16[128,128]{1,0:T(8,128)(2,1)S(1)}, u32[]{:S(2)}, u32[]{:S(2)}) collective-permute-start(bf16[128,128]{1,0:T(8,128)(2,1)S(1)} %get-tuple-element.111), channel_id=1, source_target_pairs={{0,20},{1,21},{2,22},{3,23},{4,16},{5,17},{6,18},{7,19},{8,28},{9,... | collective-permute-start | bytes 98312 | tf_op jit(solution)/shard_map/ppermute | solution.py:314
  63.2 12.4 %collective-permute-start.47 = (bf16[128,128]{1,0:T(8,128)(2,1)S(1)}, bf16[128,128]{1,0:T(8,128)(2,1)S(1)}, u32[]{:S(2)}, u32[]{:S(2)}) collective-permute-start(bf16[128,128]{1,0:T(8,128)(2,1)S(1)} %get-tuple-element.112), channel_id=1, source_target_pairs={{0,22},{1,23},{2,20},{3,21},{4,18},{5,19},{6,16},{7,17},{8,30},{9,... | collective-permute-start | bytes 98312 | tf_op jit(solution)/shard_map/ppermute | solution.py:314
  64.7 11.0 %collective-permute-start.48 = (bf16[128,128]{1,0:T(8,128)(2,1)S(1)}, bf16[128,128]{1,0:T(8,128)(2,1)S(1)}, u32[]{:S(2)}, u32[]{:S(2)}) collective-permute-start(bf16[128,128]{1,0:T(8,128)(2,1)S(1)} %get-tuple-element.113), channel_id=1, source_target_pairs={{0,24},{1,25},{2,26},{3,27},{4,28},{5,29},{6,30},{7,31},{8,16},{9,... | collective-permute-start | bytes 98312 | tf_op jit(solution)/shard_map/ppermute | solution.py:314
  66.2 9.4 %collective-permute-start.49 = (bf16[128,128]{1,0:T(8,128)(2,1)S(1)}, bf16[128,128]{1,0:T(8,128)(2,1)S(1)}, u32[]{:S(2)}, u32[]{:S(2)}) collective-permute-start(bf16[128,128]{1,0:T(8,128)(2,1)S(1)} %get-tuple-element.114), channel_id=1, source_target_pairs={{0,26},{1,27},{2,24},{3,25},{4,30},{5,31},{6,28},{7,29},{8,18},{9,... | collective-permute-start | bytes 98312 | tf_op jit(solution)/shard_map/ppermute | solution.py:314
  66.3 9.4 %collective-permute-start.50 = (bf16[128,128]{1,0:T(8,128)(2,1)S(1)}, bf16[128,128]{1,0:T(8,128)(2,1)S(1)}, u32[]{:S(2)}, u32[]{:S(2)}) collective-permute-start(bf16[128,128]{1,0:T(8,128)(2,1)S(1)} %get-tuple-element.115), channel_id=1, source_target_pairs={{0,28},{1,29},{2,30},{3,31},{4,24},{5,25},{6,26},{7,27},{8,20},{9,... | collective-permute-start | bytes 98312 | tf_op jit(solution)/shard_map/ppermute | solution.py:314
  83.9 9.9 %collective-permute-start.24 = (bf16[128,128]{1,0:T(8,128)(2,1)S(1)}, bf16[128,128]{1,0:T(8,128)(2,1)S(1)}, u32[]{:S(2)}, u32[]{:S(2)}) collective-permute-start(bf16[128,128]{1,0:T(8,128)(2,1)S(1)} %get-tuple-element.88), channel_id=1, source_target_pairs={{0,6},{1,7},{2,4},{3,5},{4,2},{5,3},{6,0},{7,1},{8,14},{9,15},{10,... | collective-permute-start | bytes 98312 | tf_op jit(solution)/shard_map/ppermute | solution.py:314
  87.7 10.5 %collective-permute-start.27 = (bf16[128,128]{1,0:T(8,128)(2,1)S(1)}, bf16[128,128]{1,0:T(8,128)(2,1)S(1)}, u32[]{:S(2)}, u32[]{:S(2)}) collective-permute-start(bf16[128,128]{1,0:T(8,128)(2,1)S(1)} %get-tuple-element.91), channel_id=1, source_target_pairs={{0,12},{1,13},{2,14},{3,15},{4,8},{5,9},{6,10},{7,11},{8,4},{9,5},... | collective-permute-start | bytes 98312 | tf_op jit(solution)/shard_map/ppermute | solution.py:314
  103.5 11.5 %collective-permute-start.58 = (bf16[128,128]{1,0:T(8,128)(2,1)S(1)}, bf16[128,128]{1,0:T(8,128)(2,1)S(1)}, u32[]{:S(2)}, u32[]{:S(2)}) collective-permute-start(bf16[128,128]{1,0:T(8,128)(2,1)S(1)} %get-tuple-element.123), channel_id=1, source_target_pairs={{0,12},{1,13},{2,14},{3,15},{4,8},{5,9},{6,10},{7,11},{8,4},{9,5},... | collective-permute-start | bytes 98312 | tf_op jit(solution)/shard_map/ppermute | solution.py:314
  110.3 12.2 %collective-permute-start.62 = (bf16[128,128]{1,0:T(8,128)(2,1)S(1)}, bf16[128,128]{1,0:T(8,128)(2,1)S(1)}, u32[]{:S(2)}, u32[]{:S(2)}) collective-permute-start(bf16[128,128]{1,0:T(8,128)(2,1)S(1)} %get-tuple-element.127), channel_id=1, source_target_pairs={{0,20},{1,21},{2,22},{3,23},{4,16},{5,17},{6,18},{7,19},{8,28},{9,... | collective-permute-start | bytes 98312 | tf_op jit(solution)/shard_map/ppermute | solution.py:314
  114.9 9.8 %collective-permute-start.63 = (bf16[128,128]{1,0:T(8,128)(2,1)S(1)}, bf16[128,128]{1,0:T(8,128)(2,1)S(1)}, u32[]{:S(2)}, u32[]{:S(2)}) collective-permute-start(bf16[128,128]{1,0:T(8,128)(2,1)S(1)} %get-tuple-element.128), channel_id=1, source_target_pairs={{0,22},{1,23},{2,20},{3,21},{4,18},{5,19},{6,16},{7,17},{8,30},{9,... | collective-permute-start | bytes 98312 | tf_op jit(solution)/shard_map/ppermute | solution.py:314
  116.2 12.0 %collective-permute-start.64 = (bf16[128,128]{1,0:T(8,128)(2,1)S(1)}, bf16[128,128]{1,0:T(8,128)(2,1)S(1)}, u32[]{:S(2)}, u32[]{:S(2)}) collective-permute-start(bf16[128,128]{1,0:T(8,128)(2,1)S(1)} %get-tuple-element.129), channel_id=1, source_target_pairs={{0,24},{1,25},{2,26},{3,27},{4,28},{5,29},{6,30},{7,31},{8,16},{9,... | collective-permute-start | bytes 98312 | tf_op jit(solution)/shard_map/ppermute | solution.py:314
  116.8 11.9 %collective-permute-start.65 = (bf16[128,128]{1,0:T(8,128)(2,1)S(1)}, bf16[128,128]{1,0:T(8,128)(2,1)S(1)}, u32[]{:S(2)}, u32[]{:S(2)}) collective-permute-start(bf16[128,128]{1,0:T(8,128)(2,1)S(1)} %get-tuple-element.130), channel_id=1, source_target_pairs={{0,26},{1,27},{2,24},{3,25},{4,30},{5,31},{6,28},{7,29},{8,18},{9,... | collective-permute-start | bytes 98312 | tf_op jit(solution)/shard_map/ppermute | solution.py:314
  117.9 10.8 %collective-permute-start.66 = (bf16[128,128]{1,0:T(8,128)(2,1)S(1)}, bf16[128,128]{1,0:T(8,128)(2,1)S(1)}, u32[]{:S(2)}, u32[]{:S(2)}) collective-permute-start(bf16[128,128]{1,0:T(8,128)(2,1)S(1)} %get-tuple-element.131), channel_id=1, source_target_pairs={{0,28},{1,29},{2,30},{3,31},{4,24},{5,25},{6,26},{7,27},{8,20},{9,... | collective-permute-start | bytes 98312 | tf_op jit(solution)/shard_map/ppermute | solution.py:314
  122.6 10.1 %collective-permute-start.67 = (bf16[128,128]{1,0:T(8,128)(2,1)S(1)}, bf16[128,128]{1,0:T(8,128)(2,1)S(1)}, u32[]{:S(2)}, u32[]{:S(2)}) collective-permute-start(bf16[128,128]{1,0:T(8,128)(2,1)S(1)} %get-tuple-element.132), channel_id=1, source_target_pairs={{0,30},{1,31},{2,28},{3,29},{4,26},{5,27},{6,24},{7,25},{8,22},{9,... | collective-permute-start | bytes 98312 | tf_op jit(solution)/shard_map/ppermute | solution.py:314
  124.8 16.6 %collective-permute-start.32 = (bf16[128,128]{1,0:T(8,128)(2,1)S(1)}, bf16[128,128]{1,0:T(8,128)(2,1)S(1)}, u32[]{:S(2)}, u32[]{:S(2)}) collective-permute-start(bf16[128,128]{1,0:T(8,128)(2,1)S(1)} %get-tuple-element.96), channel_id=1, source_target_pairs={{0,22},{1,23},{2,20},{3,21},{4,18},{5,19},{6,16},{7,17},{8,30},{9,... | collective-permute-start | bytes 98312 | tf_op jit(solution)/shard_map/ppermute | solution.py:314
  128.2 13.2 %collective-permute-start.33 = (bf16[128,128]{1,0:T(8,128)(2,1)S(1)}, bf16[128,128]{1,0:T(8,128)(2,1)S(1)}, u32[]{:S(2)}, u32[]{:S(2)}) collective-permute-start(bf16[128,128]{1,0:T(8,128)(2,1)S(1)} %get-tuple-element.97), channel_id=1, source_target_pairs={{0,24},{1,25},{2,26},{3,27},{4,28},{5,29},{6,30},{7,31},{8,16},{9,... | collective-permute-start | bytes 98312 | tf_op jit(solution)/shard_map/ppermute | solution.py:314
  128.7 12.7 %collective-permute-start.34 = (bf16[128,128]{1,0:T(8,128)(2,1)S(1)}, bf16[128,128]{1,0:T(8,128)(2,1)S(1)}, u32[]{:S(2)}, u32[]{:S(2)}) collective-permute-start(bf16[128,128]{1,0:T(8,128)(2,1)S(1)} %get-tuple-element.98), channel_id=1, source_target_pairs={{0,26},{1,27},{2,24},{3,25},{4,30},{5,31},{6,28},{7,29},{8,18},{9,... | collective-permute-start | bytes 98312 | tf_op jit(solution)/shard_map/ppermute | solution.py:314
  128.7 12.7 %collective-permute-start.35 = (bf16[128,128]{1,0:T(8,128)(2,1)S(1)}, bf16[128,128]{1,0:T(8,128)(2,1)S(1)}, u32[]{:S(2)}, u32[]{:S(2)}) collective-permute-start(bf16[128,128]{1,0:T(8,128)(2,1)S(1)} %get-tuple-element.99), channel_id=1, source_target_pairs={{0,28},{1,29},{2,30},{3,31},{4,24},{5,25},{6,26},{7,27},{8,20},{9,... | collective-permute-start | bytes 98312 | tf_op jit(solution)/shard_map/ppermute | solution.py:314
  (47 other events, 582.1 us)

commit v3 on v0

v3 whole, which is shorter than its diff:
```python
import functools
import math

import jax
import jax.numpy as jnp
import ml_dtypes
import numpy as np
from jax import lax
from jax.experimental import pallas as pl
from jax.experimental.pallas import tpu as pltpu
from jax.sharding import PartitionSpec as P

HALF = 64
WIDE = 128


def nodes():
    points = np.cos((2.0 * np.arange(8) + 1.0) * (math.pi / 16.0))
    return np.repeat(points, 8), np.tile(points, 8)


def node_weights():
    first, second = nodes()
    return (first * first + second * second).astype(np.float32)


def level_matrix(number):
    first, second = nodes()
    frequency = 9.0 + 3.0 * (number % 5)
    shifts = np.array([-0.5, 0.5])
    out_first = first[None, :] + shifts[:, None]
    in_second = second[None, :] + shifts[:, None]
    inner = (
        out_first[:, None, :, None] * first[None, None, None, :]
        + second[None, None, :, None] * in_second[None, :, None, :]
    )
    out_norm = np.sqrt(out_first**2 + second[None, :] ** 2)
    in_norm = np.sqrt(first[None, :] ** 2 + in_second**2)
    phases = frequency * (inner + 0.5 * out_norm[:, None, :, None] * in_norm[None, :, None, :])
    factor = 1.0 / math.sqrt(128.0)
    real = np.transpose(factor * np.cos(phases), (1, 3, 0, 2))
    imag = np.transpose(factor * np.sin(phases), (1, 3, 0, 2))
    upper = np.concatenate([real, imag], axis=3)
    lower = np.concatenate([-imag, real], axis=3)
    full = np.concatenate([upper, lower], axis=1)
    return full.reshape(2 * WIDE, 2 * WIDE).astype(ml_dtypes.bfloat16)


def tables(scales):
    weights = np.tile(node_weights(), 2)
    angles = scales[..., None] * weights
    signs = np.repeat(np.array([-1.0, 1.0], np.float32), HALF)
    return jnp.cos(angles), jnp.sin(angles) * signs


def shuffle_matrix():
    rows = np.arange(256)
    found = np.zeros((256, 256), np.float32)
    found[rows, rows % 16 * 16 + rows // 16] = 1.0
    return found.astype(ml_dtypes.bfloat16)


def rotated(value, cosine, sine):
    return (value * cosine + pltpu.roll(value, HALF, 1) * sine).astype(jnp.bfloat16)


def butterfly(load, store, count, apart, matrix, phase_of, group):
    lows = [i for i in range(count) if not i & apart]
    for start in range(0, len(lows), group):
        picked = lows[start : start + group]
        left = jnp.concatenate([load(i) for i in picked], axis=0)
        right = jnp.concatenate([load(i + apart) for i in picked], axis=0)
        rows = left.shape[0] // len(picked)
        both = jnp.dot(
            jnp.concatenate([left, right], axis=1), matrix, preferred_element_type=jnp.float32
        )
        for place, low in enumerate(picked):
            for child in range(2):
                index = low + child * apart
                value = both[
                    place * rows : (place + 1) * rows, child * WIDE : (child + 1) * WIDE
                ]
                store(index, rotated(value, *phase_of(index)))


def swap_axes(load, store, outer, inner, shuffle):
    for low in range(0, outer, 2):
        for at in range(inner):
            sides = [load(low + side, at).reshape(256, WIDE) for side in range(2)]
            moved = jnp.dot(
                shuffle, jnp.concatenate(sides, axis=1), preferred_element_type=jnp.float32
            ).astype(jnp.bfloat16)
            for side in range(2):
                block = moved[:, side * WIDE : (side + 1) * WIDE]
                store(at, low + side, block.reshape(16, 16, WIDE))


def block_at(first, second):
    return (slice(first * 16, first * 16 + 16), slice(second * 16, second * 16 + 16))


def source_kernel(pieces, a_ref, x_hbm, m_hbm, p_ref, o_ref, x_ref, m_ref, x_sems, m_sems):
    rows, cols, _ = x_ref.shape
    levels = m_ref.shape[0]
    each = rows // pieces
    x_copies = [
        pltpu.make_async_copy(
            x_hbm.at[pl.ds(i * each, each)], x_ref.at[pl.ds(i * each, each)], x_sems.at[i]
        )
        for i in range(pieces)
    ]
    m_copies = [
        pltpu.make_async_copy(m_hbm.at[i], m_ref.at[i], m_sems.at[i]) for i in range(levels)
    ]
    m_copies[0].start()
    for copy in x_copies:
        copy.start()
    for copy in m_copies[1:]:
        copy.start()
    angles = a_ref[...]
    cosines = jnp.cos(angles)
    lanes = lax.broadcasted_iota(jnp.int32, angles.shape, 1)
    sines = jnp.where(lanes < HALF, -jnp.sin(angles), jnp.sin(angles))
    block = 32
    for level in range(levels):
        m_copies[level].wait()
        if level == 0:
            for copy in x_copies:
                copy.wait()
        for start in range(0, cols, block):
            cosine, sine = cosines[start : start + block], sines[start : start + block]

            def store(index, value):
                x_ref[index, start : start + block, :] = value

            butterfly(
                lambda index: x_ref[index, start : start + block, :],
                store,
                rows,
                1 << level,
                m_ref[level],
                lambda index: (cosine, sine),
                16,
            )

    def store_block(first, second, block):
        o_ref[block_at(first, second)] = block

    swap_axes(
        lambda first, second: x_ref[block_at(first, second)],
        store_block,
        rows // 16,
        cols // 16,
        p_ref[...],
    )


VMEM = pl.BlockSpec(memory_space=pltpu.VMEM)
PARAMS = pltpu.CompilerParams(vmem_limit_bytes=32 << 20)


def source_levels(x, matrices, angles, shuffle):
    rows, cols, _ = x.shape
    pieces = 4
    far = pl.BlockSpec(memory_space=pltpu.HBM)
    return pl.pallas_call(
        functools.partial(source_kernel, pieces),
        out_shape=jax.ShapeDtypeStruct((cols, rows, WIDE), x.dtype),
        in_specs=[VMEM, far, far, VMEM],
        out_specs=VMEM,
        scratch_shapes=[
            pltpu.VMEM(x.shape, x.dtype),
            pltpu.VMEM(matrices.shape, x.dtype),
            pltpu.SemaphoreType.DMA((pieces,)),
            pltpu.SemaphoreType.DMA((matrices.shape[0],)),
        ],
        compiler_params=PARAMS,
    )(angles, x, matrices, shuffle)


def middle_kernel(levels, rows, x_ref, m_ref, cs_ref, ss_ref, ct_ref, st_ref, o_ref):
    count, total, _ = x_ref.shape
    run = total // rows
    tgt_count = cs_ref.shape[0] // run
    for step, (apart, by_source) in enumerate(levels):
        source = x_ref if step == 0 else o_ref
        for col in range(run):
            own = slice(col * rows, (col + 1) * rows)

            def phase_of(index):
                if by_source:
                    at = index % tgt_count * run + col
                    return cs_ref[at : at + 1, :], ss_ref[at : at + 1, :]
                at = index // tgt_count
                return ct_ref[at], st_ref[at]

            def store(index, value):
                o_ref[index, own, :] = value

            butterfly(
                lambda index: source[index, own, :],
                store,
                count,
                apart,
                m_ref[step],
                phase_of,
                16,
            )


def middle_levels(x, matrices, src_tables, tgt_tables, levels):
    rows = tgt_tables[0].shape[1]
    return pl.pallas_call(
        functools.partial(middle_kernel, levels, rows),
        out_shape=jax.ShapeDtypeStruct(x.shape, x.dtype),
        in_specs=[VMEM] * 6,
        out_specs=VMEM,
        compiler_params=PARAMS,
    )(x, matrices, *src_tables, *tgt_tables)


def target_kernel(x_ref, m_ref, c_ref, s_ref, p_ref, o_ref, state_ref):
    cols, rows, _ = x_ref.shape
    levels = m_ref.shape[0]
    for level in range(levels):
        source = x_ref if level == 0 else state_ref
        for start in range(0, rows, 16):
            own = slice(start, start + 16)
            cosine, sine = c_ref[own, :], s_ref[own, :]

            def store(index, value):
                state_ref[index, own, :] = value

            butterfly(
                lambda index: source[index, own, :],
                store,
                cols,
                1 << (levels - 1 - level),
                m_ref[level],
                lambda index: (cosine, sine),
                32,
            )

    def store_block(first, second, block):
        o_ref[block_at(first, second)] = block

    swap_axes(
        lambda first, second: state_ref[block_at(first, second)],
        store_block,
        cols // 16,
        rows // 16,
        p_ref[...],
    )


def target_levels(x, matrices, cosine, sine, shuffle):
    cols, rows, _ = x.shape
    return pl.pallas_call(
        target_kernel,
        out_shape=jax.ShapeDtypeStruct((rows, cols, WIDE), x.dtype),
        in_specs=[VMEM] * 5,
        out_specs=VMEM,
        scratch_shapes=[pltpu.VMEM(x.shape, x.dtype)],
        compiler_params=PARAMS,
    )(x, matrices, cosine, sine, shuffle)


def gathered(values, axis):
    count = lax.axis_size(axis)
    place = lax.axis_index(axis)
    values = values[None]
    apart = 1
    while apart < count:
        other = lax.ppermute(values, axis, [(i, i ^ apart) for i in range(count)])
        mine_first = (place & apart) == 0
        values = jnp.concatenate(
            [jnp.where(mine_first, values, other), jnp.where(mine_first, other, values)]
        )
        apart *= 2
    return values


def local(box_weights, slowness, dip_field):
    rows, cols, _ = box_weights.shape
    src_count = lax.axis_size("src")
    tgt_count = lax.axis_size("tgt")
    devices = src_count * tgt_count
    row_bits, col_bits = rows.bit_length() - 1, cols.bit_length() - 1
    src_bits, tgt_bits = src_count.bit_length() - 1, tgt_count.bit_length() - 1
    first_target = row_bits + src_bits
    total = first_target + tgt_bits + col_bits
    matrices = [level_matrix(number) for number in range(total)]

    def matrices_of(low, high):
        return jnp.asarray(np.stack(matrices[low:high]))

    run = cols // devices
    place = lax.axis_index("src") * tgt_count + lax.axis_index("tgt")
    shuffle = jnp.asarray(shuffle_matrix())

    angles = slowness[:, None] * np.tile(node_weights(), 2)
    state = source_levels(box_weights, matrices_of(0, row_bits), angles, shuffle)

    state, slowness, dip_field = lax.optimization_barrier((state, slowness, dip_field))
    all_dip = gathered(dip_field, "src")
    all_slowness = gathered(slowness, "tgt")
    run_slowness = lax.dynamic_slice_in_dim(all_slowness, place * run, run, 1)

    state = state.reshape(devices, run * rows, WIDE)
    state = lax.all_to_all(state, ("src", "tgt"), 0, 0, tiled=True)
    levels = [(tgt_count << bit, True) for bit in range(src_bits)]
    levels += [(1 << bit, False) for bit in reversed(range(tgt_bits))]
    state = middle_levels(
        state,
        matrices_of(row_bits, first_target + tgt_bits),
        tables(run_slowness.reshape(-1)),
        tables(all_dip),
        levels,
    )
    state = lax.all_to_all(state, ("src", "tgt"), 0, 0, tiled=True)

    return target_levels(
        state.reshape(cols, rows, WIDE),
        matrices_of(first_target + tgt_bits, total),
        *tables(dip_field),
        shuffle,
    )


def solution(mesh):
    in_specs = (P("src", "tgt", None), P("tgt"), P("src"))
    out_specs = P("src", "tgt", None)
    return jax.shard_map(local, mesh=mesh, in_specs=in_specs, out_specs=out_specs, check_vma=False)
```

time: 89 us -> 85.9 us (0.965)
  waiting for transfers between devices: 27.3 us -> 16.2 us
  blocking collectives: 22.1 us -> 30.1 us
  local copies, waits for them, and re-layouts: 8.09 us -> 4.7 us
  Pallas kernels: 12.8 us -> 15.8 us
  starting transfers between devices: 14.5 us -> 17.3 us
  other arithmetic: 3.15 us -> 1.32 us
    all_to_all x0 -> x1, blocking collectives: none -> 30.1 us  [local(): state = lax.all_to_all(state, ('src', 'tgt'), 0, 0, tiled=True)]
    all_to_all x2 -> x1, waiting for transfers between devices: 27.3 us -> 0.92 us  [local(): state = lax.all_to_all(state, ('src', 'tgt'), 0, 0, tiled=True)]
    ppermute x0 -> x5, waiting for transfers between devices: none -> 15.2 us  [gathered(): other = lax.ppermute(values, axis, [(i, i ^ apart) for i in range(count)])]
    all_gather x1 -> x0, blocking collectives: 11.8 us -> none  [local(): all_slowness = lax.all_gather(slowness, 'tgt')]
    unnamed x1 -> x0, blocking collectives: 10.3 us -> none
    ppermute x0 -> x5, starting transfers between devices: none -> 10 us  [gathered(): other = lax.ppermute(values, axis, [(i, i ^ apart) for i in range(count)])]
    all_to_all x2 -> x1, starting transfers between devices: 14.5 us -> 7.3 us  [local(): state = lax.all_to_all(state, ('src', 'tgt'), 0, 0, tiled=True)]
    pallas_call x3, Pallas kernels: 12.8 us -> 15.8 us  [the longest x1 6.48 us: source_levels(): pl.pallas_call(functools.partial(source_kernel, pieces), out_shape=jax.Sh...]
  transfers between devices with their start and end apart: 2 -> 6, of which waited for: 1 -> 5; matrix products, arithmetic and copies ran while one was open for 4% -> 1% of each run, Pallas kernels for 0% -> 0%
where the time goes in v3:
time: 85.9 us; the launch traced here: 85.6 us
  blocking collectives  30.1 us (35%)
  starting transfers between devices  17.3 us (20%)
  waiting for transfers between devices  16.2 us (19%)
  Pallas kernels  15.8 us (18%)
  local copies, waits for them, and re-layouts  4.7 us (5%)
  other arithmetic  1.32 us (2%)
    all_to_all x1, blocking collectives, local(): state = lax.all_to_all(state, ('src', 'tgt'), 0, 0, tiled=True)  30.1 us
    ppermute x5, waiting for transfers between devices, gathered(): other = lax.ppermute(values, axis, [(i, i ^ apart) for i in range(count)])  15.2 us
    ppermute x5, starting transfers between devices, gathered(): other = lax.ppermute(values, axis, [(i, i ^ apart) for i in range(count)])  10 us
    all_to_all x1, starting transfers between devices, local(): state = lax.all_to_all(state, ('src', 'tgt'), 0, 0, tiled=True)  7.3 us
    pallas_call x1, Pallas kernels, source_levels(): pl.pallas_call(functools.partial(source_kernel, pieces), out_shape=jax.Sh...  6.48 us
    pallas_call x1, Pallas kernels, target_levels(): pl.pallas_call(target_kernel, out_shape=jax.ShapeDtypeStruct((rows, cols,...  6.1 us
    unnamed x20, local copies, waits for them, and re-layouts  4.54 us
    pallas_call x1, Pallas kernels, middle_levels(): pl.pallas_call(functools.partial(middle_kernel, levels, rows), out_shape=...  3.26 us
  transfers between devices with their start and end apart: 6, of which 5 were waited for; matrix products, arithmetic and copies ran while one was open for 1% of the time, Pallas kernels for 0%

profile of v3, /device:TPU:0, one launch (start us, length us, event | category | flops | bytes accessed | tf_op | source)
XLA Modules:
  0.0 85.6 jit_solution(6556810245074555373)
XLA Ops:
  0.0 0.7 copy-done.6
  0.7 0.7 broadcast_multiply_fusion.a_ref
  1.4 0.0 copy-start
  1.4 1.1 %copy-done = bf16[5,256,256]{2,1,0:T(8,128)(2,1)S(1)} copy-done((bf16[5,256,256]{2,1,0:T(8,128)(2,1)S(1)}, bf16[5,256,256]{2,1,0:T(8,128)(2,1)}, u32[]{:S(2)}) %copy-start) | copy-done | bytes 655384
  2.5 1.2 %copy-done.2 = bf16[32,128,128]{2,1,0:T(8,128)(2,1)S(1)} copy-done((bf16[32,128,128]{2,1,0:T(8,128)(2,1)S(1)}, bf16[32,128,128]{2,1,0:T(8,128)(2,1)}, u32[]{:S(2)}) %copy-start.2) | copy-done | bytes 1048600
  3.7 0.9 %copy-done.4 = bf16[256,256]{1,0:T(8,128)(2,1)S(1)} copy-done((bf16[256,256]{1,0:T(8,128)(2,1)S(1)}, bf16[256,256]{1,0:T(8,128)(2,1)}, u32[]{:S(2)}) %copy-start.4) | copy-done | bytes 131096
  4.6 6.5 %shard_map.136 = bf16[128,32,128]{2,1,0:T(8,128)(2,1)} custom-call(f32[128,128]{1,0:T(8,128)S(1)} %broadcast_multiply_fusion.a_ref, bf16[32,128,128]{2,1,0:T(8,128)(2,1)S(1)} %copy-done.2, bf16[5,256,256]{2,1,0:T(8,128)(2,1)S(1)} %copy-done, bf16[256,256]{1,0:T(8,128)(2,1)S(1)} %copy-done.4), custom_call_target="tpu_custom_call" | custom-call | tf_op jit(solution)/shard_map/pallas_call | solution.py:166
  11.1 0.0 copy-start.1
  11.1 7.3 %all-to-all-start = ((bf16[32,128,128]{2,1,0:T(8,128)(2,1)}), bf16[32,128,128]{2,1,0:T(8,128)(2,1)S(1)}, u32[]{:S(2)}, u32[]{:S(2)}) async-start(bf16[32,128,128]{2,1,0:T(8,128)(2,1)} %bitcast), calls=%async_computation | async-start | bytes 2097152 | tf_op jit(solution)/shard_map/all_to_all | solution.py:310
  18.4 0.0 copy-start.9
  18.4 0.6 copy-done.9
  19.1 1.8 %collective-permute-start.3 = (f32[1,32]{1,0:T(1,128)S(1)}, f32[1,32]{1,0:T(1,128)S(1)}, u32[]{:S(2)}, u32[]{:S(2)}) collective-permute-start(f32[1,32]{1,0:T(1,128)S(1)} %bitcast.10), channel_id=1, source_target_pairs={{0,8},{8,0},{16,24},{24,16},{1,9},{9,1},{17,25},{25,17},{2,10},{10... | collective-permute-start | bytes 392 | tf_op jit(solution)/shard_map/ppermute | solution.py:274
  20.9 0.0 copy-done.8
  20.9 0.0 collective-permute-start
  20.9 4.6 %collective-permute-done.3 = f32[1,32]{1,0:T(1,128)S(1)} collective-permute-done((f32[1,32]{1,0:T(1,128)S(1)}, f32[1,32]{1,0:T(1,128)S(1)}, u32[]{:S(2)}, u32[]{:S(2)}) %collective-permute-start.3) | collective-permute-done | bytes 160 | tf_op jit(solution)/shard_map/ppermute | solution.py:274
  25.5 1.5 %collective-permute-start.4 = (f32[2,32]{1,0:T(2,128)S(1)}, f32[2,32]{1,0:T(2,128)S(1)}, u32[]{:S(2)}, u32[]{:S(2)}) collective-permute-start(f32[2,32]{1,0:T(2,128)S(1)} %pad_maximum_fusion.4), channel_id=1, source_target_pairs={{0,16},{8,24},{16,0},{24,8},{1,17},{9,25},{17,1},{25,9},{2,18},{10... | collective-permute-start | bytes 776 | tf_op jit(solution)/shard_map/ppermute | solution.py:274
  27.0 2.2 %collective-permute-done.4 = f32[2,32]{1,0:T(2,128)S(1)} collective-permute-done((f32[2,32]{1,0:T(2,128)S(1)}, f32[2,32]{1,0:T(2,128)S(1)}, u32[]{:S(2)}, u32[]{:S(2)}) %collective-permute-start.4) | collective-permute-done | bytes 288 | tf_op jit(solution)/shard_map/ppermute | solution.py:274
  29.2 0.0 collective-permute-done
  29.3 2.1 %collective-permute-start.1 = (f32[2,128]{1,0:T(2,128)S(1)}, f32[2,128]{1,0:T(2,128)S(1)}, u32[]{:S(2)}, u32[]{:S(2)}) collective-permute-start(f32[2,128]{1,0:T(2,128)S(1)} %pad_maximum_fusion.3), channel_id=1, source_target_pairs={{0,2},{1,3},{2,0},{3,1},{4,6},{5,7},{6,4},{7,5},{8,10},{9,11},{10,... | collective-permute-start | bytes 3080 | tf_op jit(solution)/shard_map/ppermute | solution.py:274
  31.4 4.7 %collective-permute-done.1 = f32[2,128]{1,0:T(2,128)S(1)} collective-permute-done((f32[2,128]{1,0:T(2,128)S(1)}, f32[2,128]{1,0:T(2,128)S(1)}, u32[]{:S(2)}, u32[]{:S(2)}) %collective-permute-start.1) | collective-permute-done | bytes 1056 | tf_op jit(solution)/shard_map/ppermute | solution.py:274
  36.2 4.6 %collective-permute-start.2 = (f32[4,128]{1,0:T(4,128)S(1)}, f32[4,128]{1,0:T(4,128)S(1)}, u32[]{:S(2)}, u32[]{:S(2)}) collective-permute-start(f32[4,128]{1,0:T(4,128)S(1)} %pad_maximum_fusion.1), channel_id=1, source_target_pairs={{0,4},{1,5},{2,6},{3,7},{4,0},{5,1},{6,2},{7,3},{8,12},{9,13},{10,... | collective-permute-start | bytes 6152 | tf_op jit(solution)/shard_map/ppermute | solution.py:274
  40.7 0.3 fusion
  41.0 3.7 %collective-permute-done.2 = f32[4,128]{1,0:T(4,128)S(1)} collective-permute-done((f32[4,128]{1,0:T(4,128)S(1)}, f32[4,128]{1,0:T(4,128)S(1)}, u32[]{:S(2)}, u32[]{:S(2)}) %collective-permute-start.2) | collective-permute-done | bytes 2080 | tf_op jit(solution)/shard_map/ppermute | solution.py:274
  44.8 0.1 constant_dynamic-slice_fusion
  44.9 0.1 mul.89
  44.9 0.2 fusion.2
  45.1 0.9 %all-to-all-done.x_ref = bf16[32,128,128]{2,1,0:T(8,128)(2,1)S(1)} async-done(((bf16[32,128,128]{2,1,0:T(8,128)(2,1)}), bf16[32,128,128]{2,1,0:T(8,128)(2,1)S(1)}, u32[]{:S(2)}, u32[]{:S(2)}) %all-to-all-start) | async-done | bytes 1048608 | tf_op jit(solution)/shard_map/all_to_all | solution.py:310
  46.1 3.3 %shard_map.137 = bf16[32,128,128]{2,1,0:T(8,128)(2,1)S(1)} custom-call(bf16[32,128,128]{2,1,0:T(8,128)(2,1)S(1)} %all-to-all-done.x_ref, bf16[5,256,256]{2,1,0:T(8,128)(2,1)S(1)} %copy-done.1, f32[32,128]{1,0:T(8,128)S(1)} %get-tuple-element.21.cs_ref, f32[32,128]{1,0:T(8,128)S(1)} %get-tuple-element.20.ss_ref, f32[4,32,128]{2,1,0:T(8,128)S(1)} %get-tuple-element.14.ct_ref, ...), custom_call_target="tpu_custom_call" | custom-call | tf_op jit(solution)/shard_map/pallas_call | solution.py:213
  49.3 0.0 copy-start.3
  49.3 0.0 copy-start.5
  49.3 30.1 %all_to_all.10 = bf16[32,128,128]{2,1,0:T(8,128)(2,1)S(1)} all-to-all(bf16[32,128,128]{2,1,0:T(8,128)(2,1)S(1)} %shard_map.137), channel_id=1, replica_groups=mesh['src'=4,'tgt'=8] {'src','tgt'}, dimensions={0} | all-to-all | bytes 2097152 | tf_op jit(solution)/shard_map/all_to_all | solution.py:320
  79.5 6.1 %shard_map.138 = bf16[32,128,128]{2,1,0:T(8,128)(2,1)} custom-call(bf16[128,32,128]{2,1,0:T(8,128)(2,1)S(1)} %bitcast.8, bf16[7,256,256]{2,1,0:T(8,128)(2,1)S(1)} %copy-done.3, f32[32,128]{1,0:T(8,128)S(1)} %get-tuple-element.22.c_ref, f32[32,128]{1,0:T(8,128)S(1)} %get-tuple-element.19.s_ref, bf16[256,256]{1,0:T(8,128)(2,1)S(1)} %copy-done.5), custom_call_target="tpu_custom_call" | custom-call | tf_op jit(solution)/shard_map/pallas_call | solution.py:258
  (19 shorter events, 0.1 us)
Async XLA Ops:
  0.0 0.7 copy-start.6
  1.4 1.1 %copy-start = (bf16[5,256,256]{2,1,0:T(8,128)(2,1)S(1)}, bf16[5,256,256]{2,1,0:T(8,128)(2,1)}, u32[]{:S(2)}) copy-start(bf16[5,256,256]{2,1,0:T(8,128)(2,1)} %constant.32.clone.m_hbm.m_ref) | copy-start | bytes 1966084
  2.5 1.2 %copy-start.2 = (bf16[32,128,128]{2,1,0:T(8,128)(2,1)S(1)}, bf16[32,128,128]{2,1,0:T(8,128)(2,1)}, u32[]{:S(2)}) copy-start(bf16[32,128,128]{2,1,0:T(8,128)(2,1)} %x_hbm.1) | copy-start | bytes 3145732
  3.7 0.9 %copy-start.4 = (bf16[256,256]{1,0:T(8,128)(2,1)S(1)}, bf16[256,256]{1,0:T(8,128)(2,1)}, u32[]{:S(2)}) copy-start(bf16[256,256]{1,0:T(8,128)(2,1)} %constant.30.clone.p_ref) | copy-start | bytes 393220
  11.1 35.0 %copy-start.1 = (bf16[5,256,256]{2,1,0:T(8,128)(2,1)S(1)}, bf16[5,256,256]{2,1,0:T(8,128)(2,1)}, u32[]{:S(2)}) copy-start(bf16[5,256,256]{2,1,0:T(8,128)(2,1)} %constant.32.clone.m_hbm.m_ref) | copy-start | bytes 1966084
  11.1 34.9 %all-to-all-start = ((bf16[32,128,128]{2,1,0:T(8,128)(2,1)}), bf16[32,128,128]{2,1,0:T(8,128)(2,1)S(1)}, u32[]{:S(2)}, u32[]{:S(2)}) async-start(bf16[32,128,128]{2,1,0:T(8,128)(2,1)} %bitcast), calls=%async_computation | async-start | bytes 2097152 | tf_op jit(solution)/shard_map/all_to_all | solution.py:310
  18.4 0.7 copy-start.9
  19.1 1.8 %copy-start.8 = (f32[128]{0:T(128)S(1)}, f32[128]{0:T(128)}, u32[]{:S(2)}) copy-start(f32[128]{0:T(128)} %param.15) | copy-start | bytes 1540
  19.1 6.4 %collective-permute-start.3 = (f32[1,32]{1,0:T(1,128)S(1)}, f32[1,32]{1,0:T(1,128)S(1)}, u32[]{:S(2)}, u32[]{:S(2)}) collective-permute-start(f32[1,32]{1,0:T(1,128)S(1)} %bitcast.10), channel_id=1, source_target_pairs={{0,8},{8,0},{16,24},{24,16},{1,9},{9,1},{17,25},{25,17},{2,10},{10... | collective-permute-start | bytes 392 | tf_op jit(solution)/shard_map/ppermute | solution.py:274
  20.9 8.4 %collective-permute-start = (f32[1,128]{1,0:T(1,128)S(1)}, f32[1,128]{1,0:T(1,128)S(1)}, u32[]{:S(2)}, u32[]{:S(2)}) collective-permute-start(f32[1,128]{1,0:T(1,128)S(1)} %bitcast.9), channel_id=1, source_target_pairs={{0,1},{1,0},{2,3},{3,2},{4,5},{5,4},{6,7},{7,6},{8,9},{9,8},{10,11... | collective-permute-start | bytes 1544 | tf_op jit(solution)/shard_map/ppermute | solution.py:274
  25.5 3.7 %collective-permute-start.4 = (f32[2,32]{1,0:T(2,128)S(1)}, f32[2,32]{1,0:T(2,128)S(1)}, u32[]{:S(2)}, u32[]{:S(2)}) collective-permute-start(f32[2,32]{1,0:T(2,128)S(1)} %pad_maximum_fusion.4), channel_id=1, source_target_pairs={{0,16},{8,24},{16,0},{24,8},{1,17},{9,25},{17,1},{25,9},{2,18},{10... | collective-permute-start | bytes 776 | tf_op jit(solution)/shard_map/ppermute | solution.py:274
  29.3 6.9 %collective-permute-start.1 = (f32[2,128]{1,0:T(2,128)S(1)}, f32[2,128]{1,0:T(2,128)S(1)}, u32[]{:S(2)}, u32[]{:S(2)}) collective-permute-start(f32[2,128]{1,0:T(2,128)S(1)} %pad_maximum_fusion.3), channel_id=1, source_target_pairs={{0,2},{1,3},{2,0},{3,1},{4,6},{5,7},{6,4},{7,5},{8,10},{9,11},{10,... | collective-permute-start | bytes 3080 | tf_op jit(solution)/shard_map/ppermute | solution.py:274
  36.1 4.6 %copy-start.7 = (f32[128]{0:T(128)S(1)}, f32[128]{0:T(128)}, u32[]{:S(2)}) copy-start(f32[128]{0:T(128)} %constant.33.clone) | copy-start | bytes 1540
  36.2 8.6 %collective-permute-start.2 = (f32[4,128]{1,0:T(4,128)S(1)}, f32[4,128]{1,0:T(4,128)S(1)}, u32[]{:S(2)}, u32[]{:S(2)}) collective-permute-start(f32[4,128]{1,0:T(4,128)S(1)} %pad_maximum_fusion.1), channel_id=1, source_target_pairs={{0,4},{1,5},{2,6},{3,7},{4,0},{5,1},{6,2},{7,3},{8,12},{9,13},{10,... | collective-permute-start | bytes 6152 | tf_op jit(solution)/shard_map/ppermute | solution.py:274
  49.3 30.1 %copy-start.3 = (bf16[7,256,256]{2,1,0:T(8,128)(2,1)S(1)}, bf16[7,256,256]{2,1,0:T(8,128)(2,1)}, u32[]{:S(2)}) copy-start(bf16[7,256,256]{2,1,0:T(8,128)(2,1)} %constant.34.clone.m_ref) | copy-start | bytes 2752516
  49.3 30.1 %copy-start.5 = (bf16[256,256]{1,0:T(8,128)(2,1)S(1)}, bf16[256,256]{1,0:T(8,128)(2,1)}, u32[]{:S(2)}) copy-start(bf16[256,256]{1,0:T(8,128)(2,1)} %constant.30.clone.p_ref) | copy-start | bytes 393220

commit v4 on v3

--- a/solution.py
+++ b/solution.py
@@ -58,6 +58,54 @@
     found = np.zeros((256, 256), np.float32)
     found[rows, rows % 16 * 16 + rows // 16] = 1.0
     return found.astype(ml_dtypes.bfloat16)
+
+
+def cos_sin(angles):
+    turns = jnp.floor(angles * (2.0 / math.pi) + 0.5)
+    rest = angles - turns * 1.5703125
+    rest = rest - turns * 4.837512969970703125e-4
+    rest = rest - turns * 7.54978995489188e-8
+    square = rest * rest
+    sine = 1.0 / 362880.0
+    for factor in (-1.0 / 5040.0, 1.0 / 120.0, -1.0 / 6.0, 1.0):
+        sine = sine * square + factor
+    sine = sine * rest
+    cosine = -1.0 / 3628800.0
+    for factor in (1.0 / 40320.0, -1.0 / 720.0, 1.0 / 24.0, -0.5, 1.0):
+        cosine = cosine * square + factor
+    quarter = turns.astype(jnp.int32)
+    odd = (quarter & 1) == 1
+    first = jnp.where(odd, sine, cosine)
+    second = jnp.where(odd, cosine, sine)
+    first = jnp.where(((quarter + 1) & 2) == 2, -first, first)
+    second = jnp.where((quarter & 2) == 2, -second, second)
+    return first, second
+
+
+def node_row():
+    lanes = lax.broadcasted_iota(jnp.int32, (1, WIDE), 1) % HALF
+    points = [math.cos((2 * a + 1) * math.pi / 16) ** 2 for a in range(4)]
+
+    def square(at):
+        near = jnp.minimum(at, 7 - at)
+        value = jnp.full(near.shape, points[3], jnp.float32)
+        for a in range(3):
+            value = jnp.where(near == a, jnp.float32(points[a]), value)
+        return value
+
+    return square(lanes // 8) + square(lanes % 8)
+
+
+def rotation(column):
+    cosine, sine = cos_sin(column * node_row())
+    lanes = lax.broadcasted_iota(jnp.int32, cosine.shape, 1)
+    return cosine, jnp.where(lanes < HALF, -sine, sine)
+
+
+def column_of(row, count):
+    shape = (count, WIDE)
+    here = lax.broadcasted_iota(jnp.int32, shape, 0) == lax.broadcasted_iota(jnp.int32, shape, 1)
+    return jnp.sum(jnp.where(here, jnp.broadcast_to(row, shape), 0.0), axis=1, keepdims=True)
 
 
 def rotated(value, cosine, sine):
@@ -99,42 +147,66 @@
     return (slice(first * 16, first * 16 + 16), slice(second * 16, second * 16 + 16))
 
 
-def source_kernel(pieces, a_ref, x_hbm, m_hbm, p_ref, o_ref, x_ref, m_ref, x_sems, m_sems):
+BLOCK = 32
+NOTE = 8
+VMEM = pl.BlockSpec(memory_space=pltpu.VMEM)
+FAR = pl.BlockSpec(memory_space=pltpu.HBM)
+
+
+def params(mib):
+    return pltpu.CompilerParams(vmem_limit_bytes=mib << 20)
+
+
+def source_kernel(run, side, a_ref, d_ref, x_hbm, m_hbm, p_hbm, *rest):
+    outs, (x_ref, m_ref, p_ref, note_ref, x_sems, m_sems, p_sem) = rest[:-7], rest[-7:]
     rows, cols, _ = x_ref.shape
     levels = m_ref.shape[0]
-    each = rows // pieces
-    x_copies = [
-        pltpu.make_async_copy(
-            x_hbm.at[pl.ds(i * each, each)], x_ref.at[pl.ds(i * each, each)], x_sems.at[i]
+    starts = range(0, cols, BLOCK)
+    x_copies = []
+    for piece, start in enumerate(starts):
+        own = (slice(None), pl.ds(start, BLOCK))
+        x_copies.append(
+            pltpu.make_async_copy(x_hbm.at[own], x_ref.at[own], x_sems.at[piece])
         )
-        for i in range(pieces)
-    ]
     m_copies = [
         pltpu.make_async_copy(m_hbm.at[i], m_ref.at[i], m_sems.at[i]) for i in range(levels)
     ]
+    p_copy = pltpu.make_async_copy(p_hbm, p_ref, p_sem)
     m_copies[0].start()
     for copy in x_copies:
         copy.start()
     for copy in m_copies[1:]:
         copy.start()
-    angles = a_ref[...]
-    cosines = jnp.cos(angles)
-    lanes = lax.broadcasted_iota(jnp.int32, angles.shape, 1)
-    sines = jnp.where(lanes < HALF, -jnp.sin(angles), jnp.sin(angles))
-    block = 32
+    p_copy.start()
+
+    slowness = a_ref[...]
+    note_ref[...] = jnp.zeros_like(note_ref)
+    note_ref[0:1, :rows] = d_ref[...]
+    note_ref[3:4, :] = slowness
+    for at in (0, 3):
+        left = note_ref[at : at + 1, :]
+        for part in range(3):
+            piece = left.astype(jnp.bfloat16).astype(jnp.float32)
+            note_ref[at + part : at + part + 1, :] = piece
+            left = left - piece
+    note = note_ref[...].astype(jnp.bfloat16)
+    kept = (run - side) * rows
+    for device in range(outs[0].shape[0]):
+        outs[0][device, kept : kept + NOTE, :] = note
+
+    cosines, sines = rotation(column_of(slowness, cols))
     for level in range(levels):
         m_copies[level].wait()
-        if level == 0:
-            for copy in x_copies:
-                copy.wait()
-        for start in range(0, cols, block):
-            cosine, sine = cosines[start : start + block], sines[start : start + block]
+        for piece, start in enumerate(starts):
+            if level == 0:
+                x_copies[piece].wait()
+            cosine, sine = cosines[start : start + BLOCK], sines[start : start + BLOCK]
 
             def store(index, value):
-                x_ref[index, start : start + block, :] = value
+                x_ref[index, start : start + BLOCK, :] = value
 
             butterfly(
-                lambda index: x_ref[index, start : start + block, :],
+                lambda index: x_ref[index, start : start + BLOCK, :],
                 store,
                 rows,
                 1 << level,
@@ -144,8 +216,16 @@
             )
 
     def store_block(first, second, block):
-        o_ref[block_at(first, second)] = block
-
+        for inner in range(16):
+            device, col = divmod(first * 16 + inner, run)
+            begin = second * 16
+            if col < run - side:
+                begin += col * rows
+                outs[0][device, begin : begin + 16, :] = block[inner]
+            else:
+                outs[1][device * side + col - (run - side), begin : begin + 16, :] = block[inner]
+
+    p_copy.wait()
     swap_axes(
         lambda first, second: x_ref[block_at(first, second)],
         store_block,
@@ -155,44 +235,58 @@
     )
 
 
-VMEM = pl.BlockSpec(memory_space=pltpu.VMEM)
-PARAMS = pltpu.CompilerParams(vmem_limit_bytes=32 << 20)
-
-
-def source_levels(x, matrices, angles, shuffle):
+def source_levels(x, matrices, slowness, dip_field, shuffle, devices, run, side):
     rows, cols, _ = x.shape
-    pieces = 4
-    far = pl.BlockSpec(memory_space=pltpu.HBM)
+    out_shape = [jax.ShapeDtypeStruct((devices, (run - side) * rows + NOTE, WIDE), x.dtype)]
+    if side:
+        out_shape.append(jax.ShapeDtypeStruct((devices * side, rows, WIDE), x.dtype))
     return pl.pallas_call(
-        functools.partial(source_kernel, pieces),
-        out_shape=jax.ShapeDtypeStruct((cols, rows, WIDE), x.dtype),
-        in_specs=[VMEM, far, far, VMEM],
-        out_specs=VMEM,
+        functools.partial(source_kernel, run, side),
+        out_shape=out_shape,
+        in_specs=[VMEM, VMEM, FAR, FAR, FAR],
+        out_specs=[VMEM] * len(out_shape),
         scratch_shapes=[
             pltpu.VMEM(x.shape, x.dtype),
             pltpu.VMEM(matrices.shape, x.dtype),
-            pltpu.SemaphoreType.DMA((pieces,)),
+            pltpu.VMEM(shuffle.shape, x.dtype),
+            pltpu.VMEM((NOTE, WIDE), jnp.float32),
+            pltpu.SemaphoreType.DMA((cols // BLOCK,)),
             pltpu.SemaphoreType.DMA((matrices.shape[0],)),
+            pltpu.SemaphoreType.DMA,
         ],
-        compiler_params=PARAMS,
-    )(angles, x, matrices, shuffle)
-
-
-def middle_kernel(levels, rows, x_ref, m_ref, cs_ref, ss_ref, ct_ref, st_ref, o_ref):
+        compiler_params=params(60),
+    )(slowness[None, :], dip_field[None, :], x, matrices, shuffle)
+
+
+def middle_kernel(levels, rows, run, tgt_count, x_ref, m_ref, o_ref):
     count, total, _ = x_ref.shape
-    run = total // rows
-    tgt_count = cs_ref.shape[0] // run
+    kept = (total - NOTE) // rows
+    place = lax.axis_index("src") * tgt_count + lax.axis_index("tgt")
+
+    def noted(device, at):
+        note = x_ref[device, kept * rows :, :].astype(jnp.float32)
+        return note[at : at + 1] + note[at + 1 : at + 2] + note[at + 2 : at + 3]
+
+    slowness = jnp.concatenate([noted(at, 3) for at in range(tgt_count)], axis=0)
+    lanes = lax.broadcasted_iota(jnp.int32, slowness.shape, 1)
+    by_col = []
+    for col in range(kept):
+        picked = jnp.where(lanes == place * run + col, slowness, 0.0)
+        by_col.append(rotation(jnp.sum(picked, axis=1, keepdims=True)))
+    by_src = [
+        rotation(column_of(noted(at * tgt_count, 0), rows)) for at in range(count // tgt_count)
+    ]
+
     for step, (apart, by_source) in enumerate(levels):
         source = x_ref if step == 0 else o_ref
-        for col in range(run):
+        for col in range(kept):
             own = slice(col * rows, (col + 1) * rows)
 
             def phase_of(index):
                 if by_source:
-                    at = index % tgt_count * run + col
-                    return cs_ref[at : at + 1, :], ss_ref[at : at + 1, :]
-                at = index // tgt_count
-                return ct_ref[at], st_ref[at]
+                    at = index % tgt_count
+                    return tuple(table[at : at + 1, :] for table in by_col[col])
+                return by_src[index // tgt_count]
 
             def store(index, value):
                 o_ref[index, own, :] = value
@@ -208,31 +302,78 @@
             )
 
 
-def middle_levels(x, matrices, src_tables, tgt_tables, levels):
-    rows = tgt_tables[0].shape[1]
+def middle_levels(x, matrices, levels, rows, run, tgt_count):
+    count, total, _ = x.shape
     return pl.pallas_call(
-        functools.partial(middle_kernel, levels, rows),
+        functools.partial(middle_kernel, levels, rows, run, tgt_count),
+        out_shape=jax.ShapeDtypeStruct((count, total - NOTE, WIDE), x.dtype),
+        in_specs=[VMEM] * 2,
+        out_specs=VMEM,
+        compiler_params=params(32),
+    )(x, matrices)
+
+
+def pair_kernel(axis, bit, by_row, x_ref, y_ref, m_ref, c_ref, s_ref, o_ref):
+    count, rows, _ = x_ref.shape
+    matrix = m_ref[lax.rem(lax.div(lax.axis_index(axis), 1 << bit), 2)]
+    group = 16
+    for start in range(0, count, group):
+        picked = slice(start, start + group)
+        left = x_ref[picked].reshape(-1, WIDE)
+        right = y_ref[picked].reshape(-1, WIDE)
+        both = jnp.dot(
+            jnp.concatenate([left, right], axis=1), matrix, preferred_element_type=jnp.float32
+        )
+        for place in range(left.shape[0] // rows):
+            index = start + place
+            if by_row:
+                cosine, sine = c_ref[...], s_ref[...]
+            else:
+                cosine, sine = c_ref[index : index + 1, :], s_ref[index : index + 1, :]
+            o_ref[index] = rotated(both[place * rows : (place + 1) * rows], cosine, sine)
+
+
+def pair_level(x, axis, bit, matrix, angles, by_row):
+    count = lax.axis_size(axis)
+    other = lax.ppermute(x, axis, [(i, i ^ 1 << bit) for i in range(count)])
+    flipped = np.roll(matrix, (WIDE, WIDE), (0, 1))
+    halves = jnp.asarray(np.stack([matrix[:, :WIDE], flipped[:, :WIDE]]))
+    return pl.pallas_call(
+        functools.partial(pair_kernel, axis, bit, by_row),
         out_shape=jax.ShapeDtypeStruct(x.shape, x.dtype),
-        in_specs=[VMEM] * 6,
+        in_specs=[VMEM] * 5,
         out_specs=VMEM,
-        compiler_params=PARAMS,
-    )(x, matrices, *src_tables, *tgt_tables)
-
-
-def target_kernel(x_ref, m_ref, c_ref, s_ref, p_ref, o_ref, state_ref):
-    cols, rows, _ = x_ref.shape
+        compiler_params=params(32),
+    )(x, other, halves, *angles)
+
+
+def target_kernel(run, m_ref, c_ref, s_ref, p_ref, *rest):
+    xs, (o_ref, state_ref) = rest[:-2], rest[-2:]
+    cols, rows, _ = state_ref.shape
+    kept = xs[0].shape[1] // rows
+    side = run - kept
     levels = m_ref.shape[0]
+
+    def first(index, start):
+        device, col = divmod(index, run)
+        if col < kept:
+            start += col * rows
+            return xs[0][device, start : start + 16, :]
+        return xs[1][device * side + col - kept, start : start + 16, :]
+
     for level in range(levels):
-        source = x_ref if level == 0 else state_ref
         for start in range(0, rows, 16):
             own = slice(start, start + 16)
             cosine, sine = c_ref[own, :], s_ref[own, :]
 
+            def load(index):
+                return first(index, start) if level == 0 else state_ref[index, own, :]
+
             def store(index, value):
                 state_ref[index, own, :] = value
 
             butterfly(
-                lambda index: source[index, own, :],
+                load,
                 store,
                 cols,
                 1 << (levels - 1 - level),
@@ -253,31 +394,15 @@
     )
 
 
-def target_levels(x, matrices, cosine, sine, shuffle):
-    cols, rows, _ = x.shape
+def target_levels(states, matrices, angles, shuffle, cols, rows, run):
     return pl.pallas_call(
-        target_kernel,
-        out_shape=jax.ShapeDtypeStruct((rows, cols, WIDE), x.dtype),
-        in_specs=[VMEM] * 5,
+        functools.partial(target_kernel, run),
+        out_shape=jax.ShapeDtypeStruct((rows, cols, WIDE), jnp.bfloat16),
+        in_specs=[VMEM] * (4 + len(states)),
         out_specs=VMEM,
-        scratch_shapes=[pltpu.VMEM(x.shape, x.dtype)],
-        compiler_params=PARAMS,
-    )(x, matrices, cosine, sine, shuffle)
-
-
-def gathered(values, axis):
-    count = lax.axis_size(axis)
-    place = lax.axis_index(axis)
-    values = values[None]
-    apart = 1
-    while apart < count:
-        other = lax.ppermute(values, axis, [(i, i ^ apart) for i in range(count)])
-        mine_first = (place & apart) == 0
-        values = jnp.concatenate(
-            [jnp.where(mine_first, values, other), jnp.where(mine_first, other, values)]
-        )
-        apart *= 2
-    return values
+        scratch_shapes=[pltpu.VMEM((cols, rows, WIDE), jnp.bfloat16)],
+        compiler_params=params(32),
+    )(matrices, *angles, shuffle, *states)
 
 
 def local(box_weights, slowness, dip_field):
@@ -295,35 +420,40 @@
         return jnp.asarray(np.stack(matrices[low:high]))
 
     run = cols // devices
-    place = lax.axis_index("src") * tgt_count + lax.axis_index("tgt")
+    side = run // 4
     shuffle = jnp.asarray(shuffle_matrix())
 
-    angles = slowness[:, None] * np.tile(node_weights(), 2)
-    state = source_levels(box_weights, matrices_of(0, row_bits), angles, shuffle)
-
-    state, slowness, dip_field = lax.optimization_barrier((state, slowness, dip_field))
-    all_dip = gathered(dip_field, "src")
-    all_slowness = gathered(slowness, "tgt")
-    run_slowness = lax.dynamic_slice_in_dim(all_slowness, place * run, run, 1)
-
-    state = state.reshape(devices, run * rows, WIDE)
-    state = lax.all_to_all(state, ("src", "tgt"), 0, 0, tiled=True)
+    states = source_levels(
+        box_weights, matrices_of(0, row_bits), slowness, dip_field, shuffle, devices, run, side
+    )
+    *states, slowness, dip_field = lax.optimization_barrier((*states, slowness, dip_field))
+    by_row = tables(dip_field)
+
+    if side:
+        kept = slowness.reshape(devices, run)[:, run - side :].reshape(-1)
+        by_col = tables(kept)
+        stay = states[1]
+        for bit in range(src_bits):
+            stay = pair_level(stay, "src", bit, matrices[row_bits + bit], by_col, False)
+        for at, bit in enumerate(reversed(range(tgt_bits))):
+            stay = pair_level(stay, "tgt", bit, matrices[first_target + at], by_row, True)
+
     levels = [(tgt_count << bit, True) for bit in range(src_bits)]
     levels += [(1 << bit, False) for bit in reversed(range(tgt_bits))]
+    state = lax.all_to_all(states[0], ("src", "tgt"), 0, 0, tiled=True)
     state = middle_levels(
-        state,
-        matrices_of(row_bits, first_target + tgt_bits),
-        tables(run_slowness.reshape(-1)),
-        tables(all_dip),
-        levels,
+        state, matrices_of(row_bits, first_target + tgt_bits), levels, rows, run, tgt_count
     )
     state = lax.all_to_all(state, ("src", "tgt"), 0, 0, tiled=True)
 
     return target_levels(
-        state.reshape(cols, rows, WIDE),
+        [state, stay] if side else [state],
         matrices_of(first_target + tgt_bits, total),
-        *tables(dip_field),
+        by_row,
         shuffle,
+        cols,
+        rows,
+        run,
     )
 
 

time: 85.9 us -> 99.2 us (1.15)
  waiting for transfers between devices: 16.2 us -> 38.3 us
  starting transfers between devices: 17.3 us -> 9.58 us
  local copies, waits for them, and re-layouts: 4.7 us -> 0.81 us
  Pallas kernels: 15.8 us -> 19.1 us
  other arithmetic: 1.32 us -> 0.19 us
    ppermute x5, waiting for transfers between devices: 15.2 us -> 38.3 us  [pair_level(): other = lax.ppermute(x, axis, [(i, i ^ 1 << bit) for i in range(count)])]
    all_to_all x1, starting transfers between devices: 7.3 us -> 2.94 us  [local(): state = lax.all_to_all(state, ('src', 'tgt'), 0, 0, tiled=True)]
    unnamed x20 -> x26, local copies, waits for them, and re-layouts: 4.54 us -> 0.54 us
    ppermute x5, starting transfers between devices: 10 us -> 6.65 us  [pair_level(): other = lax.ppermute(x, axis, [(i, i ^ 1 << bit) for i in range(count)])]
    pallas_call x3 -> x8, Pallas kernels: 15.8 us -> 19.1 us  [the longest x1 7.73 us: source_levels(): pl.pallas_call(functools.partial(source_kernel, run, side), out_shape=out...]
  transfers between devices with their start and end apart: 6 -> 6, of which waited for: 5 -> 5; matrix products, arithmetic and copies ran while one was open for 1% -> 0% of each run, Pallas kernels for 0% -> 2%
where the time goes in v4:
time: 99.2 us; the launch traced here: 98.9 us
  waiting for transfers between devices  38.3 us (39%)
  blocking collectives  30.7 us (31%)
  Pallas kernels  19.1 us (19%)
  starting transfers between devices  9.58 us (10%)
    ppermute x5, waiting for transfers between devices, pair_level(): other = lax.ppermute(x, axis, [(i, i ^ 1 << bit) for i in range(count)])  38.3 us
    all_to_all x1, blocking collectives, local(): state = lax.all_to_all(states[0], ('src', 'tgt'), 0, 0, tiled=True)  30.7 us
    pallas_call x1, Pallas kernels, source_levels(): pl.pallas_call(functools.partial(source_kernel, run, side), out_shape=out...  7.73 us
    ppermute x5, starting transfers between devices, pair_level(): other = lax.ppermute(x, axis, [(i, i ^ 1 << bit) for i in range(count)])  6.65 us
    pallas_call x1, Pallas kernels, target_levels(): pl.pallas_call(functools.partial(target_kernel, run), out_shape=jax.Shape...  6.1 us
    pallas_call x1, Pallas kernels, middle_levels(): pl.pallas_call(functools.partial(middle_kernel, levels, rows, run, tgt_co...  3.4 us
    all_to_all x1, starting transfers between devices, local(): state = lax.all_to_all(state, ('src', 'tgt'), 0, 0, tiled=True)  2.94 us
  transfers between devices with their start and end apart: 6, of which 5 were waited for; matrix products, arithmetic and copies ran while one was open for 0% of the time, Pallas kernels for 2%

profile of v4, /device:TPU:0, one launch (start us, length us, event | category | flops | bytes accessed | tf_op | source)
XLA Modules:
  0.0 98.9 jit_solution(13784051149547478442)
XLA Ops:
  0.0 7.7 %shard_map.154 = (bf16[32,104,128]{2,1,0:T(8,128)(2,1)}, bf16[32,32,128]{2,1,0:T(8,128)(2,1)}) custom-call(f32[1,128]{1,0:T(1,128)} %bitcast.3, f32[1,32]{1,0:T(1,128)} %bitcast.2, bf16[32,128,128]{2,1,0:T(8,128)(2,1)} %x_hbm.1, bf16[5,256,256]{2,1,0:T(8,128)(2,1)} %constant.21.clone.m_hbm.m_ref, bf16[256,256]{1,0:T(8,128)(2,1)} %constant.20.clone.p_hbm.p_ref), custom_call_target="tpu_custom_call" | custom-call | tf_op jit(solution)/shard_map/pallas_call | solution.py:243
  7.7 0.0 copy-start
  7.7 30.7 %all_to_all.10.x_ref = bf16[32,104,128]{2,1,0:T(8,128)(2,1)S(1)} all-to-all(bf16[32,104,128]{2,1,0:T(8,128)(2,1)} %get-tuple-element.14), channel_id=1, replica_groups=mesh['src'=4,'tgt'=8] {'src','tgt'}, dimensions={0} | all-to-all | bytes 1703936 | tf_op jit(solution)/shard_map/all_to_all | solution.py:443
  38.5 3.4 %shard_map.155 = bf16[32,96,128]{2,1,0:T(8,128)(2,1)} custom-call(bf16[32,104,128]{2,1,0:T(8,128)(2,1)S(1)} %all_to_all.10.x_ref, bf16[5,256,256]{2,1,0:T(8,128)(2,1)S(1)} %copy-done), custom_call_target="tpu_custom_call" | custom-call | tf_op jit(solution)/shard_map/pallas_call | solution.py:307
  41.9 2.9 %all-to-all-start.1 = ((bf16[32,96,128]{2,1,0:T(8,128)(2,1)}), bf16[32,96,128]{2,1,0:T(8,128)(2,1)S(1)}, u32[]{:S(2)}, u32[]{:S(2)}) async-start(bf16[32,96,128]{2,1,0:T(8,128)(2,1)} %shard_map.155), calls=%async_computation.1 | async-start | bytes 1572864 | tf_op jit(solution)/shard_map/all_to_all | solution.py:447
  44.8 1.5 %collective-permute-start = (bf16[32,32,128]{2,1,0:T(8,128)(2,1)S(1)}, bf16[32,32,128]{2,1,0:T(8,128)(2,1)S(1)}, u32[]{:S(2)}, u32[]{:S(2)}) collective-permute-start(bf16[32,32,128]{2,1,0:T(8,128)(2,1)S(1)} %copy-done.3), channel_id=1, source_target_pairs={{0,8},{8,0},{16,24},{24,16},{1,9},{9,1},{17,25},{25,17},{2,10},{10... | collective-permute-start | bytes 786440 | tf_op jit(solution)/shard_map/ppermute | solution.py:338
  46.4 0.1 reshape.8
  46.5 0.0 copy-start.11
  46.5 0.0 copy-start.12
  46.5 0.2 slice_reduce_fusion
  46.7 0.4 copy-done.9
  47.1 0.0 copy-done.11
  47.1 0.0 copy-done.12
  47.1 0.2 fusion.1
  47.3 12.0 %collective-permute-done.y_ref = bf16[32,32,128]{2,1,0:T(8,128)(2,1)S(1)} collective-permute-done((bf16[32,32,128]{2,1,0:T(8,128)(2,1)S(1)}, bf16[32,32,128]{2,1,0:T(8,128)(2,1)S(1)}, u32[]{:S(2)}, u32[]{:S(2)}) %collective-permute-start) | collective-permute-done | bytes 262176 | tf_op jit(solution)/shard_map/ppermute | solution.py:338
  59.3 0.4 shard_map.156.x_ref
  59.7 0.0 copy-start.6
  59.7 1.6 %collective-permute-start.1 = (bf16[32,32,128]{2,1,0:T(8,128)(2,1)S(1)}, bf16[32,32,128]{2,1,0:T(8,128)(2,1)S(1)}, u32[]{:S(2)}, u32[]{:S(2)}) collective-permute-start(bf16[32,32,128]{2,1,0:T(8,128)(2,1)S(1)} %shard_map.156.x_ref), channel_id=1, source_target_pairs={{0,16},{8,24},{16,0},{24,8},{1,17},{9,25},{17,1},{25,9},{2,18},{10... | collective-permute-start | bytes 786440 | tf_op jit(solution)/shard_map/ppermute | solution.py:338
  61.3 7.4 %collective-permute-done.1.y_ref = bf16[32,32,128]{2,1,0:T(8,128)(2,1)S(1)} collective-permute-done((bf16[32,32,128]{2,1,0:T(8,128)(2,1)S(1)}, bf16[32,32,128]{2,1,0:T(8,128)(2,1)S(1)}, u32[]{:S(2)}, u32[]{:S(2)}) %collective-permute-start.1) | collective-permute-done | bytes 262176 | tf_op jit(solution)/shard_map/ppermute | solution.py:338
  68.7 0.4 shard_map.157.x_ref
  69.1 2.7 %collective-permute-start.2 = (bf16[32,32,128]{2,1,0:T(8,128)(2,1)S(1)}, bf16[32,32,128]{2,1,0:T(8,128)(2,1)S(1)}, u32[]{:S(2)}, u32[]{:S(2)}) collective-permute-start(bf16[32,32,128]{2,1,0:T(8,128)(2,1)S(1)} %shard_map.157.x_ref), channel_id=1, source_target_pairs={{0,4},{1,5},{2,6},{3,7},{4,0},{5,1},{6,2},{7,3},{8,12},{9,13},{10,... | collective-permute-start | bytes 786440 | tf_op jit(solution)/shard_map/ppermute | solution.py:338
  71.7 10.9 %collective-permute-done.2.y_ref = bf16[32,32,128]{2,1,0:T(8,128)(2,1)S(1)} collective-permute-done((bf16[32,32,128]{2,1,0:T(8,128)(2,1)S(1)}, bf16[32,32,128]{2,1,0:T(8,128)(2,1)S(1)}, u32[]{:S(2)}, u32[]{:S(2)}) %collective-permute-start.2) | collective-permute-done | bytes 262176 | tf_op jit(solution)/shard_map/ppermute | solution.py:338
  82.7 0.4 shard_map.158.x_ref
  83.1 0.0 copy-start.1
  83.1 0.8 collective-permute-start.3
  83.9 6.5 %collective-permute-done.3.y_ref = bf16[32,32,128]{2,1,0:T(8,128)(2,1)S(1)} collective-permute-done((bf16[32,32,128]{2,1,0:T(8,128)(2,1)S(1)}, bf16[32,32,128]{2,1,0:T(8,128)(2,1)S(1)}, u32[]{:S(2)}, u32[]{:S(2)}) %collective-permute-start.3) | collective-permute-done | bytes 262176 | tf_op jit(solution)/shard_map/ppermute | solution.py:338
  90.4 0.4 shard_map.159.x_ref
  90.8 0.0 copy-start.2
  90.8 0.1 collective-permute-start.4
  90.8 1.5 %collective-permute-done.4.y_ref = bf16[32,32,128]{2,1,0:T(8,128)(2,1)S(1)} collective-permute-done((bf16[32,32,128]{2,1,0:T(8,128)(2,1)S(1)}, bf16[32,32,128]{2,1,0:T(8,128)(2,1)S(1)}, u32[]{:S(2)}, u32[]{:S(2)}) %collective-permute-start.4) | collective-permute-done | bytes 262176 | tf_op jit(solution)/shard_map/ppermute | solution.py:338
  92.4 0.4 shard_map.160.rest_1_
  92.8 6.1 %shard_map.161 = bf16[32,128,128]{2,1,0:T(8,128)(2,1)} custom-call(bf16[7,256,256]{2,1,0:T(8,128)(2,1)S(1)} %copy-done.1, f32[32,128]{1,0:T(8,128)S(1)} %get-tuple-element.19.c_ref, f32[32,128]{1,0:T(8,128)S(1)} %get-tuple-element.18.s_ref, bf16[256,256]{1,0:T(8,128)(2,1)S(1)} %copy-done.2, bf16[32,96,128]{2,1,0:T(8,128)(2,1)S(1)} %all-to-all-done.1.rest_0_, ...), custom_call_target="tpu_custom_call" | custom-call | tf_op jit(solution)/shard_map/pallas_call | solution.py:398
  (18 shorter events, 0.0 us)
Async XLA Ops:
  7.7 30.7 %copy-start = (bf16[5,256,256]{2,1,0:T(8,128)(2,1)S(1)}, bf16[5,256,256]{2,1,0:T(8,128)(2,1)}, u32[]{:S(2)}) copy-start(bf16[5,256,256]{2,1,0:T(8,128)(2,1)} %constant.21.clone.m_hbm.m_ref) | copy-start | bytes 1966084
  41.9 3.0 %copy-start.3 = (bf16[32,32,128]{2,1,0:T(8,128)(2,1)S(1)}, bf16[32,32,128]{2,1,0:T(8,128)(2,1)}, u32[]{:S(2)}) copy-start(bf16[32,32,128]{2,1,0:T(8,128)(2,1)} %get-tuple-element.15.x_ref) | copy-start | bytes 786436
  41.9 4.5 %copy-start.10 = (f32[128]{0:T(128)S(1)}, f32[128]{0:T(128)}, u32[]{:S(2)}) copy-start(f32[128]{0:T(128)} %param.17) | copy-start | bytes 1540
  41.9 17.4 %copy-start.8 = (bf16[2,256,128]{2,1,0:T(8,128)(2,1)S(1)}, bf16[2,256,128]{2,1,0:T(8,128)(2,1)}, u32[]{:S(2)}) copy-start(bf16[2,256,128]{2,1,0:T(8,128)(2,1)} %constant.24.clone.m_ref) | copy-start | bytes 393220
  41.9 50.9 %all-to-all-start.1 = ((bf16[32,96,128]{2,1,0:T(8,128)(2,1)}), bf16[32,96,128]{2,1,0:T(8,128)(2,1)S(1)}, u32[]{:S(2)}, u32[]{:S(2)}) async-start(bf16[32,96,128]{2,1,0:T(8,128)(2,1)} %shard_map.155), calls=%async_computation.1 | async-start | bytes 1572864 | tf_op jit(solution)/shard_map/all_to_all | solution.py:447
  44.8 14.5 %collective-permute-start = (bf16[32,32,128]{2,1,0:T(8,128)(2,1)S(1)}, bf16[32,32,128]{2,1,0:T(8,128)(2,1)S(1)}, u32[]{:S(2)}, u32[]{:S(2)}) collective-permute-start(bf16[32,32,128]{2,1,0:T(8,128)(2,1)S(1)} %copy-done.3), channel_id=1, source_target_pairs={{0,8},{8,0},{16,24},{24,16},{1,9},{9,1},{17,25},{25,17},{2,10},{10... | collective-permute-start | bytes 786440 | tf_op jit(solution)/shard_map/ppermute | solution.py:338
  46.5 0.7 copy-start.9
  46.5 0.7 copy-start.11
  46.5 0.7 copy-start.12
  59.3 9.4 %copy-start.7 = (bf16[2,256,128]{2,1,0:T(8,128)(2,1)S(1)}, bf16[2,256,128]{2,1,0:T(8,128)(2,1)}, u32[]{:S(2)}) copy-start(bf16[2,256,128]{2,1,0:T(8,128)(2,1)} %constant.25.clone.m_ref) | copy-start | bytes 393220
  59.7 23.0 %copy-start.6 = (bf16[2,256,128]{2,1,0:T(8,128)(2,1)S(1)}, bf16[2,256,128]{2,1,0:T(8,128)(2,1)}, u32[]{:S(2)}) copy-start(bf16[2,256,128]{2,1,0:T(8,128)(2,1)} %constant.26.clone.m_ref) | copy-start | bytes 393220
  59.7 9.0 %collective-permute-start.1 = (bf16[32,32,128]{2,1,0:T(8,128)(2,1)S(1)}, bf16[32,32,128]{2,1,0:T(8,128)(2,1)S(1)}, u32[]{:S(2)}, u32[]{:S(2)}) collective-permute-start(bf16[32,32,128]{2,1,0:T(8,128)(2,1)S(1)} %shard_map.156.x_ref), channel_id=1, source_target_pairs={{0,16},{8,24},{16,0},{24,8},{1,17},{9,25},{17,1},{25,9},{2,18},{10... | collective-permute-start | bytes 786440 | tf_op jit(solution)/shard_map/ppermute | solution.py:338
  69.1 13.6 %collective-permute-start.2 = (bf16[32,32,128]{2,1,0:T(8,128)(2,1)S(1)}, bf16[32,32,128]{2,1,0:T(8,128)(2,1)S(1)}, u32[]{:S(2)}, u32[]{:S(2)}) collective-permute-start(bf16[32,32,128]{2,1,0:T(8,128)(2,1)S(1)} %shard_map.157.x_ref), channel_id=1, source_target_pairs={{0,4},{1,5},{2,6},{3,7},{4,0},{5,1},{6,2},{7,3},{8,12},{9,13},{10,... | collective-permute-start | bytes 786440 | tf_op jit(solution)/shard_map/ppermute | solution.py:338
  82.7 7.7 %copy-start.5 = (bf16[2,256,128]{2,1,0:T(8,128)(2,1)S(1)}, bf16[2,256,128]{2,1,0:T(8,128)(2,1)}, u32[]{:S(2)}) copy-start(bf16[2,256,128]{2,1,0:T(8,128)(2,1)} %constant.27.clone.m_ref) | copy-start | bytes 393220
  82.7 9.7 %copy-start.4 = (bf16[2,256,128]{2,1,0:T(8,128)(2,1)S(1)}, bf16[2,256,128]{2,1,0:T(8,128)(2,1)}, u32[]{:S(2)}) copy-start(bf16[2,256,128]{2,1,0:T(8,128)(2,1)} %constant.28.clone.m_ref) | copy-start | bytes 393220
  83.1 9.7 %copy-start.1 = (bf16[7,256,256]{2,1,0:T(8,128)(2,1)S(1)}, bf16[7,256,256]{2,1,0:T(8,128)(2,1)}, u32[]{:S(2)}) copy-start(bf16[7,256,256]{2,1,0:T(8,128)(2,1)} %constant.29.clone.m_ref) | copy-start | bytes 2752516
  83.1 7.3 %collective-permute-start.3 = (bf16[32,32,128]{2,1,0:T(8,128)(2,1)S(1)}, bf16[32,32,128]{2,1,0:T(8,128)(2,1)S(1)}, u32[]{:S(2)}, u32[]{:S(2)}) collective-permute-start(bf16[32,32,128]{2,1,0:T(8,128)(2,1)S(1)} %shard_map.158.x_ref), channel_id=1, source_target_pairs={{0,2},{1,3},{2,0},{3,1},{4,6},{5,7},{6,4},{7,5},{8,10},{9,11},{10,... | collective-permute-start | bytes 786440 | tf_op jit(solution)/shard_map/ppermute | solution.py:338
  90.8 2.0 %copy-start.2 = (bf16[256,256]{1,0:T(8,128)(2,1)S(1)}, bf16[256,256]{1,0:T(8,128)(2,1)}, u32[]{:S(2)}) copy-start(bf16[256,256]{1,0:T(8,128)(2,1)} %constant.20.clone.p_hbm.p_ref) | copy-start | bytes 393220
  90.8 1.6 %collective-permute-start.4 = (bf16[32,32,128]{2,1,0:T(8,128)(2,1)S(1)}, bf16[32,32,128]{2,1,0:T(8,128)(2,1)S(1)}, u32[]{:S(2)}, u32[]{:S(2)}) collective-permute-start(bf16[32,32,128]{2,1,0:T(8,128)(2,1)S(1)} %shard_map.159.x_ref), channel_id=1, source_target_pairs={{0,1},{1,0},{2,3},{3,2},{4,5},{5,4},{6,7},{7,6},{8,9},{9,8},{10,11... | collective-permute-start | bytes 786440 | tf_op jit(solution)/shard_map/ppermute | solution.py:338

commit v5 on v4

--- a/solution.py
+++ b/solution.py
@@ -429,18 +429,19 @@
     *states, slowness, dip_field = lax.optimization_barrier((*states, slowness, dip_field))
     by_row = tables(dip_field)
 
+    state = lax.all_to_all(states[0], ("src", "tgt"), 0, 0, tiled=True)
     if side:
         kept = slowness.reshape(devices, run)[:, run - side :].reshape(-1)
         by_col = tables(kept)
         stay = states[1]
         for bit in range(src_bits):
             stay = pair_level(stay, "src", bit, matrices[row_bits + bit], by_col, False)
+        state, stay = lax.optimization_barrier((state, stay))
         for at, bit in enumerate(reversed(range(tgt_bits))):
             stay = pair_level(stay, "tgt", bit, matrices[first_target + at], by_row, True)
 
     levels = [(tgt_count << bit, True) for bit in range(src_bits)]
     levels += [(1 << bit, False) for bit in reversed(range(tgt_bits))]
-    state = lax.all_to_all(states[0], ("src", "tgt"), 0, 0, tiled=True)
     state = middle_levels(
         state, matrices_of(row_bits, first_target + tgt_bits), levels, rows, run, tgt_count
     )

time: 99.2 us -> 98 us (0.988)
  blocking collectives: 30.7 us -> 0 us
  waiting for transfers between devices: 38.3 us -> 58.6 us
  starting transfers between devices: 9.58 us -> 18.8 us
    all_to_all x1 -> x0, blocking collectives: 30.7 us -> none  [local(): state = lax.all_to_all(states[0], ('src', 'tgt'), 0, 0, tiled=True)]
    ppermute x5, waiting for transfers between devices: 38.3 us -> 58.5 us  [pair_level(): other = lax.ppermute(x, axis, [(i, i ^ 1 << bit) for i in range(count)])]
    all_to_all x0 -> x1, starting transfers between devices: none -> 7.32 us  [local(): state = lax.all_to_all(states[0], ('src', 'tgt'), 0, 0, tiled=True)]
    all_to_all x1, starting transfers between devices: 2.94 us -> 5.47 us  [local(): state = lax.all_to_all(state, ('src', 'tgt'), 0, 0, tiled=True)]
  transfers between devices with their start and end apart: 6 -> 7, of which waited for: 5 -> 5; matrix products, arithmetic and copies ran while one was open for 0% -> 0% of each run, Pallas kernels for 2% -> 2%
where the time goes in v5:
time: 98 us; the launch traced here: 97.7 us
  waiting for transfers between devices  58.6 us (60%)
  Pallas kernels  19.1 us (19%)
  starting transfers between devices  18.8 us (19%)
    ppermute x5, waiting for transfers between devices, pair_level(): other = lax.ppermute(x, axis, [(i, i ^ 1 << bit) for i in range(count)])  58.5 us
    pallas_call x1, Pallas kernels, source_levels(): pl.pallas_call(functools.partial(source_kernel, run, side), out_shape=out...  7.73 us
    all_to_all x1, starting transfers between devices, local(): state = lax.all_to_all(states[0], ('src', 'tgt'), 0, 0, tiled=True)  7.32 us
    pallas_call x1, Pallas kernels, target_levels(): pl.pallas_call(functools.partial(target_kernel, run), out_shape=jax.Shape...  6.1 us
    ppermute x5, starting transfers between devices, pair_level(): other = lax.ppermute(x, axis, [(i, i ^ 1 << bit) for i in range(count)])  6.05 us
    all_to_all x1, starting transfers between devices, local(): state = lax.all_to_all(state, ('src', 'tgt'), 0, 0, tiled=True)  5.47 us
    pallas_call x1, Pallas kernels, middle_levels(): pl.pallas_call(functools.partial(middle_kernel, levels, rows, run, tgt_co...  3.4 us
  transfers between devices with their start and end apart: 7, of which 5 were waited for; matrix products, arithmetic and copies ran while one was open for 0% of the time, Pallas kernels for 2%

profile of v5, /device:TPU:0, one launch (start us, length us, event | category | flops | bytes accessed | tf_op | source)
XLA Modules:
  0.0 97.7 jit_solution(10596978946290326526)
XLA Ops:
  0.0 7.7 %shard_map.154 = (bf16[32,104,128]{2,1,0:T(8,128)(2,1)}, bf16[32,32,128]{2,1,0:T(8,128)(2,1)}) custom-call(f32[1,128]{1,0:T(1,128)} %bitcast.3, f32[1,32]{1,0:T(1,128)} %bitcast.2, bf16[32,128,128]{2,1,0:T(8,128)(2,1)} %x_hbm.1, bf16[5,256,256]{2,1,0:T(8,128)(2,1)} %constant.21.clone.m_hbm.m_ref, bf16[256,256]{1,0:T(8,128)(2,1)} %constant.20.clone.p_hbm.p_ref), custom_call_target="tpu_custom_call" | custom-call | tf_op jit(solution)/shard_map/pallas_call | solution.py:243
  7.8 0.0 copy-start.8
  7.8 7.3 %all-to-all-start = ((bf16[32,104,128]{2,1,0:T(8,128)(2,1)}), bf16[32,104,128]{2,1,0:T(8,128)(2,1)S(1)}, u32[]{:S(2)}, u32[]{:S(2)}) async-start(bf16[32,104,128]{2,1,0:T(8,128)(2,1)} %get-tuple-element.16), calls=%async_computation | async-start | bytes 1703936 | tf_op jit(solution)/shard_map/all_to_all | solution.py:432
  15.1 1.8 %collective-permute-start = (bf16[32,32,128]{2,1,0:T(8,128)(2,1)S(1)}, bf16[32,32,128]{2,1,0:T(8,128)(2,1)S(1)}, u32[]{:S(2)}, u32[]{:S(2)}) collective-permute-start(bf16[32,32,128]{2,1,0:T(8,128)(2,1)S(1)} %copy-done.3), channel_id=1, source_target_pairs={{0,8},{8,0},{16,24},{24,16},{1,9},{9,1},{17,25},{25,17},{2,10},{10... | collective-permute-start | bytes 786440 | tf_op jit(solution)/shard_map/ppermute | solution.py:338
  16.9 0.1 reshape.8
  17.1 0.0 copy-start.11
  17.1 0.0 copy-start.12
  17.1 0.2 slice_reduce_fusion
  17.3 0.4 copy-done.9
  17.7 0.0 copy-done.11
  17.7 0.0 copy-done.12
  17.7 0.2 fusion.1
  17.9 12.5 %collective-permute-done.y_ref = bf16[32,32,128]{2,1,0:T(8,128)(2,1)S(1)} collective-permute-done((bf16[32,32,128]{2,1,0:T(8,128)(2,1)S(1)}, bf16[32,32,128]{2,1,0:T(8,128)(2,1)S(1)}, u32[]{:S(2)}, u32[]{:S(2)}) %collective-permute-start) | collective-permute-done | bytes 262176 | tf_op jit(solution)/shard_map/ppermute | solution.py:338
  30.5 0.4 shard_map.155.x_ref
  30.8 0.0 copy-start
  30.9 1.5 %collective-permute-start.1 = (bf16[32,32,128]{2,1,0:T(8,128)(2,1)S(1)}, bf16[32,32,128]{2,1,0:T(8,128)(2,1)S(1)}, u32[]{:S(2)}, u32[]{:S(2)}) collective-permute-start(bf16[32,32,128]{2,1,0:T(8,128)(2,1)S(1)} %shard_map.155.x_ref), channel_id=1, source_target_pairs={{0,16},{8,24},{16,0},{24,8},{1,17},{9,25},{17,1},{25,9},{2,18},{10... | collective-permute-start | bytes 786440 | tf_op jit(solution)/shard_map/ppermute | solution.py:338
  32.4 7.6 %collective-permute-done.1.y_ref = bf16[32,32,128]{2,1,0:T(8,128)(2,1)S(1)} collective-permute-done((bf16[32,32,128]{2,1,0:T(8,128)(2,1)S(1)}, bf16[32,32,128]{2,1,0:T(8,128)(2,1)S(1)}, u32[]{:S(2)}, u32[]{:S(2)}) %collective-permute-start.1) | collective-permute-done | bytes 262176 | tf_op jit(solution)/shard_map/ppermute | solution.py:338
  39.9 0.4 shard_map.156.x_ref
  40.3 3.4 %shard_map.157 = bf16[32,96,128]{2,1,0:T(8,128)(2,1)} custom-call(bf16[32,104,128]{2,1,0:T(8,128)(2,1)S(1)} %all-to-all-done.x_ref, bf16[5,256,256]{2,1,0:T(8,128)(2,1)S(1)} %copy-done), custom_call_target="tpu_custom_call" | custom-call | tf_op jit(solution)/shard_map/pallas_call | solution.py:307
  43.7 5.5 %all-to-all-start.1 = ((bf16[32,96,128]{2,1,0:T(8,128)(2,1)}), bf16[32,96,128]{2,1,0:T(8,128)(2,1)S(1)}, u32[]{:S(2)}, u32[]{:S(2)}) async-start(bf16[32,96,128]{2,1,0:T(8,128)(2,1)} %shard_map.157), calls=%async_computation.1 | async-start | bytes 1572864 | tf_op jit(solution)/shard_map/all_to_all | solution.py:448
  49.2 2.6 %collective-permute-start.2 = (bf16[32,32,128]{2,1,0:T(8,128)(2,1)S(1)}, bf16[32,32,128]{2,1,0:T(8,128)(2,1)S(1)}, u32[]{:S(2)}, u32[]{:S(2)}) collective-permute-start(bf16[32,32,128]{2,1,0:T(8,128)(2,1)S(1)} %shard_map.156.x_ref), channel_id=1, source_target_pairs={{0,4},{1,5},{2,6},{3,7},{4,0},{5,1},{6,2},{7,3},{8,12},{9,13},{10,... | collective-permute-start | bytes 786440 | tf_op jit(solution)/shard_map/ppermute | solution.py:338
  51.8 29.1 %collective-permute-done.2.y_ref = bf16[32,32,128]{2,1,0:T(8,128)(2,1)S(1)} collective-permute-done((bf16[32,32,128]{2,1,0:T(8,128)(2,1)S(1)}, bf16[32,32,128]{2,1,0:T(8,128)(2,1)S(1)}, u32[]{:S(2)}, u32[]{:S(2)}) %collective-permute-start.2) | collective-permute-done | bytes 262176 | tf_op jit(solution)/shard_map/ppermute | solution.py:338
  80.9 0.4 shard_map.158.x_ref
  81.3 0.0 copy-start.1
  81.3 0.1 collective-permute-start.3
  81.3 7.8 %collective-permute-done.3.y_ref = bf16[32,32,128]{2,1,0:T(8,128)(2,1)S(1)} collective-permute-done((bf16[32,32,128]{2,1,0:T(8,128)(2,1)S(1)}, bf16[32,32,128]{2,1,0:T(8,128)(2,1)S(1)}, u32[]{:S(2)}, u32[]{:S(2)}) %collective-permute-start.3) | collective-permute-done | bytes 262176 | tf_op jit(solution)/shard_map/ppermute | solution.py:338
  89.2 0.4 shard_map.159.x_ref
  89.6 0.0 copy-start.2
  89.6 0.1 collective-permute-start.4
  89.7 1.5 %collective-permute-done.4.y_ref = bf16[32,32,128]{2,1,0:T(8,128)(2,1)S(1)} collective-permute-done((bf16[32,32,128]{2,1,0:T(8,128)(2,1)S(1)}, bf16[32,32,128]{2,1,0:T(8,128)(2,1)S(1)}, u32[]{:S(2)}, u32[]{:S(2)}) %collective-permute-start.4) | collective-permute-done | bytes 262176 | tf_op jit(solution)/shard_map/ppermute | solution.py:338
  91.2 0.4 shard_map.160.rest_1_
  91.6 6.1 %shard_map.161 = bf16[32,128,128]{2,1,0:T(8,128)(2,1)} custom-call(bf16[7,256,256]{2,1,0:T(8,128)(2,1)S(1)} %copy-done.1, f32[32,128]{1,0:T(8,128)S(1)} %get-tuple-element.23.c_ref, f32[32,128]{1,0:T(8,128)S(1)} %get-tuple-element.22.s_ref, bf16[256,256]{1,0:T(8,128)(2,1)S(1)} %copy-done.2, bf16[32,96,128]{2,1,0:T(8,128)(2,1)S(1)} %all-to-all-done.1.rest_0_, ...), custom_call_target="tpu_custom_call" | custom-call | tf_op jit(solution)/shard_map/pallas_call | solution.py:398
  (19 shorter events, 0.0 us)
Async XLA Ops:
  7.7 7.4 %copy-start.3 = (bf16[32,32,128]{2,1,0:T(8,128)(2,1)S(1)}, bf16[32,32,128]{2,1,0:T(8,128)(2,1)}, u32[]{:S(2)}) copy-start(bf16[32,32,128]{2,1,0:T(8,128)(2,1)} %get-tuple-element.17.x_ref) | copy-start | bytes 786436
  7.7 9.2 %copy-start.10 = (f32[128]{0:T(128)S(1)}, f32[128]{0:T(128)}, u32[]{:S(2)}) copy-start(f32[128]{0:T(128)} %param.17) | copy-start | bytes 1540
  7.8 22.7 %copy-start.8 = (bf16[2,256,128]{2,1,0:T(8,128)(2,1)S(1)}, bf16[2,256,128]{2,1,0:T(8,128)(2,1)}, u32[]{:S(2)}) copy-start(bf16[2,256,128]{2,1,0:T(8,128)(2,1)} %constant.24.clone.m_ref) | copy-start | bytes 393220
  7.8 32.5 %all-to-all-start = ((bf16[32,104,128]{2,1,0:T(8,128)(2,1)}), bf16[32,104,128]{2,1,0:T(8,128)(2,1)S(1)}, u32[]{:S(2)}, u32[]{:S(2)}) async-start(bf16[32,104,128]{2,1,0:T(8,128)(2,1)} %get-tuple-element.16), calls=%async_computation | async-start | bytes 1703936 | tf_op jit(solution)/shard_map/all_to_all | solution.py:432
  15.1 15.3 %collective-permute-start = (bf16[32,32,128]{2,1,0:T(8,128)(2,1)S(1)}, bf16[32,32,128]{2,1,0:T(8,128)(2,1)S(1)}, u32[]{:S(2)}, u32[]{:S(2)}) collective-permute-start(bf16[32,32,128]{2,1,0:T(8,128)(2,1)S(1)} %copy-done.3), channel_id=1, source_target_pairs={{0,8},{8,0},{16,24},{24,16},{1,9},{9,1},{17,25},{25,17},{2,10},{10... | collective-permute-start | bytes 786440 | tf_op jit(solution)/shard_map/ppermute | solution.py:338
  17.1 0.7 copy-start.9
  17.1 0.7 copy-start.11
  17.1 0.7 copy-start.12
  30.5 9.5 %copy-start.7 = (bf16[2,256,128]{2,1,0:T(8,128)(2,1)S(1)}, bf16[2,256,128]{2,1,0:T(8,128)(2,1)}, u32[]{:S(2)}) copy-start(bf16[2,256,128]{2,1,0:T(8,128)(2,1)} %constant.25.clone.m_ref) | copy-start | bytes 393220
  30.8 9.5 %copy-start = (bf16[5,256,256]{2,1,0:T(8,128)(2,1)S(1)}, bf16[5,256,256]{2,1,0:T(8,128)(2,1)}, u32[]{:S(2)}) copy-start(bf16[5,256,256]{2,1,0:T(8,128)(2,1)} %constant.21.clone.m_hbm.m_ref) | copy-start | bytes 1966084
  30.9 9.1 %collective-permute-start.1 = (bf16[32,32,128]{2,1,0:T(8,128)(2,1)S(1)}, bf16[32,32,128]{2,1,0:T(8,128)(2,1)S(1)}, u32[]{:S(2)}, u32[]{:S(2)}) collective-permute-start(bf16[32,32,128]{2,1,0:T(8,128)(2,1)S(1)} %shard_map.155.x_ref), channel_id=1, source_target_pairs={{0,16},{8,24},{16,0},{24,8},{1,17},{9,25},{17,1},{25,9},{2,18},{10... | collective-permute-start | bytes 786440 | tf_op jit(solution)/shard_map/ppermute | solution.py:338
  43.7 37.2 %copy-start.6 = (bf16[2,256,128]{2,1,0:T(8,128)(2,1)S(1)}, bf16[2,256,128]{2,1,0:T(8,128)(2,1)}, u32[]{:S(2)}) copy-start(bf16[2,256,128]{2,1,0:T(8,128)(2,1)} %constant.26.clone.m_ref) | copy-start | bytes 393220
  43.7 47.9 %all-to-all-start.1 = ((bf16[32,96,128]{2,1,0:T(8,128)(2,1)}), bf16[32,96,128]{2,1,0:T(8,128)(2,1)S(1)}, u32[]{:S(2)}, u32[]{:S(2)}) async-start(bf16[32,96,128]{2,1,0:T(8,128)(2,1)} %shard_map.157), calls=%async_computation.1 | async-start | bytes 1572864 | tf_op jit(solution)/shard_map/all_to_all | solution.py:448
  49.2 31.7 %collective-permute-start.2 = (bf16[32,32,128]{2,1,0:T(8,128)(2,1)S(1)}, bf16[32,32,128]{2,1,0:T(8,128)(2,1)S(1)}, u32[]{:S(2)}, u32[]{:S(2)}) collective-permute-start(bf16[32,32,128]{2,1,0:T(8,128)(2,1)S(1)} %shard_map.156.x_ref), channel_id=1, source_target_pairs={{0,4},{1,5},{2,6},{3,7},{4,0},{5,1},{6,2},{7,3},{8,12},{9,13},{10,... | collective-permute-start | bytes 786440 | tf_op jit(solution)/shard_map/ppermute | solution.py:338
  80.9 8.3 %copy-start.5 = (bf16[2,256,128]{2,1,0:T(8,128)(2,1)S(1)}, bf16[2,256,128]{2,1,0:T(8,128)(2,1)}, u32[]{:S(2)}) copy-start(bf16[2,256,128]{2,1,0:T(8,128)(2,1)} %constant.27.clone.m_ref) | copy-start | bytes 393220
  80.9 10.3 %copy-start.4 = (bf16[2,256,128]{2,1,0:T(8,128)(2,1)S(1)}, bf16[2,256,128]{2,1,0:T(8,128)(2,1)}, u32[]{:S(2)}) copy-start(bf16[2,256,128]{2,1,0:T(8,128)(2,1)} %constant.28.clone.m_ref) | copy-start | bytes 393220
  81.3 10.3 %copy-start.1 = (bf16[7,256,256]{2,1,0:T(8,128)(2,1)S(1)}, bf16[7,256,256]{2,1,0:T(8,128)(2,1)}, u32[]{:S(2)}) copy-start(bf16[7,256,256]{2,1,0:T(8,128)(2,1)} %constant.29.clone.m_ref) | copy-start | bytes 2752516
  81.3 7.9 %collective-permute-start.3 = (bf16[32,32,128]{2,1,0:T(8,128)(2,1)S(1)}, bf16[32,32,128]{2,1,0:T(8,128)(2,1)S(1)}, u32[]{:S(2)}, u32[]{:S(2)}) collective-permute-start(bf16[32,32,128]{2,1,0:T(8,128)(2,1)S(1)} %shard_map.158.x_ref), channel_id=1, source_target_pairs={{0,2},{1,3},{2,0},{3,1},{4,6},{5,7},{6,4},{7,5},{8,10},{9,11},{10,... | collective-permute-start | bytes 786440 | tf_op jit(solution)/shard_map/ppermute | solution.py:338
  89.6 2.0 %copy-start.2 = (bf16[256,256]{1,0:T(8,128)(2,1)S(1)}, bf16[256,256]{1,0:T(8,128)(2,1)}, u32[]{:S(2)}) copy-start(bf16[256,256]{1,0:T(8,128)(2,1)} %constant.20.clone.p_hbm.p_ref) | copy-start | bytes 393220
  89.6 1.6 %collective-permute-start.4 = (bf16[32,32,128]{2,1,0:T(8,128)(2,1)S(1)}, bf16[32,32,128]{2,1,0:T(8,128)(2,1)S(1)}, u32[]{:S(2)}, u32[]{:S(2)}) collective-permute-start(bf16[32,32,128]{2,1,0:T(8,128)(2,1)S(1)} %shard_map.159.x_ref), channel_id=1, source_target_pairs={{0,1},{1,0},{2,3},{3,2},{4,5},{5,4},{6,7},{7,6},{8,9},{9,8},{10,11... | collective-permute-start | bytes 786440 | tf_op jit(solution)/shard_map/ppermute | solution.py:338

commit v6 on v5

--- a/solution.py
+++ b/solution.py
@@ -157,17 +157,23 @@
     return pltpu.CompilerParams(vmem_limit_bytes=mib << 20)
 
 
-def source_kernel(run, side, a_ref, d_ref, x_hbm, m_hbm, p_hbm, *rest):
-    outs, (x_ref, m_ref, p_ref, note_ref, x_sems, m_sems, p_sem) = rest[:-7], rest[-7:]
+def weighed(flops):
+    return pl.CostEstimate(flops=flops, bytes_accessed=1 << 20, transcendentals=0)
+
+
+def source_kernel(first_col, keep, a_ref, d_ref, x_hbm, m_hbm, p_hbm, *rest):
+    o_ref, x_ref, m_ref, p_ref, note_ref, x_sems, m_sems, p_sem = rest
     rows, cols, _ = x_ref.shape
     levels = m_ref.shape[0]
     starts = range(0, cols, BLOCK)
-    x_copies = []
-    for piece, start in enumerate(starts):
-        own = (slice(None), pl.ds(start, BLOCK))
-        x_copies.append(
-            pltpu.make_async_copy(x_hbm.at[own], x_ref.at[own], x_sems.at[piece])
+    x_copies = [
+        pltpu.make_async_copy(
+            x_hbm.at[:, pl.ds(first_col + start, BLOCK)],
+            x_ref.at[:, pl.ds(start, BLOCK)],
+            x_sems.at[piece],
         )
+        for piece, start in enumerate(starts)
+    ]
     m_copies = [
         pltpu.make_async_copy(m_hbm.at[i], m_ref.at[i], m_sems.at[i]) for i in range(levels)
     ]
@@ -180,21 +186,21 @@
     p_copy.start()
 
     slowness = a_ref[...]
-    note_ref[...] = jnp.zeros_like(note_ref)
-    note_ref[0:1, :rows] = d_ref[...]
-    note_ref[3:4, :] = slowness
-    for at in (0, 3):
-        left = note_ref[at : at + 1, :]
-        for part in range(3):
-            piece = left.astype(jnp.bfloat16).astype(jnp.float32)
-            note_ref[at + part : at + part + 1, :] = piece
-            left = left - piece
-    note = note_ref[...].astype(jnp.bfloat16)
-    kept = (run - side) * rows
-    for device in range(outs[0].shape[0]):
-        outs[0][device, kept : kept + NOTE, :] = note
-
-    cosines, sines = rotation(column_of(slowness, cols))
+    if keep:
+        note_ref[...] = jnp.zeros_like(note_ref)
+        note_ref[0:1, :rows] = d_ref[...]
+        note_ref[3:4, :] = slowness
+        for at in (0, 3):
+            left = note_ref[at : at + 1, :]
+            for part in range(3):
+                piece = left.astype(jnp.bfloat16).astype(jnp.float32)
+                note_ref[at + part : at + part + 1, :] = piece
+                left = left - piece
+        note = note_ref[...].astype(jnp.bfloat16)
+        for device in range(o_ref.shape[0]):
+            o_ref[device, keep * rows : keep * rows + NOTE, :] = note
+
+    cosines, sines = rotation(column_of(slowness, first_col + cols)[first_col:])
     for level in range(levels):
         m_copies[level].wait()
         for piece, start in enumerate(starts):
@@ -216,14 +222,14 @@
             )
 
     def store_block(first, second, block):
+        begin = second * 16
+        if not keep:
+            o_ref[first * 16 : first * 16 + 16, begin : begin + 16, :] = block
+            return
         for inner in range(16):
-            device, col = divmod(first * 16 + inner, run)
-            begin = second * 16
-            if col < run - side:
-                begin += col * rows
-                outs[0][device, begin : begin + 16, :] = block[inner]
-            else:
-                outs[1][device * side + col - (run - side), begin : begin + 16, :] = block[inner]
+            device, col = divmod(first * 16 + inner, keep)
+            at = col * rows + begin
+            o_ref[device, at : at + 16, :] = block[inner]
 
     p_copy.wait()
     swap_axes(
@@ -235,30 +241,29 @@
     )
 
 
-def source_levels(x, matrices, slowness, dip_field, shuffle, devices, run, side):
-    rows, cols, _ = x.shape
-    out_shape = [jax.ShapeDtypeStruct((devices, (run - side) * rows + NOTE, WIDE), x.dtype)]
-    if side:
-        out_shape.append(jax.ShapeDtypeStruct((devices * side, rows, WIDE), x.dtype))
+def source_levels(x, matrices, slowness, dip_field, shuffle, first_col, count, keep):
+    rows = x.shape[0]
+    shape = (count // keep, keep * rows + NOTE, WIDE) if keep else (count, rows, WIDE)
     return pl.pallas_call(
-        functools.partial(source_kernel, run, side),
-        out_shape=out_shape,
+        functools.partial(source_kernel, first_col, keep),
+        out_shape=jax.ShapeDtypeStruct(shape, x.dtype),
         in_specs=[VMEM, VMEM, FAR, FAR, FAR],
-        out_specs=[VMEM] * len(out_shape),
+        out_specs=VMEM,
         scratch_shapes=[
-            pltpu.VMEM(x.shape, x.dtype),
+            pltpu.VMEM((rows, count, WIDE), x.dtype),
             pltpu.VMEM(matrices.shape, x.dtype),
             pltpu.VMEM(shuffle.shape, x.dtype),
             pltpu.VMEM((NOTE, WIDE), jnp.float32),
-            pltpu.SemaphoreType.DMA((cols // BLOCK,)),
+            pltpu.SemaphoreType.DMA((count // BLOCK,)),
             pltpu.SemaphoreType.DMA((matrices.shape[0],)),
             pltpu.SemaphoreType.DMA,
         ],
+        cost_estimate=weighed(10**10),
         compiler_params=params(60),
     )(slowness[None, :], dip_field[None, :], x, matrices, shuffle)
 
 
-def middle_kernel(levels, rows, run, tgt_count, x_ref, m_ref, o_ref):
+def middle_kernel(levels, rows, tgt_count, x_ref, m_ref, o_ref):
     count, total, _ = x_ref.shape
     kept = (total - NOTE) // rows
     place = lax.axis_index("src") * tgt_count + lax.axis_index("tgt")
@@ -271,7 +276,7 @@
     lanes = lax.broadcasted_iota(jnp.int32, slowness.shape, 1)
     by_col = []
     for col in range(kept):
-        picked = jnp.where(lanes == place * run + col, slowness, 0.0)
+        picked = jnp.where(lanes == place * kept + col, slowness, 0.0)
         by_col.append(rotation(jnp.sum(picked, axis=1, keepdims=True)))
     by_src = [
         rotation(column_of(noted(at * tgt_count, 0), rows)) for at in range(count // tgt_count)
@@ -302,13 +307,14 @@
             )
 
 
-def middle_levels(x, matrices, levels, rows, run, tgt_count):
+def middle_levels(x, matrices, levels, rows, tgt_count):
     count, total, _ = x.shape
     return pl.pallas_call(
-        functools.partial(middle_kernel, levels, rows, run, tgt_count),
+        functools.partial(middle_kernel, levels, rows, tgt_count),
         out_shape=jax.ShapeDtypeStruct((count, total - NOTE, WIDE), x.dtype),
         in_specs=[VMEM] * 2,
         out_specs=VMEM,
+        cost_estimate=weighed(2 * 10**10),
         compiler_params=params(32),
     )(x, matrices)
 
@@ -347,19 +353,18 @@
     )(x, other, halves, *angles)
 
 
-def target_kernel(run, m_ref, c_ref, s_ref, p_ref, *rest):
+def target_kernel(m_ref, c_ref, s_ref, p_ref, *rest):
     xs, (o_ref, state_ref) = rest[:-2], rest[-2:]
     cols, rows, _ = state_ref.shape
-    kept = xs[0].shape[1] // rows
-    side = run - kept
+    devices, kept = xs[0].shape[0], xs[0].shape[1] // rows
     levels = m_ref.shape[0]
 
     def first(index, start):
-        device, col = divmod(index, run)
-        if col < kept:
-            start += col * rows
-            return xs[0][device, start : start + 16, :]
-        return xs[1][device * side + col - kept, start : start + 16, :]
+        if index >= devices * kept:
+            return xs[1][index - devices * kept, start : start + 16, :]
+        device, col = divmod(index, kept)
+        start += col * rows
+        return xs[0][device, start : start + 16, :]
 
     for level in range(levels):
         for start in range(0, rows, 16):
@@ -394,9 +399,9 @@
     )
 
 
-def target_levels(states, matrices, angles, shuffle, cols, rows, run):
+def target_levels(states, matrices, angles, shuffle, cols, rows):
     return pl.pallas_call(
-        functools.partial(target_kernel, run),
+        target_kernel,
         out_shape=jax.ShapeDtypeStruct((rows, cols, WIDE), jnp.bfloat16),
         in_specs=[VMEM] * (4 + len(states)),
         out_specs=VMEM,
@@ -421,19 +426,21 @@
 
     run = cols // devices
     side = run // 4
+    keep = run - side
+    sent = devices * keep
     shuffle = jnp.asarray(shuffle_matrix())
 
-    states = source_levels(
-        box_weights, matrices_of(0, row_bits), slowness, dip_field, shuffle, devices, run, side
-    )
-    *states, slowness, dip_field = lax.optimization_barrier((*states, slowness, dip_field))
+    first = matrices_of(0, row_bits)
+    sources = (box_weights, first, slowness, dip_field, shuffle)
+    if side:
+        stay = source_levels(*sources, sent, cols - sent, 0)
+    state = source_levels(*sources, 0, sent, keep)
+    state, slowness, dip_field = lax.optimization_barrier((state, slowness, dip_field))
     by_row = tables(dip_field)
 
-    state = lax.all_to_all(states[0], ("src", "tgt"), 0, 0, tiled=True)
+    state = lax.all_to_all(state, ("src", "tgt"), 0, 0, tiled=True)
     if side:
-        kept = slowness.reshape(devices, run)[:, run - side :].reshape(-1)
-        by_col = tables(kept)
-        stay = states[1]
+        by_col = tables(slowness[sent:])
         for bit in range(src_bits):
             stay = pair_level(stay, "src", bit, matrices[row_bits + bit], by_col, False)
         state, stay = lax.optimization_barrier((state, stay))
@@ -443,7 +450,7 @@
     levels = [(tgt_count << bit, True) for bit in range(src_bits)]
     levels += [(1 << bit, False) for bit in reversed(range(tgt_bits))]
     state = middle_levels(
-        state, matrices_of(row_bits, first_target + tgt_bits), levels, rows, run, tgt_count
+        state, matrices_of(row_bits, first_target + tgt_bits), levels, rows, tgt_count
     )
     state = lax.all_to_all(state, ("src", "tgt"), 0, 0, tiled=True)
 
@@ -454,7 +461,6 @@
         shuffle,
         cols,
         rows,
-        run,
     )
 
 

time: 98 us -> 98.5 us (level)
  Pallas kernels: 19.1 us -> 22.9 us
  waiting for transfers between devices: 58.6 us -> 55.4 us
    all_to_all x1 -> x0, starting transfers between devices: 7.32 us -> none  [local(): state = lax.all_to_all(states[0], ('src', 'tgt'), 0, 0, tiled=True)]
    all_to_all x1 -> x2, starting transfers between devices: 5.47 us -> 12.3 us  [local(): state = lax.all_to_all(state, ('src', 'tgt'), 0, 0, tiled=True)]
    pallas_call x3 -> x4, Pallas kernels: 17.2 us -> 21 us  [the longest x2 11.5 us: source_levels(): pl.pallas_call(functools.partial(source_kernel, first_col, keep), out_sha...]
    ppermute x5, waiting for transfers between devices: 58.5 us -> 55.4 us  [pair_level(): other = lax.ppermute(x, axis, [(i, i ^ 1 << bit) for i in range(count)])]
  transfers between devices with their start and end apart: 7 -> 7, of which waited for: 5 -> 5; matrix products, arithmetic and copies ran while one was open for 0% -> 0% of each run, Pallas kernels for 2% -> 7%
where the time goes in v6:
time: 98.5 us; the launch traced here: 98.1 us
  waiting for transfers between devices  55.4 us (56%)
  Pallas kernels  22.9 us (23%)
  starting transfers between devices  18.3 us (19%)
  local copies, waits for them, and re-layouts  1.09 us (1%)
    ppermute x5, waiting for transfers between devices, pair_level(): other = lax.ppermute(x, axis, [(i, i ^ 1 << bit) for i in range(count)])  55.4 us
    all_to_all x2, starting transfers between devices, local(): state = lax.all_to_all(state, ('src', 'tgt'), 0, 0, tiled=True)  12.3 us
    pallas_call x2, Pallas kernels, source_levels(): pl.pallas_call(functools.partial(source_kernel, first_col, keep), out_sha...  11.5 us
    pallas_call x1, Pallas kernels, target_levels(): pl.pallas_call(target_kernel, out_shape=jax.ShapeDtypeStruct((rows, cols,...  6.09 us
    ppermute x5, starting transfers between devices, pair_level(): other = lax.ppermute(x, axis, [(i, i ^ 1 << bit) for i in range(count)])  6.08 us
    pallas_call x1, Pallas kernels, middle_levels(): pl.pallas_call(functools.partial(middle_kernel, levels, rows, tgt_count),...  3.4 us
  transfers between devices with their start and end apart: 7, of which 5 were waited for; matrix products, arithmetic and copies ran while one was open for 0% of the time, Pallas kernels for 7%

profile of v6, /device:TPU:0, one launch (start us, length us, event | category | flops | bytes accessed | tf_op | source)
XLA Modules:
  0.0 98.1 jit_solution(5605948841022055009)
XLA Ops:
  0.0 6.8 %shard_map.154 = bf16[32,104,128]{2,1,0:T(8,128)(2,1)} custom-call(f32[1,128]{1,0:T(1,128)} %bitcast.4, f32[1,32]{1,0:T(1,128)} %bitcast.2, bf16[32,128,128]{2,1,0:T(8,128)(2,1)} %x_hbm.3, bf16[5,256,256]{2,1,0:T(8,128)(2,1)} %constant.21.clone.m_hbm.m_ref, bf16[256,256]{1,0:T(8,128)(2,1)} %constant.20.clone.p_hbm.p_ref), custom_call_target="tpu_custom_call" | custom-call | flops 10000000000 | bytes 1048576 | tf_op jit(solution)/shard_map/pallas_call | solution.py:247
  6.8 7.3 %all-to-all-start = ((bf16[32,104,128]{2,1,0:T(8,128)(2,1)}), bf16[32,104,128]{2,1,0:T(8,128)(2,1)S(1)}, u32[]{:S(2)}, u32[]{:S(2)}) async-start(bf16[32,104,128]{2,1,0:T(8,128)(2,1)} %shard_map.154), calls=%async_computation | async-start | bytes 1703936 | tf_op jit(solution)/shard_map/all_to_all | solution.py:441
  14.1 0.0 copy-start.12
  14.1 0.0 copy-start.7
  14.1 4.7 %shard_map.155.x_ref = bf16[32,32,128]{2,1,0:T(8,128)(2,1)} custom-call(f32[1,128]{1,0:T(1,128)} %bitcast.5, f32[1,32]{1,0:T(1,128)} %bitcast.3, bf16[32,128,128]{2,1,0:T(8,128)(2,1)} %x_hbm.3, bf16[5,256,256]{2,1,0:T(8,128)(2,1)} %constant.21.clone.m_hbm.m_ref, bf16[256,256]{1,0:T(8,128)(2,1)} %constant.20.clone.p_hbm.p_ref), custom_call_target="tpu_custom_call" | custom-call | flops 10000000000 | bytes 1048576 | tf_op jit(solution)/shard_map/pallas_call | solution.py:247
  18.9 0.0 copy-start.9
  18.9 0.0 copy-start.10
  18.9 0.0 copy-start.11
  18.9 1.8 %collective-permute-start = (bf16[32,32,128]{2,1,0:T(8,128)(2,1)}, bf16[32,32,128]{2,1,0:T(8,128)(2,1)S(1)}, u32[]{:S(2)}, u32[]{:S(2)}) collective-permute-start(bf16[32,32,128]{2,1,0:T(8,128)(2,1)} %shard_map.155.x_ref), channel_id=1, source_target_pairs={{0,8},{8,0},{16,24},{24,16},{1,9},{9,1},{17,25},{25,17},{2,10},{10... | collective-permute-start | bytes 786440 | tf_op jit(solution)/shard_map/ppermute | solution.py:344
  20.8 0.1 slice.3
  20.9 0.2 fusion.1
  21.1 9.5 %collective-permute-done.y_ref = bf16[32,32,128]{2,1,0:T(8,128)(2,1)S(1)} collective-permute-done((bf16[32,32,128]{2,1,0:T(8,128)(2,1)}, bf16[32,32,128]{2,1,0:T(8,128)(2,1)S(1)}, u32[]{:S(2)}, u32[]{:S(2)}) %collective-permute-start) | collective-permute-done | bytes 262176 | tf_op jit(solution)/shard_map/ppermute | solution.py:344
  30.5 0.9 copy-done.1
  31.5 0.4 shard_map.156.x_ref
  31.9 0.0 copy-start.8
  31.9 1.5 %collective-permute-start.1 = (bf16[32,32,128]{2,1,0:T(8,128)(2,1)S(1)}, bf16[32,32,128]{2,1,0:T(8,128)(2,1)S(1)}, u32[]{:S(2)}, u32[]{:S(2)}) collective-permute-start(bf16[32,32,128]{2,1,0:T(8,128)(2,1)S(1)} %shard_map.156.x_ref), channel_id=1, source_target_pairs={{0,16},{8,24},{16,0},{24,8},{1,17},{9,25},{17,1},{25,9},{2,18},{10... | collective-permute-start | bytes 786440 | tf_op jit(solution)/shard_map/ppermute | solution.py:344
  33.4 7.4 %collective-permute-done.1.y_ref = bf16[32,32,128]{2,1,0:T(8,128)(2,1)S(1)} collective-permute-done((bf16[32,32,128]{2,1,0:T(8,128)(2,1)S(1)}, bf16[32,32,128]{2,1,0:T(8,128)(2,1)S(1)}, u32[]{:S(2)}, u32[]{:S(2)}) %collective-permute-start.1) | collective-permute-done | bytes 262176 | tf_op jit(solution)/shard_map/ppermute | solution.py:344
  40.9 0.4 shard_map.157.x_ref
  41.3 3.4 %shard_map.158 = bf16[32,96,128]{2,1,0:T(8,128)(2,1)} custom-call(bf16[32,104,128]{2,1,0:T(8,128)(2,1)S(1)} %all-to-all-done.x_ref, bf16[5,256,256]{2,1,0:T(8,128)(2,1)S(1)} %copy-done.8), custom_call_target="tpu_custom_call" | custom-call | flops 20000000000 | bytes 1048576 | tf_op jit(solution)/shard_map/pallas_call | solution.py:312
  44.7 5.0 %all-to-all-start.1 = ((bf16[32,96,128]{2,1,0:T(8,128)(2,1)}), bf16[32,96,128]{2,1,0:T(8,128)(2,1)S(1)}, u32[]{:S(2)}, u32[]{:S(2)}) async-start(bf16[32,96,128]{2,1,0:T(8,128)(2,1)} %shard_map.158), calls=%async_computation.1 | async-start | bytes 1572864 | tf_op jit(solution)/shard_map/all_to_all | solution.py:455
  49.6 2.6 %collective-permute-start.2 = (bf16[32,32,128]{2,1,0:T(8,128)(2,1)S(1)}, bf16[32,32,128]{2,1,0:T(8,128)(2,1)S(1)}, u32[]{:S(2)}, u32[]{:S(2)}) collective-permute-start(bf16[32,32,128]{2,1,0:T(8,128)(2,1)S(1)} %shard_map.157.x_ref), channel_id=1, source_target_pairs={{0,4},{1,5},{2,6},{3,7},{4,0},{5,1},{6,2},{7,3},{8,12},{9,13},{10,... | collective-permute-start | bytes 786440 | tf_op jit(solution)/shard_map/ppermute | solution.py:344
  52.2 29.1 %collective-permute-done.2.y_ref = bf16[32,32,128]{2,1,0:T(8,128)(2,1)S(1)} collective-permute-done((bf16[32,32,128]{2,1,0:T(8,128)(2,1)S(1)}, bf16[32,32,128]{2,1,0:T(8,128)(2,1)S(1)}, u32[]{:S(2)}, u32[]{:S(2)}) %collective-permute-start.2) | collective-permute-done | bytes 262176 | tf_op jit(solution)/shard_map/ppermute | solution.py:344
  81.3 0.4 shard_map.159.x_ref
  81.7 0.0 copy-start
  81.7 0.1 collective-permute-start.3
  81.8 7.8 %collective-permute-done.3.y_ref = bf16[32,32,128]{2,1,0:T(8,128)(2,1)S(1)} collective-permute-done((bf16[32,32,128]{2,1,0:T(8,128)(2,1)S(1)}, bf16[32,32,128]{2,1,0:T(8,128)(2,1)S(1)}, u32[]{:S(2)}, u32[]{:S(2)}) %collective-permute-start.3) | collective-permute-done | bytes 262176 | tf_op jit(solution)/shard_map/ppermute | solution.py:344
  89.6 0.4 shard_map.160.x_ref
  90.0 0.0 copy-start.2
  90.0 0.1 collective-permute-start.4
  90.1 1.5 %collective-permute-done.4.y_ref = bf16[32,32,128]{2,1,0:T(8,128)(2,1)S(1)} collective-permute-done((bf16[32,32,128]{2,1,0:T(8,128)(2,1)S(1)}, bf16[32,32,128]{2,1,0:T(8,128)(2,1)S(1)}, u32[]{:S(2)}, u32[]{:S(2)}) %collective-permute-start.4) | collective-permute-done | bytes 262176 | tf_op jit(solution)/shard_map/ppermute | solution.py:344
  91.6 0.4 shard_map.161.rest_1_
  92.1 6.1 %shard_map.162 = bf16[32,128,128]{2,1,0:T(8,128)(2,1)} custom-call(bf16[7,256,256]{2,1,0:T(8,128)(2,1)S(1)} %copy-done, f32[32,128]{1,0:T(8,128)S(1)} %get-tuple-element.17.c_ref, f32[32,128]{1,0:T(8,128)S(1)} %get-tuple-element.16.s_ref, bf16[256,256]{1,0:T(8,128)(2,1)S(1)} %copy-done.2, bf16[32,96,128]{2,1,0:T(8,128)(2,1)S(1)} %all-to-all-done.1.rest_0_, ...), custom_call_target="tpu_custom_call" | custom-call | tf_op jit(solution)/shard_map/pallas_call | solution.py:403
  (19 shorter events, 0.0 us)
Async XLA Ops:
  6.8 34.4 %all-to-all-start = ((bf16[32,104,128]{2,1,0:T(8,128)(2,1)}), bf16[32,104,128]{2,1,0:T(8,128)(2,1)S(1)}, u32[]{:S(2)}, u32[]{:S(2)}) async-start(bf16[32,104,128]{2,1,0:T(8,128)(2,1)} %shard_map.154), calls=%async_computation | async-start | bytes 1703936 | tf_op jit(solution)/shard_map/all_to_all | solution.py:441
  14.1 6.7 %copy-start.12 = (f32[128]{0:T(128)S(1)}, f32[128]{0:T(128)}, u32[]{:S(2)}) copy-start(f32[128]{0:T(128)} %param.17) | copy-start | bytes 1540
  14.1 16.4 %copy-start.7 = (bf16[2,256,128]{2,1,0:T(8,128)(2,1)S(1)}, bf16[2,256,128]{2,1,0:T(8,128)(2,1)}, u32[]{:S(2)}) copy-start(bf16[2,256,128]{2,1,0:T(8,128)(2,1)} %constant.24.clone.m_ref) | copy-start | bytes 393220
  18.9 1.9 %copy-start.9 = (f32[32]{0:T(128)S(1)}, f32[32]{0:T(128)}, u32[]{:S(2)}) copy-start(f32[32]{0:T(128)} %param.18) | copy-start | bytes 388
  18.9 1.9 %copy-start.10 = (f32[128]{0:T(128)S(1)}, f32[128]{0:T(128)}, u32[]{:S(2)}) copy-start(f32[128]{0:T(128)} %constant.22.clone) | copy-start | bytes 1540
  18.9 1.9 %copy-start.11 = (f32[128]{0:T(128)S(1)}, f32[128]{0:T(128)}, u32[]{:S(2)}) copy-start(f32[128]{0:T(128)} %constant.23.clone) | copy-start | bytes 1540
  18.9 11.6 %collective-permute-start = (bf16[32,32,128]{2,1,0:T(8,128)(2,1)}, bf16[32,32,128]{2,1,0:T(8,128)(2,1)S(1)}, u32[]{:S(2)}, u32[]{:S(2)}) collective-permute-start(bf16[32,32,128]{2,1,0:T(8,128)(2,1)} %shard_map.155.x_ref), channel_id=1, source_target_pairs={{0,8},{8,0},{16,24},{24,16},{1,9},{9,1},{17,25},{25,17},{2,10},{10... | collective-permute-start | bytes 786440 | tf_op jit(solution)/shard_map/ppermute | solution.py:344
  30.5 1.0 copy-start.1
  31.5 9.4 %copy-start.6 = (bf16[2,256,128]{2,1,0:T(8,128)(2,1)S(1)}, bf16[2,256,128]{2,1,0:T(8,128)(2,1)}, u32[]{:S(2)}) copy-start(bf16[2,256,128]{2,1,0:T(8,128)(2,1)} %constant.25.clone.m_ref) | copy-start | bytes 393220
  31.9 9.4 %copy-start.8 = (bf16[5,256,256]{2,1,0:T(8,128)(2,1)S(1)}, bf16[5,256,256]{2,1,0:T(8,128)(2,1)}, u32[]{:S(2)}) copy-start(bf16[5,256,256]{2,1,0:T(8,128)(2,1)} %constant.21.clone.m_hbm.m_ref) | copy-start | bytes 1966084
  31.9 9.0 %collective-permute-start.1 = (bf16[32,32,128]{2,1,0:T(8,128)(2,1)S(1)}, bf16[32,32,128]{2,1,0:T(8,128)(2,1)S(1)}, u32[]{:S(2)}, u32[]{:S(2)}) collective-permute-start(bf16[32,32,128]{2,1,0:T(8,128)(2,1)S(1)} %shard_map.156.x_ref), channel_id=1, source_target_pairs={{0,16},{8,24},{16,0},{24,8},{1,17},{9,25},{17,1},{25,9},{2,18},{10... | collective-permute-start | bytes 786440 | tf_op jit(solution)/shard_map/ppermute | solution.py:344
  44.7 36.6 %copy-start.5 = (bf16[2,256,128]{2,1,0:T(8,128)(2,1)S(1)}, bf16[2,256,128]{2,1,0:T(8,128)(2,1)}, u32[]{:S(2)}) copy-start(bf16[2,256,128]{2,1,0:T(8,128)(2,1)} %constant.26.clone.m_ref) | copy-start | bytes 393220
  44.7 47.3 %all-to-all-start.1 = ((bf16[32,96,128]{2,1,0:T(8,128)(2,1)}), bf16[32,96,128]{2,1,0:T(8,128)(2,1)S(1)}, u32[]{:S(2)}, u32[]{:S(2)}) async-start(bf16[32,96,128]{2,1,0:T(8,128)(2,1)} %shard_map.158), calls=%async_computation.1 | async-start | bytes 1572864 | tf_op jit(solution)/shard_map/all_to_all | solution.py:455
  49.6 31.7 %collective-permute-start.2 = (bf16[32,32,128]{2,1,0:T(8,128)(2,1)S(1)}, bf16[32,32,128]{2,1,0:T(8,128)(2,1)S(1)}, u32[]{:S(2)}, u32[]{:S(2)}) collective-permute-start(bf16[32,32,128]{2,1,0:T(8,128)(2,1)S(1)} %shard_map.157.x_ref), channel_id=1, source_target_pairs={{0,4},{1,5},{2,6},{3,7},{4,0},{5,1},{6,2},{7,3},{8,12},{9,13},{10,... | collective-permute-start | bytes 786440 | tf_op jit(solution)/shard_map/ppermute | solution.py:344
  81.3 8.3 %copy-start.4 = (bf16[2,256,128]{2,1,0:T(8,128)(2,1)S(1)}, bf16[2,256,128]{2,1,0:T(8,128)(2,1)}, u32[]{:S(2)}) copy-start(bf16[2,256,128]{2,1,0:T(8,128)(2,1)} %constant.27.clone.m_ref) | copy-start | bytes 393220
  81.3 10.3 %copy-start.3 = (bf16[2,256,128]{2,1,0:T(8,128)(2,1)S(1)}, bf16[2,256,128]{2,1,0:T(8,128)(2,1)}, u32[]{:S(2)}) copy-start(bf16[2,256,128]{2,1,0:T(8,128)(2,1)} %constant.28.clone.m_ref) | copy-start | bytes 393220
  81.7 10.3 %copy-start = (bf16[7,256,256]{2,1,0:T(8,128)(2,1)S(1)}, bf16[7,256,256]{2,1,0:T(8,128)(2,1)}, u32[]{:S(2)}) copy-start(bf16[7,256,256]{2,1,0:T(8,128)(2,1)} %constant.29.clone.m_ref) | copy-start | bytes 2752516
  81.7 7.9 %collective-permute-start.3 = (bf16[32,32,128]{2,1,0:T(8,128)(2,1)S(1)}, bf16[32,32,128]{2,1,0:T(8,128)(2,1)S(1)}, u32[]{:S(2)}, u32[]{:S(2)}) collective-permute-start(bf16[32,32,128]{2,1,0:T(8,128)(2,1)S(1)} %shard_map.159.x_ref), channel_id=1, source_target_pairs={{0,2},{1,3},{2,0},{3,1},{4,6},{5,7},{6,4},{7,5},{8,10},{9,11},{10,... | collective-permute-start | bytes 786440 | tf_op jit(solution)/shard_map/ppermute | solution.py:344
  90.0 2.0 %copy-start.2 = (bf16[256,256]{1,0:T(8,128)(2,1)S(1)}, bf16[256,256]{1,0:T(8,128)(2,1)}, u32[]{:S(2)}) copy-start(bf16[256,256]{1,0:T(8,128)(2,1)} %constant.20.clone.p_hbm.p_ref) | copy-start | bytes 393220
  90.0 1.6 %collective-permute-start.4 = (bf16[32,32,128]{2,1,0:T(8,128)(2,1)S(1)}, bf16[32,32,128]{2,1,0:T(8,128)(2,1)S(1)}, u32[]{:S(2)}, u32[]{:S(2)}) collective-permute-start(bf16[32,32,128]{2,1,0:T(8,128)(2,1)S(1)} %shard_map.160.x_ref), channel_id=1, source_target_pairs={{0,1},{1,0},{2,3},{3,2},{4,5},{5,4},{6,7},{7,6},{8,9},{9,8},{10,11... | collective-permute-start | bytes 786440 | tf_op jit(solution)/shard_map/ppermute | solution.py:344

commit v7 on v6

--- a/solution.py
+++ b/solution.py
@@ -43,7 +43,9 @@
     upper = np.concatenate([real, imag], axis=3)
     lower = np.concatenate([-imag, real], axis=3)
     full = np.concatenate([upper, lower], axis=1)
-    return full.reshape(2 * WIDE, 2 * WIDE).astype(ml_dtypes.bfloat16)
+    swapped = np.concatenate([full[..., HALF:], full[..., :HALF]], axis=3)
+    whole = [part.reshape(2 * WIDE, 2 * WIDE) for part in (full, swapped)]
+    return np.concatenate(whole, axis=1).astype(ml_dtypes.bfloat16)
 
 
 def tables(scales):
@@ -108,10 +110,6 @@
     return jnp.sum(jnp.where(here, jnp.broadcast_to(row, shape), 0.0), axis=1, keepdims=True)
 
 
-def rotated(value, cosine, sine):
-    return (value * cosine + pltpu.roll(value, HALF, 1) * sine).astype(jnp.bfloat16)
-
-
 def butterfly(load, store, count, apart, matrix, phase_of, group):
     lows = [i for i in range(count) if not i & apart]
     for start in range(0, len(lows), group):
@@ -125,10 +123,12 @@
         for place, low in enumerate(picked):
             for child in range(2):
                 index = low + child * apart
-                value = both[
-                    place * rows : (place + 1) * rows, child * WIDE : (child + 1) * WIDE
-                ]
-                store(index, rotated(value, *phase_of(index)))
+                cosine, sine = phase_of(index)
+                mine = slice(place * rows, (place + 1) * rows)
+                at = child * WIDE
+                value = both[mine, at : at + WIDE] * cosine
+                value += both[mine, at + 2 * WIDE : at + 3 * WIDE] * sine
+                store(index, value.astype(jnp.bfloat16))
 
 
 def swap_axes(load, store, outer, inner, shuffle):
@@ -218,7 +218,7 @@
                 1 << level,
                 m_ref[level],
                 lambda index: (cosine, sine),
-                16,
+                8,
             )
 
     def store_block(first, second, block):
@@ -303,7 +303,7 @@
                 apart,
                 m_ref[step],
                 phase_of,
-                16,
+                8,
             )
 
 
@@ -319,52 +319,15 @@
     )(x, matrices)
 
 
-def pair_kernel(axis, bit, by_row, x_ref, y_ref, m_ref, c_ref, s_ref, o_ref):
-    count, rows, _ = x_ref.shape
-    matrix = m_ref[lax.rem(lax.div(lax.axis_index(axis), 1 << bit), 2)]
-    group = 16
-    for start in range(0, count, group):
-        picked = slice(start, start + group)
-        left = x_ref[picked].reshape(-1, WIDE)
-        right = y_ref[picked].reshape(-1, WIDE)
-        both = jnp.dot(
-            jnp.concatenate([left, right], axis=1), matrix, preferred_element_type=jnp.float32
-        )
-        for place in range(left.shape[0] // rows):
-            index = start + place
-            if by_row:
-                cosine, sine = c_ref[...], s_ref[...]
-            else:
-                cosine, sine = c_ref[index : index + 1, :], s_ref[index : index + 1, :]
-            o_ref[index] = rotated(both[place * rows : (place + 1) * rows], cosine, sine)
-
-
-def pair_level(x, axis, bit, matrix, angles, by_row):
-    count = lax.axis_size(axis)
-    other = lax.ppermute(x, axis, [(i, i ^ 1 << bit) for i in range(count)])
-    flipped = np.roll(matrix, (WIDE, WIDE), (0, 1))
-    halves = jnp.asarray(np.stack([matrix[:, :WIDE], flipped[:, :WIDE]]))
-    return pl.pallas_call(
-        functools.partial(pair_kernel, axis, bit, by_row),
-        out_shape=jax.ShapeDtypeStruct(x.shape, x.dtype),
-        in_specs=[VMEM] * 5,
-        out_specs=VMEM,
-        compiler_params=params(32),
-    )(x, other, halves, *angles)
-
-
-def target_kernel(m_ref, c_ref, s_ref, p_ref, *rest):
-    xs, (o_ref, state_ref) = rest[:-2], rest[-2:]
+def target_kernel(m_ref, c_ref, s_ref, p_ref, x_ref, o_ref, state_ref):
     cols, rows, _ = state_ref.shape
-    devices, kept = xs[0].shape[0], xs[0].shape[1] // rows
+    kept = x_ref.shape[1] // rows
     levels = m_ref.shape[0]
 
     def first(index, start):
-        if index >= devices * kept:
-            return xs[1][index - devices * kept, start : start + 16, :]
         device, col = divmod(index, kept)
         start += col * rows
-        return xs[0][device, start : start + 16, :]
+        return x_ref[device, start : start + 16, :]
 
     for level in range(levels):
         for start in range(0, rows, 16):
@@ -384,7 +347,7 @@
                 1 << (levels - 1 - level),
                 m_ref[level],
                 lambda index: (cosine, sine),
-                32,
+                16,
             )
 
     def store_block(first, second, block):
@@ -399,15 +362,15 @@
     )
 
 
-def target_levels(states, matrices, angles, shuffle, cols, rows):
+def target_levels(x, matrices, angles, shuffle, cols, rows):
     return pl.pallas_call(
         target_kernel,
         out_shape=jax.ShapeDtypeStruct((rows, cols, WIDE), jnp.bfloat16),
-        in_specs=[VMEM] * (4 + len(states)),
+        in_specs=[VMEM] * 5,
         out_specs=VMEM,
         scratch_shapes=[pltpu.VMEM((cols, rows, WIDE), jnp.bfloat16)],
         compiler_params=params(32),
-    )(matrices, *angles, shuffle, *states)
+    )(matrices, *angles, shuffle, x)
 
 
 def local(box_weights, slowness, dip_field):
@@ -424,29 +387,16 @@
     def matrices_of(low, high):
         return jnp.asarray(np.stack(matrices[low:high]))
 
-    run = cols // devices
-    side = run // 4
-    keep = run - side
-    sent = devices * keep
+    keep = cols // devices
     shuffle = jnp.asarray(shuffle_matrix())
 
-    first = matrices_of(0, row_bits)
-    sources = (box_weights, first, slowness, dip_field, shuffle)
-    if side:
-        stay = source_levels(*sources, sent, cols - sent, 0)
-    state = source_levels(*sources, 0, sent, keep)
-    state, slowness, dip_field = lax.optimization_barrier((state, slowness, dip_field))
+    state = source_levels(
+        box_weights, matrices_of(0, row_bits), slowness, dip_field, shuffle, 0, cols, keep
+    )
+    state, dip_field = lax.optimization_barrier((state, dip_field))
     by_row = tables(dip_field)
 
     state = lax.all_to_all(state, ("src", "tgt"), 0, 0, tiled=True)
-    if side:
-        by_col = tables(slowness[sent:])
-        for bit in range(src_bits):
-            stay = pair_level(stay, "src", bit, matrices[row_bits + bit], by_col, False)
-        state, stay = lax.optimization_barrier((state, stay))
-        for at, bit in enumerate(reversed(range(tgt_bits))):
-            stay = pair_level(stay, "tgt", bit, matrices[first_target + at], by_row, True)
-
     levels = [(tgt_count << bit, True) for bit in range(src_bits)]
     levels += [(1 << bit, False) for bit in reversed(range(tgt_bits))]
     state = middle_levels(
@@ -455,7 +405,7 @@
     state = lax.all_to_all(state, ("src", "tgt"), 0, 0, tiled=True)
 
     return target_levels(
-        [state, stay] if side else [state],
+        state,
         matrices_of(first_target + tgt_bits, total),
         by_row,
         shuffle,

time: 98.5 us -> 83.6 us (0.85)
  blocking collectives: 0 us -> 36.5 us
  waiting for transfers between devices: 55.4 us -> 27.2 us
  starting transfers between devices: 18.3 us -> 2.98 us
  Pallas kernels: 22.9 us -> 15.4 us
    ppermute x5 -> x0, waiting for transfers between devices: 55.4 us -> none  [pair_level(): other = lax.ppermute(x, axis, [(i, i ^ 1 << bit) for i in range(count)])]
    all_to_all x0 -> x1, blocking collectives: none -> 36.5 us  [local(): state = lax.all_to_all(state, ('src', 'tgt'), 0, 0, tiled=True)]
    all_to_all x2 -> x1, waiting for transfers between devices: 0.01 us -> 27.2 us  [local(): state = lax.all_to_all(state, ('src', 'tgt'), 0, 0, tiled=True)]
    all_to_all x2 -> x1, starting transfers between devices: 12.3 us -> 2.98 us  [local(): state = lax.all_to_all(state, ('src', 'tgt'), 0, 0, tiled=True)]
    ppermute x5 -> x0, starting transfers between devices: 6.08 us -> none  [pair_level(): other = lax.ppermute(x, axis, [(i, i ^ 1 << bit) for i in range(count)])]
    pallas_call x2 -> x1, Pallas kernels: 11.5 us -> 7.3 us  [source_levels(): pl.pallas_call(functools.partial(source_kernel, first_col, keep), out_sha...]
    pallas_call x5 -> x0, Pallas kernels: 1.88 us -> none  [pair_level(): pl.pallas_call(functools.partial(pair_kernel, axis, bit, by_row), out_sha...]
  transfers between devices with their start and end apart: 7 -> 1, of which waited for: 5 -> 1; matrix products, arithmetic and copies ran while one was open for 0% -> 0% of each run, Pallas kernels for 7% -> 0%
where the time goes in v7:
time: 83.6 us; the launch traced here: 83.4 us
  blocking collectives  36.5 us (44%)
  waiting for transfers between devices  27.2 us (33%)
  Pallas kernels  15.4 us (18%)
  starting transfers between devices  2.98 us (4%)
  local copies, waits for them, and re-layouts  0.99 us (1%)
    all_to_all x1, blocking collectives, local(): state = lax.all_to_all(state, ('src', 'tgt'), 0, 0, tiled=True)  36.5 us
    all_to_all x1, waiting for transfers between devices, local(): state = lax.all_to_all(state, ('src', 'tgt'), 0, 0, tiled=True)  27.2 us
    pallas_call x1, Pallas kernels, source_levels(): pl.pallas_call(functools.partial(source_kernel, first_col, keep), out_sha...  7.3 us
    pallas_call x1, Pallas kernels, target_levels(): pl.pallas_call(target_kernel, out_shape=jax.ShapeDtypeStruct((rows, cols,...  5.24 us
    all_to_all x1, starting transfers between devices, local(): state = lax.all_to_all(state, ('src', 'tgt'), 0, 0, tiled=True)  2.98 us
    pallas_call x1, Pallas kernels, middle_levels(): pl.pallas_call(functools.partial(middle_kernel, levels, rows, tgt_count),...  2.9 us
  transfers between devices with their start and end apart: 1, of which 1 were waited for; matrix products, arithmetic and copies ran while one was open for 0% of the time, Pallas kernels for 0%

profile of v7, /device:TPU:0, one launch (start us, length us, event | category | flops | bytes accessed | tf_op | source)
XLA Modules:
  0.0 83.4 jit_solution(1695391049509148836)
XLA Ops:
  0.0 7.3 %shard_map.91 = bf16[32,136,128]{2,1,0:T(8,128)(2,1)} custom-call(f32[1,128]{1,0:T(1,128)} %bitcast.3, f32[1,32]{1,0:T(1,128)} %bitcast.2, bf16[32,128,128]{2,1,0:T(8,128)(2,1)} %x_hbm.1, bf16[5,256,512]{2,1,0:T(8,128)(2,1)} %constant.11.clone.m_hbm.m_ref, bf16[256,256]{1,0:T(8,128)(2,1)} %constant.10.clone.p_hbm.p_ref), custom_call_target="tpu_custom_call" | custom-call | flops 10000000000 | bytes 1048576 | tf_op jit(solution)/shard_map/pallas_call | solution.py:247
  7.3 0.0 copy-start.3
  7.3 36.5 %all_to_all.10.x_ref = bf16[32,136,128]{2,1,0:T(8,128)(2,1)S(1)} all-to-all(bf16[32,136,128]{2,1,0:T(8,128)(2,1)} %shard_map.91), channel_id=1, replica_groups=mesh['src'=4,'tgt'=8] {'src','tgt'}, dimensions={0} | all-to-all | bytes 2228224 | tf_op jit(solution)/shard_map/all_to_all | solution.py:399
  43.9 0.0 copy-done.3
  43.9 2.9 %shard_map.92 = bf16[32,128,128]{2,1,0:T(8,128)(2,1)S(1)} custom-call(bf16[32,136,128]{2,1,0:T(8,128)(2,1)S(1)} %all_to_all.10.x_ref, bf16[5,256,512]{2,1,0:T(8,128)(2,1)S(1)} %copy-done.3), custom_call_target="tpu_custom_call" | custom-call | flops 20000000000 | bytes 1048576 | tf_op jit(solution)/shard_map/pallas_call | solution.py:312
  46.8 0.0 copy-start.1
  46.8 1.0 %copy-done.1 = bf16[32,128,128]{2,1,0:T(8,128)(2,1)} copy-done((bf16[32,128,128]{2,1,0:T(8,128)(2,1)}, bf16[32,128,128]{2,1,0:T(8,128)(2,1)S(1)}, u32[]{:S(2)}) %copy-start.1) | copy-done | bytes 1048600
  47.8 0.0 copy-start.4
  47.8 0.0 copy-start.5
  47.8 0.0 copy-start.6
  47.8 0.0 copy-start
  47.8 0.0 copy-start.2
  47.8 3.0 %all-to-all-start.1 = ((bf16[32,128,128]{2,1,0:T(8,128)(2,1)}), bf16[32,128,128]{2,1,0:T(8,128)(2,1)S(1)}, u32[]{:S(2)}, u32[]{:S(2)}) async-start(bf16[32,128,128]{2,1,0:T(8,128)(2,1)} %copy-done.1), calls=%async_computation.1 | async-start | bytes 2097152 | tf_op jit(solution)/shard_map/all_to_all | solution.py:405
  50.8 0.0 copy-done.4
  50.8 0.0 copy-done.5
  50.8 0.0 copy-done.6
  50.8 0.1 fusion
  50.9 27.2 %all-to-all-done.1.x_ref = bf16[32,128,128]{2,1,0:T(8,128)(2,1)S(1)} async-done(((bf16[32,128,128]{2,1,0:T(8,128)(2,1)}), bf16[32,128,128]{2,1,0:T(8,128)(2,1)S(1)}, u32[]{:S(2)}, u32[]{:S(2)}) %all-to-all-start.1) | async-done | bytes 1048608 | tf_op jit(solution)/shard_map/all_to_all | solution.py:405
  78.2 0.0 copy-done
  78.2 0.0 copy-done.2
  78.2 5.2 %shard_map.93 = bf16[32,128,128]{2,1,0:T(8,128)(2,1)} custom-call(bf16[7,256,512]{2,1,0:T(8,128)(2,1)S(1)} %copy-done, f32[32,128]{1,0:T(8,128)S(1)} %get-tuple-element.10.c_ref, f32[32,128]{1,0:T(8,128)S(1)} %get-tuple-element.9.s_ref, bf16[256,256]{1,0:T(8,128)(2,1)S(1)} %copy-done.2, bf16[32,128,128]{2,1,0:T(8,128)(2,1)S(1)} %all-to-all-done.1.x_ref), custom_call_target="tpu_custom_call" | custom-call | tf_op jit(solution)/shard_map/pallas_call | solution.py:366
Async XLA Ops:
  7.3 36.6 %copy-start.3 = (bf16[5,256,512]{2,1,0:T(8,128)(2,1)S(1)}, bf16[5,256,512]{2,1,0:T(8,128)(2,1)}, u32[]{:S(2)}) copy-start(bf16[5,256,512]{2,1,0:T(8,128)(2,1)} %constant.11.clone.m_hbm.m_ref) | copy-start | bytes 3932164
  46.8 1.0 %copy-start.1 = (bf16[32,128,128]{2,1,0:T(8,128)(2,1)}, bf16[32,128,128]{2,1,0:T(8,128)(2,1)S(1)}, u32[]{:S(2)}) copy-start(bf16[32,128,128]{2,1,0:T(8,128)(2,1)S(1)} %shard_map.92) | copy-start | bytes 3145732
  47.8 3.0 %copy-start.4 = (f32[32]{0:T(128)S(1)}, f32[32]{0:T(128)}, u32[]{:S(2)}) copy-start(f32[32]{0:T(128)} %param.11) | copy-start | bytes 388
  47.8 3.0 %copy-start.5 = (f32[128]{0:T(128)S(1)}, f32[128]{0:T(128)}, u32[]{:S(2)}) copy-start(f32[128]{0:T(128)} %constant.13.clone) | copy-start | bytes 1540
  47.8 3.0 %copy-start.6 = (f32[128]{0:T(128)S(1)}, f32[128]{0:T(128)}, u32[]{:S(2)}) copy-start(f32[128]{0:T(128)} %constant.12.clone) | copy-start | bytes 1540
  47.8 30.4 %copy-start = (bf16[7,256,512]{2,1,0:T(8,128)(2,1)S(1)}, bf16[7,256,512]{2,1,0:T(8,128)(2,1)}, u32[]{:S(2)}) copy-start(bf16[7,256,512]{2,1,0:T(8,128)(2,1)} %constant.14.clone.m_ref) | copy-start | bytes 5505028
  47.8 30.4 %copy-start.2 = (bf16[256,256]{1,0:T(8,128)(2,1)S(1)}, bf16[256,256]{1,0:T(8,128)(2,1)}, u32[]{:S(2)}) copy-start(bf16[256,256]{1,0:T(8,128)(2,1)} %constant.10.clone.p_hbm.p_ref) | copy-start | bytes 393220
  47.8 30.4 %all-to-all-start.1 = ((bf16[32,128,128]{2,1,0:T(8,128)(2,1)}), bf16[32,128,128]{2,1,0:T(8,128)(2,1)S(1)}, u32[]{:S(2)}, u32[]{:S(2)}) async-start(bf16[32,128,128]{2,1,0:T(8,128)(2,1)} %copy-done.1), calls=%async_computation.1 | async-start | bytes 2097152 | tf_op jit(solution)/shard_map/all_to_all | solution.py:405

commit v8 on v3

--- a/solution.py
+++ b/solution.py
@@ -60,27 +60,79 @@
     return found.astype(ml_dtypes.bfloat16)
 
 
-def rotated(value, cosine, sine):
-    return (value * cosine + pltpu.roll(value, HALF, 1) * sine).astype(jnp.bfloat16)
-
-
-def butterfly(load, store, count, apart, matrix, phase_of, group):
+def cos_sin(angles):
+    turns = jnp.floor(angles * (2.0 / math.pi) + 0.5)
+    rest = angles - turns * 1.5703125
+    rest = rest - turns * 4.837512969970703125e-4
+    rest = rest - turns * 7.54978995489188e-8
+    square = rest * rest
+    sine = 1.0 / 362880.0
+    for factor in (-1.0 / 5040.0, 1.0 / 120.0, -1.0 / 6.0, 1.0):
+        sine = sine * square + factor
+    sine = sine * rest
+    cosine = -1.0 / 3628800.0
+    for factor in (1.0 / 40320.0, -1.0 / 720.0, 1.0 / 24.0, -0.5, 1.0):
+        cosine = cosine * square + factor
+    quarter = turns.astype(jnp.int32)
+    odd = (quarter & 1) == 1
+    first = jnp.where(odd, sine, cosine)
+    second = jnp.where(odd, cosine, sine)
+    first = jnp.where(((quarter + 1) & 2) == 2, -first, first)
+    second = jnp.where((quarter & 2) == 2, -second, second)
+    return first, second
+
+
+def node_row():
+    lanes = lax.broadcasted_iota(jnp.int32, (1, WIDE), 1) % HALF
+    points = [math.cos((2 * a + 1) * math.pi / 16) ** 2 for a in range(4)]
+
+    def square(at):
+        near = jnp.minimum(at, 7 - at)
+        value = jnp.full(near.shape, points[3], jnp.float32)
+        for a in range(3):
+            value = jnp.where(near == a, jnp.float32(points[a]), value)
+        return value
+
+    return square(lanes // 8) + square(lanes % 8)
+
+
+def rotation(column):
+    cosine, sine = cos_sin(column * node_row())
+    lanes = lax.broadcasted_iota(jnp.int32, cosine.shape, 1)
+    return cosine, jnp.where(lanes < HALF, -sine, sine)
+
+
+def column_of(row, count):
+    shape = (count, WIDE)
+    here = lax.broadcasted_iota(jnp.int32, shape, 0) == lax.broadcasted_iota(jnp.int32, shape, 1)
+    return jnp.sum(jnp.where(here, jnp.broadcast_to(row, shape), 0.0), axis=1, keepdims=True)
+
+
+def swapped_columns(matrix):
+    parts = [matrix[:, at : at + HALF] for at in (HALF, 0, 3 * HALF, 2 * HALF)]
+    return jnp.concatenate(parts, axis=1)
+
+
+def butterfly(load, store, count, apart, matrix, swapped, phase_of, group):
     lows = [i for i in range(count) if not i & apart]
-    for start in range(0, len(lows), group):
+    for turn, start in enumerate(range(0, len(lows), group)):
         picked = lows[start : start + group]
         left = jnp.concatenate([load(i) for i in picked], axis=0)
         right = jnp.concatenate([load(i + apart) for i in picked], axis=0)
         rows = left.shape[0] // len(picked)
-        both = jnp.dot(
-            jnp.concatenate([left, right], axis=1), matrix, preferred_element_type=jnp.float32
-        )
+        pair = jnp.concatenate([left, right], axis=1)
+        both = jnp.dot(pair, matrix, preferred_element_type=jnp.float32)
+        if turn % 2 == 0:
+            other = jnp.dot(pair, swapped, preferred_element_type=jnp.float32)
         for place, low in enumerate(picked):
             for child in range(2):
                 index = low + child * apart
-                value = both[
-                    place * rows : (place + 1) * rows, child * WIDE : (child + 1) * WIDE
-                ]
-                store(index, rotated(value, *phase_of(index)))
+                cosine, sine = phase_of(index)
+                mine = slice(place * rows, (place + 1) * rows)
+                own = slice(child * WIDE, (child + 1) * WIDE)
+                value = both[mine, own]
+                turned = other[mine, own] if turn % 2 == 0 else pltpu.roll(value, HALF, 1)
+                store(index, (value * cosine + turned * sine).astype(jnp.bfloat16))
 
 
 def swap_axes(load, store, outer, inner, shuffle):
@@ -99,53 +151,61 @@
     return (slice(first * 16, first * 16 + 16), slice(second * 16, second * 16 + 16))
 
 
-def source_kernel(pieces, a_ref, x_hbm, m_hbm, p_ref, o_ref, x_ref, m_ref, x_sems, m_sems):
+BLOCK = 32
+VMEM = pl.BlockSpec(memory_space=pltpu.VMEM)
+FAR = pl.BlockSpec(memory_space=pltpu.HBM)
+PARAMS = pltpu.CompilerParams(vmem_limit_bytes=32 << 20)
+
+
+def source_kernel(a_ref, x_hbm, m_hbm, p_hbm, o_ref, x_ref, m_ref, p_ref, x_sems, m_sems, p_sem):
     rows, cols, _ = x_ref.shape
     levels = m_ref.shape[0]
-    each = rows // pieces
+    starts = range(0, cols, BLOCK)
     x_copies = [
         pltpu.make_async_copy(
-            x_hbm.at[pl.ds(i * each, each)], x_ref.at[pl.ds(i * each, each)], x_sems.at[i]
+            x_hbm.at[:, pl.ds(start, BLOCK)], x_ref.at[:, pl.ds(start, BLOCK)], x_sems.at[piece]
         )
-        for i in range(pieces)
+        for piece, start in enumerate(starts)
     ]
     m_copies = [
         pltpu.make_async_copy(m_hbm.at[i], m_ref.at[i], m_sems.at[i]) for i in range(levels)
     ]
+    p_copy = pltpu.make_async_copy(p_hbm, p_ref, p_sem)
     m_copies[0].start()
     for copy in x_copies:
         copy.start()
     for copy in m_copies[1:]:
         copy.start()
-    angles = a_ref[...]
-    cosines = jnp.cos(angles)
-    lanes = lax.broadcasted_iota(jnp.int32, angles.shape, 1)
-    sines = jnp.where(lanes < HALF, -jnp.sin(angles), jnp.sin(angles))
-    block = 32
+    p_copy.start()
+
+    cosines, sines = rotation(column_of(a_ref[...], cols))
     for level in range(levels):
         m_copies[level].wait()
-        if level == 0:
-            for copy in x_copies:
-                copy.wait()
-        for start in range(0, cols, block):
-            cosine, sine = cosines[start : start + block], sines[start : start + block]
+        matrix = m_ref[level]
+        swapped = swapped_columns(matrix)
+        for piece, start in enumerate(starts):
+            if level == 0:
+                x_copies[piece].wait()
+            cosine, sine = cosines[start : start + BLOCK], sines[start : start + BLOCK]
 
             def store(index, value):
-                x_ref[index, start : start + block, :] = value
+                x_ref[index, start : start + BLOCK, :] = value
 
             butterfly(
-                lambda index: x_ref[index, start : start + block, :],
+                lambda index: x_ref[index, start : start + BLOCK, :],
                 store,
                 rows,
                 1 << level,
-                m_ref[level],
+                matrix,
+                swapped,
                 lambda index: (cosine, sine),
-                16,
+                8,
             )
 
     def store_block(first, second, block):
         o_ref[block_at(first, second)] = block
 
+    p_copy.wait()
     swap_axes(
         lambda first, second: x_ref[block_at(first, second)],
         store_block,
@@ -155,27 +215,24 @@
     )
 
 
-VMEM = pl.BlockSpec(memory_space=pltpu.VMEM)
-PARAMS = pltpu.CompilerParams(vmem_limit_bytes=32 << 20)
-
-
-def source_levels(x, matrices, angles, shuffle):
+def source_levels(x, matrices, slowness, shuffle):
     rows, cols, _ = x.shape
-    pieces = 4
-    far = pl.BlockSpec(memory_space=pltpu.HBM)
+    far = [pltpu.with_memory_space_constraint(v, pltpu.HBM) for v in (x, matrices, shuffle)]
     return pl.pallas_call(
-        functools.partial(source_kernel, pieces),
+        source_kernel,
         out_shape=jax.ShapeDtypeStruct((cols, rows, WIDE), x.dtype),
-        in_specs=[VMEM, far, far, VMEM],
+        in_specs=[VMEM, FAR, FAR, FAR],
         out_specs=VMEM,
         scratch_shapes=[
             pltpu.VMEM(x.shape, x.dtype),
             pltpu.VMEM(matrices.shape, x.dtype),
-            pltpu.SemaphoreType.DMA((pieces,)),
+            pltpu.VMEM(shuffle.shape, x.dtype),
+            pltpu.SemaphoreType.DMA((cols // BLOCK,)),
             pltpu.SemaphoreType.DMA((matrices.shape[0],)),
+            pltpu.SemaphoreType.DMA,
         ],
         compiler_params=PARAMS,
-    )(angles, x, matrices, shuffle)
+    )(slowness[None, :], *far)
 
 
 def middle_kernel(levels, rows, x_ref, m_ref, cs_ref, ss_ref, ct_ref, st_ref, o_ref):
@@ -184,6 +241,8 @@
     tgt_count = cs_ref.shape[0] // run
     for step, (apart, by_source) in enumerate(levels):
         source = x_ref if step == 0 else o_ref
+        matrix = m_ref[step]
+        swapped = swapped_columns(matrix)
         for col in range(run):
             own = slice(col * rows, (col + 1) * rows)
 
@@ -202,9 +261,10 @@
                 store,
                 count,
                 apart,
-                m_ref[step],
+                matrix,
+                swapped,
                 phase_of,
-                16,
+                8,
             )
 
 
@@ -219,11 +279,13 @@
     )(x, matrices, *src_tables, *tgt_tables)
 
 
-def target_kernel(x_ref, m_ref, c_ref, s_ref, p_ref, o_ref, state_ref):
+def target_kernel(m_ref, c_ref, s_ref, p_ref, x_ref, o_hbm, state_ref, o_ref, o_sems):
     cols, rows, _ = x_ref.shape
     levels = m_ref.shape[0]
     for level in range(levels):
         source = x_ref if level == 0 else state_ref
+        matrix = m_ref[level]
+        swapped = swapped_columns(matrix)
         for start in range(0, rows, 16):
             own = slice(start, start + 16)
             cosine, sine = c_ref[own, :], s_ref[own, :]
@@ -236,33 +298,47 @@
                 store,
                 cols,
                 1 << (levels - 1 - level),
-                m_ref[level],
+                matrix,
+                swapped,
                 lambda index: (cosine, sine),
-                32,
+                16,
             )
 
-    def store_block(first, second, block):
-        o_ref[block_at(first, second)] = block
-
-    swap_axes(
-        lambda first, second: state_ref[block_at(first, second)],
-        store_block,
-        cols // 16,
-        rows // 16,
-        p_ref[...],
-    )
-
-
-def target_levels(x, matrices, cosine, sine, shuffle):
+    copies = []
+    for piece in range(rows // 16):
+        own = pl.ds(piece * 16, 16)
+        copies.append(pltpu.make_async_copy(o_ref.at[own], o_hbm.at[own], o_sems.at[piece]))
+
+        def store_block(first, second, block):
+            o_ref[block_at(piece, second)] = block
+
+        swap_axes(
+            lambda first, second: state_ref[block_at(first, piece)],
+            store_block,
+            cols // 16,
+            1,
+            p_ref[...],
+        )
+        copies[-1].start()
+    for copy in copies:
+        copy.wait()
+
+
+def target_levels(x, matrices, angles, shuffle):
     cols, rows, _ = x.shape
+    shape = (rows, cols, WIDE)
     return pl.pallas_call(
         target_kernel,
-        out_shape=jax.ShapeDtypeStruct((rows, cols, WIDE), x.dtype),
+        out_shape=jax.ShapeDtypeStruct(shape, x.dtype),
         in_specs=[VMEM] * 5,
-        out_specs=VMEM,
-        scratch_shapes=[pltpu.VMEM(x.shape, x.dtype)],
+        out_specs=FAR,
+        scratch_shapes=[
+            pltpu.VMEM(x.shape, x.dtype),
+            pltpu.VMEM(shape, x.dtype),
+            pltpu.SemaphoreType.DMA((rows // 16,)),
+        ],
         compiler_params=PARAMS,
-    )(x, matrices, cosine, sine, shuffle)
+    )(matrices, *angles, shuffle, x)
 
 
 def gathered(values, axis):
@@ -298,8 +374,7 @@
     place = lax.axis_index("src") * tgt_count + lax.axis_index("tgt")
     shuffle = jnp.asarray(shuffle_matrix())
 
-    angles = slowness[:, None] * np.tile(node_weights(), 2)
-    state = source_levels(box_weights, matrices_of(0, row_bits), angles, shuffle)
+    state = source_levels(box_weights, matrices_of(0, row_bits), slowness, shuffle)
 
     state, slowness, dip_field = lax.optimization_barrier((state, slowness, dip_field))
     all_dip = gathered(dip_field, "src")
@@ -322,7 +397,7 @@
     return target_levels(
         state.reshape(cols, rows, WIDE),
         matrices_of(first_target + tgt_bits, total),
-        *tables(dip_field),
+        tables(dip_field),
         shuffle,
     )
 

time: 85.9 us -> 79.6 us (0.927)
  local copies, waits for them, and re-layouts: 4.7 us -> 1.5 us
  Pallas kernels: 15.8 us -> 13.6 us
    unnamed x20 -> x14, local copies, waits for them, and re-layouts: 4.54 us -> 1.34 us
    pallas_call x2, Pallas kernels: 12.6 us -> 11.2 us  [the longest x1 6.84 us: source_levels(): pl.pallas_call(source_kernel, out_shape=jax.ShapeDtypeStruct((cols, rows,...]
where the time goes in v8:
time: 79.6 us; the launch traced here: 79.3 us
  blocking collectives  30.1 us (38%)
  starting transfers between devices  17.3 us (22%)
  waiting for transfers between devices  16.1 us (20%)
  Pallas kernels  13.6 us (17%)
  local copies, waits for them, and re-layouts  1.5 us (2%)
    all_to_all x1, blocking collectives, local(): state = lax.all_to_all(state, ('src', 'tgt'), 0, 0, tiled=True)  30.1 us
    ppermute x5, waiting for transfers between devices, gathered(): other = lax.ppermute(values, axis, [(i, i ^ apart) for i in range(count)])  15.2 us
    ppermute x5, starting transfers between devices, gathered(): other = lax.ppermute(values, axis, [(i, i ^ apart) for i in range(count)])  10 us
    all_to_all x1, starting transfers between devices, local(): state = lax.all_to_all(state, ('src', 'tgt'), 0, 0, tiled=True)  7.3 us
    pallas_call x1, Pallas kernels, source_levels(): pl.pallas_call(source_kernel, out_shape=jax.ShapeDtypeStruct((cols, rows,...  6.84 us
    pallas_call x1, Pallas kernels, target_levels(): pl.pallas_call(target_kernel, out_shape=jax.ShapeDtypeStruct(shape, x.dty...  4.32 us
    pallas_call x1, Pallas kernels, middle_levels(): pl.pallas_call(functools.partial(middle_kernel, levels, rows), out_shape=...  2.41 us
  transfers between devices with their start and end apart: 6, of which 5 were waited for; matrix products, arithmetic and copies ran while one was open for 1% of the time, Pallas kernels for 0%

profile of v8, /device:TPU:0, one launch (start us, length us, event | category | flops | bytes accessed | tf_op | source)
XLA Modules:
  0.0 79.3 jit_solution(3039814393321897367)
XLA Ops:
  0.0 0.7 copy-done.3
  0.7 6.8 %shard_map.127 = bf16[128,32,128]{2,1,0:T(8,128)(2,1)} custom-call(f32[1,128]{1,0:T(1,128)S(1)} %bitcast.10, bf16[32,128,128]{2,1,0:T(8,128)(2,1)} %x_hbm.1, bf16[5,256,256]{2,1,0:T(8,128)(2,1)} %constant.31.clone.m_hbm.m_ref, bf16[256,256]{1,0:T(8,128)(2,1)} %constant.30.clone.p_hbm.p_ref), custom_call_target="tpu_custom_call" | custom-call | tf_op jit(solution)/shard_map/pallas_call | solution.py:221
  7.5 0.0 copy-start
  7.5 7.3 %all-to-all-start = ((bf16[32,128,128]{2,1,0:T(8,128)(2,1)}), bf16[32,128,128]{2,1,0:T(8,128)(2,1)S(1)}, u32[]{:S(2)}, u32[]{:S(2)}) async-start(bf16[32,128,128]{2,1,0:T(8,128)(2,1)} %bitcast.1), calls=%async_computation | async-start | bytes 2097152 | tf_op jit(solution)/shard_map/all_to_all | solution.py:385
  14.8 0.0 copy-start.6
  14.8 0.6 copy-done.6
  15.5 1.8 %collective-permute-start.3 = (f32[1,32]{1,0:T(1,128)S(1)}, f32[1,32]{1,0:T(1,128)S(1)}, u32[]{:S(2)}, u32[]{:S(2)}) collective-permute-start(f32[1,32]{1,0:T(1,128)S(1)} %bitcast.12), channel_id=1, source_target_pairs={{0,8},{8,0},{16,24},{24,16},{1,9},{9,1},{17,25},{25,17},{2,10},{10... | collective-permute-start | bytes 392 | tf_op jit(solution)/shard_map/ppermute | solution.py:350
  17.3 0.0 collective-permute-start
  17.3 4.6 %collective-permute-done.3 = f32[1,32]{1,0:T(1,128)S(1)} collective-permute-done((f32[1,32]{1,0:T(1,128)S(1)}, f32[1,32]{1,0:T(1,128)S(1)}, u32[]{:S(2)}, u32[]{:S(2)}) %collective-permute-start.3) | collective-permute-done | bytes 160 | tf_op jit(solution)/shard_map/ppermute | solution.py:350
  21.9 1.5 %collective-permute-start.4 = (f32[2,32]{1,0:T(2,128)S(1)}, f32[2,32]{1,0:T(2,128)S(1)}, u32[]{:S(2)}, u32[]{:S(2)}) collective-permute-start(f32[2,32]{1,0:T(2,128)S(1)} %pad_maximum_fusion.4), channel_id=1, source_target_pairs={{0,16},{8,24},{16,0},{24,8},{1,17},{9,25},{17,1},{25,9},{2,18},{10... | collective-permute-start | bytes 776 | tf_op jit(solution)/shard_map/ppermute | solution.py:350
  23.4 2.2 %collective-permute-done.4 = f32[2,32]{1,0:T(2,128)S(1)} collective-permute-done((f32[2,32]{1,0:T(2,128)S(1)}, f32[2,32]{1,0:T(2,128)S(1)}, u32[]{:S(2)}, u32[]{:S(2)}) %collective-permute-start.4) | collective-permute-done | bytes 288 | tf_op jit(solution)/shard_map/ppermute | solution.py:350
  25.6 0.0 collective-permute-done
  25.7 2.1 %collective-permute-start.1 = (f32[2,128]{1,0:T(2,128)S(1)}, f32[2,128]{1,0:T(2,128)S(1)}, u32[]{:S(2)}, u32[]{:S(2)}) collective-permute-start(f32[2,128]{1,0:T(2,128)S(1)} %pad_maximum_fusion.3), channel_id=1, source_target_pairs={{0,2},{1,3},{2,0},{3,1},{4,6},{5,7},{6,4},{7,5},{8,10},{9,11},{10,... | collective-permute-start | bytes 3080 | tf_op jit(solution)/shard_map/ppermute | solution.py:350
  27.8 4.7 %collective-permute-done.1 = f32[2,128]{1,0:T(2,128)S(1)} collective-permute-done((f32[2,128]{1,0:T(2,128)S(1)}, f32[2,128]{1,0:T(2,128)S(1)}, u32[]{:S(2)}, u32[]{:S(2)}) %collective-permute-start.1) | collective-permute-done | bytes 1056 | tf_op jit(solution)/shard_map/ppermute | solution.py:350
  32.6 0.0 copy-start.5
  32.6 4.6 %collective-permute-start.2 = (f32[4,128]{1,0:T(4,128)S(1)}, f32[4,128]{1,0:T(4,128)S(1)}, u32[]{:S(2)}, u32[]{:S(2)}) collective-permute-start(f32[4,128]{1,0:T(4,128)S(1)} %pad_maximum_fusion.1), channel_id=1, source_target_pairs={{0,4},{1,5},{2,6},{3,7},{4,0},{5,1},{6,2},{7,3},{8,12},{9,13},{10,... | collective-permute-start | bytes 6152 | tf_op jit(solution)/shard_map/ppermute | solution.py:350
  37.1 0.0 copy-done.4
  37.1 0.0 copy-done.5
  37.1 0.3 fusion
  37.5 3.7 %collective-permute-done.2 = f32[4,128]{1,0:T(4,128)S(1)} collective-permute-done((f32[4,128]{1,0:T(4,128)S(1)}, f32[4,128]{1,0:T(4,128)S(1)}, u32[]{:S(2)}, u32[]{:S(2)}) %collective-permute-start.2) | collective-permute-done | bytes 2080 | tf_op jit(solution)/shard_map/ppermute | solution.py:350
  41.2 0.1 constant_dynamic-slice_fusion
  41.3 0.1 mul.78
  41.3 0.2 fusion.2
  41.5 0.9 %all-to-all-done.x_ref = bf16[32,128,128]{2,1,0:T(8,128)(2,1)S(1)} async-done(((bf16[32,128,128]{2,1,0:T(8,128)(2,1)}), bf16[32,128,128]{2,1,0:T(8,128)(2,1)S(1)}, u32[]{:S(2)}, u32[]{:S(2)}) %all-to-all-start) | async-done | bytes 1048608 | tf_op jit(solution)/shard_map/all_to_all | solution.py:385
  42.5 0.0 copy-done
  42.5 2.4 %shard_map.128 = bf16[32,128,128]{2,1,0:T(8,128)(2,1)S(1)} custom-call(bf16[32,128,128]{2,1,0:T(8,128)(2,1)S(1)} %all-to-all-done.x_ref, bf16[5,256,256]{2,1,0:T(8,128)(2,1)S(1)} %copy-done, f32[32,128]{1,0:T(8,128)S(1)} %get-tuple-element.24.cs_ref, f32[32,128]{1,0:T(8,128)S(1)} %get-tuple-element.21.ss_ref, f32[4,32,128]{2,1,0:T(8,128)S(1)} %get-tuple-element.14.ct_ref, ...), custom_call_target="tpu_custom_call" | custom-call | tf_op jit(solution)/shard_map/pallas_call | solution.py:273
  44.9 0.0 copy-start.1
  44.9 0.0 copy-start.2
  44.9 30.1 %all_to_all.10 = bf16[32,128,128]{2,1,0:T(8,128)(2,1)S(1)} all-to-all(bf16[32,128,128]{2,1,0:T(8,128)(2,1)S(1)} %shard_map.128), channel_id=1, replica_groups=mesh['src'=4,'tgt'=8] {'src','tgt'}, dimensions={0} | all-to-all | bytes 2097152 | tf_op jit(solution)/shard_map/all_to_all | solution.py:395
  75.0 0.0 copy-done.1
  75.0 0.0 copy-done.2
  75.0 4.3 %shard_map.129 = bf16[32,128,128]{2,1,0:T(8,128)(2,1)} custom-call(bf16[7,256,256]{2,1,0:T(8,128)(2,1)S(1)} %copy-done.1, f32[32,128]{1,0:T(8,128)S(1)} %get-tuple-element.23.c_ref, f32[32,128]{1,0:T(8,128)S(1)} %get-tuple-element.22.s_ref, bf16[256,256]{1,0:T(8,128)(2,1)S(1)} %copy-done.2, bf16[128,32,128]{2,1,0:T(8,128)(2,1)S(1)} %bitcast.9), custom_call_target="tpu_custom_call" | custom-call | tf_op jit(solution)/shard_map/pallas_call | solution.py:330
  (12 shorter events, 0.1 us)
Async XLA Ops:
  0.0 0.7 copy-start.3
  7.5 35.0 %copy-start = (bf16[5,256,256]{2,1,0:T(8,128)(2,1)S(1)}, bf16[5,256,256]{2,1,0:T(8,128)(2,1)}, u32[]{:S(2)}) copy-start(bf16[5,256,256]{2,1,0:T(8,128)(2,1)} %constant.31.clone.m_hbm.m_ref) | copy-start | bytes 1966084
  7.5 34.9 %all-to-all-start = ((bf16[32,128,128]{2,1,0:T(8,128)(2,1)}), bf16[32,128,128]{2,1,0:T(8,128)(2,1)S(1)}, u32[]{:S(2)}, u32[]{:S(2)}) async-start(bf16[32,128,128]{2,1,0:T(8,128)(2,1)} %bitcast.1), calls=%async_computation | async-start | bytes 2097152 | tf_op jit(solution)/shard_map/all_to_all | solution.py:385
  14.8 0.7 copy-start.6
  15.5 6.4 %collective-permute-start.3 = (f32[1,32]{1,0:T(1,128)S(1)}, f32[1,32]{1,0:T(1,128)S(1)}, u32[]{:S(2)}, u32[]{:S(2)}) collective-permute-start(f32[1,32]{1,0:T(1,128)S(1)} %bitcast.12), channel_id=1, source_target_pairs={{0,8},{8,0},{16,24},{24,16},{1,9},{9,1},{17,25},{25,17},{2,10},{10... | collective-permute-start | bytes 392 | tf_op jit(solution)/shard_map/ppermute | solution.py:350
  17.3 8.4 %collective-permute-start = (f32[1,128]{1,0:T(1,128)S(1)}, f32[1,128]{1,0:T(1,128)S(1)}, u32[]{:S(2)}, u32[]{:S(2)}) collective-permute-start(f32[1,128]{1,0:T(1,128)S(1)} %bitcast.11), channel_id=1, source_target_pairs={{0,1},{1,0},{2,3},{3,2},{4,5},{5,4},{6,7},{7,6},{8,9},{9,8},{10,11... | collective-permute-start | bytes 1544 | tf_op jit(solution)/shard_map/ppermute | solution.py:350
  21.9 3.7 %collective-permute-start.4 = (f32[2,32]{1,0:T(2,128)S(1)}, f32[2,32]{1,0:T(2,128)S(1)}, u32[]{:S(2)}, u32[]{:S(2)}) collective-permute-start(f32[2,32]{1,0:T(2,128)S(1)} %pad_maximum_fusion.4), channel_id=1, source_target_pairs={{0,16},{8,24},{16,0},{24,8},{1,17},{9,25},{17,1},{25,9},{2,18},{10... | collective-permute-start | bytes 776 | tf_op jit(solution)/shard_map/ppermute | solution.py:350
  25.7 6.9 %collective-permute-start.1 = (f32[2,128]{1,0:T(2,128)S(1)}, f32[2,128]{1,0:T(2,128)S(1)}, u32[]{:S(2)}, u32[]{:S(2)}) collective-permute-start(f32[2,128]{1,0:T(2,128)S(1)} %pad_maximum_fusion.3), channel_id=1, source_target_pairs={{0,2},{1,3},{2,0},{3,1},{4,6},{5,7},{6,4},{7,5},{8,10},{9,11},{10,... | collective-permute-start | bytes 3080 | tf_op jit(solution)/shard_map/ppermute | solution.py:350
  32.5 4.6 %copy-start.4 = (f32[128]{0:T(128)S(1)}, f32[128]{0:T(128)}, u32[]{:S(2)}) copy-start(f32[128]{0:T(128)} %constant.33.clone) | copy-start | bytes 1540
  32.6 4.6 %copy-start.5 = (f32[128]{0:T(128)S(1)}, f32[128]{0:T(128)}, u32[]{:S(2)}) copy-start(f32[128]{0:T(128)} %constant.32.clone) | copy-start | bytes 1540
  32.6 8.6 %collective-permute-start.2 = (f32[4,128]{1,0:T(4,128)S(1)}, f32[4,128]{1,0:T(4,128)S(1)}, u32[]{:S(2)}, u32[]{:S(2)}) collective-permute-start(f32[4,128]{1,0:T(4,128)S(1)} %pad_maximum_fusion.1), channel_id=1, source_target_pairs={{0,4},{1,5},{2,6},{3,7},{4,0},{5,1},{6,2},{7,3},{8,12},{9,13},{10,... | collective-permute-start | bytes 6152 | tf_op jit(solution)/shard_map/ppermute | solution.py:350
  44.9 30.1 %copy-start.1 = (bf16[7,256,256]{2,1,0:T(8,128)(2,1)S(1)}, bf16[7,256,256]{2,1,0:T(8,128)(2,1)}, u32[]{:S(2)}) copy-start(bf16[7,256,256]{2,1,0:T(8,128)(2,1)} %constant.34.clone.m_ref) | copy-start | bytes 2752516
  44.9 30.1 %copy-start.2 = (bf16[256,256]{1,0:T(8,128)(2,1)S(1)}, bf16[256,256]{1,0:T(8,128)(2,1)}, u32[]{:S(2)}) copy-start(bf16[256,256]{1,0:T(8,128)(2,1)} %constant.30.clone.p_hbm.p_ref) | copy-start | bytes 393220

commit v9 on v8

--- a/solution.py
+++ b/solution.py
@@ -41,9 +41,7 @@
     real = np.transpose(factor * np.cos(phases), (1, 3, 0, 2))
     imag = np.transpose(factor * np.sin(phases), (1, 3, 0, 2))
     upper = np.concatenate([real, imag], axis=3)
-    lower = np.concatenate([-imag, real], axis=3)
-    full = np.concatenate([upper, lower], axis=1)
-    return full.reshape(2 * WIDE, 2 * WIDE).astype(ml_dtypes.bfloat16)
+    return upper.reshape(WIDE, 2 * WIDE).astype(ml_dtypes.bfloat16)
 
 
 def tables(scales):
@@ -54,10 +52,10 @@
 
 
 def shuffle_matrix():
-    rows = np.arange(256)
-    found = np.zeros((256, 256), np.float32)
-    found[rows, rows % 16 * 16 + rows // 16] = 1.0
-    return found.astype(ml_dtypes.bfloat16)
+    to = lax.broadcasted_iota(jnp.int32, (256, 256), 0)
+    source = lax.broadcasted_iota(jnp.int32, (256, 256), 1)
+    here = source == (to & 15) * 16 + (to >> 4)
+    return jnp.where(here, 1.0, 0.0).astype(jnp.bfloat16)
 
 
 def cos_sin(angles):
@@ -108,14 +106,23 @@
     return jnp.sum(jnp.where(here, jnp.broadcast_to(row, shape), 0.0), axis=1, keepdims=True)
 
 
-def swapped_columns(matrix):
-    parts = [matrix[:, at : at + HALF] for at in (HALF, 0, 3 * HALF, 2 * HALF)]
-    return jnp.concatenate(parts, axis=1)
-
-
-def butterfly(load, store, count, apart, matrix, swapped, phase_of, group):
+def whole_matrix(upper):
+    parts = [upper[:, at : at + HALF] for at in (HALF, 0, 3 * HALF, 2 * HALF)]
+    traded = jnp.concatenate(parts, axis=1)
+    im_lane = (lax.broadcasted_iota(jnp.int32, upper.shape, 1) & HALF) != 0
+    below = jnp.where(im_lane, traded, -traded)
+    traded_below = jnp.where(im_lane, -upper, upper)
+
+    def stacked(first, second):
+        children = (slice(0, HALF), slice(HALF, WIDE))
+        return jnp.concatenate([half[rows] for rows in children for half in (first, second)], axis=0)
+
+    return stacked(upper, below), stacked(traded, traded_below)
+
+
+def butterfly(load, store, count, apart, matrix, swapped, phase_of, group, turn=0):
     lows = [i for i in range(count) if not i & apart]
-    for turn, start in enumerate(range(0, len(lows), group)):
+    for start in range(0, len(lows), group):
         picked = lows[start : start + group]
         left = jnp.concatenate([load(i) for i in picked], axis=0)
         right = jnp.concatenate([load(i + apart) for i in picked], axis=0)
@@ -133,6 +140,7 @@
                 value = both[mine, own]
                 turned = other[mine, own] if turn % 2 == 0 else pltpu.roll(value, HALF, 1)
                 store(index, (value * cosine + turned * sine).astype(jnp.bfloat16))
+        turn += 1
 
 
 def swap_axes(load, store, outer, inner, shuffle):
@@ -151,98 +159,105 @@
     return (slice(first * 16, first * 16 + 16), slice(second * 16, second * 16 + 16))
 
 
-BLOCK = 32
+PIECE = 8
 VMEM = pl.BlockSpec(memory_space=pltpu.VMEM)
 FAR = pl.BlockSpec(memory_space=pltpu.HBM)
 PARAMS = pltpu.CompilerParams(vmem_limit_bytes=32 << 20)
 
 
-def source_kernel(a_ref, x_hbm, m_hbm, p_hbm, o_ref, x_ref, m_ref, p_ref, x_sems, m_sems, p_sem):
+def source_kernel(a_hbm, x_hbm, m_hbm, o_ref, a_ref, x_ref, m_ref, w_ref, a_sem, x_sems, m_sems):
     rows, cols, _ = x_ref.shape
     levels = m_ref.shape[0]
-    starts = range(0, cols, BLOCK)
-    x_copies = [
-        pltpu.make_async_copy(
-            x_hbm.at[:, pl.ds(start, BLOCK)], x_ref.at[:, pl.ds(start, BLOCK)], x_sems.at[piece]
-        )
-        for piece, start in enumerate(starts)
-    ]
+    low_levels = PIECE.bit_length() - 1
+    a_copy = pltpu.make_async_copy(a_hbm, a_ref, a_sem)
+    x_copies = []
+    for piece in range(rows // PIECE):
+        own = pl.ds(piece * PIECE, PIECE)
+        x_copies.append(pltpu.make_async_copy(x_hbm.at[own], x_ref.at[own], x_sems.at[piece]))
     m_copies = [
         pltpu.make_async_copy(m_hbm.at[i], m_ref.at[i], m_sems.at[i]) for i in range(levels)
     ]
-    p_copy = pltpu.make_async_copy(p_hbm, p_ref, p_sem)
-    m_copies[0].start()
-    for copy in x_copies:
+    first = [a_copy, m_copies[0], x_copies[0], *m_copies[1:low_levels], *x_copies[1:]]
+    for copy in first + m_copies[low_levels:]:
         copy.start()
-    for copy in m_copies[1:]:
-        copy.start()
-    p_copy.start()
-
+
+    def ready(level):
+        m_copies[level].wait()
+        w_ref[2 * level], w_ref[2 * level + 1] = whole_matrix(m_ref[level])
+
+    def level_on(level, base, count, begin, block, group, turn):
+        own = slice(begin, begin + block)
+
+        def store(index, value):
+            x_ref[base + index, own, :] = value
+
+        butterfly(
+            lambda index: x_ref[base + index, own, :],
+            store,
+            count,
+            1 << level,
+            w_ref[2 * level],
+            w_ref[2 * level + 1],
+            lambda index: (cosines[own], sines[own]),
+            group,
+            turn,
+        )
+
+    a_copy.wait()
     cosines, sines = rotation(column_of(a_ref[...], cols))
-    for level in range(levels):
-        m_copies[level].wait()
-        matrix = m_ref[level]
-        swapped = swapped_columns(matrix)
-        for piece, start in enumerate(starts):
-            if level == 0:
-                x_copies[piece].wait()
-            cosine, sine = cosines[start : start + BLOCK], sines[start : start + BLOCK]
-
-            def store(index, value):
-                x_ref[index, start : start + BLOCK, :] = value
-
-            butterfly(
-                lambda index: x_ref[index, start : start + BLOCK, :],
-                store,
-                rows,
-                1 << level,
-                matrix,
-                swapped,
-                lambda index: (cosine, sine),
-                8,
-            )
+    for piece in range(rows // PIECE):
+        x_copies[piece].wait()
+        for level in range(low_levels):
+            if piece == 0:
+                ready(level)
+            for turn, begin in enumerate(range(0, cols, 64)):
+                level_on(level, piece * PIECE, PIECE, begin, 64, PIECE // 2, turn)
+    for level in range(low_levels, levels):
+        ready(level)
+        for begin in range(0, cols, 32):
+            level_on(level, 0, rows, begin, 32, 8, 0)
 
     def store_block(first, second, block):
         o_ref[block_at(first, second)] = block
 
-    p_copy.wait()
     swap_axes(
         lambda first, second: x_ref[block_at(first, second)],
         store_block,
         rows // 16,
         cols // 16,
-        p_ref[...],
+        shuffle_matrix(),
     )
 
 
-def source_levels(x, matrices, slowness, shuffle):
+def source_levels(x, matrices, slowness):
     rows, cols, _ = x.shape
-    far = [pltpu.with_memory_space_constraint(v, pltpu.HBM) for v in (x, matrices, shuffle)]
+    levels = matrices.shape[0]
+    far = [pltpu.with_memory_space_constraint(v, pltpu.HBM) for v in (slowness[None, :], x, matrices)]
     return pl.pallas_call(
         source_kernel,
         out_shape=jax.ShapeDtypeStruct((cols, rows, WIDE), x.dtype),
-        in_specs=[VMEM, FAR, FAR, FAR],
+        in_specs=[FAR, FAR, FAR],
         out_specs=VMEM,
         scratch_shapes=[
+            pltpu.VMEM((1, cols), jnp.float32),
             pltpu.VMEM(x.shape, x.dtype),
             pltpu.VMEM(matrices.shape, x.dtype),
-            pltpu.VMEM(shuffle.shape, x.dtype),
-            pltpu.SemaphoreType.DMA((cols // BLOCK,)),
-            pltpu.SemaphoreType.DMA((matrices.shape[0],)),
+            pltpu.VMEM((2 * levels, 2 * WIDE, 2 * WIDE), x.dtype),
             pltpu.SemaphoreType.DMA,
+            pltpu.SemaphoreType.DMA((rows // PIECE,)),
+            pltpu.SemaphoreType.DMA((levels,)),
         ],
         compiler_params=PARAMS,
-    )(slowness[None, :], *far)
-
-
-def middle_kernel(levels, rows, x_ref, m_ref, cs_ref, ss_ref, ct_ref, st_ref, o_ref):
+    )(*far)
+
+
+def middle_kernel(levels, spots, rows, x_ref, m_ref, cs_ref, ss_ref, ct_ref, st_ref, o_ref):
     count, total, _ = x_ref.shape
     run = total // rows
     tgt_count = cs_ref.shape[0] // run
     for step, (apart, by_source) in enumerate(levels):
         source = x_ref if step == 0 else o_ref
-        matrix = m_ref[step]
-        swapped = swapped_columns(matrix)
+        matrix, swapped = whole_matrix(m_ref[step])
         for col in range(run):
             own = slice(col * rows, (col + 1) * rows)
 
@@ -254,10 +269,10 @@
                 return ct_ref[at], st_ref[at]
 
             def store(index, value):
-                o_ref[index, own, :] = value
+                o_ref[spots[index], own, :] = value
 
             butterfly(
-                lambda index: source[index, own, :],
+                lambda index: source[spots[index], own, :],
                 store,
                 count,
                 apart,
@@ -268,10 +283,10 @@
             )
 
 
-def middle_levels(x, matrices, src_tables, tgt_tables, levels):
+def middle_levels(x, matrices, src_tables, tgt_tables, levels, spots):
     rows = tgt_tables[0].shape[1]
     return pl.pallas_call(
-        functools.partial(middle_kernel, levels, rows),
+        functools.partial(middle_kernel, levels, spots, rows),
         out_shape=jax.ShapeDtypeStruct(x.shape, x.dtype),
         in_specs=[VMEM] * 6,
         out_specs=VMEM,
@@ -279,13 +294,12 @@
     )(x, matrices, *src_tables, *tgt_tables)
 
 
-def target_kernel(m_ref, c_ref, s_ref, p_ref, x_ref, o_hbm, state_ref, o_ref, o_sems):
+def target_kernel(m_ref, c_ref, s_ref, x_ref, o_hbm, state_ref, o_ref, o_sems):
     cols, rows, _ = x_ref.shape
     levels = m_ref.shape[0]
     for level in range(levels):
         source = x_ref if level == 0 else state_ref
-        matrix = m_ref[level]
-        swapped = swapped_columns(matrix)
+        matrix, swapped = whole_matrix(m_ref[level])
         for start in range(0, rows, 16):
             own = slice(start, start + 16)
             cosine, sine = c_ref[own, :], s_ref[own, :]
@@ -304,6 +318,7 @@
                 16,
             )
 
+    shuffle = shuffle_matrix()
     copies = []
     for piece in range(rows // 16):
         own = pl.ds(piece * 16, 16)
@@ -317,20 +332,20 @@
             store_block,
             cols // 16,
             1,
-            p_ref[...],
+            shuffle,
         )
         copies[-1].start()
     for copy in copies:
         copy.wait()
 
 
-def target_levels(x, matrices, angles, shuffle):
+def target_levels(x, matrices, angles):
     cols, rows, _ = x.shape
     shape = (rows, cols, WIDE)
     return pl.pallas_call(
         target_kernel,
         out_shape=jax.ShapeDtypeStruct(shape, x.dtype),
-        in_specs=[VMEM] * 5,
+        in_specs=[VMEM] * 4,
         out_specs=FAR,
         scratch_shapes=[
             pltpu.VMEM(x.shape, x.dtype),
@@ -338,7 +353,7 @@
             pltpu.SemaphoreType.DMA((rows // 16,)),
         ],
         compiler_params=PARAMS,
-    )(matrices, *angles, shuffle, x)
+    )(matrices, *angles, x)
 
 
 def gathered(values, axis):
@@ -371,10 +386,18 @@
         return jnp.asarray(np.stack(matrices[low:high]))
 
     run = cols // devices
-    place = lax.axis_index("src") * tgt_count + lax.axis_index("tgt")
-    shuffle = jnp.asarray(shuffle_matrix())
-
-    state = source_levels(box_weights, matrices_of(0, row_bits), slowness, shuffle)
+    pairs = sorted(range(tgt_count // 2), key=lambda at: abs(2 * at + 1 - tgt_count // 2))
+    tgt_order = [2 * at + side for at in pairs for side in range(2)]
+    order = [src * tgt_count + tgt for src in range(src_count) for tgt in tgt_order]
+    spots = [order.index(device) for device in range(devices)]
+    place = jnp.asarray(spots)[lax.axis_index("src") * tgt_count + lax.axis_index("tgt")]
+
+    def traded(state):
+        return lax.all_to_all(
+            state, ("src", "tgt"), 0, 0, axis_index_groups=[order], tiled=True
+        )
+
+    state = source_levels(box_weights, matrices_of(0, row_bits), slowness)
 
     state, slowness, dip_field = lax.optimization_barrier((state, slowness, dip_field))
     all_dip = gathered(dip_field, "src")
@@ -382,7 +405,7 @@
     run_slowness = lax.dynamic_slice_in_dim(all_slowness, place * run, run, 1)
 
     state = state.reshape(devices, run * rows, WIDE)
-    state = lax.all_to_all(state, ("src", "tgt"), 0, 0, tiled=True)
+    state = traded(state)
     levels = [(tgt_count << bit, True) for bit in range(src_bits)]
     levels += [(1 << bit, False) for bit in reversed(range(tgt_bits))]
     state = middle_levels(
@@ -391,14 +414,14 @@
         tables(run_slowness.reshape(-1)),
         tables(all_dip),
         levels,
+        spots,
     )
-    state = lax.all_to_all(state, ("src", "tgt"), 0, 0, tiled=True)
+    state = traded(state)
 
     return target_levels(
         state.reshape(cols, rows, WIDE),
         matrices_of(first_target + tgt_bits, total),
         tables(dip_field),
-        shuffle,
     )
 
 

time: 79.6 us -> 79.4 us (level)
  starting transfers between devices: 17.3 us -> 15.3 us
  Pallas kernels: 13.6 us -> 14.7 us
  waiting for transfers between devices: 16.1 us -> 16.9 us
    ppermute x5, starting transfers between devices: 10 us -> 7.96 us  [gathered(): other = lax.ppermute(values, axis, [(i, i ^ apart) for i in range(count)])]
    ppermute x5, waiting for transfers between devices: 15.2 us -> 16.7 us  [gathered(): other = lax.ppermute(values, axis, [(i, i ^ apart) for i in range(count)])]
    unnamed x14, local copies, waits for them, and re-layouts: 1.34 us -> 0.05 us
    pallas_call x1, Pallas kernels: 6.84 us -> 7.86 us  [source_levels(): pl.pallas_call(source_kernel, out_shape=jax.ShapeDtypeStruct((cols, rows,...]
  transfers between devices with their start and end apart: 6 -> 6, of which waited for: 5 -> 5; matrix products, arithmetic and copies ran while one was open for 1% -> 2% of each run, Pallas kernels for 0% -> 0%
where the time goes in v9:
time: 79.4 us; the launch traced here: 79.2 us
  blocking collectives  30.1 us (38%)
  waiting for transfers between devices  16.9 us (21%)
  starting transfers between devices  15.3 us (19%)
  Pallas kernels  14.7 us (19%)
  between operations  0.89 us (1%)
    all_to_all x1, blocking collectives, traded(): lax.all_to_all(state, ('src', 'tgt'), 0, 0, axis_index_groups=[order], ti...  30.1 us
    ppermute x5, waiting for transfers between devices, gathered(): other = lax.ppermute(values, axis, [(i, i ^ apart) for i in range(count)])  16.7 us
    ppermute x5, starting transfers between devices, gathered(): other = lax.ppermute(values, axis, [(i, i ^ apart) for i in range(count)])  7.96 us
    pallas_call x1, Pallas kernels, source_levels(): pl.pallas_call(source_kernel, out_shape=jax.ShapeDtypeStruct((cols, rows,...  7.86 us
    all_to_all x1, starting transfers between devices, traded(): lax.all_to_all(state, ('src', 'tgt'), 0, 0, axis_index_groups=[order], ti...  7.3 us
    pallas_call x1, Pallas kernels, target_levels(): pl.pallas_call(target_kernel, out_shape=jax.ShapeDtypeStruct(shape, x.dty...  4.39 us
    pallas_call x1, Pallas kernels, middle_levels(): pl.pallas_call(functools.partial(middle_kernel, levels, spots, rows), out...  2.43 us
  transfers between devices with their start and end apart: 6, of which 5 were waited for; matrix products, arithmetic and copies ran while one was open for 2% of the time, Pallas kernels for 0%

profile of v9, /device:TPU:0, one launch (start us, length us, event | category | flops | bytes accessed | tf_op | source)
XLA Modules:
  0.0 79.2 jit_solution(12970144681537845120)
XLA Ops:
  0.0 7.9 %shard_map.127 = bf16[128,32,128]{2,1,0:T(8,128)(2,1)} custom-call(f32[1,128]{1,0:T(1,128)} %bitcast.12, bf16[32,128,128]{2,1,0:T(8,128)(2,1)} %x_hbm.1, bf16[5,128,256]{2,1,0:T(8,128)(2,1)} %constant.35.clone.m_hbm.m_ref), custom_call_target="tpu_custom_call" | custom-call | tf_op jit(solution)/shard_map/pallas_call | solution.py:236
  7.9 0.0 copy-start.4
  7.9 0.0 copy-start.5
  7.9 0.0 copy-start.6
  7.9 0.0 copy-start.2
  7.9 0.0 copy-start.3
  7.9 7.3 %all-to-all-start = ((bf16[32,128,128]{2,1,0:T(8,128)(2,1)}), bf16[32,128,128]{2,1,0:T(8,128)(2,1)S(1)}, u32[]{:S(2)}, u32[]{:S(2)}) async-start(bf16[32,128,128]{2,1,0:T(8,128)(2,1)} %bitcast.1), calls=%async_computation | async-start | bytes 2097152 | tf_op jit(solution)/shard_map/all_to_all | solution.py:396
  15.2 0.0 copy-start
  15.3 1.8 %collective-permute-start.3 = (f32[1,32]{1,0:T(1,128)S(1)}, f32[1,32]{1,0:T(1,128)S(1)}, u32[]{:S(2)}, u32[]{:S(2)}) collective-permute-start(f32[1,32]{1,0:T(1,128)S(1)} %bitcast.11), channel_id=1, source_target_pairs={{0,8},{8,0},{16,24},{24,16},{1,9},{9,1},{17,25},{25,17},{2,10},{10... | collective-permute-start | bytes 392 | tf_op jit(solution)/shard_map/ppermute | solution.py:365
  17.1 0.0 copy-done.5
  17.1 0.0 collective-permute-start
  17.1 0.6 dynamic_slice.6
  18.3 5.5 %collective-permute-done.3 = f32[1,32]{1,0:T(1,128)S(1)} collective-permute-done((f32[1,32]{1,0:T(1,128)S(1)}, f32[1,32]{1,0:T(1,128)S(1)}, u32[]{:S(2)}, u32[]{:S(2)}) %collective-permute-start.3) | collective-permute-done | bytes 160 | tf_op jit(solution)/shard_map/ppermute | solution.py:365
  23.7 1.5 %collective-permute-start.4 = (f32[2,32]{1,0:T(2,128)S(1)}, f32[2,32]{1,0:T(2,128)S(1)}, u32[]{:S(2)}, u32[]{:S(2)}) collective-permute-start(f32[2,32]{1,0:T(2,128)S(1)} %pad_maximum_fusion.4), channel_id=1, source_target_pairs={{0,16},{8,24},{16,0},{24,8},{1,17},{9,25},{17,1},{25,9},{2,18},{10... | collective-permute-start | bytes 776 | tf_op jit(solution)/shard_map/ppermute | solution.py:365
  25.3 2.1 %collective-permute-done.4 = f32[2,32]{1,0:T(2,128)S(1)} collective-permute-done((f32[2,32]{1,0:T(2,128)S(1)}, f32[2,32]{1,0:T(2,128)S(1)}, u32[]{:S(2)}, u32[]{:S(2)}) %collective-permute-start.4) | collective-permute-done | bytes 288 | tf_op jit(solution)/shard_map/ppermute | solution.py:365
  27.4 0.0 collective-permute-done
  27.4 0.1 collective-permute-start.1
  27.5 5.4 %collective-permute-done.1 = f32[2,128]{1,0:T(2,128)S(1)} collective-permute-done((f32[2,128]{1,0:T(2,128)S(1)}, f32[2,128]{1,0:T(2,128)S(1)}, u32[]{:S(2)}, u32[]{:S(2)}) %collective-permute-start.1) | collective-permute-done | bytes 1056 | tf_op jit(solution)/shard_map/ppermute | solution.py:365
  33.0 4.5 %collective-permute-start.2 = (f32[4,128]{1,0:T(4,128)S(1)}, f32[4,128]{1,0:T(4,128)S(1)}, u32[]{:S(2)}, u32[]{:S(2)}) collective-permute-start(f32[4,128]{1,0:T(4,128)S(1)} %pad_maximum_fusion.1), channel_id=1, source_target_pairs={{0,4},{1,5},{2,6},{3,7},{4,0},{5,1},{6,2},{7,3},{8,12},{9,13},{10,... | collective-permute-start | bytes 6152 | tf_op jit(solution)/shard_map/ppermute | solution.py:365
  37.5 0.0 copy-done.2
  37.5 0.3 fusion
  37.8 3.8 %collective-permute-done.2 = f32[4,128]{1,0:T(4,128)S(1)} collective-permute-done((f32[4,128]{1,0:T(4,128)S(1)}, f32[4,128]{1,0:T(4,128)S(1)}, u32[]{:S(2)}, u32[]{:S(2)}) %collective-permute-start.2) | collective-permute-done | bytes 2080 | tf_op jit(solution)/shard_map/ppermute | solution.py:365
  41.6 0.1 constant_dynamic-slice_fusion
  41.7 0.1 mul.82
  41.7 0.2 fusion.2
  42.0 0.1 all-to-all-done.x_ref
  42.1 0.0 copy-done
  42.1 2.4 %shard_map.128 = bf16[32,128,128]{2,1,0:T(8,128)(2,1)S(1)} custom-call(bf16[32,128,128]{2,1,0:T(8,128)(2,1)S(1)} %all-to-all-done.x_ref, bf16[5,128,256]{2,1,0:T(8,128)(2,1)S(1)} %copy-done, f32[32,128]{1,0:T(8,128)S(1)} %get-tuple-element.24.cs_ref, f32[32,128]{1,0:T(8,128)S(1)} %get-tuple-element.21.ss_ref, f32[4,32,128]{2,1,0:T(8,128)S(1)} %get-tuple-element.14.ct_ref, ...), custom_call_target="tpu_custom_call" | custom-call | tf_op jit(solution)/shard_map/pallas_call | solution.py:288
  44.5 0.0 copy-start.1
  44.5 30.1 %all_to_all.10 = bf16[32,128,128]{2,1,0:T(8,128)(2,1)S(1)} all-to-all(bf16[32,128,128]{2,1,0:T(8,128)(2,1)S(1)} %shard_map.128), channel_id=1, replica_groups={{2,3,4,5,0,1,6,7,10,11,12,13,8,9,14,15,18,19,20,21,16,17,22,23,26,27,28..., dimensions={0} | all-to-all | bytes 2097152 | tf_op jit(solution)/shard_map/all_to_all | solution.py:396
  74.6 0.0 copy-done.1
  74.6 4.4 %shard_map.129 = bf16[32,128,128]{2,1,0:T(8,128)(2,1)} custom-call(bf16[7,128,256]{2,1,0:T(8,128)(2,1)S(1)} %copy-done.1, f32[32,128]{1,0:T(8,128)S(1)} %get-tuple-element.23.c_ref, f32[32,128]{1,0:T(8,128)S(1)} %get-tuple-element.22.s_ref, bf16[128,32,128]{2,1,0:T(8,128)(2,1)S(1)} %bitcast.10), custom_call_target="tpu_custom_call" | custom-call | tf_op jit(solution)/shard_map/pallas_call | solution.py:345
  (13 shorter events, 0.1 us)
Async XLA Ops:
  7.9 7.4 %copy-start.4 = (f32[32]{0:T(128)S(1)}, f32[32]{0:T(128)}, u32[]{:S(2)}) copy-start(f32[32]{0:T(128)} %param.15) | copy-start | bytes 388
  7.9 9.2 %copy-start.5 = (f32[128]{0:T(128)S(1)}, f32[128]{0:T(128)}, u32[]{:S(2)}) copy-start(f32[128]{0:T(128)} %param.14) | copy-start | bytes 1540
  7.9 9.2 %copy-start.6 = (s32[32]{0:T(128)S(1)}, s32[32]{0:T(128)}, u32[]{:S(2)}) copy-start(s32[32]{0:T(128)} %constant.34.clone) | copy-start | bytes 388
  7.9 29.6 %copy-start.2 = (f32[128]{0:T(128)S(1)}, f32[128]{0:T(128)}, u32[]{:S(2)}) copy-start(f32[128]{0:T(128)} %constant.37.clone) | copy-start | bytes 1540
  7.9 29.6 %copy-start.3 = (f32[128]{0:T(128)S(1)}, f32[128]{0:T(128)}, u32[]{:S(2)}) copy-start(f32[128]{0:T(128)} %constant.36.clone) | copy-start | bytes 1540
  7.9 34.2 %all-to-all-start = ((bf16[32,128,128]{2,1,0:T(8,128)(2,1)}), bf16[32,128,128]{2,1,0:T(8,128)(2,1)S(1)}, u32[]{:S(2)}, u32[]{:S(2)}) async-start(bf16[32,128,128]{2,1,0:T(8,128)(2,1)} %bitcast.1), calls=%async_computation | async-start | bytes 2097152 | tf_op jit(solution)/shard_map/all_to_all | solution.py:396
  15.2 26.9 %copy-start = (bf16[5,128,256]{2,1,0:T(8,128)(2,1)S(1)}, bf16[5,128,256]{2,1,0:T(8,128)(2,1)}, u32[]{:S(2)}) copy-start(bf16[5,128,256]{2,1,0:T(8,128)(2,1)} %constant.35.clone.m_hbm.m_ref) | copy-start | bytes 983044
  15.3 8.5 %collective-permute-start.3 = (f32[1,32]{1,0:T(1,128)S(1)}, f32[1,32]{1,0:T(1,128)S(1)}, u32[]{:S(2)}, u32[]{:S(2)}) collective-permute-start(f32[1,32]{1,0:T(1,128)S(1)} %bitcast.11), channel_id=1, source_target_pairs={{0,8},{8,0},{16,24},{24,16},{1,9},{9,1},{17,25},{25,17},{2,10},{10... | collective-permute-start | bytes 392 | tf_op jit(solution)/shard_map/ppermute | solution.py:365
  17.1 10.3 %collective-permute-start = (f32[1,128]{1,0:T(1,128)S(1)}, f32[1,128]{1,0:T(1,128)S(1)}, u32[]{:S(2)}, u32[]{:S(2)}) collective-permute-start(f32[1,128]{1,0:T(1,128)S(1)} %bitcast.13), channel_id=1, source_target_pairs={{0,1},{1,0},{2,3},{3,2},{4,5},{5,4},{6,7},{7,6},{8,9},{9,8},{10,11... | collective-permute-start | bytes 1544 | tf_op jit(solution)/shard_map/ppermute | solution.py:365
  23.7 3.6 %collective-permute-start.4 = (f32[2,32]{1,0:T(2,128)S(1)}, f32[2,32]{1,0:T(2,128)S(1)}, u32[]{:S(2)}, u32[]{:S(2)}) collective-permute-start(f32[2,32]{1,0:T(2,128)S(1)} %pad_maximum_fusion.4), channel_id=1, source_target_pairs={{0,16},{8,24},{16,0},{24,8},{1,17},{9,25},{17,1},{25,9},{2,18},{10... | collective-permute-start | bytes 776 | tf_op jit(solution)/shard_map/ppermute | solution.py:365
  27.4 5.5 %collective-permute-start.1 = (f32[2,128]{1,0:T(2,128)S(1)}, f32[2,128]{1,0:T(2,128)S(1)}, u32[]{:S(2)}, u32[]{:S(2)}) collective-permute-start(f32[2,128]{1,0:T(2,128)S(1)} %pad_maximum_fusion.3), channel_id=1, source_target_pairs={{0,2},{1,3},{2,0},{3,1},{4,6},{5,7},{6,4},{7,5},{8,10},{9,11},{10,... | collective-permute-start | bytes 3080 | tf_op jit(solution)/shard_map/ppermute | solution.py:365
  33.0 8.6 %collective-permute-start.2 = (f32[4,128]{1,0:T(4,128)S(1)}, f32[4,128]{1,0:T(4,128)S(1)}, u32[]{:S(2)}, u32[]{:S(2)}) collective-permute-start(f32[4,128]{1,0:T(4,128)S(1)} %pad_maximum_fusion.1), channel_id=1, source_target_pairs={{0,4},{1,5},{2,6},{3,7},{4,0},{5,1},{6,2},{7,3},{8,12},{9,13},{10,... | collective-permute-start | bytes 6152 | tf_op jit(solution)/shard_map/ppermute | solution.py:365
  44.5 30.1 %copy-start.1 = (bf16[7,128,256]{2,1,0:T(8,128)(2,1)S(1)}, bf16[7,128,256]{2,1,0:T(8,128)(2,1)}, u32[]{:S(2)}) copy-start(bf16[7,128,256]{2,1,0:T(8,128)(2,1)} %constant.38.clone.m_ref) | copy-start | bytes 1376260

commit v10 on v9

--- a/solution.py
+++ b/solution.py
@@ -159,7 +159,8 @@
     return (slice(first * 16, first * 16 + 16), slice(second * 16, second * 16 + 16))
 
 
-PIECE = 8
+PIECE = 64
+BLOCK = 32
 VMEM = pl.BlockSpec(memory_space=pltpu.VMEM)
 FAR = pl.BlockSpec(memory_space=pltpu.HBM)
 PARAMS = pltpu.CompilerParams(vmem_limit_bytes=32 << 20)
@@ -168,54 +169,52 @@
 def source_kernel(a_hbm, x_hbm, m_hbm, o_ref, a_ref, x_ref, m_ref, w_ref, a_sem, x_sems, m_sems):
     rows, cols, _ = x_ref.shape
     levels = m_ref.shape[0]
-    low_levels = PIECE.bit_length() - 1
     a_copy = pltpu.make_async_copy(a_hbm, a_ref, a_sem)
     x_copies = []
-    for piece in range(rows // PIECE):
-        own = pl.ds(piece * PIECE, PIECE)
+    for piece in range(cols // PIECE):
+        own = (slice(None), pl.ds(piece * PIECE, PIECE))
         x_copies.append(pltpu.make_async_copy(x_hbm.at[own], x_ref.at[own], x_sems.at[piece]))
     m_copies = [
         pltpu.make_async_copy(m_hbm.at[i], m_ref.at[i], m_sems.at[i]) for i in range(levels)
     ]
-    first = [a_copy, m_copies[0], x_copies[0], *m_copies[1:low_levels], *x_copies[1:]]
-    for copy in first + m_copies[low_levels:]:
+    for copy in (a_copy, m_copies[0], *x_copies, *m_copies[1:]):
         copy.start()
 
-    def ready(level):
-        m_copies[level].wait()
+    def expand(level):
         w_ref[2 * level], w_ref[2 * level + 1] = whole_matrix(m_ref[level])
 
-    def level_on(level, base, count, begin, block, group, turn):
-        own = slice(begin, begin + block)
+    def level_on(level, begin):
+        own = slice(begin, begin + BLOCK)
 
         def store(index, value):
-            x_ref[base + index, own, :] = value
+            x_ref[index, own, :] = value
 
         butterfly(
-            lambda index: x_ref[base + index, own, :],
+            lambda index: x_ref[index, own, :],
             store,
-            count,
+            rows,
             1 << level,
             w_ref[2 * level],
             w_ref[2 * level + 1],
             lambda index: (cosines[own], sines[own]),
-            group,
-            turn,
+            8,
         )
 
     a_copy.wait()
     cosines, sines = rotation(column_of(a_ref[...], cols))
-    for piece in range(rows // PIECE):
-        x_copies[piece].wait()
-        for level in range(low_levels):
-            if piece == 0:
-                ready(level)
-            for turn, begin in enumerate(range(0, cols, 64)):
-                level_on(level, piece * PIECE, PIECE, begin, 64, PIECE // 2, turn)
-    for level in range(low_levels, levels):
-        ready(level)
-        for begin in range(0, cols, 32):
-            level_on(level, 0, rows, begin, 32, 8, 0)
+    m_copies[0].wait()
+    expand(0)
+    for piece, copy in enumerate(x_copies):
+        copy.wait()
+        for begin in range(piece * PIECE, (piece + 1) * PIECE, BLOCK):
+            level_on(0, begin)
+    for copy in m_copies[1:]:
+        copy.wait()
+    for level in range(1, levels):
+        expand(level)
+    for level in range(1, levels):
+        for begin in range(0, cols, BLOCK):
+            level_on(level, begin)
 
     def store_block(first, second, block):
         o_ref[block_at(first, second)] = block
@@ -232,7 +231,8 @@
 def source_levels(x, matrices, slowness):
     rows, cols, _ = x.shape
     levels = matrices.shape[0]
-    far = [pltpu.with_memory_space_constraint(v, pltpu.HBM) for v in (slowness[None, :], x, matrices)]
+    operands = (slowness[None, :], x, matrices)
+    far = [pltpu.with_memory_space_constraint(value, pltpu.HBM) for value in operands]
     return pl.pallas_call(
         source_kernel,
         out_shape=jax.ShapeDtypeStruct((cols, rows, WIDE), x.dtype),
@@ -244,14 +244,14 @@
             pltpu.VMEM(matrices.shape, x.dtype),
             pltpu.VMEM((2 * levels, 2 * WIDE, 2 * WIDE), x.dtype),
             pltpu.SemaphoreType.DMA,
-            pltpu.SemaphoreType.DMA((rows // PIECE,)),
+            pltpu.SemaphoreType.DMA((cols // PIECE,)),
             pltpu.SemaphoreType.DMA((levels,)),
         ],
         compiler_params=PARAMS,
     )(*far)
 
 
-def middle_kernel(levels, spots, rows, x_ref, m_ref, cs_ref, ss_ref, ct_ref, st_ref, o_ref):
+def middle_kernel(levels, rows, x_ref, m_ref, cs_ref, ss_ref, ct_ref, st_ref, o_ref):
     count, total, _ = x_ref.shape
     run = total // rows
     tgt_count = cs_ref.shape[0] // run
@@ -269,10 +269,10 @@
                 return ct_ref[at], st_ref[at]
 
             def store(index, value):
-                o_ref[spots[index], own, :] = value
+                o_ref[index, own, :] = value
 
             butterfly(
-                lambda index: source[spots[index], own, :],
+                lambda index: source[index, own, :],
                 store,
                 count,
                 apart,
@@ -283,10 +283,10 @@
             )
 
 
-def middle_levels(x, matrices, src_tables, tgt_tables, levels, spots):
+def middle_levels(x, matrices, src_tables, tgt_tables, levels):
     rows = tgt_tables[0].shape[1]
     return pl.pallas_call(
-        functools.partial(middle_kernel, levels, spots, rows),
+        functools.partial(middle_kernel, levels, rows),
         out_shape=jax.ShapeDtypeStruct(x.shape, x.dtype),
         in_specs=[VMEM] * 6,
         out_specs=VMEM,
@@ -297,30 +297,35 @@
 def target_kernel(m_ref, c_ref, s_ref, x_ref, o_hbm, state_ref, o_ref, o_sems):
     cols, rows, _ = x_ref.shape
     levels = m_ref.shape[0]
-    for level in range(levels):
+
+    def level_on(level, start, weights):
         source = x_ref if level == 0 else state_ref
-        matrix, swapped = whole_matrix(m_ref[level])
+        own = slice(start, start + 16)
+        cosine, sine = c_ref[own, :], s_ref[own, :]
+
+        def store(index, value):
+            state_ref[index, own, :] = value
+
+        butterfly(
+            lambda index: source[index, own, :],
+            store,
+            cols,
+            1 << (levels - 1 - level),
+            *weights,
+            lambda index: (cosine, sine),
+            16,
+        )
+
+    for level in range(levels - 1):
+        weights = whole_matrix(m_ref[level])
         for start in range(0, rows, 16):
-            own = slice(start, start + 16)
-            cosine, sine = c_ref[own, :], s_ref[own, :]
-
-            def store(index, value):
-                state_ref[index, own, :] = value
-
-            butterfly(
-                lambda index: source[index, own, :],
-                store,
-                cols,
-                1 << (levels - 1 - level),
-                matrix,
-                swapped,
-                lambda index: (cosine, sine),
-                16,
-            )
-
+            level_on(level, start, weights)
+
+    weights = whole_matrix(m_ref[levels - 1])
     shuffle = shuffle_matrix()
     copies = []
     for piece in range(rows // 16):
+        level_on(levels - 1, piece * 16, weights)
         own = pl.ds(piece * 16, 16)
         copies.append(pltpu.make_async_copy(o_ref.at[own], o_hbm.at[own], o_sems.at[piece]))
 
@@ -386,16 +391,10 @@
         return jnp.asarray(np.stack(matrices[low:high]))
 
     run = cols // devices
-    pairs = sorted(range(tgt_count // 2), key=lambda at: abs(2 * at + 1 - tgt_count // 2))
-    tgt_order = [2 * at + side for at in pairs for side in range(2)]
-    order = [src * tgt_count + tgt for src in range(src_count) for tgt in tgt_order]
-    spots = [order.index(device) for device in range(devices)]
-    place = jnp.asarray(spots)[lax.axis_index("src") * tgt_count + lax.axis_index("tgt")]
+    place = lax.axis_index("src") * tgt_count + lax.axis_index("tgt")
 
     def traded(state):
-        return lax.all_to_all(
-            state, ("src", "tgt"), 0, 0, axis_index_groups=[order], tiled=True
-        )
+        return lax.all_to_all(state, ("src", "tgt"), 0, 0, tiled=True)
 
     state = source_levels(box_weights, matrices_of(0, row_bits), slowness)
 
@@ -414,7 +413,6 @@
         tables(run_slowness.reshape(-1)),
         tables(all_dip),
         levels,
-        spots,
     )
     state = traded(state)
 

time: 79.4 us -> 77.9 us (0.981)
  Pallas kernels: 14.7 us -> 12.5 us
  starting transfers between devices: 15.3 us -> 17.4 us
    pallas_call x1, Pallas kernels: 7.86 us -> 5.38 us  [source_levels(): pl.pallas_call(source_kernel, out_shape=jax.ShapeDtypeStruct((cols, rows,...]
    ppermute x5, starting transfers between devices: 7.96 us -> 10.1 us  [gathered(): other = lax.ppermute(values, axis, [(i, i ^ apart) for i in range(count)])]
    ppermute x5, waiting for transfers between devices: 16.7 us -> 15.8 us  [gathered(): other = lax.ppermute(values, axis, [(i, i ^ apart) for i in range(count)])]
  transfers between devices with their start and end apart: 6 -> 6, of which waited for: 5 -> 5; matrix products, arithmetic and copies ran while one was open for 2% -> 1% of each run, Pallas kernels for 0% -> 0%
where the time goes in v10:
time: 77.9 us; the launch traced here: 77.6 us
  blocking collectives  30.1 us (39%)
  starting transfers between devices  17.4 us (22%)
  waiting for transfers between devices  16.7 us (21%)
  Pallas kernels  12.5 us (16%)
    all_to_all x1, blocking collectives, traded(): return lax.all_to_all(state, ('src', 'tgt'), 0, 0, tiled=True)  30.1 us
    ppermute x5, waiting for transfers between devices, gathered(): other = lax.ppermute(values, axis, [(i, i ^ apart) for i in range(count)])  15.8 us
    ppermute x5, starting transfers between devices, gathered(): other = lax.ppermute(values, axis, [(i, i ^ apart) for i in range(count)])  10.1 us
    all_to_all x1, starting transfers between devices, traded(): return lax.all_to_all(state, ('src', 'tgt'), 0, 0, tiled=True)  7.3 us
    pallas_call x1, Pallas kernels, source_levels(): pl.pallas_call(source_kernel, out_shape=jax.ShapeDtypeStruct((cols, rows,...  5.38 us
    pallas_call x1, Pallas kernels, target_levels(): pl.pallas_call(target_kernel, out_shape=jax.ShapeDtypeStruct(shape, x.dty...  4.67 us
    pallas_call x1, Pallas kernels, middle_levels(): pl.pallas_call(functools.partial(middle_kernel, levels, rows), out_shape=...  2.43 us
  transfers between devices with their start and end apart: 6, of which 5 were waited for; matrix products, arithmetic and copies ran while one was open for 1% of the time, Pallas kernels for 0%

profile of v10, /device:TPU:0, one launch (start us, length us, event | category | flops | bytes accessed | tf_op | source)
XLA Modules:
  0.0 77.6 jit_solution(16809581735985691557)
XLA Ops:
  0.0 5.4 %shard_map.118 = bf16[128,32,128]{2,1,0:T(8,128)(2,1)} custom-call(f32[1,128]{1,0:T(1,128)} %bitcast.11, bf16[32,128,128]{2,1,0:T(8,128)(2,1)} %x_hbm.1, bf16[5,128,256]{2,1,0:T(8,128)(2,1)} %constant.28.clone.m_hbm.m_ref), custom_call_target="tpu_custom_call" | custom-call | tf_op jit(solution)/shard_map/pallas_call | solution.py:236
  5.4 0.0 copy-start.4
  5.4 0.0 copy-start.5
  5.4 0.0 copy-start.2
  5.4 0.0 copy-start.3
  5.4 7.3 %all-to-all-start = ((bf16[32,128,128]{2,1,0:T(8,128)(2,1)}), bf16[32,128,128]{2,1,0:T(8,128)(2,1)S(1)}, u32[]{:S(2)}, u32[]{:S(2)}) async-start(bf16[32,128,128]{2,1,0:T(8,128)(2,1)} %bitcast.1), calls=%async_computation | async-start | bytes 2097152 | tf_op jit(solution)/shard_map/all_to_all | solution.py:397
  12.7 0.0 copy-start
  12.8 0.0 copy-done.4
  12.8 1.8 %collective-permute-start.3 = (f32[1,32]{1,0:T(1,128)S(1)}, f32[1,32]{1,0:T(1,128)S(1)}, u32[]{:S(2)}, u32[]{:S(2)}) collective-permute-start(f32[1,32]{1,0:T(1,128)S(1)} %bitcast.10), channel_id=1, source_target_pairs={{0,8},{8,0},{16,24},{24,16},{1,9},{9,1},{17,25},{25,17},{2,10},{10... | collective-permute-start | bytes 392 | tf_op jit(solution)/shard_map/ppermute | solution.py:370
  14.6 0.0 copy-done.5
  14.6 0.0 collective-permute-start
  14.6 5.2 %collective-permute-done.3 = f32[1,32]{1,0:T(1,128)S(1)} collective-permute-done((f32[1,32]{1,0:T(1,128)S(1)}, f32[1,32]{1,0:T(1,128)S(1)}, u32[]{:S(2)}, u32[]{:S(2)}) %collective-permute-start.3) | collective-permute-done | bytes 160 | tf_op jit(solution)/shard_map/ppermute | solution.py:370
  19.8 1.5 %collective-permute-start.4 = (f32[2,32]{1,0:T(2,128)S(1)}, f32[2,32]{1,0:T(2,128)S(1)}, u32[]{:S(2)}, u32[]{:S(2)}) collective-permute-start(f32[2,32]{1,0:T(2,128)S(1)} %pad_maximum_fusion.4), channel_id=1, source_target_pairs={{0,16},{8,24},{16,0},{24,8},{1,17},{9,25},{17,1},{25,9},{2,18},{10... | collective-permute-start | bytes 776 | tf_op jit(solution)/shard_map/ppermute | solution.py:370
  21.3 2.2 %collective-permute-done.4 = f32[2,32]{1,0:T(2,128)S(1)} collective-permute-done((f32[2,32]{1,0:T(2,128)S(1)}, f32[2,32]{1,0:T(2,128)S(1)}, u32[]{:S(2)}, u32[]{:S(2)}) %collective-permute-start.4) | collective-permute-done | bytes 288 | tf_op jit(solution)/shard_map/ppermute | solution.py:370
  23.5 0.0 collective-permute-done
  23.6 2.1 %collective-permute-start.1 = (f32[2,128]{1,0:T(2,128)S(1)}, f32[2,128]{1,0:T(2,128)S(1)}, u32[]{:S(2)}, u32[]{:S(2)}) collective-permute-start(f32[2,128]{1,0:T(2,128)S(1)} %pad_maximum_fusion.3), channel_id=1, source_target_pairs={{0,2},{1,3},{2,0},{3,1},{4,6},{5,7},{6,4},{7,5},{8,10},{9,11},{10,... | collective-permute-start | bytes 3080 | tf_op jit(solution)/shard_map/ppermute | solution.py:370
  25.7 4.7 %collective-permute-done.1 = f32[2,128]{1,0:T(2,128)S(1)} collective-permute-done((f32[2,128]{1,0:T(2,128)S(1)}, f32[2,128]{1,0:T(2,128)S(1)}, u32[]{:S(2)}, u32[]{:S(2)}) %collective-permute-start.1) | collective-permute-done | bytes 1056 | tf_op jit(solution)/shard_map/ppermute | solution.py:370
  30.5 4.6 %collective-permute-start.2 = (f32[4,128]{1,0:T(4,128)S(1)}, f32[4,128]{1,0:T(4,128)S(1)}, u32[]{:S(2)}, u32[]{:S(2)}) collective-permute-start(f32[4,128]{1,0:T(4,128)S(1)} %pad_maximum_fusion.1), channel_id=1, source_target_pairs={{0,4},{1,5},{2,6},{3,7},{4,0},{5,1},{6,2},{7,3},{8,12},{9,13},{10,... | collective-permute-start | bytes 6152 | tf_op jit(solution)/shard_map/ppermute | solution.py:370
  35.0 0.0 copy-done.2
  35.0 0.0 copy-done.3
  35.0 0.3 fusion
  35.4 3.7 %collective-permute-done.2 = f32[4,128]{1,0:T(4,128)S(1)} collective-permute-done((f32[4,128]{1,0:T(4,128)S(1)}, f32[4,128]{1,0:T(4,128)S(1)}, u32[]{:S(2)}, u32[]{:S(2)}) %collective-permute-start.2) | collective-permute-done | bytes 2080 | tf_op jit(solution)/shard_map/ppermute | solution.py:370
  39.1 0.1 constant_dynamic-slice_fusion
  39.2 0.1 mul.78
  39.3 0.2 fusion.2
  39.5 0.9 %all-to-all-done.x_ref = bf16[32,128,128]{2,1,0:T(8,128)(2,1)S(1)} async-done(((bf16[32,128,128]{2,1,0:T(8,128)(2,1)}), bf16[32,128,128]{2,1,0:T(8,128)(2,1)S(1)}, u32[]{:S(2)}, u32[]{:S(2)}) %all-to-all-start) | async-done | bytes 1048608 | tf_op jit(solution)/shard_map/all_to_all | solution.py:397
  40.4 0.0 copy-done
  40.4 2.4 %shard_map.119 = bf16[32,128,128]{2,1,0:T(8,128)(2,1)S(1)} custom-call(bf16[32,128,128]{2,1,0:T(8,128)(2,1)S(1)} %all-to-all-done.x_ref, bf16[5,128,256]{2,1,0:T(8,128)(2,1)S(1)} %copy-done, f32[32,128]{1,0:T(8,128)S(1)} %get-tuple-element.24.cs_ref, f32[32,128]{1,0:T(8,128)S(1)} %get-tuple-element.21.ss_ref, f32[4,32,128]{2,1,0:T(8,128)S(1)} %get-tuple-element.14.ct_ref, ...), custom_call_target="tpu_custom_call" | custom-call | tf_op jit(solution)/shard_map/pallas_call | solution.py:288
  42.8 0.0 copy-start.1
  42.8 30.1 %all_to_all.10 = bf16[32,128,128]{2,1,0:T(8,128)(2,1)S(1)} all-to-all(bf16[32,128,128]{2,1,0:T(8,128)(2,1)S(1)} %shard_map.119), channel_id=1, replica_groups=mesh['src'=4,'tgt'=8] {'src','tgt'}, dimensions={0} | all-to-all | bytes 2097152 | tf_op jit(solution)/shard_map/all_to_all | solution.py:397
  72.9 0.0 copy-done.1
  72.9 4.7 %shard_map.120 = bf16[32,128,128]{2,1,0:T(8,128)(2,1)} custom-call(bf16[7,128,256]{2,1,0:T(8,128)(2,1)S(1)} %copy-done.1, f32[32,128]{1,0:T(8,128)S(1)} %get-tuple-element.23.c_ref, f32[32,128]{1,0:T(8,128)S(1)} %get-tuple-element.22.s_ref, bf16[128,32,128]{2,1,0:T(8,128)(2,1)S(1)} %bitcast.9), custom_call_target="tpu_custom_call" | custom-call | tf_op jit(solution)/shard_map/pallas_call | solution.py:350
  (10 shorter events, 0.1 us)
Async XLA Ops:
  5.4 7.4 %copy-start.4 = (f32[32]{0:T(128)S(1)}, f32[32]{0:T(128)}, u32[]{:S(2)}) copy-start(f32[32]{0:T(128)} %param.14) | copy-start | bytes 388
  5.4 9.2 %copy-start.5 = (f32[128]{0:T(128)S(1)}, f32[128]{0:T(128)}, u32[]{:S(2)}) copy-start(f32[128]{0:T(128)} %param.13) | copy-start | bytes 1540
  5.4 29.6 %copy-start.2 = (f32[128]{0:T(128)S(1)}, f32[128]{0:T(128)}, u32[]{:S(2)}) copy-start(f32[128]{0:T(128)} %constant.30.clone) | copy-start | bytes 1540
  5.4 29.6 %copy-start.3 = (f32[128]{0:T(128)S(1)}, f32[128]{0:T(128)}, u32[]{:S(2)}) copy-start(f32[128]{0:T(128)} %constant.29.clone) | copy-start | bytes 1540
  5.4 34.9 %all-to-all-start = ((bf16[32,128,128]{2,1,0:T(8,128)(2,1)}), bf16[32,128,128]{2,1,0:T(8,128)(2,1)S(1)}, u32[]{:S(2)}, u32[]{:S(2)}) async-start(bf16[32,128,128]{2,1,0:T(8,128)(2,1)} %bitcast.1), calls=%async_computation | async-start | bytes 2097152 | tf_op jit(solution)/shard_map/all_to_all | solution.py:397
  12.7 27.6 %copy-start = (bf16[5,128,256]{2,1,0:T(8,128)(2,1)S(1)}, bf16[5,128,256]{2,1,0:T(8,128)(2,1)}, u32[]{:S(2)}) copy-start(bf16[5,128,256]{2,1,0:T(8,128)(2,1)} %constant.28.clone.m_hbm.m_ref) | copy-start | bytes 983044
  12.8 7.0 %collective-permute-start.3 = (f32[1,32]{1,0:T(1,128)S(1)}, f32[1,32]{1,0:T(1,128)S(1)}, u32[]{:S(2)}, u32[]{:S(2)}) collective-permute-start(f32[1,32]{1,0:T(1,128)S(1)} %bitcast.10), channel_id=1, source_target_pairs={{0,8},{8,0},{16,24},{24,16},{1,9},{9,1},{17,25},{25,17},{2,10},{10... | collective-permute-start | bytes 392 | tf_op jit(solution)/shard_map/ppermute | solution.py:370
  14.6 8.9 %collective-permute-start = (f32[1,128]{1,0:T(1,128)S(1)}, f32[1,128]{1,0:T(1,128)S(1)}, u32[]{:S(2)}, u32[]{:S(2)}) collective-permute-start(f32[1,128]{1,0:T(1,128)S(1)} %bitcast.12), channel_id=1, source_target_pairs={{0,1},{1,0},{2,3},{3,2},{4,5},{5,4},{6,7},{7,6},{8,9},{9,8},{10,11... | collective-permute-start | bytes 1544 | tf_op jit(solution)/shard_map/ppermute | solution.py:370
  19.8 3.7 %collective-permute-start.4 = (f32[2,32]{1,0:T(2,128)S(1)}, f32[2,32]{1,0:T(2,128)S(1)}, u32[]{:S(2)}, u32[]{:S(2)}) collective-permute-start(f32[2,32]{1,0:T(2,128)S(1)} %pad_maximum_fusion.4), channel_id=1, source_target_pairs={{0,16},{8,24},{16,0},{24,8},{1,17},{9,25},{17,1},{25,9},{2,18},{10... | collective-permute-start | bytes 776 | tf_op jit(solution)/shard_map/ppermute | solution.py:370
  23.6 6.9 %collective-permute-start.1 = (f32[2,128]{1,0:T(2,128)S(1)}, f32[2,128]{1,0:T(2,128)S(1)}, u32[]{:S(2)}, u32[]{:S(2)}) collective-permute-start(f32[2,128]{1,0:T(2,128)S(1)} %pad_maximum_fusion.3), channel_id=1, source_target_pairs={{0,2},{1,3},{2,0},{3,1},{4,6},{5,7},{6,4},{7,5},{8,10},{9,11},{10,... | collective-permute-start | bytes 3080 | tf_op jit(solution)/shard_map/ppermute | solution.py:370
  30.5 8.6 %collective-permute-start.2 = (f32[4,128]{1,0:T(4,128)S(1)}, f32[4,128]{1,0:T(4,128)S(1)}, u32[]{:S(2)}, u32[]{:S(2)}) collective-permute-start(f32[4,128]{1,0:T(4,128)S(1)} %pad_maximum_fusion.1), channel_id=1, source_target_pairs={{0,4},{1,5},{2,6},{3,7},{4,0},{5,1},{6,2},{7,3},{8,12},{9,13},{10,... | collective-permute-start | bytes 6152 | tf_op jit(solution)/shard_map/ppermute | solution.py:370
  42.8 30.1 %copy-start.1 = (bf16[7,128,256]{2,1,0:T(8,128)(2,1)S(1)}, bf16[7,128,256]{2,1,0:T(8,128)(2,1)}, u32[]{:S(2)}) copy-start(bf16[7,128,256]{2,1,0:T(8,128)(2,1)} %constant.31.clone.m_ref) | copy-start | bytes 1376260

commit v11 on v10

--- a/solution.py
+++ b/solution.py
@@ -197,7 +197,8 @@
             w_ref[2 * level],
             w_ref[2 * level + 1],
             lambda index: (cosines[own], sines[own]),
-            8,
+            16,
+            begin // BLOCK,
         )
 
     a_copy.wait()
@@ -279,7 +280,8 @@
                 matrix,
                 swapped,
                 phase_of,
-                8,
+                16,
+                col,
             )
 
 
@@ -298,34 +300,29 @@
     cols, rows, _ = x_ref.shape
     levels = m_ref.shape[0]
 
-    def level_on(level, start, weights):
+    for level in range(levels):
         source = x_ref if level == 0 else state_ref
-        own = slice(start, start + 16)
-        cosine, sine = c_ref[own, :], s_ref[own, :]
-
-        def store(index, value):
-            state_ref[index, own, :] = value
-
-        butterfly(
-            lambda index: source[index, own, :],
-            store,
-            cols,
-            1 << (levels - 1 - level),
-            *weights,
-            lambda index: (cosine, sine),
-            16,
-        )
-
-    for level in range(levels - 1):
         weights = whole_matrix(m_ref[level])
         for start in range(0, rows, 16):
-            level_on(level, start, weights)
-
-    weights = whole_matrix(m_ref[levels - 1])
+            own = slice(start, start + 16)
+            cosine, sine = c_ref[own, :], s_ref[own, :]
+
+            def store(index, value):
+                state_ref[index, own, :] = value
+
+            butterfly(
+                lambda index: source[index, own, :],
+                store,
+                cols,
+                1 << (levels - 1 - level),
+                *weights,
+                lambda index: (cosine, sine),
+                32,
+            )
+
     shuffle = shuffle_matrix()
     copies = []
     for piece in range(rows // 16):
-        level_on(levels - 1, piece * 16, weights)
         own = pl.ds(piece * 16, 16)
         copies.append(pltpu.make_async_copy(o_ref.at[own], o_hbm.at[own], o_sems.at[piece]))
 

time: 77.9 us -> 77.7 us (level)
  no operation moved by 1% of the time
where the time goes in v11:
time: 77.7 us; the launch traced here: 77.4 us
  blocking collectives  30.1 us (39%)
  starting transfers between devices  17.4 us (22%)
  waiting for transfers between devices  16.7 us (21%)
  Pallas kernels  12.3 us (16%)
    all_to_all x1, blocking collectives, traded(): return lax.all_to_all(state, ('src', 'tgt'), 0, 0, tiled=True)  30.1 us
    ppermute x5, waiting for transfers between devices, gathered(): other = lax.ppermute(values, axis, [(i, i ^ apart) for i in range(count)])  15.8 us
    ppermute x5, starting transfers between devices, gathered(): other = lax.ppermute(values, axis, [(i, i ^ apart) for i in range(count)])  10.1 us
    all_to_all x1, starting transfers between devices, traded(): return lax.all_to_all(state, ('src', 'tgt'), 0, 0, tiled=True)  7.3 us
    pallas_call x1, Pallas kernels, source_levels(): pl.pallas_call(source_kernel, out_shape=jax.ShapeDtypeStruct((cols, rows,...  5.52 us
    pallas_call x1, Pallas kernels, target_levels(): pl.pallas_call(target_kernel, out_shape=jax.ShapeDtypeStruct(shape, x.dty...  4.39 us
    pallas_call x1, Pallas kernels, middle_levels(): pl.pallas_call(functools.partial(middle_kernel, levels, rows), out_shape=...  2.39 us
  transfers between devices with their start and end apart: 6, of which 5 were waited for; matrix products, arithmetic and copies ran while one was open for 1% of the time, Pallas kernels for 0%

profile of v11, /device:TPU:0, one launch (start us, length us, event | category | flops | bytes accessed | tf_op | source)
XLA Modules:
  0.0 77.4 jit_solution(16935355934004478454)
XLA Ops:
  0.0 5.5 %shard_map.118 = bf16[128,32,128]{2,1,0:T(8,128)(2,1)} custom-call(f32[1,128]{1,0:T(1,128)} %bitcast.11, bf16[32,128,128]{2,1,0:T(8,128)(2,1)} %x_hbm.1, bf16[5,128,256]{2,1,0:T(8,128)(2,1)} %constant.28.clone.m_hbm.m_ref), custom_call_target="tpu_custom_call" | custom-call | tf_op jit(solution)/shard_map/pallas_call | solution.py:237
  5.5 0.0 copy-start.4
  5.5 0.0 copy-start.5
  5.5 0.0 copy-start.2
  5.6 0.0 copy-start.3
  5.6 7.3 %all-to-all-start = ((bf16[32,128,128]{2,1,0:T(8,128)(2,1)}), bf16[32,128,128]{2,1,0:T(8,128)(2,1)S(1)}, u32[]{:S(2)}, u32[]{:S(2)}) async-start(bf16[32,128,128]{2,1,0:T(8,128)(2,1)} %bitcast.1), calls=%async_computation | async-start | bytes 2097152 | tf_op jit(solution)/shard_map/all_to_all | solution.py:394
  12.9 0.0 copy-start
  12.9 0.0 copy-done.4
  12.9 1.8 %collective-permute-start.3 = (f32[1,32]{1,0:T(1,128)S(1)}, f32[1,32]{1,0:T(1,128)S(1)}, u32[]{:S(2)}, u32[]{:S(2)}) collective-permute-start(f32[1,32]{1,0:T(1,128)S(1)} %bitcast.10), channel_id=1, source_target_pairs={{0,8},{8,0},{16,24},{24,16},{1,9},{9,1},{17,25},{25,17},{2,10},{10... | collective-permute-start | bytes 392 | tf_op jit(solution)/shard_map/ppermute | solution.py:367
  14.7 0.0 copy-done.5
  14.7 0.0 collective-permute-start
  14.7 5.2 %collective-permute-done.3 = f32[1,32]{1,0:T(1,128)S(1)} collective-permute-done((f32[1,32]{1,0:T(1,128)S(1)}, f32[1,32]{1,0:T(1,128)S(1)}, u32[]{:S(2)}, u32[]{:S(2)}) %collective-permute-start.3) | collective-permute-done | bytes 160 | tf_op jit(solution)/shard_map/ppermute | solution.py:367
  19.9 1.5 %collective-permute-start.4 = (f32[2,32]{1,0:T(2,128)S(1)}, f32[2,32]{1,0:T(2,128)S(1)}, u32[]{:S(2)}, u32[]{:S(2)}) collective-permute-start(f32[2,32]{1,0:T(2,128)S(1)} %pad_maximum_fusion.4), channel_id=1, source_target_pairs={{0,16},{8,24},{16,0},{24,8},{1,17},{9,25},{17,1},{25,9},{2,18},{10... | collective-permute-start | bytes 776 | tf_op jit(solution)/shard_map/ppermute | solution.py:367
  21.5 2.2 %collective-permute-done.4 = f32[2,32]{1,0:T(2,128)S(1)} collective-permute-done((f32[2,32]{1,0:T(2,128)S(1)}, f32[2,32]{1,0:T(2,128)S(1)}, u32[]{:S(2)}, u32[]{:S(2)}) %collective-permute-start.4) | collective-permute-done | bytes 288 | tf_op jit(solution)/shard_map/ppermute | solution.py:367
  23.7 0.0 collective-permute-done
  23.7 2.1 %collective-permute-start.1 = (f32[2,128]{1,0:T(2,128)S(1)}, f32[2,128]{1,0:T(2,128)S(1)}, u32[]{:S(2)}, u32[]{:S(2)}) collective-permute-start(f32[2,128]{1,0:T(2,128)S(1)} %pad_maximum_fusion.3), channel_id=1, source_target_pairs={{0,2},{1,3},{2,0},{3,1},{4,6},{5,7},{6,4},{7,5},{8,10},{9,11},{10,... | collective-permute-start | bytes 3080 | tf_op jit(solution)/shard_map/ppermute | solution.py:367
  25.9 4.7 %collective-permute-done.1 = f32[2,128]{1,0:T(2,128)S(1)} collective-permute-done((f32[2,128]{1,0:T(2,128)S(1)}, f32[2,128]{1,0:T(2,128)S(1)}, u32[]{:S(2)}, u32[]{:S(2)}) %collective-permute-start.1) | collective-permute-done | bytes 1056 | tf_op jit(solution)/shard_map/ppermute | solution.py:367
  30.6 4.6 %collective-permute-start.2 = (f32[4,128]{1,0:T(4,128)S(1)}, f32[4,128]{1,0:T(4,128)S(1)}, u32[]{:S(2)}, u32[]{:S(2)}) collective-permute-start(f32[4,128]{1,0:T(4,128)S(1)} %pad_maximum_fusion.1), channel_id=1, source_target_pairs={{0,4},{1,5},{2,6},{3,7},{4,0},{5,1},{6,2},{7,3},{8,12},{9,13},{10,... | collective-permute-start | bytes 6152 | tf_op jit(solution)/shard_map/ppermute | solution.py:367
  35.2 0.0 copy-done.2
  35.2 0.0 copy-done.3
  35.2 0.3 fusion
  35.5 3.7 %collective-permute-done.2 = f32[4,128]{1,0:T(4,128)S(1)} collective-permute-done((f32[4,128]{1,0:T(4,128)S(1)}, f32[4,128]{1,0:T(4,128)S(1)}, u32[]{:S(2)}, u32[]{:S(2)}) %collective-permute-start.2) | collective-permute-done | bytes 2080 | tf_op jit(solution)/shard_map/ppermute | solution.py:367
  39.2 0.1 constant_dynamic-slice_fusion
  39.3 0.1 mul.78
  39.4 0.2 fusion.2
  39.6 0.9 %all-to-all-done.x_ref = bf16[32,128,128]{2,1,0:T(8,128)(2,1)S(1)} async-done(((bf16[32,128,128]{2,1,0:T(8,128)(2,1)}), bf16[32,128,128]{2,1,0:T(8,128)(2,1)S(1)}, u32[]{:S(2)}, u32[]{:S(2)}) %all-to-all-start) | async-done | bytes 1048608 | tf_op jit(solution)/shard_map/all_to_all | solution.py:394
  40.5 0.0 copy-done
  40.5 2.4 %shard_map.119 = bf16[32,128,128]{2,1,0:T(8,128)(2,1)S(1)} custom-call(bf16[32,128,128]{2,1,0:T(8,128)(2,1)S(1)} %all-to-all-done.x_ref, bf16[5,128,256]{2,1,0:T(8,128)(2,1)S(1)} %copy-done, f32[32,128]{1,0:T(8,128)S(1)} %get-tuple-element.24.cs_ref, f32[32,128]{1,0:T(8,128)S(1)} %get-tuple-element.21.ss_ref, f32[4,32,128]{2,1,0:T(8,128)S(1)} %get-tuple-element.14.ct_ref, ...), custom_call_target="tpu_custom_call" | custom-call | tf_op jit(solution)/shard_map/pallas_call | solution.py:290
  42.9 0.0 copy-start.1
  42.9 30.1 %all_to_all.10 = bf16[32,128,128]{2,1,0:T(8,128)(2,1)S(1)} all-to-all(bf16[32,128,128]{2,1,0:T(8,128)(2,1)S(1)} %shard_map.119), channel_id=1, replica_groups=mesh['src'=4,'tgt'=8] {'src','tgt'}, dimensions={0} | all-to-all | bytes 2097152 | tf_op jit(solution)/shard_map/all_to_all | solution.py:394
  73.0 0.0 copy-done.1
  73.0 4.4 %shard_map.120 = bf16[32,128,128]{2,1,0:T(8,128)(2,1)} custom-call(bf16[7,128,256]{2,1,0:T(8,128)(2,1)S(1)} %copy-done.1, f32[32,128]{1,0:T(8,128)S(1)} %get-tuple-element.23.c_ref, f32[32,128]{1,0:T(8,128)S(1)} %get-tuple-element.22.s_ref, bf16[128,32,128]{2,1,0:T(8,128)(2,1)S(1)} %bitcast.9), custom_call_target="tpu_custom_call" | custom-call | tf_op jit(solution)/shard_map/pallas_call | solution.py:347
  (10 shorter events, 0.1 us)
Async XLA Ops:
  5.5 7.4 %copy-start.4 = (f32[32]{0:T(128)S(1)}, f32[32]{0:T(128)}, u32[]{:S(2)}) copy-start(f32[32]{0:T(128)} %param.14) | copy-start | bytes 388
  5.5 9.2 %copy-start.5 = (f32[128]{0:T(128)S(1)}, f32[128]{0:T(128)}, u32[]{:S(2)}) copy-start(f32[128]{0:T(128)} %param.13) | copy-start | bytes 1540
  5.5 29.6 %copy-start.2 = (f32[128]{0:T(128)S(1)}, f32[128]{0:T(128)}, u32[]{:S(2)}) copy-start(f32[128]{0:T(128)} %constant.30.clone) | copy-start | bytes 1540
  5.6 29.6 %copy-start.3 = (f32[128]{0:T(128)S(1)}, f32[128]{0:T(128)}, u32[]{:S(2)}) copy-start(f32[128]{0:T(128)} %constant.29.clone) | copy-start | bytes 1540
  5.6 34.9 %all-to-all-start = ((bf16[32,128,128]{2,1,0:T(8,128)(2,1)}), bf16[32,128,128]{2,1,0:T(8,128)(2,1)S(1)}, u32[]{:S(2)}, u32[]{:S(2)}) async-start(bf16[32,128,128]{2,1,0:T(8,128)(2,1)} %bitcast.1), calls=%async_computation | async-start | bytes 2097152 | tf_op jit(solution)/shard_map/all_to_all | solution.py:394
  12.9 27.6 %copy-start = (bf16[5,128,256]{2,1,0:T(8,128)(2,1)S(1)}, bf16[5,128,256]{2,1,0:T(8,128)(2,1)}, u32[]{:S(2)}) copy-start(bf16[5,128,256]{2,1,0:T(8,128)(2,1)} %constant.28.clone.m_hbm.m_ref) | copy-start | bytes 983044
  12.9 7.0 %collective-permute-start.3 = (f32[1,32]{1,0:T(1,128)S(1)}, f32[1,32]{1,0:T(1,128)S(1)}, u32[]{:S(2)}, u32[]{:S(2)}) collective-permute-start(f32[1,32]{1,0:T(1,128)S(1)} %bitcast.10), channel_id=1, source_target_pairs={{0,8},{8,0},{16,24},{24,16},{1,9},{9,1},{17,25},{25,17},{2,10},{10... | collective-permute-start | bytes 392 | tf_op jit(solution)/shard_map/ppermute | solution.py:367
  14.7 8.9 %collective-permute-start = (f32[1,128]{1,0:T(1,128)S(1)}, f32[1,128]{1,0:T(1,128)S(1)}, u32[]{:S(2)}, u32[]{:S(2)}) collective-permute-start(f32[1,128]{1,0:T(1,128)S(1)} %bitcast.12), channel_id=1, source_target_pairs={{0,1},{1,0},{2,3},{3,2},{4,5},{5,4},{6,7},{7,6},{8,9},{9,8},{10,11... | collective-permute-start | bytes 1544 | tf_op jit(solution)/shard_map/ppermute | solution.py:367
  19.9 3.7 %collective-permute-start.4 = (f32[2,32]{1,0:T(2,128)S(1)}, f32[2,32]{1,0:T(2,128)S(1)}, u32[]{:S(2)}, u32[]{:S(2)}) collective-permute-start(f32[2,32]{1,0:T(2,128)S(1)} %pad_maximum_fusion.4), channel_id=1, source_target_pairs={{0,16},{8,24},{16,0},{24,8},{1,17},{9,25},{17,1},{25,9},{2,18},{10... | collective-permute-start | bytes 776 | tf_op jit(solution)/shard_map/ppermute | solution.py:367
  23.7 6.9 %collective-permute-start.1 = (f32[2,128]{1,0:T(2,128)S(1)}, f32[2,128]{1,0:T(2,128)S(1)}, u32[]{:S(2)}, u32[]{:S(2)}) collective-permute-start(f32[2,128]{1,0:T(2,128)S(1)} %pad_maximum_fusion.3), channel_id=1, source_target_pairs={{0,2},{1,3},{2,0},{3,1},{4,6},{5,7},{6,4},{7,5},{8,10},{9,11},{10,... | collective-permute-start | bytes 3080 | tf_op jit(solution)/shard_map/ppermute | solution.py:367
  30.6 8.6 %collective-permute-start.2 = (f32[4,128]{1,0:T(4,128)S(1)}, f32[4,128]{1,0:T(4,128)S(1)}, u32[]{:S(2)}, u32[]{:S(2)}) collective-permute-start(f32[4,128]{1,0:T(4,128)S(1)} %pad_maximum_fusion.1), channel_id=1, source_target_pairs={{0,4},{1,5},{2,6},{3,7},{4,0},{5,1},{6,2},{7,3},{8,12},{9,13},{10,... | collective-permute-start | bytes 6152 | tf_op jit(solution)/shard_map/ppermute | solution.py:367
  42.9 30.1 %copy-start.1 = (bf16[7,128,256]{2,1,0:T(8,128)(2,1)S(1)}, bf16[7,128,256]{2,1,0:T(8,128)(2,1)}, u32[]{:S(2)}) copy-start(bf16[7,128,256]{2,1,0:T(8,128)(2,1)} %constant.31.clone.m_ref) | copy-start | bytes 1376260

commit v12 on v11

--- a/solution.py
+++ b/solution.py
@@ -252,48 +252,97 @@
     )(*far)
 
 
-def middle_kernel(levels, rows, x_ref, m_ref, cs_ref, ss_ref, ct_ref, st_ref, o_ref):
-    count, total, _ = x_ref.shape
-    run = total // rows
-    tgt_count = cs_ref.shape[0] // run
+def middle_kernel(levels, cols, x_ref, m_ref, cs_ref, ss_ref, ct_ref, st_ref, o_ref):
+    count = x_ref.shape[0]
+    rows = ct_ref.shape[1]
+    run = x_ref.shape[1] // rows
+    tgt_chips = cs_ref.shape[0] // run
     for step, (apart, by_source) in enumerate(levels):
-        source = x_ref if step == 0 else o_ref
-        matrix, swapped = whole_matrix(m_ref[step])
-        for col in range(run):
-            own = slice(col * rows, (col + 1) * rows)
+        weights = whole_matrix(m_ref[step])
+        for turn, col in enumerate(cols):
+            first = col if step == 0 else turn
+            source = x_ref if step == 0 else o_ref
+            taken = slice(first * rows, (first + 1) * rows)
+            own = slice(turn * rows, (turn + 1) * rows)
 
             def phase_of(index):
                 if by_source:
-                    at = index % tgt_count * run + col
+                    at = index % tgt_chips * run + col
                     return cs_ref[at : at + 1, :], ss_ref[at : at + 1, :]
-                at = index // tgt_count
+                at = index // tgt_chips
                 return ct_ref[at], st_ref[at]
 
             def store(index, value):
                 o_ref[index, own, :] = value
 
             butterfly(
-                lambda index: source[index, own, :],
+                lambda index: source[index, taken, :],
                 store,
                 count,
                 apart,
-                matrix,
-                swapped,
+                *weights,
                 phase_of,
-                16,
-                col,
+                8,
+                turn,
             )
 
 
-def middle_levels(x, matrices, src_tables, tgt_tables, levels):
+def middle_levels(x, matrices, src_tables, tgt_tables, levels, cols):
     rows = tgt_tables[0].shape[1]
     return pl.pallas_call(
-        functools.partial(middle_kernel, levels, rows),
-        out_shape=jax.ShapeDtypeStruct(x.shape, x.dtype),
+        functools.partial(middle_kernel, levels, cols),
+        out_shape=jax.ShapeDtypeStruct((x.shape[0], len(cols) * rows, WIDE), x.dtype),
         in_specs=[VMEM] * 6,
         out_specs=VMEM,
         compiler_params=PARAMS,
     )(x, matrices, *src_tables, *tgt_tables)
+
+
+def core_kernel(parts, m_ref, ct_ref, st_ref, *rest):
+    o_ref = rest[-1]
+    matrix = m_ref[lax.rem(lax.axis_index("tgt"), 2)]
+    count = o_ref.shape[0]
+    rows = ct_ref.shape[1]
+    tgt_chips = count // ct_ref.shape[0]
+    at = 0
+    for own_ref, other_ref in zip(rest[:parts], rest[parts : 2 * parts]):
+        total = own_ref.shape[1]
+        group = max(1, 512 // total)
+        for start in range(0, count, group):
+            picked = slice(start, start + group)
+            pair = [ref[picked].reshape(-1, WIDE) for ref in (own_ref, other_ref)]
+            both = jnp.dot(
+                jnp.concatenate(pair, axis=1), matrix, preferred_element_type=jnp.float32
+            )
+            for begin in range(0, both.shape[0], rows):
+                index, row = divmod(begin, total)
+                src = (start + index) // tgt_chips
+                mine = slice(begin, begin + rows)
+                value = both[mine, :WIDE] * ct_ref[src] + both[mine, WIDE:] * st_ref[src]
+                o_ref[start + index, at + row : at + row + rows, :] = value.astype(jnp.bfloat16)
+        at += total
+
+
+def core_level(owns, upper, tgt_tables):
+    devices = lax.axis_size("tgt")
+    others = [lax.ppermute(own, "tgt", [(i, i ^ 1) for i in range(devices)]) for own in owns]
+    real, imag = upper[..., :HALF], upper[..., HALF:]
+    below = np.concatenate([-imag, real], axis=3)
+    whole = np.concatenate([upper, below], axis=1).reshape(2, WIDE, 2, 2, HALF)
+    choices = []
+    for core in range(2):
+        picked = whole[[core, 1 - core], :, core].reshape(2 * WIDE, 2, HALF)
+        both = np.concatenate([picked, picked[:, ::-1]], axis=1).reshape(2 * WIDE, -1)
+        choices.append(both.astype(ml_dtypes.bfloat16))
+    shape = owns[0].shape
+    total = sum(own.shape[1] for own in owns)
+    return pl.pallas_call(
+        functools.partial(core_kernel, len(owns)),
+        out_shape=jax.ShapeDtypeStruct((shape[0], total, WIDE), owns[0].dtype),
+        in_specs=[VMEM] * (3 + 2 * len(owns)),
+        out_specs=VMEM,
+        compiler_params=PARAMS,
+    )(jnp.asarray(np.stack(choices)), *tgt_tables, *owns, *others)
 
 
 def target_kernel(m_ref, c_ref, s_ref, x_ref, o_hbm, state_ref, o_ref, o_sems):
@@ -358,18 +407,16 @@
     )(matrices, *angles, x)
 
 
-def gathered(values, axis):
+def gathered(values, axis, bits):
     count = lax.axis_size(axis)
     place = lax.axis_index(axis)
     values = values[None]
-    apart = 1
-    while apart < count:
-        other = lax.ppermute(values, axis, [(i, i ^ apart) for i in range(count)])
-        mine_first = (place & apart) == 0
+    for bit in bits:
+        other = lax.ppermute(values, axis, [(i, i ^ 1 << bit) for i in range(count)])
+        mine_first = (place >> bit & 1) == 0
         values = jnp.concatenate(
             [jnp.where(mine_first, values, other), jnp.where(mine_first, other, values)]
         )
-        apart *= 2
     return values
 
 
@@ -377,46 +424,53 @@
     rows, cols, _ = box_weights.shape
     src_count = lax.axis_size("src")
     tgt_count = lax.axis_size("tgt")
-    devices = src_count * tgt_count
+    tgt_chips = tgt_count // 2
+    chips = src_count * tgt_chips
     row_bits, col_bits = rows.bit_length() - 1, cols.bit_length() - 1
-    src_bits, tgt_bits = src_count.bit_length() - 1, tgt_count.bit_length() - 1
+    src_bits, chip_bits = src_count.bit_length() - 1, tgt_chips.bit_length() - 1
     first_target = row_bits + src_bits
-    total = first_target + tgt_bits + col_bits
+    core = first_target + chip_bits
+    total = core + 1 + col_bits
     matrices = [level_matrix(number) for number in range(total)]
 
     def matrices_of(low, high):
         return jnp.asarray(np.stack(matrices[low:high]))
 
-    run = cols // devices
-    place = lax.axis_index("src") * tgt_count + lax.axis_index("tgt")
+    run = cols // chips
+    place = lax.axis_index("src") * tgt_chips + lax.axis_index("tgt") // 2
+    groups = [
+        [src * tgt_count + 2 * at + side for src in range(src_count) for at in range(tgt_chips)]
+        for side in range(2)
+    ]
 
     def traded(state):
-        return lax.all_to_all(state, ("src", "tgt"), 0, 0, tiled=True)
+        return lax.all_to_all(
+            state, ("src", "tgt"), 0, 0, axis_index_groups=groups, tiled=True
+        )
 
     state = source_levels(box_weights, matrices_of(0, row_bits), slowness)
 
     state, slowness, dip_field = lax.optimization_barrier((state, slowness, dip_field))
-    all_dip = gathered(dip_field, "src")
-    all_slowness = gathered(slowness, "tgt")
+    all_dip = gathered(dip_field, "src", range(src_bits))
+    all_slowness = gathered(slowness, "tgt", range(1, 1 + chip_bits))
     run_slowness = lax.dynamic_slice_in_dim(all_slowness, place * run, run, 1)
-
-    state = state.reshape(devices, run * rows, WIDE)
+    src_tables, tgt_tables = tables(run_slowness.reshape(-1)), tables(all_dip)
+
+    state = traded(state.reshape(chips, run * rows, WIDE))
+    levels = [(tgt_chips << bit, True) for bit in range(src_bits)]
+    levels += [(1 << bit, False) for bit in reversed(range(chip_bits))]
+    half = max(1, run // 2)
+    middle = matrices_of(row_bits, core)
+    owns = [
+        middle_levels(state, middle, src_tables, tgt_tables, levels, range(start, start + half))
+        for start in range(0, run, half)
+    ]
+    upper = matrices[core].astype(np.float32).reshape(2, HALF, 2, WIDE)
+    state = core_level(owns, upper, tgt_tables)
     state = traded(state)
-    levels = [(tgt_count << bit, True) for bit in range(src_bits)]
-    levels += [(1 << bit, False) for bit in reversed(range(tgt_bits))]
-    state = middle_levels(
-        state,
-        matrices_of(row_bits, first_target + tgt_bits),
-        tables(run_slowness.reshape(-1)),
-        tables(all_dip),
-        levels,
-    )
-    state = traded(state)
 
     return target_levels(
-        state.reshape(cols, rows, WIDE),
-        matrices_of(first_target + tgt_bits, total),
-        tables(dip_field),
+        state.reshape(cols, rows, WIDE), matrices_of(core + 1, total), tables(dip_field)
     )
 
 

time: 77.7 us -> 82.9 us (1.067)
  waiting for transfers between devices: 16.7 us -> 18.6 us
  starting transfers between devices: 17.4 us -> 18.7 us
  blocking collectives: 30.1 us -> 31.1 us
  Pallas kernels: 12.3 us -> 13.2 us
    ppermute x5 -> x6, waiting for transfers between devices: 15.8 us -> 17.2 us  [the longest x4 15.7 us: gathered(): lax.ppermute(values, axis, [(i, i ^ 1 << bit) for i in range(count)])]
    all_to_all x1, starting transfers between devices: 7.3 us -> 8.46 us  [traded(): lax.all_to_all(state, ('src', 'tgt'), 0, 0, axis_index_groups=groups, til...]
    all_to_all x1, blocking collectives: 30.1 us -> 31.1 us  [traded(): lax.all_to_all(state, ('src', 'tgt'), 0, 0, axis_index_groups=groups, til...]
    pallas_call x1 -> x3, Pallas kernels: 2.39 us -> 3.33 us  [the longest x2 2.61 us: middle_levels(): pl.pallas_call(functools.partial(middle_kernel, levels, cols), out_shape=...]
    ppermute x5 -> x6, starting transfers between devices: 10.1 us -> 10.2 us  [the longest x4 9.61 us: gathered(): lax.ppermute(values, axis, [(i, i ^ 1 << bit) for i in range(count)])]
  transfers between devices with their start and end apart: 6 -> 7, of which waited for: 5 -> 6; matrix products, arithmetic and copies ran while one was open for 1% -> 1% of each run, Pallas kernels for 0% -> 2%
where the time goes in v12:
time: 82.9 us; the launch traced here: 82.6 us
  blocking collectives  31.1 us (38%)
  starting transfers between devices  18.7 us (23%)
  waiting for transfers between devices  18.6 us (22%)
  Pallas kernels  13.2 us (16%)
    all_to_all x1, blocking collectives, traded(): lax.all_to_all(state, ('src', 'tgt'), 0, 0, axis_index_groups=groups, til...  31.1 us
    ppermute x4, waiting for transfers between devices, gathered(): lax.ppermute(values, axis, [(i, i ^ 1 << bit) for i in range(count)])  15.7 us
    ppermute x4, starting transfers between devices, gathered(): lax.ppermute(values, axis, [(i, i ^ 1 << bit) for i in range(count)])  9.61 us
    all_to_all x1, starting transfers between devices, traded(): lax.all_to_all(state, ('src', 'tgt'), 0, 0, axis_index_groups=groups, til...  8.46 us
    pallas_call x1, Pallas kernels, source_levels(): pl.pallas_call(source_kernel, out_shape=jax.ShapeDtypeStruct((cols, rows,...  5.52 us
    pallas_call x1, Pallas kernels, target_levels(): pl.pallas_call(target_kernel, out_shape=jax.ShapeDtypeStruct(shape, x.dty...  4.39 us
    pallas_call x2, Pallas kernels, middle_levels(): pl.pallas_call(functools.partial(middle_kernel, levels, cols), out_shape=...  2.61 us
  transfers between devices with their start and end apart: 7, of which 6 were waited for; matrix products, arithmetic and copies ran while one was open for 1% of the time, Pallas kernels for 2%

profile of v12, /device:TPU:0, one launch (start us, length us, event | category | flops | bytes accessed | tf_op | source)
XLA Modules:
  0.0 82.6 jit_solution(1818267270099615836)
XLA Ops:
  0.0 5.5 %shard_map.127 = bf16[128,32,128]{2,1,0:T(8,128)(2,1)} custom-call(f32[1,128]{1,0:T(1,128)} %bitcast.11, bf16[32,128,128]{2,1,0:T(8,128)(2,1)} %x_hbm.1, bf16[5,128,256]{2,1,0:T(8,128)(2,1)} %constant.43.clone.m_hbm), custom_call_target="tpu_custom_call" | custom-call | tf_op jit(solution)/shard_map/pallas_call | solution.py:237
  5.5 0.0 copy-start.5
  5.5 0.0 copy-start.6
  5.5 0.0 copy-start.3
  5.6 0.0 copy-start.4
  5.6 8.5 %all-to-all-start = ((bf16[16,256,128]{2,1,0:T(8,128)(2,1)}), bf16[16,256,128]{2,1,0:T(8,128)(2,1)S(1)}, u32[]{:S(2)}, u32[]{:S(2)}) async-start(bf16[16,256,128]{2,1,0:T(8,128)(2,1)} %bitcast.2), calls=%async_computation | async-start | bytes 2097152 | tf_op jit(solution)/shard_map/all_to_all | solution.py:447
  14.0 0.0 copy-start
  14.1 0.0 copy-done.5
  14.1 2.0 %collective-permute-start = (f32[1,32]{1,0:T(1,128)S(1)}, f32[1,32]{1,0:T(1,128)S(1)}, u32[]{:S(2)}, u32[]{:S(2)}) collective-permute-start(f32[1,32]{1,0:T(1,128)S(1)} %bitcast.10), channel_id=1, source_target_pairs={{0,8},{8,0},{16,24},{24,16},{1,9},{9,1},{17,25},{25,17},{2,10},{10... | collective-permute-start | bytes 392 | tf_op jit(solution)/shard_map/ppermute | solution.py:415
  16.1 1.5 %collective-permute-start.2 = (f32[1,128]{1,0:T(1,128)S(1)}, f32[1,128]{1,0:T(1,128)S(1)}, u32[]{:S(2)}, u32[]{:S(2)}) collective-permute-start(f32[1,128]{1,0:T(1,128)S(1)} %bitcast.12), channel_id=1, source_target_pairs={{0,2},{1,3},{2,0},{3,1},{4,6},{5,7},{6,4},{7,5},{8,10},{9,11},{10,... | collective-permute-start | bytes 1544 | tf_op jit(solution)/shard_map/ppermute | solution.py:415
  17.5 4.1 %collective-permute-done = f32[1,32]{1,0:T(1,128)S(1)} collective-permute-done((f32[1,32]{1,0:T(1,128)S(1)}, f32[1,32]{1,0:T(1,128)S(1)}, u32[]{:S(2)}, u32[]{:S(2)}) %collective-permute-start) | collective-permute-done | bytes 160 | tf_op jit(solution)/shard_map/ppermute | solution.py:415
  21.6 1.5 %collective-permute-start.1 = (f32[2,32]{1,0:T(2,128)S(1)}, f32[2,32]{1,0:T(2,128)S(1)}, u32[]{:S(2)}, u32[]{:S(2)}) collective-permute-start(f32[2,32]{1,0:T(2,128)S(1)} %pad_maximum_fusion.2), channel_id=1, source_target_pairs={{0,16},{8,24},{16,0},{24,8},{1,17},{9,25},{17,1},{25,9},{2,18},{10... | collective-permute-start | bytes 776 | tf_op jit(solution)/shard_map/ppermute | solution.py:415
  23.1 2.1 %collective-permute-done.1 = f32[2,32]{1,0:T(2,128)S(1)} collective-permute-done((f32[2,32]{1,0:T(2,128)S(1)}, f32[2,32]{1,0:T(2,128)S(1)}, u32[]{:S(2)}, u32[]{:S(2)}) %collective-permute-start.1) | collective-permute-done | bytes 288 | tf_op jit(solution)/shard_map/ppermute | solution.py:415
  25.3 5.8 %collective-permute-done.2 = f32[1,128]{1,0:T(1,128)S(1)} collective-permute-done((f32[1,128]{1,0:T(1,128)S(1)}, f32[1,128]{1,0:T(1,128)S(1)}, u32[]{:S(2)}, u32[]{:S(2)}) %collective-permute-start.2) | collective-permute-done | bytes 544 | tf_op jit(solution)/shard_map/ppermute | solution.py:415
  31.1 4.6 %collective-permute-start.3 = (f32[2,128]{1,0:T(2,128)S(1)}, f32[2,128]{1,0:T(2,128)S(1)}, u32[]{:S(2)}, u32[]{:S(2)}) collective-permute-start(f32[2,128]{1,0:T(2,128)S(1)} %pad_maximum_fusion.3), channel_id=1, source_target_pairs={{0,4},{1,5},{2,6},{3,7},{4,0},{5,1},{6,2},{7,3},{8,12},{9,13},{10,... | collective-permute-start | bytes 3080 | tf_op jit(solution)/shard_map/ppermute | solution.py:415
  35.8 0.3 fusion
  36.1 3.7 %collective-permute-done.3 = f32[2,128]{1,0:T(2,128)S(1)} collective-permute-done((f32[2,128]{1,0:T(2,128)S(1)}, f32[2,128]{1,0:T(2,128)S(1)}, u32[]{:S(2)}, u32[]{:S(2)}) %collective-permute-start.3) | collective-permute-done | bytes 1056 | tf_op jit(solution)/shard_map/ppermute | solution.py:415
  39.8 0.1 constant_dynamic-slice_fusion
  39.9 0.1 mul.83
  39.9 0.2 fusion.2
  40.1 1.4 %all-to-all-done.x_ref = bf16[16,256,128]{2,1,0:T(8,128)(2,1)S(1)} async-done(((bf16[16,256,128]{2,1,0:T(8,128)(2,1)}), bf16[16,256,128]{2,1,0:T(8,128)(2,1)S(1)}, u32[]{:S(2)}, u32[]{:S(2)}) %all-to-all-start) | async-done | bytes 1048608 | tf_op jit(solution)/shard_map/all_to_all | solution.py:447
  41.6 1.3 %shard_map.128.rest_0_ = bf16[16,128,128]{2,1,0:T(8,128)(2,1)S(1)} custom-call(bf16[16,256,128]{2,1,0:T(8,128)(2,1)S(1)} %all-to-all-done.x_ref, bf16[4,128,256]{2,1,0:T(8,128)(2,1)S(1)} %copy-done, f32[32,128]{1,0:T(8,128)S(1)} %get-tuple-element.20.cs_ref, f32[32,128]{1,0:T(8,128)S(1)} %get-tuple-element.17.ss_ref, ...), custom_call_target="tpu_custom_call" | custom-call | tf_op jit(solution)/shard_map/pallas_call | solution.py:292
  42.9 0.0 copy-start.2
  42.9 0.1 collective-permute-start.4
  43.0 1.3 %shard_map.129.rest_1_ = bf16[16,128,128]{2,1,0:T(8,128)(2,1)S(1)} custom-call(bf16[16,256,128]{2,1,0:T(8,128)(2,1)S(1)} %all-to-all-done.x_ref, bf16[4,128,256]{2,1,0:T(8,128)(2,1)S(1)} %copy-done, f32[32,128]{1,0:T(8,128)S(1)} %get-tuple-element.20.cs_ref, f32[32,128]{1,0:T(8,128)S(1)} %get-tuple-element.17.ss_ref, ...), custom_call_target="tpu_custom_call" | custom-call | tf_op jit(solution)/shard_map/pallas_call | solution.py:292
  44.3 0.6 collective-permute-start.5
  44.8 0.0 collective-permute-done.4.rest_2_
  44.9 1.5 %collective-permute-done.5.rest_3_ = bf16[16,128,128]{2,1,0:T(8,128)(2,1)S(1)} collective-permute-done((bf16[16,128,128]{2,1,0:T(8,128)(2,1)S(1)}, bf16[16,128,128]{2,1,0:T(8,128)(2,1)S(1)}, u32[]{:S(2)}, u32[]{:S(2)}) %collective-permute-start.5) | collective-permute-done | bytes 524320 | tf_op jit(solution)/shard_map/ppermute | solution.py:328
  46.4 0.7 shard_map.130
  47.1 0.0 copy-start.1
  47.1 31.1 %all_to_all.10 = bf16[16,256,128]{2,1,0:T(8,128)(2,1)S(1)} all-to-all(bf16[16,256,128]{2,1,0:T(8,128)(2,1)S(1)} %shard_map.130), channel_id=1, replica_groups={{0,2,4,6,8,10,12,14,16,18,20,22,24,26,28,30},{1,3,5,7,9,11,13,15,17,19,..., dimensions={0} | all-to-all | bytes 2097152 | tf_op jit(solution)/shard_map/all_to_all | solution.py:447
  78.3 4.4 %shard_map.131 = bf16[32,128,128]{2,1,0:T(8,128)(2,1)} custom-call(bf16[7,128,256]{2,1,0:T(8,128)(2,1)S(1)} %copy-done.1, f32[32,128]{1,0:T(8,128)S(1)} %get-tuple-element.19.c_ref, f32[32,128]{1,0:T(8,128)S(1)} %get-tuple-element.18.s_ref, bf16[128,32,128]{2,1,0:T(8,128)(2,1)S(1)} %bitcast.9), custom_call_target="tpu_custom_call" | custom-call | tf_op jit(solution)/shard_map/pallas_call | solution.py:396
  (14 shorter events, 0.1 us)
Async XLA Ops:
  5.5 8.5 %copy-start.5 = (f32[32]{0:T(128)S(1)}, f32[32]{0:T(128)}, u32[]{:S(2)}) copy-start(f32[32]{0:T(128)} %param.15) | copy-start | bytes 388
  5.5 10.5 %copy-start.6 = (f32[128]{0:T(128)S(1)}, f32[128]{0:T(128)}, u32[]{:S(2)}) copy-start(f32[128]{0:T(128)} %param.14) | copy-start | bytes 1540
  5.5 30.2 %copy-start.3 = (f32[128]{0:T(128)S(1)}, f32[128]{0:T(128)}, u32[]{:S(2)}) copy-start(f32[128]{0:T(128)} %constant.45.clone) | copy-start | bytes 1540
  5.6 30.2 %copy-start.4 = (f32[128]{0:T(128)S(1)}, f32[128]{0:T(128)}, u32[]{:S(2)}) copy-start(f32[128]{0:T(128)} %constant.44.clone) | copy-start | bytes 1540
  5.6 36.0 %all-to-all-start = ((bf16[16,256,128]{2,1,0:T(8,128)(2,1)}), bf16[16,256,128]{2,1,0:T(8,128)(2,1)S(1)}, u32[]{:S(2)}, u32[]{:S(2)}) async-start(bf16[16,256,128]{2,1,0:T(8,128)(2,1)} %bitcast.2), calls=%async_computation | async-start | bytes 2097152 | tf_op jit(solution)/shard_map/all_to_all | solution.py:447
  14.0 27.5 %copy-start = (bf16[4,128,256]{2,1,0:T(8,128)(2,1)S(1)}, bf16[4,128,256]{2,1,0:T(8,128)(2,1)}, u32[]{:S(2)}) copy-start(bf16[4,128,256]{2,1,0:T(8,128)(2,1)} %constant.46.clone.m_ref) | copy-start | bytes 786436
  14.1 7.5 %collective-permute-start = (f32[1,32]{1,0:T(1,128)S(1)}, f32[1,32]{1,0:T(1,128)S(1)}, u32[]{:S(2)}, u32[]{:S(2)}) collective-permute-start(f32[1,32]{1,0:T(1,128)S(1)} %bitcast.10), channel_id=1, source_target_pairs={{0,8},{8,0},{16,24},{24,16},{1,9},{9,1},{17,25},{25,17},{2,10},{10... | collective-permute-start | bytes 392 | tf_op jit(solution)/shard_map/ppermute | solution.py:415
  16.1 15.1 %collective-permute-start.2 = (f32[1,128]{1,0:T(1,128)S(1)}, f32[1,128]{1,0:T(1,128)S(1)}, u32[]{:S(2)}, u32[]{:S(2)}) collective-permute-start(f32[1,128]{1,0:T(1,128)S(1)} %bitcast.12), channel_id=1, source_target_pairs={{0,2},{1,3},{2,0},{3,1},{4,6},{5,7},{6,4},{7,5},{8,10},{9,11},{10,... | collective-permute-start | bytes 1544 | tf_op jit(solution)/shard_map/ppermute | solution.py:415
  21.6 3.6 %collective-permute-start.1 = (f32[2,32]{1,0:T(2,128)S(1)}, f32[2,32]{1,0:T(2,128)S(1)}, u32[]{:S(2)}, u32[]{:S(2)}) collective-permute-start(f32[2,32]{1,0:T(2,128)S(1)} %pad_maximum_fusion.2), channel_id=1, source_target_pairs={{0,16},{8,24},{16,0},{24,8},{1,17},{9,25},{17,1},{25,9},{2,18},{10... | collective-permute-start | bytes 776 | tf_op jit(solution)/shard_map/ppermute | solution.py:415
  31.1 8.6 %collective-permute-start.3 = (f32[2,128]{1,0:T(2,128)S(1)}, f32[2,128]{1,0:T(2,128)S(1)}, u32[]{:S(2)}, u32[]{:S(2)}) collective-permute-start(f32[2,128]{1,0:T(2,128)S(1)} %pad_maximum_fusion.3), channel_id=1, source_target_pairs={{0,4},{1,5},{2,6},{3,7},{4,0},{5,1},{6,2},{7,3},{8,12},{9,13},{10,... | collective-permute-start | bytes 3080 | tf_op jit(solution)/shard_map/ppermute | solution.py:415
  42.9 3.5 %copy-start.2 = (bf16[2,256,256]{2,1,0:T(8,128)(2,1)S(1)}, bf16[2,256,256]{2,1,0:T(8,128)(2,1)}, u32[]{:S(2)}) copy-start(bf16[2,256,256]{2,1,0:T(8,128)(2,1)} %constant.47.clone.m_ref) | copy-start | bytes 786436
  42.9 2.0 %collective-permute-start.4 = (bf16[16,128,128]{2,1,0:T(8,128)(2,1)S(1)}, bf16[16,128,128]{2,1,0:T(8,128)(2,1)S(1)}, u32[]{:S(2)}, u32[]{:S(2)}) collective-permute-start(bf16[16,128,128]{2,1,0:T(8,128)(2,1)S(1)} %shard_map.128.rest_0_), channel_id=1, source_target_pairs={{0,1},{1,0},{2,3},{3,2},{4,5},{5,4},{6,7},{7,6},{8,9},{9,8},{10,11... | collective-permute-start | bytes 1572872 | tf_op jit(solution)/shard_map/ppermute | solution.py:328
  44.3 2.1 %collective-permute-start.5 = (bf16[16,128,128]{2,1,0:T(8,128)(2,1)S(1)}, bf16[16,128,128]{2,1,0:T(8,128)(2,1)S(1)}, u32[]{:S(2)}, u32[]{:S(2)}) collective-permute-start(bf16[16,128,128]{2,1,0:T(8,128)(2,1)S(1)} %shard_map.129.rest_1_), channel_id=1, source_target_pairs={{0,1},{1,0},{2,3},{3,2},{4,5},{5,4},{6,7},{7,6},{8,9},{9,8},{10,11... | collective-permute-start | bytes 1572872 | tf_op jit(solution)/shard_map/ppermute | solution.py:328
  47.1 31.2 %copy-start.1 = (bf16[7,128,256]{2,1,0:T(8,128)(2,1)S(1)}, bf16[7,128,256]{2,1,0:T(8,128)(2,1)}, u32[]{:S(2)}) copy-start(bf16[7,128,256]{2,1,0:T(8,128)(2,1)} %constant.48.clone.m_ref) | copy-start | bytes 1376260

commit v13 on v11

--- a/solution.py
+++ b/solution.py
@@ -161,13 +161,28 @@
 
 PIECE = 64
 BLOCK = 32
+NOTE = 8
 VMEM = pl.BlockSpec(memory_space=pltpu.VMEM)
 FAR = pl.BlockSpec(memory_space=pltpu.HBM)
 PARAMS = pltpu.CompilerParams(vmem_limit_bytes=32 << 20)
 
 
-def source_kernel(a_hbm, x_hbm, m_hbm, o_ref, a_ref, x_ref, m_ref, w_ref, a_sem, x_sems, m_sems):
+def write_note(note_ref, dip_ref, slowness):
+    note_ref[...] = jnp.zeros_like(note_ref)
+    note_ref[0:1, : dip_ref.shape[1]] = dip_ref[...]
+    note_ref[3:4, :] = slowness
+    for at in (0, 3):
+        left = note_ref[at : at + 1, :]
+        for part in range(3):
+            piece = left.astype(jnp.bfloat16).astype(jnp.float32)
+            note_ref[at + part : at + part + 1, :] = piece
+            left = left - piece
+
+
+def source_kernel(keep, a_hbm, d_ref, x_hbm, m_hbm, *rest):
+    outs, (a_ref, x_ref, m_ref, w_ref, note_ref, a_sem, x_sems, m_sems) = rest[:-8], rest[-8:]
     rows, cols, _ = x_ref.shape
+    devices = outs[0].shape[0]
     levels = m_ref.shape[0]
     a_copy = pltpu.make_async_copy(a_hbm, a_ref, a_sem)
     x_copies = []
@@ -197,12 +212,16 @@
             w_ref[2 * level],
             w_ref[2 * level + 1],
             lambda index: (cosines[own], sines[own]),
-            16,
-            begin // BLOCK,
+            8,
         )
 
     a_copy.wait()
-    cosines, sines = rotation(column_of(a_ref[...], cols))
+    slowness = a_ref[...]
+    cosines, sines = rotation(column_of(slowness, cols))
+    write_note(note_ref, d_ref, slowness)
+    note = note_ref[...].astype(jnp.bfloat16)
+    for device in range(devices):
+        outs[0][device, keep * rows :, :] = note
     m_copies[0].wait()
     expand(0)
     for piece, copy in enumerate(x_copies):
@@ -218,7 +237,15 @@
             level_on(level, begin)
 
     def store_block(first, second, block):
-        o_ref[block_at(first, second)] = block
+        begin = second * 16
+        for inner in range(16):
+            col = first * 16 + inner
+            if col < devices * keep:
+                device, at = divmod(col, keep)
+                at = at * rows + begin
+                outs[0][device, at : at + 16, :] = block[inner]
+            else:
+                outs[1][col - devices * keep, begin : begin + 16, :] = block[inner]
 
     swap_axes(
         lambda first, second: x_ref[block_at(first, second)],
@@ -229,45 +256,150 @@
     )
 
 
-def source_levels(x, matrices, slowness):
+def source_levels(x, matrices, slowness, dip_field, devices, keep):
     rows, cols, _ = x.shape
     levels = matrices.shape[0]
-    operands = (slowness[None, :], x, matrices)
-    far = [pltpu.with_memory_space_constraint(value, pltpu.HBM) for value in operands]
+    out_shape = [jax.ShapeDtypeStruct((devices, keep * rows + NOTE, WIDE), x.dtype)]
+    if devices * keep < cols:
+        out_shape.append(jax.ShapeDtypeStruct((cols - devices * keep, rows, WIDE), x.dtype))
+    a, x, matrices = (
+        pltpu.with_memory_space_constraint(value, pltpu.HBM)
+        for value in (slowness[None, :], x, matrices)
+    )
     return pl.pallas_call(
-        source_kernel,
-        out_shape=jax.ShapeDtypeStruct((cols, rows, WIDE), x.dtype),
-        in_specs=[FAR, FAR, FAR],
-        out_specs=VMEM,
+        functools.partial(source_kernel, keep),
+        out_shape=out_shape,
+        in_specs=[FAR, VMEM, FAR, FAR],
+        out_specs=[VMEM] * len(out_shape),
         scratch_shapes=[
             pltpu.VMEM((1, cols), jnp.float32),
             pltpu.VMEM(x.shape, x.dtype),
             pltpu.VMEM(matrices.shape, x.dtype),
             pltpu.VMEM((2 * levels, 2 * WIDE, 2 * WIDE), x.dtype),
+            pltpu.VMEM((NOTE, WIDE), jnp.float32),
             pltpu.SemaphoreType.DMA,
             pltpu.SemaphoreType.DMA((cols // PIECE,)),
             pltpu.SemaphoreType.DMA((levels,)),
         ],
         compiler_params=PARAMS,
-    )(*far)
-
-
-def middle_kernel(levels, rows, x_ref, m_ref, cs_ref, ss_ref, ct_ref, st_ref, o_ref):
+    )(a, dip_field[None, :], x, matrices)
+
+
+def partner_kernel(first_col, a_ref, x_ref, m_ref, y_ref, o_ref, state_ref):
+    rows, cols, _ = x_ref.shape
+    o_ref[:cols] = y_ref[...]
+    cosines, sines = rotation(column_of(a_ref[...], first_col + cols)[first_col:])
+    for level in range(m_ref.shape[0]):
+        source = x_ref if level == 0 else state_ref
+        weights = whole_matrix(m_ref[level])
+
+        def store(index, value):
+            state_ref[index] = value
+
+        butterfly(
+            lambda index: source[index],
+            store,
+            rows,
+            1 << level,
+            *weights,
+            lambda index: (cosines, sines),
+            max(1, 256 // cols),
+        )
+
+    def store_block(first, second, block):
+        o_ref[cols + first * 16 : cols + first * 16 + 16, second * 16 : second * 16 + 16] = block
+
+    swap_axes(
+        lambda first, second: state_ref[block_at(first, second)],
+        store_block,
+        rows // 16,
+        cols // 16,
+        shuffle_matrix(),
+    )
+
+
+def partner_levels(x, matrices, slowness, own, first_col):
+    rows, cols, _ = x.shape
+    return pl.pallas_call(
+        functools.partial(partner_kernel, first_col),
+        out_shape=jax.ShapeDtypeStruct((2 * cols, rows, WIDE), x.dtype),
+        in_specs=[VMEM] * 4,
+        out_specs=VMEM,
+        scratch_shapes=[pltpu.VMEM(x.shape, x.dtype)],
+        compiler_params=PARAMS,
+    )(slowness[None, :], x, matrices, own)
+
+
+def pair_kernel(axis, bit, by_row, x_ref, y_ref, m_ref, c_ref, s_ref, o_ref):
+    count, rows, _ = x_ref.shape
+    matrix = m_ref[lax.rem(lax.div(lax.axis_index(axis), 1 << bit), 2)]
+    group = max(1, 512 // rows)
+    for start in range(0, count, group):
+        picked = slice(start, start + group)
+        pair = [ref[picked].reshape(-1, WIDE) for ref in (x_ref, y_ref)]
+        both = jnp.dot(
+            jnp.concatenate(pair, axis=1), matrix, preferred_element_type=jnp.float32
+        )
+        for index in range(start, min(start + group, count)):
+            own = slice((index - start) * rows, (index - start + 1) * rows)
+            phase = slice(None) if by_row else slice(index, index + 1)
+            value = both[own, :WIDE] * c_ref[phase, :] + both[own, WIDE:] * s_ref[phase, :]
+            o_ref[index] = value.astype(jnp.bfloat16)
+
+
+def joined(own, other, axis, bit, upper, angles, by_row):
+    upper = upper.astype(np.float32).reshape(2, HALF, 2, WIDE)
+    below = np.concatenate([-upper[..., HALF:], upper[..., :HALF]], axis=3)
+    whole = np.concatenate([upper, below], axis=1).reshape(2, WIDE, 2, 2, HALF)
+    choices = []
+    for child in range(2):
+        picked = whole[[child, 1 - child], :, child].reshape(2 * WIDE, 2, HALF)
+        both = np.concatenate([picked, picked[:, ::-1]], axis=1).reshape(2 * WIDE, -1)
+        choices.append(both.astype(ml_dtypes.bfloat16))
+    return pl.pallas_call(
+        functools.partial(pair_kernel, axis, bit, by_row),
+        out_shape=jax.ShapeDtypeStruct(own.shape, own.dtype),
+        in_specs=[VMEM] * 5,
+        out_specs=VMEM,
+        compiler_params=PARAMS,
+    )(own, other, jnp.asarray(np.stack(choices)), *angles)
+
+
+def exchanged(value, axis, bit):
+    count = lax.axis_size(axis)
+    return lax.ppermute(value, axis, [(i, i ^ 1 << bit) for i in range(count)])
+
+
+def middle_kernel(levels, rows, tgt_count, x_ref, m_ref, o_ref):
     count, total, _ = x_ref.shape
-    run = total // rows
-    tgt_count = cs_ref.shape[0] // run
+    kept = (total - NOTE) // rows
+    place = lax.axis_index("src") * tgt_count + lax.axis_index("tgt")
+
+    def noted(device, at):
+        note = x_ref[device, kept * rows :, :].astype(jnp.float32)
+        return note[at : at + 1] + note[at + 1 : at + 2] + note[at + 2 : at + 3]
+
+    slowness = jnp.concatenate([noted(at, 3) for at in range(tgt_count)], axis=0)
+    lanes = lax.broadcasted_iota(jnp.int32, slowness.shape, 1)
+    by_col = []
+    for col in range(kept):
+        picked = jnp.where(lanes == place * kept + col, slowness, 0.0)
+        by_col.append(rotation(jnp.sum(picked, axis=1, keepdims=True)))
+    by_src = [
+        rotation(column_of(noted(at * tgt_count, 0), rows)) for at in range(count // tgt_count)
+    ]
+
     for step, (apart, by_source) in enumerate(levels):
         source = x_ref if step == 0 else o_ref
-        matrix, swapped = whole_matrix(m_ref[step])
-        for col in range(run):
+        weights = whole_matrix(m_ref[step])
+        for col in range(kept):
             own = slice(col * rows, (col + 1) * rows)
 
             def phase_of(index):
                 if by_source:
-                    at = index % tgt_count * run + col
-                    return cs_ref[at : at + 1, :], ss_ref[at : at + 1, :]
-                at = index // tgt_count
-                return ct_ref[at], st_ref[at]
+                    at = index % tgt_count
+                    return tuple(table[at : at + 1, :] for table in by_col[col])
+                return by_src[index // tgt_count]
 
             def store(index, value):
                 o_ref[index, own, :] = value
@@ -277,41 +409,51 @@
                 store,
                 count,
                 apart,
-                matrix,
-                swapped,
+                *weights,
                 phase_of,
-                16,
-                col,
+                8,
             )
 
 
-def middle_levels(x, matrices, src_tables, tgt_tables, levels):
-    rows = tgt_tables[0].shape[1]
+def middle_levels(x, matrices, levels, rows, tgt_count):
+    count, total, _ = x.shape
     return pl.pallas_call(
-        functools.partial(middle_kernel, levels, rows),
-        out_shape=jax.ShapeDtypeStruct(x.shape, x.dtype),
-        in_specs=[VMEM] * 6,
+        functools.partial(middle_kernel, levels, rows, tgt_count),
+        out_shape=jax.ShapeDtypeStruct((count, total - NOTE, WIDE), x.dtype),
+        in_specs=[VMEM] * 2,
         out_specs=VMEM,
         compiler_params=PARAMS,
-    )(x, matrices, *src_tables, *tgt_tables)
-
-
-def target_kernel(m_ref, c_ref, s_ref, x_ref, o_hbm, state_ref, o_ref, o_sems):
-    cols, rows, _ = x_ref.shape
+    )(x, matrices)
+
+
+def target_kernel(m_ref, c_ref, s_ref, *rest):
+    xs, (o_hbm, state_ref, o_ref, o_sems) = rest[:-4], rest[-4:]
+    cols, rows, _ = state_ref.shape
+    devices, kept = xs[0].shape[0], xs[0].shape[1] // rows
+
+    def arrived(index, start):
+        if index >= devices * kept:
+            return xs[1][index - devices * kept, start : start + 16, :]
+        device, col = divmod(index, kept)
+        start += col * rows
+        return xs[0][device, start : start + 16, :]
+
     levels = m_ref.shape[0]
 
     for level in range(levels):
-        source = x_ref if level == 0 else state_ref
         weights = whole_matrix(m_ref[level])
         for start in range(0, rows, 16):
             own = slice(start, start + 16)
             cosine, sine = c_ref[own, :], s_ref[own, :]
 
+            def load(index):
+                return arrived(index, start) if level == 0 else state_ref[index, own, :]
+
             def store(index, value):
                 state_ref[index, own, :] = value
 
             butterfly(
-                lambda index: source[index, own, :],
+                load,
                 store,
                 cols,
                 1 << (levels - 1 - level),
@@ -341,36 +483,20 @@
         copy.wait()
 
 
-def target_levels(x, matrices, angles):
-    cols, rows, _ = x.shape
+def target_levels(xs, matrices, angles, cols, rows):
     shape = (rows, cols, WIDE)
     return pl.pallas_call(
         target_kernel,
-        out_shape=jax.ShapeDtypeStruct(shape, x.dtype),
-        in_specs=[VMEM] * 4,
+        out_shape=jax.ShapeDtypeStruct(shape, jnp.bfloat16),
+        in_specs=[VMEM] * (3 + len(xs)),
         out_specs=FAR,
         scratch_shapes=[
-            pltpu.VMEM(x.shape, x.dtype),
-            pltpu.VMEM(shape, x.dtype),
+            pltpu.VMEM((cols, rows, WIDE), jnp.bfloat16),
+            pltpu.VMEM(shape, jnp.bfloat16),
             pltpu.SemaphoreType.DMA((rows // 16,)),
         ],
         compiler_params=PARAMS,
-    )(matrices, *angles, x)
-
-
-def gathered(values, axis):
-    count = lax.axis_size(axis)
-    place = lax.axis_index(axis)
-    values = values[None]
-    apart = 1
-    while apart < count:
-        other = lax.ppermute(values, axis, [(i, i ^ apart) for i in range(count)])
-        mine_first = (place & apart) == 0
-        values = jnp.concatenate(
-            [jnp.where(mine_first, values, other), jnp.where(mine_first, other, values)]
-        )
-        apart *= 2
-    return values
+    )(matrices, *angles, *xs)
 
 
 def local(box_weights, slowness, dip_field):
@@ -388,36 +514,47 @@
         return jnp.asarray(np.stack(matrices[low:high]))
 
     run = cols // devices
-    place = lax.axis_index("src") * tgt_count + lax.axis_index("tgt")
+    keep = run - run // 4
+    sent = devices * keep
+    stays = sent < cols
+    top = tgt_bits - 1
+
+    if stays:
+        raw = exchanged(box_weights[:, sent:], "tgt", top)
+        far_slowness = exchanged(slowness, "tgt", top)
+
+    first = matrices_of(0, row_bits)
+    state, *stay = source_levels(box_weights, first, slowness, dip_field, devices, keep)
+    state, slowness, dip_field = lax.optimization_barrier((state, slowness, dip_field))
+    by_row = tables(dip_field)
 
     def traded(state):
         return lax.all_to_all(state, ("src", "tgt"), 0, 0, tiled=True)
 
-    state = source_levels(box_weights, matrices_of(0, row_bits), slowness)
-
-    state, slowness, dip_field = lax.optimization_barrier((state, slowness, dip_field))
-    all_dip = gathered(dip_field, "src")
-    all_slowness = gathered(slowness, "tgt")
-    run_slowness = lax.dynamic_slice_in_dim(all_slowness, place * run, run, 1)
-
-    state = state.reshape(devices, run * rows, WIDE)
     state = traded(state)
+
+    if stays:
+        by_col = tables(jnp.concatenate([slowness[sent:], far_slowness[sent:]]))
+        both = partner_levels(raw, first, far_slowness, stay[0], sent)
+        for bit in range(src_bits):
+            other = exchanged(both, "src", bit)
+            both = joined(both, other, "src", bit, matrices[row_bits + bit], by_col, False)
+            if bit == 0:
+                state, both = lax.optimization_barrier((state, both))
+        here, there = both[: cols - sent], both[cols - sent :]
+        here = joined(here, there, "tgt", top, matrices[first_target], by_row, True)
+        for at, bit in enumerate(reversed(range(top))):
+            other = exchanged(here, "tgt", bit)
+            here = joined(here, other, "tgt", bit, matrices[first_target + 1 + at], by_row, True)
+        stay = [here]
+
     levels = [(tgt_count << bit, True) for bit in range(src_bits)]
     levels += [(1 << bit, False) for bit in reversed(range(tgt_bits))]
-    state = middle_levels(
-        state,
-        matrices_of(row_bits, first_target + tgt_bits),
-        tables(run_slowness.reshape(-1)),
-        tables(all_dip),
-        levels,
-    )
-    state = traded(state)
-
-    return target_levels(
-        state.reshape(cols, rows, WIDE),
-        matrices_of(first_target + tgt_bits, total),
-        tables(dip_field),
-    )
+    middle = matrices_of(row_bits, first_target + tgt_bits)
+    state = traded(middle_levels(state, middle, levels, rows, tgt_count))
+
+    last = matrices_of(first_target + tgt_bits, total)
+    return target_levels([state, *stay], last, by_row, cols, rows)
 
 
 def solution(mesh):

time: 77.7 us -> 109 us (1.40)
  waiting for transfers between devices: 16.7 us -> 68.7 us
  blocking collectives: 30.1 us -> 0 us
  Pallas kernels: 12.3 us -> 16.3 us
  local copies, waits for them, and re-layouts: 0.2 us -> 3.39 us
  starting transfers between devices: 17.4 us -> 19.3 us
    ppermute x5 -> x6, waiting for transfers between devices: 15.8 us -> 68.7 us  [exchanged(): return lax.ppermute(value, axis, [(i, i ^ 1 << bit) for i in range(count)])]
    all_to_all x1 -> x0, blocking collectives: 30.1 us -> none  [traded(): return lax.all_to_all(state, ('src', 'tgt'), 0, 0, tiled=True)]
    all_to_all x1 -> x2, starting transfers between devices: 7.3 us -> 11.5 us  [traded(): return lax.all_to_all(state, ('src', 'tgt'), 0, 0, tiled=True)]
    pallas_call x3 -> x9, Pallas kernels: 12.3 us -> 16.3 us  [the longest x1 5.24 us: source_levels(): pl.pallas_call(functools.partial(source_kernel, keep), out_shape=out_shap...]
    ppermute x5 -> x6, starting transfers between devices: 10.1 us -> 7.78 us  [exchanged(): return lax.ppermute(value, axis, [(i, i ^ 1 << bit) for i in range(count)])]
    unnamed x12 -> x22, local copies, waits for them, and re-layouts: 0.04 us -> 2.19 us
    slice x0 -> x4, local copies, waits for them, and re-layouts: none -> 1.2 us  [the longest x1 1.02 us: local(): raw = exchanged(box_weights[:, sent:], 'tgt', top)]
  transfers between devices with their start and end apart: 6 -> 8, of which waited for: 5 -> 5; matrix products, arithmetic and copies ran while one was open for 1% -> 1% of each run, Pallas kernels for 0% -> 3%
where the time goes in v13:
time: 109 us; the launch traced here: 108 us
  waiting for transfers between devices  68.7 us (63%)
  starting transfers between devices  19.3 us (18%)
  Pallas kernels  16.3 us (15%)
  local copies, waits for them, and re-layouts  3.39 us (3%)
    ppermute x6, waiting for transfers between devices, exchanged(): return lax.ppermute(value, axis, [(i, i ^ 1 << bit) for i in range(count)])  68.7 us
    all_to_all x2, starting transfers between devices, traded(): return lax.all_to_all(state, ('src', 'tgt'), 0, 0, tiled=True)  11.5 us
    ppermute x6, starting transfers between devices, exchanged(): return lax.ppermute(value, axis, [(i, i ^ 1 << bit) for i in range(count)])  7.78 us
    pallas_call x1, Pallas kernels, source_levels(): pl.pallas_call(functools.partial(source_kernel, keep), out_shape=out_shap...  5.24 us
    pallas_call x1, Pallas kernels, target_levels(): pl.pallas_call(target_kernel, out_shape=jax.ShapeDtypeStruct(shape, jnp.b...  4.39 us
    pallas_call x1, Pallas kernels, middle_levels(): pl.pallas_call(functools.partial(middle_kernel, levels, rows, tgt_count),...  3.13 us
    unnamed x22, local copies, waits for them, and re-layouts  2.19 us
  transfers between devices with their start and end apart: 8, of which 5 were waited for; matrix products, arithmetic and copies ran while one was open for 1% of the time, Pallas kernels for 3%

profile of v13, /device:TPU:0, one launch (start us, length us, event | category | flops | bytes accessed | tf_op | source)
XLA Modules:
  0.0 108.4 jit_solution(15633010145443971385)
XLA Ops:
  0.0 0.7 copy-done.7
  0.7 5.2 %shard_map.145 = (bf16[32,104,128]{2,1,0:T(8,128)(2,1)}, bf16[32,32,128]{2,1,0:T(8,128)(2,1)S(1)}) custom-call(f32[1,128]{1,0:T(1,128)} %bitcast.5, f32[1,32]{1,0:T(1,128)S(1)} %bitcast.3, bf16[32,128,128]{2,1,0:T(8,128)(2,1)} %x_hbm.1, bf16[5,128,256]{2,1,0:T(8,128)(2,1)} %constant.18.clone.m_hbm.m_ref), custom_call_target="tpu_custom_call" | custom-call | tf_op jit(solution)/shard_map/pallas_call | solution.py:269
  5.9 7.3 %all-to-all-start = ((bf16[32,104,128]{2,1,0:T(8,128)(2,1)}), bf16[32,104,128]{2,1,0:T(8,128)(2,1)S(1)}, u32[]{:S(2)}, u32[]{:S(2)}) async-start(bf16[32,104,128]{2,1,0:T(8,128)(2,1)} %get-tuple-element.14), calls=%async_computation | async-start | bytes 1703936 | tf_op jit(solution)/shard_map/all_to_all | solution.py:532
  13.2 1.0 slice.15
  14.3 2.7 %collective-permute-start.1 = (bf16[32,32,128]{2,1,0:T(8,128)(2,1)S(1)}, bf16[32,32,128]{2,1,0:T(8,128)(2,1)S(1)}, u32[]{:S(2)}, u32[]{:S(2)}) collective-permute-start(bf16[32,32,128]{2,1,0:T(8,128)(2,1)S(1)} %slice.15), channel_id=1, source_target_pairs={{0,4},{1,5},{2,6},{3,7},{4,0},{5,1},{6,2},{7,3},{8,12},{9,13},{10,... | collective-permute-start | bytes 786440 | tf_op jit(solution)/shard_map/ppermute | solution.py:370
  17.0 0.3 collective-permute-start
  17.3 29.3 %collective-permute-done = f32[128]{0:T(128)S(1)} collective-permute-done((f32[128]{0:T(128)S(1)}, f32[128]{0:T(128)S(1)}, u32[]{:S(2)}, u32[]{:S(2)}) %collective-permute-start) | collective-permute-done | bytes 544 | tf_op jit(solution)/shard_map/ppermute | solution.py:370
  46.6 1.7 %shard_map.146.x_ref = bf16[64,32,128]{2,1,0:T(8,128)(2,1)S(1)} custom-call(f32[1,128]{1,0:T(1,128)S(1)} %bitcast.4, bf16[32,32,128]{2,1,0:T(8,128)(2,1)S(1)} %collective-permute-done.1.x_ref, bf16[5,128,256]{2,1,0:T(8,128)(2,1)S(1)} %copy-done, bf16[32,32,128]{2,1,0:T(8,128)(2,1)S(1)} %get-tuple-element.15.y_ref), custom_call_target="tpu_custom_call" | custom-call | tf_op jit(solution)/shard_map/pallas_call | solution.py:323
  48.3 1.5 %collective-permute-start.2 = (bf16[64,32,128]{2,1,0:T(8,128)(2,1)S(1)}, bf16[64,32,128]{2,1,0:T(8,128)(2,1)S(1)}, u32[]{:S(2)}, u32[]{:S(2)}) collective-permute-start(bf16[64,32,128]{2,1,0:T(8,128)(2,1)S(1)} %shard_map.146.x_ref), channel_id=1, source_target_pairs={{0,8},{8,0},{16,24},{24,16},{1,9},{9,1},{17,25},{25,17},{2,10},{10... | collective-permute-start | bytes 1572872 | tf_op jit(solution)/shard_map/ppermute | solution.py:370
  49.8 0.1 slice.16
  49.9 0.1 slice.17
  50.0 0.1 pad_maximum_fusion
  50.1 0.6 copy-done.8
  50.6 0.0 copy-done.9
  50.7 0.2 fusion
  50.9 10.9 %collective-permute-done.2.y_ref = bf16[64,32,128]{2,1,0:T(8,128)(2,1)S(1)} collective-permute-done((bf16[64,32,128]{2,1,0:T(8,128)(2,1)S(1)}, bf16[64,32,128]{2,1,0:T(8,128)(2,1)S(1)}, u32[]{:S(2)}, u32[]{:S(2)}) %collective-permute-start.2) | collective-permute-done | bytes 524320 | tf_op jit(solution)/shard_map/ppermute | solution.py:370
  61.8 0.4 shard_map.147.x_ref
  62.2 3.1 %shard_map.148 = bf16[32,96,128]{2,1,0:T(8,128)(2,1)} custom-call(bf16[32,104,128]{2,1,0:T(8,128)(2,1)S(1)} %all-to-all-done.x_ref, bf16[5,128,256]{2,1,0:T(8,128)(2,1)S(1)} %copy-done), custom_call_target="tpu_custom_call" | custom-call | tf_op jit(solution)/shard_map/pallas_call | solution.py:420
  65.4 4.2 %all-to-all-start.1 = ((bf16[32,96,128]{2,1,0:T(8,128)(2,1)}), bf16[32,96,128]{2,1,0:T(8,128)(2,1)S(1)}, u32[]{:S(2)}, u32[]{:S(2)}) async-start(bf16[32,96,128]{2,1,0:T(8,128)(2,1)} %shard_map.148), calls=%async_computation.1 | async-start | bytes 1572864 | tf_op jit(solution)/shard_map/all_to_all | solution.py:532
  69.6 1.7 %collective-permute-start.3 = (bf16[64,32,128]{2,1,0:T(8,128)(2,1)S(1)}, bf16[64,32,128]{2,1,0:T(8,128)(2,1)S(1)}, u32[]{:S(2)}, u32[]{:S(2)}) collective-permute-start(bf16[64,32,128]{2,1,0:T(8,128)(2,1)S(1)} %shard_map.147.x_ref), channel_id=1, source_target_pairs={{0,16},{8,24},{16,0},{24,8},{1,17},{9,25},{17,1},{25,9},{2,18},{10... | collective-permute-start | bytes 1572872 | tf_op jit(solution)/shard_map/ppermute | solution.py:370
  71.3 0.1 fusion.1
  71.4 20.6 %collective-permute-done.3.y_ref = bf16[64,32,128]{2,1,0:T(8,128)(2,1)S(1)} collective-permute-done((bf16[64,32,128]{2,1,0:T(8,128)(2,1)S(1)}, bf16[64,32,128]{2,1,0:T(8,128)(2,1)S(1)}, u32[]{:S(2)}, u32[]{:S(2)}) %collective-permute-start.3) | collective-permute-done | bytes 524320 | tf_op jit(solution)/shard_map/ppermute | solution.py:370
  92.0 0.4 shard_map.149
  92.5 0.9 copy-done.4
  93.4 0.3 shard_map.150.x_ref
  93.7 1.5 %collective-permute-start.4 = (bf16[32,32,128]{2,1,0:T(8,128)(2,1)S(1)}, bf16[32,32,128]{2,1,0:T(8,128)(2,1)S(1)}, u32[]{:S(2)}, u32[]{:S(2)}) collective-permute-start(bf16[32,32,128]{2,1,0:T(8,128)(2,1)S(1)} %shard_map.150.x_ref), channel_id=1, source_target_pairs={{0,2},{1,3},{2,0},{3,1},{4,6},{5,7},{6,4},{7,5},{8,10},{9,11},{10,... | collective-permute-start | bytes 786440 | tf_op jit(solution)/shard_map/ppermute | solution.py:370
  95.2 6.4 %collective-permute-done.4.y_ref = bf16[32,32,128]{2,1,0:T(8,128)(2,1)S(1)} collective-permute-done((bf16[32,32,128]{2,1,0:T(8,128)(2,1)S(1)}, bf16[32,32,128]{2,1,0:T(8,128)(2,1)S(1)}, u32[]{:S(2)}, u32[]{:S(2)}) %collective-permute-start.4) | collective-permute-done | bytes 262176 | tf_op jit(solution)/shard_map/ppermute | solution.py:370
  101.6 0.3 shard_map.151.x_ref
  102.0 0.1 collective-permute-start.5
  102.0 1.5 %collective-permute-done.5.y_ref = bf16[32,32,128]{2,1,0:T(8,128)(2,1)S(1)} collective-permute-done((bf16[32,32,128]{2,1,0:T(8,128)(2,1)S(1)}, bf16[32,32,128]{2,1,0:T(8,128)(2,1)S(1)}, u32[]{:S(2)}, u32[]{:S(2)}) %collective-permute-start.5) | collective-permute-done | bytes 262176 | tf_op jit(solution)/shard_map/ppermute | solution.py:370
  103.6 0.3 shard_map.152.rest_1_
  103.9 4.4 %shard_map.153 = bf16[32,128,128]{2,1,0:T(8,128)(2,1)} custom-call(bf16[7,128,256]{2,1,0:T(8,128)(2,1)S(1)} %copy-done.1, f32[32,128]{1,0:T(8,128)S(1)} %get-tuple-element.24.c_ref, f32[32,128]{1,0:T(8,128)S(1)} %get-tuple-element.23.s_ref, bf16[32,96,128]{2,1,0:T(8,128)(2,1)S(1)} %all-to-all-done.1.rest_0_, bf16[32,32,128]{2,1,0:T(8,128)(2,1)S(1)} %shard_map.152.rest_1_), custom_call_target="tpu_custom_call" | custom-call | tf_op jit(solution)/shard_map/pallas_call | solution.py:488
  (22 shorter events, 0.1 us)
Async XLA Ops:
  0.0 0.7 copy-start.7
  5.9 56.3 %all-to-all-start = ((bf16[32,104,128]{2,1,0:T(8,128)(2,1)}), bf16[32,104,128]{2,1,0:T(8,128)(2,1)S(1)}, u32[]{:S(2)}, u32[]{:S(2)}) async-start(bf16[32,104,128]{2,1,0:T(8,128)(2,1)} %get-tuple-element.14), calls=%async_computation | async-start | bytes 1703936 | tf_op jit(solution)/shard_map/all_to_all | solution.py:532
  13.2 3.8 %copy-start.10 = (f32[128]{0:T(128)S(1)}, f32[128]{0:T(128)}, u32[]{:S(2)}) copy-start(f32[128]{0:T(128)} %param.16) | copy-start | bytes 1540
  13.2 33.3 %copy-start = (bf16[5,128,256]{2,1,0:T(8,128)(2,1)S(1)}, bf16[5,128,256]{2,1,0:T(8,128)(2,1)}, u32[]{:S(2)}) copy-start(bf16[5,128,256]{2,1,0:T(8,128)(2,1)} %constant.18.clone.m_hbm.m_ref) | copy-start | bytes 983044
  14.3 32.3 %collective-permute-start.1 = (bf16[32,32,128]{2,1,0:T(8,128)(2,1)S(1)}, bf16[32,32,128]{2,1,0:T(8,128)(2,1)S(1)}, u32[]{:S(2)}, u32[]{:S(2)}) collective-permute-start(bf16[32,32,128]{2,1,0:T(8,128)(2,1)S(1)} %slice.15), channel_id=1, source_target_pairs={{0,4},{1,5},{2,6},{3,7},{4,0},{5,1},{6,2},{7,3},{8,12},{9,13},{10,... | collective-permute-start | bytes 786440 | tf_op jit(solution)/shard_map/ppermute | solution.py:370
  17.0 29.5 %collective-permute-start = (f32[128]{0:T(128)S(1)}, f32[128]{0:T(128)S(1)}, u32[]{:S(2)}, u32[]{:S(2)}) collective-permute-start(f32[128]{0:T(128)S(1)} %copy-done.10), channel_id=1, source_target_pairs={{0,4},{1,5},{2,6},{3,7},{4,0},{5,1},{6,2},{7,3},{8,12},{9,13},{10,... | collective-permute-start | bytes 1544 | tf_op jit(solution)/shard_map/ppermute | solution.py:370
  46.6 15.2 %copy-start.6 = (bf16[2,256,256]{2,1,0:T(8,128)(2,1)S(1)}, bf16[2,256,256]{2,1,0:T(8,128)(2,1)}, u32[]{:S(2)}) copy-start(bf16[2,256,256]{2,1,0:T(8,128)(2,1)} %constant.21.clone.m_ref) | copy-start | bytes 786436
  48.3 13.5 %collective-permute-start.2 = (bf16[64,32,128]{2,1,0:T(8,128)(2,1)S(1)}, bf16[64,32,128]{2,1,0:T(8,128)(2,1)S(1)}, u32[]{:S(2)}, u32[]{:S(2)}) collective-permute-start(bf16[64,32,128]{2,1,0:T(8,128)(2,1)S(1)} %shard_map.146.x_ref), channel_id=1, source_target_pairs={{0,8},{8,0},{16,24},{24,16},{1,9},{9,1},{17,25},{25,17},{2,10},{10... | collective-permute-start | bytes 1572872 | tf_op jit(solution)/shard_map/ppermute | solution.py:370
  50.0 0.7 copy-start.8
  50.0 0.7 copy-start.9
  65.4 26.6 %copy-start.5 = (bf16[2,256,256]{2,1,0:T(8,128)(2,1)S(1)}, bf16[2,256,256]{2,1,0:T(8,128)(2,1)}, u32[]{:S(2)}) copy-start(bf16[2,256,256]{2,1,0:T(8,128)(2,1)} %constant.22.clone.m_ref) | copy-start | bytes 786436
  65.4 38.5 %all-to-all-start.1 = ((bf16[32,96,128]{2,1,0:T(8,128)(2,1)}), bf16[32,96,128]{2,1,0:T(8,128)(2,1)S(1)}, u32[]{:S(2)}, u32[]{:S(2)}) async-start(bf16[32,96,128]{2,1,0:T(8,128)(2,1)} %shard_map.148), calls=%async_computation.1 | async-start | bytes 1572864 | tf_op jit(solution)/shard_map/all_to_all | solution.py:532
  69.6 22.4 %collective-permute-start.3 = (bf16[64,32,128]{2,1,0:T(8,128)(2,1)S(1)}, bf16[64,32,128]{2,1,0:T(8,128)(2,1)S(1)}, u32[]{:S(2)}, u32[]{:S(2)}) collective-permute-start(bf16[64,32,128]{2,1,0:T(8,128)(2,1)S(1)} %shard_map.147.x_ref), channel_id=1, source_target_pairs={{0,16},{8,24},{16,0},{24,8},{1,17},{9,25},{17,1},{25,9},{2,18},{10... | collective-permute-start | bytes 1572872 | tf_op jit(solution)/shard_map/ppermute | solution.py:370
  92.4 1.0 copy-start.4
  93.4 8.2 %copy-start.3 = (bf16[2,256,256]{2,1,0:T(8,128)(2,1)S(1)}, bf16[2,256,256]{2,1,0:T(8,128)(2,1)}, u32[]{:S(2)}) copy-start(bf16[2,256,256]{2,1,0:T(8,128)(2,1)} %constant.24.clone.m_ref) | copy-start | bytes 786436
  93.7 9.9 %copy-start.2 = (bf16[2,256,256]{2,1,0:T(8,128)(2,1)S(1)}, bf16[2,256,256]{2,1,0:T(8,128)(2,1)}, u32[]{:S(2)}) copy-start(bf16[2,256,256]{2,1,0:T(8,128)(2,1)} %constant.25.clone.m_ref) | copy-start | bytes 786436
  93.7 7.9 %collective-permute-start.4 = (bf16[32,32,128]{2,1,0:T(8,128)(2,1)S(1)}, bf16[32,32,128]{2,1,0:T(8,128)(2,1)S(1)}, u32[]{:S(2)}, u32[]{:S(2)}) collective-permute-start(bf16[32,32,128]{2,1,0:T(8,128)(2,1)S(1)} %shard_map.150.x_ref), channel_id=1, source_target_pairs={{0,2},{1,3},{2,0},{3,1},{4,6},{5,7},{6,4},{7,5},{8,10},{9,11},{10,... | collective-permute-start | bytes 786440 | tf_op jit(solution)/shard_map/ppermute | solution.py:370
  101.9 1.9 %copy-start.1 = (bf16[7,128,256]{2,1,0:T(8,128)(2,1)S(1)}, bf16[7,128,256]{2,1,0:T(8,128)(2,1)}, u32[]{:S(2)}) copy-start(bf16[7,128,256]{2,1,0:T(8,128)(2,1)} %constant.26.clone.m_ref) | copy-start | bytes 1376260
  102.0 1.6 %collective-permute-start.5 = (bf16[32,32,128]{2,1,0:T(8,128)(2,1)S(1)}, bf16[32,32,128]{2,1,0:T(8,128)(2,1)S(1)}, u32[]{:S(2)}, u32[]{:S(2)}) collective-permute-start(bf16[32,32,128]{2,1,0:T(8,128)(2,1)S(1)} %shard_map.151.x_ref), channel_id=1, source_target_pairs={{0,1},{1,0},{2,3},{3,2},{4,5},{5,4},{6,7},{7,6},{8,9},{9,8},{10,11... | collective-permute-start | bytes 786440 | tf_op jit(solution)/shard_map/ppermute | solution.py:370

commit v14 on v11

--- a/solution.py
+++ b/solution.py
@@ -160,6 +160,7 @@
 
 
 PIECE = 64
+SPAN = 8
 BLOCK = 32
 VMEM = pl.BlockSpec(memory_space=pltpu.VMEM)
 FAR = pl.BlockSpec(memory_space=pltpu.HBM)
@@ -172,8 +173,10 @@
     a_copy = pltpu.make_async_copy(a_hbm, a_ref, a_sem)
     x_copies = []
     for piece in range(cols // PIECE):
-        own = (slice(None), pl.ds(piece * PIECE, PIECE))
-        x_copies.append(pltpu.make_async_copy(x_hbm.at[own], x_ref.at[own], x_sems.at[piece]))
+        for at in range(0, rows, SPAN):
+            own = (pl.ds(at, SPAN), pl.ds(piece * PIECE, PIECE))
+            sem = x_sems.at[len(x_copies)]
+            x_copies.append(pltpu.make_async_copy(x_hbm.at[own], x_ref.at[own], sem))
     m_copies = [
         pltpu.make_async_copy(m_hbm.at[i], m_ref.at[i], m_sems.at[i]) for i in range(levels)
     ]
@@ -197,16 +200,17 @@
             w_ref[2 * level],
             w_ref[2 * level + 1],
             lambda index: (cosines[own], sines[own]),
-            16,
-            begin // BLOCK,
+            8,
         )
 
     a_copy.wait()
     cosines, sines = rotation(column_of(a_ref[...], cols))
     m_copies[0].wait()
     expand(0)
-    for piece, copy in enumerate(x_copies):
-        copy.wait()
+    each = rows // SPAN
+    for piece in range(cols // PIECE):
+        for copy in x_copies[piece * each : (piece + 1) * each]:
+            copy.wait()
         for begin in range(piece * PIECE, (piece + 1) * PIECE, BLOCK):
             level_on(0, begin)
     for copy in m_copies[1:]:
@@ -245,7 +249,7 @@
             pltpu.VMEM(matrices.shape, x.dtype),
             pltpu.VMEM((2 * levels, 2 * WIDE, 2 * WIDE), x.dtype),
             pltpu.SemaphoreType.DMA,
-            pltpu.SemaphoreType.DMA((cols // PIECE,)),
+            pltpu.SemaphoreType.DMA((cols // PIECE * (rows // SPAN),)),
             pltpu.SemaphoreType.DMA((levels,)),
         ],
         compiler_params=PARAMS,
@@ -280,8 +284,7 @@
                 matrix,
                 swapped,
                 phase_of,
-                16,
-                col,
+                8,
             )
 
 
@@ -322,21 +325,25 @@
 
     shuffle = shuffle_matrix()
     copies = []
+    half = cols // 2
     for piece in range(rows // 16):
-        own = pl.ds(piece * 16, 16)
-        copies.append(pltpu.make_async_copy(o_ref.at[own], o_hbm.at[own], o_sems.at[piece]))
-
-        def store_block(first, second, block):
-            o_ref[block_at(piece, second)] = block
-
-        swap_axes(
-            lambda first, second: state_ref[block_at(first, piece)],
-            store_block,
-            cols // 16,
-            1,
-            shuffle,
-        )
-        copies[-1].start()
+        for side in range(2):
+            own = (pl.ds(piece * 16, 16), pl.ds(side * half, half))
+            copies.append(
+                pltpu.make_async_copy(o_ref.at[own], o_hbm.at[own], o_sems.at[len(copies)])
+            )
+
+            def store_block(first, second, block):
+                o_ref[block_at(piece, side * half // 16 + second)] = block
+
+            swap_axes(
+                lambda first, second: state_ref[block_at(side * half // 16 + first, piece)],
+                store_block,
+                half // 16,
+                1,
+                shuffle,
+            )
+            copies[-1].start()
     for copy in copies:
         copy.wait()
 
@@ -352,7 +359,7 @@
         scratch_shapes=[
             pltpu.VMEM(x.shape, x.dtype),
             pltpu.VMEM(shape, x.dtype),
-            pltpu.SemaphoreType.DMA((rows // 16,)),
+            pltpu.SemaphoreType.DMA((rows // 8,)),
         ],
         compiler_params=PARAMS,
     )(matrices, *angles, x)

time: 77.7 us -> 77.8 us (level)
  no operation moved by 1% of the time
where the time goes in v14:
time: 77.8 us; the launch traced here: 77.5 us
  blocking collectives  30.1 us (39%)
  starting transfers between devices  17.4 us (22%)
  waiting for transfers between devices  16.7 us (21%)
  Pallas kernels  12.4 us (16%)
    all_to_all x1, blocking collectives, traded(): return lax.all_to_all(state, ('src', 'tgt'), 0, 0, tiled=True)  30.1 us
    ppermute x5, waiting for transfers between devices, gathered(): other = lax.ppermute(values, axis, [(i, i ^ apart) for i in range(count)])  15.8 us
    ppermute x5, starting transfers between devices, gathered(): other = lax.ppermute(values, axis, [(i, i ^ apart) for i in range(count)])  10.1 us
    all_to_all x1, starting transfers between devices, traded(): return lax.all_to_all(state, ('src', 'tgt'), 0, 0, tiled=True)  7.3 us
    pallas_call x1, Pallas kernels, source_levels(): pl.pallas_call(source_kernel, out_shape=jax.ShapeDtypeStruct((cols, rows,...  5.63 us
    pallas_call x1, Pallas kernels, target_levels(): pl.pallas_call(target_kernel, out_shape=jax.ShapeDtypeStruct(shape, x.dty...  4.32 us
    pallas_call x1, Pallas kernels, middle_levels(): pl.pallas_call(functools.partial(middle_kernel, levels, rows), out_shape=...  2.43 us
  transfers between devices with their start and end apart: 6, of which 5 were waited for; matrix products, arithmetic and copies ran while one was open for 1% of the time, Pallas kernels for 0%

profile of v14, /device:TPU:0, one launch (start us, length us, event | category | flops | bytes accessed | tf_op | source)
XLA Modules:
  0.0 77.5 jit_solution(13392068027338379571)
XLA Ops:
  0.0 5.6 %shard_map.118 = bf16[128,32,128]{2,1,0:T(8,128)(2,1)} custom-call(f32[1,128]{1,0:T(1,128)} %bitcast.11, bf16[32,128,128]{2,1,0:T(8,128)(2,1)} %x_hbm.1, bf16[5,128,256]{2,1,0:T(8,128)(2,1)} %constant.28.clone.m_hbm.m_ref), custom_call_target="tpu_custom_call" | custom-call | tf_op jit(solution)/shard_map/pallas_call | solution.py:241
  5.6 0.0 copy-start.4
  5.6 0.0 copy-start.5
  5.7 0.0 copy-start.2
  5.7 0.0 copy-start.3
  5.7 7.3 %all-to-all-start = ((bf16[32,128,128]{2,1,0:T(8,128)(2,1)}), bf16[32,128,128]{2,1,0:T(8,128)(2,1)S(1)}, u32[]{:S(2)}, u32[]{:S(2)}) async-start(bf16[32,128,128]{2,1,0:T(8,128)(2,1)} %bitcast.1), calls=%async_computation | async-start | bytes 2097152 | tf_op jit(solution)/shard_map/all_to_all | solution.py:401
  13.0 0.0 copy-start
  13.0 0.0 copy-done.4
  13.0 1.8 %collective-permute-start.3 = (f32[1,32]{1,0:T(1,128)S(1)}, f32[1,32]{1,0:T(1,128)S(1)}, u32[]{:S(2)}, u32[]{:S(2)}) collective-permute-start(f32[1,32]{1,0:T(1,128)S(1)} %bitcast.10), channel_id=1, source_target_pairs={{0,8},{8,0},{16,24},{24,16},{1,9},{9,1},{17,25},{25,17},{2,10},{10... | collective-permute-start | bytes 392 | tf_op jit(solution)/shard_map/ppermute | solution.py:374
  14.9 0.0 copy-done.5
  14.9 0.0 collective-permute-start
  14.9 5.2 %collective-permute-done.3 = f32[1,32]{1,0:T(1,128)S(1)} collective-permute-done((f32[1,32]{1,0:T(1,128)S(1)}, f32[1,32]{1,0:T(1,128)S(1)}, u32[]{:S(2)}, u32[]{:S(2)}) %collective-permute-start.3) | collective-permute-done | bytes 160 | tf_op jit(solution)/shard_map/ppermute | solution.py:374
  20.0 1.5 %collective-permute-start.4 = (f32[2,32]{1,0:T(2,128)S(1)}, f32[2,32]{1,0:T(2,128)S(1)}, u32[]{:S(2)}, u32[]{:S(2)}) collective-permute-start(f32[2,32]{1,0:T(2,128)S(1)} %pad_maximum_fusion.4), channel_id=1, source_target_pairs={{0,16},{8,24},{16,0},{24,8},{1,17},{9,25},{17,1},{25,9},{2,18},{10... | collective-permute-start | bytes 776 | tf_op jit(solution)/shard_map/ppermute | solution.py:374
  21.6 2.2 %collective-permute-done.4 = f32[2,32]{1,0:T(2,128)S(1)} collective-permute-done((f32[2,32]{1,0:T(2,128)S(1)}, f32[2,32]{1,0:T(2,128)S(1)}, u32[]{:S(2)}, u32[]{:S(2)}) %collective-permute-start.4) | collective-permute-done | bytes 288 | tf_op jit(solution)/shard_map/ppermute | solution.py:374
  23.8 0.0 collective-permute-done
  23.8 2.1 %collective-permute-start.1 = (f32[2,128]{1,0:T(2,128)S(1)}, f32[2,128]{1,0:T(2,128)S(1)}, u32[]{:S(2)}, u32[]{:S(2)}) collective-permute-start(f32[2,128]{1,0:T(2,128)S(1)} %pad_maximum_fusion.3), channel_id=1, source_target_pairs={{0,2},{1,3},{2,0},{3,1},{4,6},{5,7},{6,4},{7,5},{8,10},{9,11},{10,... | collective-permute-start | bytes 3080 | tf_op jit(solution)/shard_map/ppermute | solution.py:374
  26.0 4.7 %collective-permute-done.1 = f32[2,128]{1,0:T(2,128)S(1)} collective-permute-done((f32[2,128]{1,0:T(2,128)S(1)}, f32[2,128]{1,0:T(2,128)S(1)}, u32[]{:S(2)}, u32[]{:S(2)}) %collective-permute-start.1) | collective-permute-done | bytes 1056 | tf_op jit(solution)/shard_map/ppermute | solution.py:374
  30.7 4.6 %collective-permute-start.2 = (f32[4,128]{1,0:T(4,128)S(1)}, f32[4,128]{1,0:T(4,128)S(1)}, u32[]{:S(2)}, u32[]{:S(2)}) collective-permute-start(f32[4,128]{1,0:T(4,128)S(1)} %pad_maximum_fusion.1), channel_id=1, source_target_pairs={{0,4},{1,5},{2,6},{3,7},{4,0},{5,1},{6,2},{7,3},{8,12},{9,13},{10,... | collective-permute-start | bytes 6152 | tf_op jit(solution)/shard_map/ppermute | solution.py:374
  35.3 0.0 copy-done.2
  35.3 0.0 copy-done.3
  35.3 0.3 fusion
  35.6 3.7 %collective-permute-done.2 = f32[4,128]{1,0:T(4,128)S(1)} collective-permute-done((f32[4,128]{1,0:T(4,128)S(1)}, f32[4,128]{1,0:T(4,128)S(1)}, u32[]{:S(2)}, u32[]{:S(2)}) %collective-permute-start.2) | collective-permute-done | bytes 2080 | tf_op jit(solution)/shard_map/ppermute | solution.py:374
  39.3 0.1 constant_dynamic-slice_fusion
  39.4 0.1 mul.78
  39.5 0.2 fusion.2
  39.7 0.9 %all-to-all-done.x_ref = bf16[32,128,128]{2,1,0:T(8,128)(2,1)S(1)} async-done(((bf16[32,128,128]{2,1,0:T(8,128)(2,1)}), bf16[32,128,128]{2,1,0:T(8,128)(2,1)S(1)}, u32[]{:S(2)}, u32[]{:S(2)}) %all-to-all-start) | async-done | bytes 1048608 | tf_op jit(solution)/shard_map/all_to_all | solution.py:401
  40.6 0.0 copy-done
  40.6 2.4 %shard_map.119 = bf16[32,128,128]{2,1,0:T(8,128)(2,1)S(1)} custom-call(bf16[32,128,128]{2,1,0:T(8,128)(2,1)S(1)} %all-to-all-done.x_ref, bf16[5,128,256]{2,1,0:T(8,128)(2,1)S(1)} %copy-done, f32[32,128]{1,0:T(8,128)S(1)} %get-tuple-element.24.cs_ref, f32[32,128]{1,0:T(8,128)S(1)} %get-tuple-element.21.ss_ref, f32[4,32,128]{2,1,0:T(8,128)S(1)} %get-tuple-element.14.ct_ref, ...), custom_call_target="tpu_custom_call" | custom-call | tf_op jit(solution)/shard_map/pallas_call | solution.py:293
  43.1 0.0 copy-start.1
  43.1 30.1 %all_to_all.10 = bf16[32,128,128]{2,1,0:T(8,128)(2,1)S(1)} all-to-all(bf16[32,128,128]{2,1,0:T(8,128)(2,1)S(1)} %shard_map.119), channel_id=1, replica_groups=mesh['src'=4,'tgt'=8] {'src','tgt'}, dimensions={0} | all-to-all | bytes 2097152 | tf_op jit(solution)/shard_map/all_to_all | solution.py:401
  73.2 0.0 copy-done.1
  73.2 4.3 %shard_map.120 = bf16[32,128,128]{2,1,0:T(8,128)(2,1)} custom-call(bf16[7,128,256]{2,1,0:T(8,128)(2,1)S(1)} %copy-done.1, f32[32,128]{1,0:T(8,128)S(1)} %get-tuple-element.23.c_ref, f32[32,128]{1,0:T(8,128)S(1)} %get-tuple-element.22.s_ref, bf16[128,32,128]{2,1,0:T(8,128)(2,1)S(1)} %bitcast.9), custom_call_target="tpu_custom_call" | custom-call | tf_op jit(solution)/shard_map/pallas_call | solution.py:354
  (10 shorter events, 0.1 us)
Async XLA Ops:
  5.6 7.4 %copy-start.4 = (f32[32]{0:T(128)S(1)}, f32[32]{0:T(128)}, u32[]{:S(2)}) copy-start(f32[32]{0:T(128)} %param.14) | copy-start | bytes 388
  5.6 9.2 %copy-start.5 = (f32[128]{0:T(128)S(1)}, f32[128]{0:T(128)}, u32[]{:S(2)}) copy-start(f32[128]{0:T(128)} %param.13) | copy-start | bytes 1540
  5.7 29.6 %copy-start.2 = (f32[128]{0:T(128)S(1)}, f32[128]{0:T(128)}, u32[]{:S(2)}) copy-start(f32[128]{0:T(128)} %constant.30.clone) | copy-start | bytes 1540
  5.7 29.6 %copy-start.3 = (f32[128]{0:T(128)S(1)}, f32[128]{0:T(128)}, u32[]{:S(2)}) copy-start(f32[128]{0:T(128)} %constant.29.clone) | copy-start | bytes 1540
  5.7 34.9 %all-to-all-start = ((bf16[32,128,128]{2,1,0:T(8,128)(2,1)}), bf16[32,128,128]{2,1,0:T(8,128)(2,1)S(1)}, u32[]{:S(2)}, u32[]{:S(2)}) async-start(bf16[32,128,128]{2,1,0:T(8,128)(2,1)} %bitcast.1), calls=%async_computation | async-start | bytes 2097152 | tf_op jit(solution)/shard_map/all_to_all | solution.py:401
  13.0 27.6 %copy-start = (bf16[5,128,256]{2,1,0:T(8,128)(2,1)S(1)}, bf16[5,128,256]{2,1,0:T(8,128)(2,1)}, u32[]{:S(2)}) copy-start(bf16[5,128,256]{2,1,0:T(8,128)(2,1)} %constant.28.clone.m_hbm.m_ref) | copy-start | bytes 983044
  13.0 7.0 %collective-permute-start.3 = (f32[1,32]{1,0:T(1,128)S(1)}, f32[1,32]{1,0:T(1,128)S(1)}, u32[]{:S(2)}, u32[]{:S(2)}) collective-permute-start(f32[1,32]{1,0:T(1,128)S(1)} %bitcast.10), channel_id=1, source_target_pairs={{0,8},{8,0},{16,24},{24,16},{1,9},{9,1},{17,25},{25,17},{2,10},{10... | collective-permute-start | bytes 392 | tf_op jit(solution)/shard_map/ppermute | solution.py:374
  14.9 8.9 %collective-permute-start = (f32[1,128]{1,0:T(1,128)S(1)}, f32[1,128]{1,0:T(1,128)S(1)}, u32[]{:S(2)}, u32[]{:S(2)}) collective-permute-start(f32[1,128]{1,0:T(1,128)S(1)} %bitcast.12), channel_id=1, source_target_pairs={{0,1},{1,0},{2,3},{3,2},{4,5},{5,4},{6,7},{7,6},{8,9},{9,8},{10,11... | collective-permute-start | bytes 1544 | tf_op jit(solution)/shard_map/ppermute | solution.py:374
  20.0 3.7 %collective-permute-start.4 = (f32[2,32]{1,0:T(2,128)S(1)}, f32[2,32]{1,0:T(2,128)S(1)}, u32[]{:S(2)}, u32[]{:S(2)}) collective-permute-start(f32[2,32]{1,0:T(2,128)S(1)} %pad_maximum_fusion.4), channel_id=1, source_target_pairs={{0,16},{8,24},{16,0},{24,8},{1,17},{9,25},{17,1},{25,9},{2,18},{10... | collective-permute-start | bytes 776 | tf_op jit(solution)/shard_map/ppermute | solution.py:374
  23.8 6.9 %collective-permute-start.1 = (f32[2,128]{1,0:T(2,128)S(1)}, f32[2,128]{1,0:T(2,128)S(1)}, u32[]{:S(2)}, u32[]{:S(2)}) collective-permute-start(f32[2,128]{1,0:T(2,128)S(1)} %pad_maximum_fusion.3), channel_id=1, source_target_pairs={{0,2},{1,3},{2,0},{3,1},{4,6},{5,7},{6,4},{7,5},{8,10},{9,11},{10,... | collective-permute-start | bytes 3080 | tf_op jit(solution)/shard_map/ppermute | solution.py:374
  30.7 8.6 %collective-permute-start.2 = (f32[4,128]{1,0:T(4,128)S(1)}, f32[4,128]{1,0:T(4,128)S(1)}, u32[]{:S(2)}, u32[]{:S(2)}) collective-permute-start(f32[4,128]{1,0:T(4,128)S(1)} %pad_maximum_fusion.1), channel_id=1, source_target_pairs={{0,4},{1,5},{2,6},{3,7},{4,0},{5,1},{6,2},{7,3},{8,12},{9,13},{10,... | collective-permute-start | bytes 6152 | tf_op jit(solution)/shard_map/ppermute | solution.py:374
  43.1 30.1 %copy-start.1 = (bf16[7,128,256]{2,1,0:T(8,128)(2,1)S(1)}, bf16[7,128,256]{2,1,0:T(8,128)(2,1)}, u32[]{:S(2)}) copy-start(bf16[7,128,256]{2,1,0:T(8,128)(2,1)} %constant.31.clone.m_ref) | copy-start | bytes 1376260

commit v15 on v14

--- a/solution.py
+++ b/solution.py
@@ -80,6 +80,10 @@
     return first, second
 
 
+def halved(table):
+    return tuple(part.astype(jnp.bfloat16) for part in table)
+
+
 def node_row():
     lanes = lax.broadcasted_iota(jnp.int32, (1, WIDE), 1) % HALF
     points = [math.cos((2 * a + 1) * math.pi / 16) ** 2 for a in range(4)]
@@ -128,9 +132,10 @@
         right = jnp.concatenate([load(i + apart) for i in picked], axis=0)
         rows = left.shape[0] // len(picked)
         pair = jnp.concatenate([left, right], axis=1)
-        both = jnp.dot(pair, matrix, preferred_element_type=jnp.float32)
+        both = jnp.dot(pair, matrix, preferred_element_type=jnp.float32).astype(jnp.bfloat16)
         if turn % 2 == 0:
             other = jnp.dot(pair, swapped, preferred_element_type=jnp.float32)
+            other = other.astype(jnp.bfloat16)
         for place, low in enumerate(picked):
             for child in range(2):
                 index = low + child * apart
@@ -138,8 +143,11 @@
                 mine = slice(place * rows, (place + 1) * rows)
                 own = slice(child * WIDE, (child + 1) * WIDE)
                 value = both[mine, own]
-                turned = other[mine, own] if turn % 2 == 0 else pltpu.roll(value, HALF, 1)
-                store(index, (value * cosine + turned * sine).astype(jnp.bfloat16))
+                if turn % 2 == 0:
+                    turned = other[mine, own]
+                else:
+                    turned = jnp.concatenate([value[:, HALF:], value[:, :HALF]], axis=1)
+                store(index, value * cosine + turned * sine)
         turn += 1
 
 
@@ -203,14 +211,15 @@
             8,
         )
 
-    a_copy.wait()
-    cosines, sines = rotation(column_of(a_ref[...], cols))
     m_copies[0].wait()
-    expand(0)
     each = rows // SPAN
     for piece in range(cols // PIECE):
         for copy in x_copies[piece * each : (piece + 1) * each]:
             copy.wait()
+        if piece == 0:
+            a_copy.wait()
+            expand(0)
+            cosines, sines = halved(rotation(column_of(a_ref[...], cols)))
         for begin in range(piece * PIECE, (piece + 1) * PIECE, BLOCK):
             level_on(0, begin)
     for copy in m_copies[1:]:
@@ -269,9 +278,10 @@
             def phase_of(index):
                 if by_source:
                     at = index % tgt_count * run + col
-                    return cs_ref[at : at + 1, :], ss_ref[at : at + 1, :]
+                    row = (cs_ref[at : at + 1, :], ss_ref[at : at + 1, :])
+                    return halved(jnp.broadcast_to(part, (rows, WIDE)) for part in row)
                 at = index // tgt_count
-                return ct_ref[at], st_ref[at]
+                return halved((ct_ref[at], st_ref[at]))
 
             def store(index, value):
                 o_ref[index, own, :] = value
@@ -308,7 +318,7 @@
         weights = whole_matrix(m_ref[level])
         for start in range(0, rows, 16):
             own = slice(start, start + 16)
-            cosine, sine = c_ref[own, :], s_ref[own, :]
+            cosine, sine = halved((c_ref[own, :], s_ref[own, :]))
 
             def store(index, value):
                 state_ref[index, own, :] = value

time: 77.8 us -> 77.5 us (level)
  no operation moved by 1% of the time
where the time goes in v15:
time: 77.5 us; the launch traced here: 77.3 us
  blocking collectives  30.1 us (39%)
  starting transfers between devices  17.4 us (22%)
  waiting for transfers between devices  16.7 us (22%)
  Pallas kernels  12.2 us (16%)
    all_to_all x1, blocking collectives, traded(): return lax.all_to_all(state, ('src', 'tgt'), 0, 0, tiled=True)  30.1 us
    ppermute x5, waiting for transfers between devices, gathered(): other = lax.ppermute(values, axis, [(i, i ^ apart) for i in range(count)])  15.8 us
    ppermute x5, starting transfers between devices, gathered(): other = lax.ppermute(values, axis, [(i, i ^ apart) for i in range(count)])  10.1 us
    all_to_all x1, starting transfers between devices, traded(): return lax.all_to_all(state, ('src', 'tgt'), 0, 0, tiled=True)  7.31 us
    pallas_call x1, Pallas kernels, source_levels(): pl.pallas_call(source_kernel, out_shape=jax.ShapeDtypeStruct((cols, rows,...  5.41 us
    pallas_call x1, Pallas kernels, target_levels(): pl.pallas_call(target_kernel, out_shape=jax.ShapeDtypeStruct(shape, x.dty...  4.29 us
    pallas_call x1, Pallas kernels, middle_levels(): pl.pallas_call(functools.partial(middle_kernel, levels, rows), out_shape=...  2.47 us
  transfers between devices with their start and end apart: 6, of which 5 were waited for; matrix products, arithmetic and copies ran while one was open for 1% of the time, Pallas kernels for 0%

profile of v15, /device:TPU:0, one launch (start us, length us, event | category | flops | bytes accessed | tf_op | source)
XLA Modules:
  0.0 77.3 jit_solution(7424567362143299100)
XLA Ops:
  0.0 5.4 %shard_map.118 = bf16[128,32,128]{2,1,0:T(8,128)(2,1)} custom-call(f32[1,128]{1,0:T(1,128)} %bitcast.11, bf16[32,128,128]{2,1,0:T(8,128)(2,1)} %x_hbm.1, bf16[5,128,256]{2,1,0:T(8,128)(2,1)} %constant.28.clone.m_hbm.m_ref), custom_call_target="tpu_custom_call" | custom-call | tf_op jit(solution)/shard_map/pallas_call | solution.py:250
  5.4 0.0 copy-start.4
  5.4 0.0 copy-start.5
  5.4 0.0 copy-start.2
  5.5 0.0 copy-start.3
  5.5 7.3 %all-to-all-start = ((bf16[32,128,128]{2,1,0:T(8,128)(2,1)}), bf16[32,128,128]{2,1,0:T(8,128)(2,1)S(1)}, u32[]{:S(2)}, u32[]{:S(2)}) async-start(bf16[32,128,128]{2,1,0:T(8,128)(2,1)} %bitcast.1), calls=%async_computation | async-start | bytes 2097152 | tf_op jit(solution)/shard_map/all_to_all | solution.py:411
  12.8 0.0 copy-start
  12.8 0.0 copy-done.4
  12.8 1.8 %collective-permute-start.3 = (f32[1,32]{1,0:T(1,128)S(1)}, f32[1,32]{1,0:T(1,128)S(1)}, u32[]{:S(2)}, u32[]{:S(2)}) collective-permute-start(f32[1,32]{1,0:T(1,128)S(1)} %bitcast.10), channel_id=1, source_target_pairs={{0,8},{8,0},{16,24},{24,16},{1,9},{9,1},{17,25},{25,17},{2,10},{10... | collective-permute-start | bytes 392 | tf_op jit(solution)/shard_map/ppermute | solution.py:384
  14.6 0.0 copy-done.5
  14.6 0.0 collective-permute-start
  14.7 5.2 %collective-permute-done.3 = f32[1,32]{1,0:T(1,128)S(1)} collective-permute-done((f32[1,32]{1,0:T(1,128)S(1)}, f32[1,32]{1,0:T(1,128)S(1)}, u32[]{:S(2)}, u32[]{:S(2)}) %collective-permute-start.3) | collective-permute-done | bytes 160 | tf_op jit(solution)/shard_map/ppermute | solution.py:384
  19.8 1.5 %collective-permute-start.4 = (f32[2,32]{1,0:T(2,128)S(1)}, f32[2,32]{1,0:T(2,128)S(1)}, u32[]{:S(2)}, u32[]{:S(2)}) collective-permute-start(f32[2,32]{1,0:T(2,128)S(1)} %pad_maximum_fusion.4), channel_id=1, source_target_pairs={{0,16},{8,24},{16,0},{24,8},{1,17},{9,25},{17,1},{25,9},{2,18},{10... | collective-permute-start | bytes 776 | tf_op jit(solution)/shard_map/ppermute | solution.py:384
  21.4 2.2 %collective-permute-done.4 = f32[2,32]{1,0:T(2,128)S(1)} collective-permute-done((f32[2,32]{1,0:T(2,128)S(1)}, f32[2,32]{1,0:T(2,128)S(1)}, u32[]{:S(2)}, u32[]{:S(2)}) %collective-permute-start.4) | collective-permute-done | bytes 288 | tf_op jit(solution)/shard_map/ppermute | solution.py:384
  23.6 0.0 collective-permute-done
  23.6 2.1 %collective-permute-start.1 = (f32[2,128]{1,0:T(2,128)S(1)}, f32[2,128]{1,0:T(2,128)S(1)}, u32[]{:S(2)}, u32[]{:S(2)}) collective-permute-start(f32[2,128]{1,0:T(2,128)S(1)} %pad_maximum_fusion.3), channel_id=1, source_target_pairs={{0,2},{1,3},{2,0},{3,1},{4,6},{5,7},{6,4},{7,5},{8,10},{9,11},{10,... | collective-permute-start | bytes 3080 | tf_op jit(solution)/shard_map/ppermute | solution.py:384
  25.8 4.7 %collective-permute-done.1 = f32[2,128]{1,0:T(2,128)S(1)} collective-permute-done((f32[2,128]{1,0:T(2,128)S(1)}, f32[2,128]{1,0:T(2,128)S(1)}, u32[]{:S(2)}, u32[]{:S(2)}) %collective-permute-start.1) | collective-permute-done | bytes 1056 | tf_op jit(solution)/shard_map/ppermute | solution.py:384
  30.5 4.6 %collective-permute-start.2 = (f32[4,128]{1,0:T(4,128)S(1)}, f32[4,128]{1,0:T(4,128)S(1)}, u32[]{:S(2)}, u32[]{:S(2)}) collective-permute-start(f32[4,128]{1,0:T(4,128)S(1)} %pad_maximum_fusion.1), channel_id=1, source_target_pairs={{0,4},{1,5},{2,6},{3,7},{4,0},{5,1},{6,2},{7,3},{8,12},{9,13},{10,... | collective-permute-start | bytes 6152 | tf_op jit(solution)/shard_map/ppermute | solution.py:384
  35.1 0.0 copy-done.2
  35.1 0.0 copy-done.3
  35.1 0.3 fusion
  35.4 3.7 %collective-permute-done.2 = f32[4,128]{1,0:T(4,128)S(1)} collective-permute-done((f32[4,128]{1,0:T(4,128)S(1)}, f32[4,128]{1,0:T(4,128)S(1)}, u32[]{:S(2)}, u32[]{:S(2)}) %collective-permute-start.2) | collective-permute-done | bytes 2080 | tf_op jit(solution)/shard_map/ppermute | solution.py:384
  39.1 0.1 constant_dynamic-slice_fusion
  39.2 0.1 mul.78
  39.3 0.2 fusion.2
  39.5 0.9 %all-to-all-done.x_ref = bf16[32,128,128]{2,1,0:T(8,128)(2,1)S(1)} async-done(((bf16[32,128,128]{2,1,0:T(8,128)(2,1)}), bf16[32,128,128]{2,1,0:T(8,128)(2,1)S(1)}, u32[]{:S(2)}, u32[]{:S(2)}) %all-to-all-start) | async-done | bytes 1048608 | tf_op jit(solution)/shard_map/all_to_all | solution.py:411
  40.4 0.0 copy-done
  40.4 2.5 %shard_map.119 = bf16[32,128,128]{2,1,0:T(8,128)(2,1)S(1)} custom-call(bf16[32,128,128]{2,1,0:T(8,128)(2,1)S(1)} %all-to-all-done.x_ref, bf16[5,128,256]{2,1,0:T(8,128)(2,1)S(1)} %copy-done, f32[32,128]{1,0:T(8,128)S(1)} %get-tuple-element.24.cs_ref, f32[32,128]{1,0:T(8,128)S(1)} %get-tuple-element.21.ss_ref, f32[4,32,128]{2,1,0:T(8,128)S(1)} %get-tuple-element.14.ct_ref, ...), custom_call_target="tpu_custom_call" | custom-call | tf_op jit(solution)/shard_map/pallas_call | solution.py:303
  42.9 0.0 copy-start.1
  42.9 30.1 %all_to_all.10 = bf16[32,128,128]{2,1,0:T(8,128)(2,1)S(1)} all-to-all(bf16[32,128,128]{2,1,0:T(8,128)(2,1)S(1)} %shard_map.119), channel_id=1, replica_groups=mesh['src'=4,'tgt'=8] {'src','tgt'}, dimensions={0} | all-to-all | bytes 2097152 | tf_op jit(solution)/shard_map/all_to_all | solution.py:411
  73.0 0.0 copy-done.1
  73.0 4.3 %shard_map.120 = bf16[32,128,128]{2,1,0:T(8,128)(2,1)} custom-call(bf16[7,128,256]{2,1,0:T(8,128)(2,1)S(1)} %copy-done.1, f32[32,128]{1,0:T(8,128)S(1)} %get-tuple-element.23.c_ref, f32[32,128]{1,0:T(8,128)S(1)} %get-tuple-element.22.s_ref, bf16[128,32,128]{2,1,0:T(8,128)(2,1)S(1)} %bitcast.9), custom_call_target="tpu_custom_call" | custom-call | tf_op jit(solution)/shard_map/pallas_call | solution.py:364
  (10 shorter events, 0.1 us)
Async XLA Ops:
  5.4 7.4 %copy-start.4 = (f32[32]{0:T(128)S(1)}, f32[32]{0:T(128)}, u32[]{:S(2)}) copy-start(f32[32]{0:T(128)} %param.14) | copy-start | bytes 388
  5.4 9.2 %copy-start.5 = (f32[128]{0:T(128)S(1)}, f32[128]{0:T(128)}, u32[]{:S(2)}) copy-start(f32[128]{0:T(128)} %param.13) | copy-start | bytes 1540
  5.4 29.6 %copy-start.2 = (f32[128]{0:T(128)S(1)}, f32[128]{0:T(128)}, u32[]{:S(2)}) copy-start(f32[128]{0:T(128)} %constant.30.clone) | copy-start | bytes 1540
  5.5 29.6 %copy-start.3 = (f32[128]{0:T(128)S(1)}, f32[128]{0:T(128)}, u32[]{:S(2)}) copy-start(f32[128]{0:T(128)} %constant.29.clone) | copy-start | bytes 1540
  5.5 34.9 %all-to-all-start = ((bf16[32,128,128]{2,1,0:T(8,128)(2,1)}), bf16[32,128,128]{2,1,0:T(8,128)(2,1)S(1)}, u32[]{:S(2)}, u32[]{:S(2)}) async-start(bf16[32,128,128]{2,1,0:T(8,128)(2,1)} %bitcast.1), calls=%async_computation | async-start | bytes 2097152 | tf_op jit(solution)/shard_map/all_to_all | solution.py:411
  12.8 27.6 %copy-start = (bf16[5,128,256]{2,1,0:T(8,128)(2,1)S(1)}, bf16[5,128,256]{2,1,0:T(8,128)(2,1)}, u32[]{:S(2)}) copy-start(bf16[5,128,256]{2,1,0:T(8,128)(2,1)} %constant.28.clone.m_hbm.m_ref) | copy-start | bytes 983044
  12.8 7.0 %collective-permute-start.3 = (f32[1,32]{1,0:T(1,128)S(1)}, f32[1,32]{1,0:T(1,128)S(1)}, u32[]{:S(2)}, u32[]{:S(2)}) collective-permute-start(f32[1,32]{1,0:T(1,128)S(1)} %bitcast.10), channel_id=1, source_target_pairs={{0,8},{8,0},{16,24},{24,16},{1,9},{9,1},{17,25},{25,17},{2,10},{10... | collective-permute-start | bytes 392 | tf_op jit(solution)/shard_map/ppermute | solution.py:384
  14.6 8.9 %collective-permute-start = (f32[1,128]{1,0:T(1,128)S(1)}, f32[1,128]{1,0:T(1,128)S(1)}, u32[]{:S(2)}, u32[]{:S(2)}) collective-permute-start(f32[1,128]{1,0:T(1,128)S(1)} %bitcast.12), channel_id=1, source_target_pairs={{0,1},{1,0},{2,3},{3,2},{4,5},{5,4},{6,7},{7,6},{8,9},{9,8},{10,11... | collective-permute-start | bytes 1544 | tf_op jit(solution)/shard_map/ppermute | solution.py:384
  19.8 3.7 %collective-permute-start.4 = (f32[2,32]{1,0:T(2,128)S(1)}, f32[2,32]{1,0:T(2,128)S(1)}, u32[]{:S(2)}, u32[]{:S(2)}) collective-permute-start(f32[2,32]{1,0:T(2,128)S(1)} %pad_maximum_fusion.4), channel_id=1, source_target_pairs={{0,16},{8,24},{16,0},{24,8},{1,17},{9,25},{17,1},{25,9},{2,18},{10... | collective-permute-start | bytes 776 | tf_op jit(solution)/shard_map/ppermute | solution.py:384
  23.6 6.9 %collective-permute-start.1 = (f32[2,128]{1,0:T(2,128)S(1)}, f32[2,128]{1,0:T(2,128)S(1)}, u32[]{:S(2)}, u32[]{:S(2)}) collective-permute-start(f32[2,128]{1,0:T(2,128)S(1)} %pad_maximum_fusion.3), channel_id=1, source_target_pairs={{0,2},{1,3},{2,0},{3,1},{4,6},{5,7},{6,4},{7,5},{8,10},{9,11},{10,... | collective-permute-start | bytes 3080 | tf_op jit(solution)/shard_map/ppermute | solution.py:384
  30.5 8.6 %collective-permute-start.2 = (f32[4,128]{1,0:T(4,128)S(1)}, f32[4,128]{1,0:T(4,128)S(1)}, u32[]{:S(2)}, u32[]{:S(2)}) collective-permute-start(f32[4,128]{1,0:T(4,128)S(1)} %pad_maximum_fusion.1), channel_id=1, source_target_pairs={{0,4},{1,5},{2,6},{3,7},{4,0},{5,1},{6,2},{7,3},{8,12},{9,13},{10,... | collective-permute-start | bytes 6152 | tf_op jit(solution)/shard_map/ppermute | solution.py:384
  42.9 30.1 %copy-start.1 = (bf16[7,128,256]{2,1,0:T(8,128)(2,1)S(1)}, bf16[7,128,256]{2,1,0:T(8,128)(2,1)}, u32[]{:S(2)}) copy-start(bf16[7,128,256]{2,1,0:T(8,128)(2,1)} %constant.31.clone.m_ref) | copy-start | bytes 1376260

commit v16 on v15

--- a/solution.py
+++ b/solution.py
@@ -133,7 +133,7 @@
         rows = left.shape[0] // len(picked)
         pair = jnp.concatenate([left, right], axis=1)
         both = jnp.dot(pair, matrix, preferred_element_type=jnp.float32).astype(jnp.bfloat16)
-        if turn % 2 == 0:
+        if turn % 4 == 0:
             other = jnp.dot(pair, swapped, preferred_element_type=jnp.float32)
             other = other.astype(jnp.bfloat16)
         for place, low in enumerate(picked):
@@ -143,7 +143,7 @@
                 mine = slice(place * rows, (place + 1) * rows)
                 own = slice(child * WIDE, (child + 1) * WIDE)
                 value = both[mine, own]
-                if turn % 2 == 0:
+                if turn % 4 == 0:
                     turned = other[mine, own]
                 else:
                     turned = jnp.concatenate([value[:, HALF:], value[:, :HALF]], axis=1)
@@ -209,6 +209,7 @@
             w_ref[2 * level + 1],
             lambda index: (cosines[own], sines[own]),
             8,
+            begin // BLOCK * 2,
         )
 
     m_copies[0].wait()
@@ -295,6 +296,7 @@
                 swapped,
                 phase_of,
                 8,
+                col * 2,
             )
 
 
@@ -330,7 +332,7 @@
                 1 << (levels - 1 - level),
                 *weights,
                 lambda index: (cosine, sine),
-                32,
+                16,
             )
 
     shuffle = shuffle_matrix()

time: 77.5 us -> 76.8 us (level)
  no operation moved by 1% of the time
where the time goes in v16:
time: 76.8 us; the launch traced here: 76.6 us
  blocking collectives  30.1 us (39%)
  starting transfers between devices  17.4 us (23%)
  waiting for transfers between devices  16.7 us (22%)
  Pallas kernels  11.5 us (15%)
    all_to_all x1, blocking collectives, traded(): return lax.all_to_all(state, ('src', 'tgt'), 0, 0, tiled=True)  30.1 us
    ppermute x5, waiting for transfers between devices, gathered(): other = lax.ppermute(values, axis, [(i, i ^ apart) for i in range(count)])  15.8 us
    ppermute x5, starting transfers between devices, gathered(): other = lax.ppermute(values, axis, [(i, i ^ apart) for i in range(count)])  10.1 us
    all_to_all x1, starting transfers between devices, traded(): return lax.all_to_all(state, ('src', 'tgt'), 0, 0, tiled=True)  7.31 us
    pallas_call x1, Pallas kernels, source_levels(): pl.pallas_call(source_kernel, out_shape=jax.ShapeDtypeStruct((cols, rows,...  5.25 us
    pallas_call x1, Pallas kernels, target_levels(): pl.pallas_call(target_kernel, out_shape=jax.ShapeDtypeStruct(shape, x.dty...  4 us
    pallas_call x1, Pallas kernels, middle_levels(): pl.pallas_call(functools.partial(middle_kernel, levels, rows), out_shape=...  2.22 us
  transfers between devices with their start and end apart: 6, of which 5 were waited for; matrix products, arithmetic and copies ran while one was open for 1% of the time, Pallas kernels for 0%

profile of v16, /device:TPU:0, one launch (start us, length us, event | category | flops | bytes accessed | tf_op | source)
XLA Modules:
  0.0 76.6 jit_solution(3603971492593187480)
XLA Ops:
  0.0 5.3 %shard_map.118 = bf16[128,32,128]{2,1,0:T(8,128)(2,1)} custom-call(f32[1,128]{1,0:T(1,128)} %bitcast.11, bf16[32,128,128]{2,1,0:T(8,128)(2,1)} %x_hbm.1, bf16[5,128,256]{2,1,0:T(8,128)(2,1)} %constant.28.clone.m_hbm.m_ref), custom_call_target="tpu_custom_call" | custom-call | tf_op jit(solution)/shard_map/pallas_call | solution.py:251
  5.3 0.0 copy-start.4
  5.3 0.0 copy-start.5
  5.3 0.0 copy-start.2
  5.3 0.0 copy-start.3
  5.3 7.3 %all-to-all-start = ((bf16[32,128,128]{2,1,0:T(8,128)(2,1)}), bf16[32,128,128]{2,1,0:T(8,128)(2,1)S(1)}, u32[]{:S(2)}, u32[]{:S(2)}) async-start(bf16[32,128,128]{2,1,0:T(8,128)(2,1)} %bitcast.1), calls=%async_computation | async-start | bytes 2097152 | tf_op jit(solution)/shard_map/all_to_all | solution.py:413
  12.6 0.0 copy-start
  12.6 0.0 copy-done.4
  12.6 1.8 %collective-permute-start.3 = (f32[1,32]{1,0:T(1,128)S(1)}, f32[1,32]{1,0:T(1,128)S(1)}, u32[]{:S(2)}, u32[]{:S(2)}) collective-permute-start(f32[1,32]{1,0:T(1,128)S(1)} %bitcast.10), channel_id=1, source_target_pairs={{0,8},{8,0},{16,24},{24,16},{1,9},{9,1},{17,25},{25,17},{2,10},{10... | collective-permute-start | bytes 392 | tf_op jit(solution)/shard_map/ppermute | solution.py:386
  14.5 0.0 copy-done.5
  14.5 0.0 collective-permute-start
  14.5 5.2 %collective-permute-done.3 = f32[1,32]{1,0:T(1,128)S(1)} collective-permute-done((f32[1,32]{1,0:T(1,128)S(1)}, f32[1,32]{1,0:T(1,128)S(1)}, u32[]{:S(2)}, u32[]{:S(2)}) %collective-permute-start.3) | collective-permute-done | bytes 160 | tf_op jit(solution)/shard_map/ppermute | solution.py:386
  19.7 1.5 %collective-permute-start.4 = (f32[2,32]{1,0:T(2,128)S(1)}, f32[2,32]{1,0:T(2,128)S(1)}, u32[]{:S(2)}, u32[]{:S(2)}) collective-permute-start(f32[2,32]{1,0:T(2,128)S(1)} %pad_maximum_fusion.4), channel_id=1, source_target_pairs={{0,16},{8,24},{16,0},{24,8},{1,17},{9,25},{17,1},{25,9},{2,18},{10... | collective-permute-start | bytes 776 | tf_op jit(solution)/shard_map/ppermute | solution.py:386
  21.2 2.2 %collective-permute-done.4 = f32[2,32]{1,0:T(2,128)S(1)} collective-permute-done((f32[2,32]{1,0:T(2,128)S(1)}, f32[2,32]{1,0:T(2,128)S(1)}, u32[]{:S(2)}, u32[]{:S(2)}) %collective-permute-start.4) | collective-permute-done | bytes 288 | tf_op jit(solution)/shard_map/ppermute | solution.py:386
  23.4 0.0 collective-permute-done
  23.5 2.1 %collective-permute-start.1 = (f32[2,128]{1,0:T(2,128)S(1)}, f32[2,128]{1,0:T(2,128)S(1)}, u32[]{:S(2)}, u32[]{:S(2)}) collective-permute-start(f32[2,128]{1,0:T(2,128)S(1)} %pad_maximum_fusion.3), channel_id=1, source_target_pairs={{0,2},{1,3},{2,0},{3,1},{4,6},{5,7},{6,4},{7,5},{8,10},{9,11},{10,... | collective-permute-start | bytes 3080 | tf_op jit(solution)/shard_map/ppermute | solution.py:386
  25.6 4.7 %collective-permute-done.1 = f32[2,128]{1,0:T(2,128)S(1)} collective-permute-done((f32[2,128]{1,0:T(2,128)S(1)}, f32[2,128]{1,0:T(2,128)S(1)}, u32[]{:S(2)}, u32[]{:S(2)}) %collective-permute-start.1) | collective-permute-done | bytes 1056 | tf_op jit(solution)/shard_map/ppermute | solution.py:386
  30.4 4.6 %collective-permute-start.2 = (f32[4,128]{1,0:T(4,128)S(1)}, f32[4,128]{1,0:T(4,128)S(1)}, u32[]{:S(2)}, u32[]{:S(2)}) collective-permute-start(f32[4,128]{1,0:T(4,128)S(1)} %pad_maximum_fusion.1), channel_id=1, source_target_pairs={{0,4},{1,5},{2,6},{3,7},{4,0},{5,1},{6,2},{7,3},{8,12},{9,13},{10,... | collective-permute-start | bytes 6152 | tf_op jit(solution)/shard_map/ppermute | solution.py:386
  34.9 0.0 copy-done.2
  34.9 0.0 copy-done.3
  34.9 0.3 fusion
  35.2 3.7 %collective-permute-done.2 = f32[4,128]{1,0:T(4,128)S(1)} collective-permute-done((f32[4,128]{1,0:T(4,128)S(1)}, f32[4,128]{1,0:T(4,128)S(1)}, u32[]{:S(2)}, u32[]{:S(2)}) %collective-permute-start.2) | collective-permute-done | bytes 2080 | tf_op jit(solution)/shard_map/ppermute | solution.py:386
  39.0 0.1 constant_dynamic-slice_fusion
  39.1 0.1 mul.78
  39.1 0.2 fusion.2
  39.3 0.9 %all-to-all-done.x_ref = bf16[32,128,128]{2,1,0:T(8,128)(2,1)S(1)} async-done(((bf16[32,128,128]{2,1,0:T(8,128)(2,1)}), bf16[32,128,128]{2,1,0:T(8,128)(2,1)S(1)}, u32[]{:S(2)}, u32[]{:S(2)}) %all-to-all-start) | async-done | bytes 1048608 | tf_op jit(solution)/shard_map/all_to_all | solution.py:413
  40.3 0.0 copy-done
  40.3 2.2 %shard_map.119 = bf16[32,128,128]{2,1,0:T(8,128)(2,1)S(1)} custom-call(bf16[32,128,128]{2,1,0:T(8,128)(2,1)S(1)} %all-to-all-done.x_ref, bf16[5,128,256]{2,1,0:T(8,128)(2,1)S(1)} %copy-done, f32[32,128]{1,0:T(8,128)S(1)} %get-tuple-element.24.cs_ref, f32[32,128]{1,0:T(8,128)S(1)} %get-tuple-element.21.ss_ref, f32[4,32,128]{2,1,0:T(8,128)S(1)} %get-tuple-element.14.ct_ref, ...), custom_call_target="tpu_custom_call" | custom-call | tf_op jit(solution)/shard_map/pallas_call | solution.py:305
  42.5 0.0 copy-start.1
  42.5 30.1 %all_to_all.10 = bf16[32,128,128]{2,1,0:T(8,128)(2,1)S(1)} all-to-all(bf16[32,128,128]{2,1,0:T(8,128)(2,1)S(1)} %shard_map.119), channel_id=1, replica_groups=mesh['src'=4,'tgt'=8] {'src','tgt'}, dimensions={0} | all-to-all | bytes 2097152 | tf_op jit(solution)/shard_map/all_to_all | solution.py:413
  72.6 0.0 copy-done.1
  72.6 4.0 %shard_map.120 = bf16[32,128,128]{2,1,0:T(8,128)(2,1)} custom-call(bf16[7,128,256]{2,1,0:T(8,128)(2,1)S(1)} %copy-done.1, f32[32,128]{1,0:T(8,128)S(1)} %get-tuple-element.23.c_ref, f32[32,128]{1,0:T(8,128)S(1)} %get-tuple-element.22.s_ref, bf16[128,32,128]{2,1,0:T(8,128)(2,1)S(1)} %bitcast.9), custom_call_target="tpu_custom_call" | custom-call | tf_op jit(solution)/shard_map/pallas_call | solution.py:366
  (10 shorter events, 0.1 us)
Async XLA Ops:
  5.3 7.4 %copy-start.4 = (f32[32]{0:T(128)S(1)}, f32[32]{0:T(128)}, u32[]{:S(2)}) copy-start(f32[32]{0:T(128)} %param.14) | copy-start | bytes 388
  5.3 9.2 %copy-start.5 = (f32[128]{0:T(128)S(1)}, f32[128]{0:T(128)}, u32[]{:S(2)}) copy-start(f32[128]{0:T(128)} %param.13) | copy-start | bytes 1540
  5.3 29.6 %copy-start.2 = (f32[128]{0:T(128)S(1)}, f32[128]{0:T(128)}, u32[]{:S(2)}) copy-start(f32[128]{0:T(128)} %constant.30.clone) | copy-start | bytes 1540
  5.3 29.6 %copy-start.3 = (f32[128]{0:T(128)S(1)}, f32[128]{0:T(128)}, u32[]{:S(2)}) copy-start(f32[128]{0:T(128)} %constant.29.clone) | copy-start | bytes 1540
  5.3 34.9 %all-to-all-start = ((bf16[32,128,128]{2,1,0:T(8,128)(2,1)}), bf16[32,128,128]{2,1,0:T(8,128)(2,1)S(1)}, u32[]{:S(2)}, u32[]{:S(2)}) async-start(bf16[32,128,128]{2,1,0:T(8,128)(2,1)} %bitcast.1), calls=%async_computation | async-start | bytes 2097152 | tf_op jit(solution)/shard_map/all_to_all | solution.py:413
  12.6 27.6 %copy-start = (bf16[5,128,256]{2,1,0:T(8,128)(2,1)S(1)}, bf16[5,128,256]{2,1,0:T(8,128)(2,1)}, u32[]{:S(2)}) copy-start(bf16[5,128,256]{2,1,0:T(8,128)(2,1)} %constant.28.clone.m_hbm.m_ref) | copy-start | bytes 983044
  12.6 7.0 %collective-permute-start.3 = (f32[1,32]{1,0:T(1,128)S(1)}, f32[1,32]{1,0:T(1,128)S(1)}, u32[]{:S(2)}, u32[]{:S(2)}) collective-permute-start(f32[1,32]{1,0:T(1,128)S(1)} %bitcast.10), channel_id=1, source_target_pairs={{0,8},{8,0},{16,24},{24,16},{1,9},{9,1},{17,25},{25,17},{2,10},{10... | collective-permute-start | bytes 392 | tf_op jit(solution)/shard_map/ppermute | solution.py:386
  14.5 8.9 %collective-permute-start = (f32[1,128]{1,0:T(1,128)S(1)}, f32[1,128]{1,0:T(1,128)S(1)}, u32[]{:S(2)}, u32[]{:S(2)}) collective-permute-start(f32[1,128]{1,0:T(1,128)S(1)} %bitcast.12), channel_id=1, source_target_pairs={{0,1},{1,0},{2,3},{3,2},{4,5},{5,4},{6,7},{7,6},{8,9},{9,8},{10,11... | collective-permute-start | bytes 1544 | tf_op jit(solution)/shard_map/ppermute | solution.py:386
  19.7 3.7 %collective-permute-start.4 = (f32[2,32]{1,0:T(2,128)S(1)}, f32[2,32]{1,0:T(2,128)S(1)}, u32[]{:S(2)}, u32[]{:S(2)}) collective-permute-start(f32[2,32]{1,0:T(2,128)S(1)} %pad_maximum_fusion.4), channel_id=1, source_target_pairs={{0,16},{8,24},{16,0},{24,8},{1,17},{9,25},{17,1},{25,9},{2,18},{10... | collective-permute-start | bytes 776 | tf_op jit(solution)/shard_map/ppermute | solution.py:386
  23.5 6.9 %collective-permute-start.1 = (f32[2,128]{1,0:T(2,128)S(1)}, f32[2,128]{1,0:T(2,128)S(1)}, u32[]{:S(2)}, u32[]{:S(2)}) collective-permute-start(f32[2,128]{1,0:T(2,128)S(1)} %pad_maximum_fusion.3), channel_id=1, source_target_pairs={{0,2},{1,3},{2,0},{3,1},{4,6},{5,7},{6,4},{7,5},{8,10},{9,11},{10,... | collective-permute-start | bytes 3080 | tf_op jit(solution)/shard_map/ppermute | solution.py:386
  30.4 8.6 %collective-permute-start.2 = (f32[4,128]{1,0:T(4,128)S(1)}, f32[4,128]{1,0:T(4,128)S(1)}, u32[]{:S(2)}, u32[]{:S(2)}) collective-permute-start(f32[4,128]{1,0:T(4,128)S(1)} %pad_maximum_fusion.1), channel_id=1, source_target_pairs={{0,4},{1,5},{2,6},{3,7},{4,0},{5,1},{6,2},{7,3},{8,12},{9,13},{10,... | collective-permute-start | bytes 6152 | tf_op jit(solution)/shard_map/ppermute | solution.py:386
  42.5 30.1 %copy-start.1 = (bf16[7,128,256]{2,1,0:T(8,128)(2,1)S(1)}, bf16[7,128,256]{2,1,0:T(8,128)(2,1)}, u32[]{:S(2)}) copy-start(bf16[7,128,256]{2,1,0:T(8,128)(2,1)} %constant.31.clone.m_ref) | copy-start | bytes 1376260

commit v17 on v16

--- a/solution.py
+++ b/solution.py
@@ -115,16 +115,11 @@
     traded = jnp.concatenate(parts, axis=1)
     im_lane = (lax.broadcasted_iota(jnp.int32, upper.shape, 1) & HALF) != 0
     below = jnp.where(im_lane, traded, -traded)
-    traded_below = jnp.where(im_lane, -upper, upper)
-
-    def stacked(first, second):
-        children = (slice(0, HALF), slice(HALF, WIDE))
-        return jnp.concatenate([half[rows] for rows in children for half in (first, second)], axis=0)
-
-    return stacked(upper, below), stacked(traded, traded_below)
-
-
-def butterfly(load, store, count, apart, matrix, swapped, phase_of, group, turn=0):
+    children = (slice(0, HALF), slice(HALF, WIDE))
+    return jnp.concatenate([half[rows] for rows in children for half in (upper, below)], axis=0)
+
+
+def butterfly(load, store, count, apart, matrix, phase_of, group):
     lows = [i for i in range(count) if not i & apart]
     for start in range(0, len(lows), group):
         picked = lows[start : start + group]
@@ -133,22 +128,15 @@
         rows = left.shape[0] // len(picked)
         pair = jnp.concatenate([left, right], axis=1)
         both = jnp.dot(pair, matrix, preferred_element_type=jnp.float32).astype(jnp.bfloat16)
-        if turn % 4 == 0:
-            other = jnp.dot(pair, swapped, preferred_element_type=jnp.float32)
-            other = other.astype(jnp.bfloat16)
         for place, low in enumerate(picked):
             for child in range(2):
                 index = low + child * apart
                 cosine, sine = phase_of(index)
-                mine = slice(place * rows, (place + 1) * rows)
-                own = slice(child * WIDE, (child + 1) * WIDE)
-                value = both[mine, own]
-                if turn % 4 == 0:
-                    turned = other[mine, own]
-                else:
-                    turned = jnp.concatenate([value[:, HALF:], value[:, :HALF]], axis=1)
+                value = both[
+                    place * rows : (place + 1) * rows, child * WIDE : (child + 1) * WIDE
+                ]
+                turned = jnp.concatenate([value[:, HALF:], value[:, :HALF]], axis=1)
                 store(index, value * cosine + turned * sine)
-        turn += 1
 
 
 def swap_axes(load, store, outer, inner, shuffle):
@@ -192,7 +180,7 @@
         copy.start()
 
     def expand(level):
-        w_ref[2 * level], w_ref[2 * level + 1] = whole_matrix(m_ref[level])
+        w_ref[level] = whole_matrix(m_ref[level])
 
     def level_on(level, begin):
         own = slice(begin, begin + BLOCK)
@@ -205,11 +193,9 @@
             store,
             rows,
             1 << level,
-            w_ref[2 * level],
-            w_ref[2 * level + 1],
+            w_ref[level],
             lambda index: (cosines[own], sines[own]),
             8,
-            begin // BLOCK * 2,
         )
 
     m_copies[0].wait()
@@ -257,7 +243,7 @@
             pltpu.VMEM((1, cols), jnp.float32),
             pltpu.VMEM(x.shape, x.dtype),
             pltpu.VMEM(matrices.shape, x.dtype),
-            pltpu.VMEM((2 * levels, 2 * WIDE, 2 * WIDE), x.dtype),
+            pltpu.VMEM((levels, 2 * WIDE, 2 * WIDE), x.dtype),
             pltpu.SemaphoreType.DMA,
             pltpu.SemaphoreType.DMA((cols // PIECE * (rows // SPAN),)),
             pltpu.SemaphoreType.DMA((levels,)),
@@ -272,7 +258,7 @@
     tgt_count = cs_ref.shape[0] // run
     for step, (apart, by_source) in enumerate(levels):
         source = x_ref if step == 0 else o_ref
-        matrix, swapped = whole_matrix(m_ref[step])
+        matrix = whole_matrix(m_ref[step])
         for col in range(run):
             own = slice(col * rows, (col + 1) * rows)
 
@@ -293,10 +279,8 @@
                 count,
                 apart,
                 matrix,
-                swapped,
                 phase_of,
                 8,
-                col * 2,
             )
 
 
@@ -317,7 +301,7 @@
 
     for level in range(levels):
         source = x_ref if level == 0 else state_ref
-        weights = whole_matrix(m_ref[level])
+        matrix = whole_matrix(m_ref[level])
         for start in range(0, rows, 16):
             own = slice(start, start + 16)
             cosine, sine = halved((c_ref[own, :], s_ref[own, :]))
@@ -330,7 +314,7 @@
                 store,
                 cols,
                 1 << (levels - 1 - level),
-                *weights,
+                matrix,
                 lambda index: (cosine, sine),
                 16,
             )

time: 76.8 us -> 75.5 us (0.983)
  Pallas kernels: 11.5 us -> 10.1 us
where the time goes in v17:
time: 75.5 us; the launch traced here: 75.2 us
  blocking collectives  30.1 us (40%)
  starting transfers between devices  17.4 us (23%)
  waiting for transfers between devices  16.7 us (22%)
  Pallas kernels  10.1 us (13%)
    all_to_all x1, blocking collectives, traded(): return lax.all_to_all(state, ('src', 'tgt'), 0, 0, tiled=True)  30.1 us
    ppermute x5, waiting for transfers between devices, gathered(): other = lax.ppermute(values, axis, [(i, i ^ apart) for i in range(count)])  15.8 us
    ppermute x5, starting transfers between devices, gathered(): other = lax.ppermute(values, axis, [(i, i ^ apart) for i in range(count)])  10.1 us
    all_to_all x1, starting transfers between devices, traded(): return lax.all_to_all(state, ('src', 'tgt'), 0, 0, tiled=True)  7.3 us
    pallas_call x1, Pallas kernels, source_levels(): pl.pallas_call(source_kernel, out_shape=jax.ShapeDtypeStruct((cols, rows,...  4.85 us
    pallas_call x1, Pallas kernels, target_levels(): pl.pallas_call(target_kernel, out_shape=jax.ShapeDtypeStruct(shape, x.dty...  3.45 us
    pallas_call x1, Pallas kernels, middle_levels(): pl.pallas_call(functools.partial(middle_kernel, levels, rows), out_shape=...  1.81 us
  transfers between devices with their start and end apart: 6, of which 5 were waited for; matrix products, arithmetic and copies ran while one was open for 1% of the time, Pallas kernels for 0%

profile of v17, /device:TPU:0, one launch (start us, length us, event | category | flops | bytes accessed | tf_op | source)
XLA Modules:
  0.0 75.2 jit_solution(4864257243415845493)
XLA Ops:
  0.0 4.9 %shard_map.118 = bf16[128,32,128]{2,1,0:T(8,128)(2,1)} custom-call(f32[1,128]{1,0:T(1,128)} %bitcast.11, bf16[32,128,128]{2,1,0:T(8,128)(2,1)} %x_hbm.1, bf16[5,128,256]{2,1,0:T(8,128)(2,1)} %constant.28.clone.m_hbm.m_ref), custom_call_target="tpu_custom_call" | custom-call | tf_op jit(solution)/shard_map/pallas_call | solution.py:237
  4.9 0.0 copy-start.4
  4.9 0.0 copy-start.5
  4.9 0.0 copy-start.2
  4.9 0.0 copy-start.3
  4.9 7.3 %all-to-all-start = ((bf16[32,128,128]{2,1,0:T(8,128)(2,1)}), bf16[32,128,128]{2,1,0:T(8,128)(2,1)S(1)}, u32[]{:S(2)}, u32[]{:S(2)}) async-start(bf16[32,128,128]{2,1,0:T(8,128)(2,1)} %bitcast.1), calls=%async_computation | async-start | bytes 2097152 | tf_op jit(solution)/shard_map/all_to_all | solution.py:397
  12.2 0.0 copy-start
  12.2 0.0 copy-done.4
  12.2 1.8 %collective-permute-start.3 = (f32[1,32]{1,0:T(1,128)S(1)}, f32[1,32]{1,0:T(1,128)S(1)}, u32[]{:S(2)}, u32[]{:S(2)}) collective-permute-start(f32[1,32]{1,0:T(1,128)S(1)} %bitcast.10), channel_id=1, source_target_pairs={{0,8},{8,0},{16,24},{24,16},{1,9},{9,1},{17,25},{25,17},{2,10},{10... | collective-permute-start | bytes 392 | tf_op jit(solution)/shard_map/ppermute | solution.py:370
  14.1 0.0 copy-done.5
  14.1 0.0 collective-permute-start
  14.1 5.2 %collective-permute-done.3 = f32[1,32]{1,0:T(1,128)S(1)} collective-permute-done((f32[1,32]{1,0:T(1,128)S(1)}, f32[1,32]{1,0:T(1,128)S(1)}, u32[]{:S(2)}, u32[]{:S(2)}) %collective-permute-start.3) | collective-permute-done | bytes 160 | tf_op jit(solution)/shard_map/ppermute | solution.py:370
  19.3 1.5 %collective-permute-start.4 = (f32[2,32]{1,0:T(2,128)S(1)}, f32[2,32]{1,0:T(2,128)S(1)}, u32[]{:S(2)}, u32[]{:S(2)}) collective-permute-start(f32[2,32]{1,0:T(2,128)S(1)} %pad_maximum_fusion.4), channel_id=1, source_target_pairs={{0,16},{8,24},{16,0},{24,8},{1,17},{9,25},{17,1},{25,9},{2,18},{10... | collective-permute-start | bytes 776 | tf_op jit(solution)/shard_map/ppermute | solution.py:370
  20.8 2.2 %collective-permute-done.4 = f32[2,32]{1,0:T(2,128)S(1)} collective-permute-done((f32[2,32]{1,0:T(2,128)S(1)}, f32[2,32]{1,0:T(2,128)S(1)}, u32[]{:S(2)}, u32[]{:S(2)}) %collective-permute-start.4) | collective-permute-done | bytes 288 | tf_op jit(solution)/shard_map/ppermute | solution.py:370
  23.0 0.0 collective-permute-done
  23.1 2.1 %collective-permute-start.1 = (f32[2,128]{1,0:T(2,128)S(1)}, f32[2,128]{1,0:T(2,128)S(1)}, u32[]{:S(2)}, u32[]{:S(2)}) collective-permute-start(f32[2,128]{1,0:T(2,128)S(1)} %pad_maximum_fusion.3), channel_id=1, source_target_pairs={{0,2},{1,3},{2,0},{3,1},{4,6},{5,7},{6,4},{7,5},{8,10},{9,11},{10,... | collective-permute-start | bytes 3080 | tf_op jit(solution)/shard_map/ppermute | solution.py:370
  25.2 4.7 %collective-permute-done.1 = f32[2,128]{1,0:T(2,128)S(1)} collective-permute-done((f32[2,128]{1,0:T(2,128)S(1)}, f32[2,128]{1,0:T(2,128)S(1)}, u32[]{:S(2)}, u32[]{:S(2)}) %collective-permute-start.1) | collective-permute-done | bytes 1056 | tf_op jit(solution)/shard_map/ppermute | solution.py:370
  30.0 4.6 %collective-permute-start.2 = (f32[4,128]{1,0:T(4,128)S(1)}, f32[4,128]{1,0:T(4,128)S(1)}, u32[]{:S(2)}, u32[]{:S(2)}) collective-permute-start(f32[4,128]{1,0:T(4,128)S(1)} %pad_maximum_fusion.1), channel_id=1, source_target_pairs={{0,4},{1,5},{2,6},{3,7},{4,0},{5,1},{6,2},{7,3},{8,12},{9,13},{10,... | collective-permute-start | bytes 6152 | tf_op jit(solution)/shard_map/ppermute | solution.py:370
  34.5 0.0 copy-done.2
  34.5 0.0 copy-done.3
  34.5 0.3 fusion
  34.8 3.7 %collective-permute-done.2 = f32[4,128]{1,0:T(4,128)S(1)} collective-permute-done((f32[4,128]{1,0:T(4,128)S(1)}, f32[4,128]{1,0:T(4,128)S(1)}, u32[]{:S(2)}, u32[]{:S(2)}) %collective-permute-start.2) | collective-permute-done | bytes 2080 | tf_op jit(solution)/shard_map/ppermute | solution.py:370
  38.6 0.1 constant_dynamic-slice_fusion
  38.7 0.1 mul.78
  38.7 0.2 fusion.2
  38.9 0.9 %all-to-all-done.x_ref = bf16[32,128,128]{2,1,0:T(8,128)(2,1)S(1)} async-done(((bf16[32,128,128]{2,1,0:T(8,128)(2,1)}), bf16[32,128,128]{2,1,0:T(8,128)(2,1)S(1)}, u32[]{:S(2)}, u32[]{:S(2)}) %all-to-all-start) | async-done | bytes 1048608 | tf_op jit(solution)/shard_map/all_to_all | solution.py:397
  39.9 0.0 copy-done
  39.9 1.8 %shard_map.119 = bf16[32,128,128]{2,1,0:T(8,128)(2,1)S(1)} custom-call(bf16[32,128,128]{2,1,0:T(8,128)(2,1)S(1)} %all-to-all-done.x_ref, bf16[5,128,256]{2,1,0:T(8,128)(2,1)S(1)} %copy-done, f32[32,128]{1,0:T(8,128)S(1)} %get-tuple-element.24.cs_ref, f32[32,128]{1,0:T(8,128)S(1)} %get-tuple-element.21.ss_ref, f32[4,32,128]{2,1,0:T(8,128)S(1)} %get-tuple-element.14.ct_ref, ...), custom_call_target="tpu_custom_call" | custom-call | tf_op jit(solution)/shard_map/pallas_call | solution.py:289
  41.7 0.0 copy-start.1
  41.7 30.1 %all_to_all.10 = bf16[32,128,128]{2,1,0:T(8,128)(2,1)S(1)} all-to-all(bf16[32,128,128]{2,1,0:T(8,128)(2,1)S(1)} %shard_map.119), channel_id=1, replica_groups=mesh['src'=4,'tgt'=8] {'src','tgt'}, dimensions={0} | all-to-all | bytes 2097152 | tf_op jit(solution)/shard_map/all_to_all | solution.py:397
  71.8 0.0 copy-done.1
  71.8 3.4 %shard_map.120 = bf16[32,128,128]{2,1,0:T(8,128)(2,1)} custom-call(bf16[7,128,256]{2,1,0:T(8,128)(2,1)S(1)} %copy-done.1, f32[32,128]{1,0:T(8,128)S(1)} %get-tuple-element.23.c_ref, f32[32,128]{1,0:T(8,128)S(1)} %get-tuple-element.22.s_ref, bf16[128,32,128]{2,1,0:T(8,128)(2,1)S(1)} %bitcast.9), custom_call_target="tpu_custom_call" | custom-call | tf_op jit(solution)/shard_map/pallas_call | solution.py:350
  (10 shorter events, 0.1 us)
Async XLA Ops:
  4.9 7.4 %copy-start.4 = (f32[32]{0:T(128)S(1)}, f32[32]{0:T(128)}, u32[]{:S(2)}) copy-start(f32[32]{0:T(128)} %param.14) | copy-start | bytes 388
  4.9 9.2 %copy-start.5 = (f32[128]{0:T(128)S(1)}, f32[128]{0:T(128)}, u32[]{:S(2)}) copy-start(f32[128]{0:T(128)} %param.13) | copy-start | bytes 1540
  4.9 29.6 %copy-start.2 = (f32[128]{0:T(128)S(1)}, f32[128]{0:T(128)}, u32[]{:S(2)}) copy-start(f32[128]{0:T(128)} %constant.30.clone) | copy-start | bytes 1540
  4.9 29.6 %copy-start.3 = (f32[128]{0:T(128)S(1)}, f32[128]{0:T(128)}, u32[]{:S(2)}) copy-start(f32[128]{0:T(128)} %constant.29.clone) | copy-start | bytes 1540
  4.9 34.9 %all-to-all-start = ((bf16[32,128,128]{2,1,0:T(8,128)(2,1)}), bf16[32,128,128]{2,1,0:T(8,128)(2,1)S(1)}, u32[]{:S(2)}, u32[]{:S(2)}) async-start(bf16[32,128,128]{2,1,0:T(8,128)(2,1)} %bitcast.1), calls=%async_computation | async-start | bytes 2097152 | tf_op jit(solution)/shard_map/all_to_all | solution.py:397
  12.2 27.6 %copy-start = (bf16[5,128,256]{2,1,0:T(8,128)(2,1)S(1)}, bf16[5,128,256]{2,1,0:T(8,128)(2,1)}, u32[]{:S(2)}) copy-start(bf16[5,128,256]{2,1,0:T(8,128)(2,1)} %constant.28.clone.m_hbm.m_ref) | copy-start | bytes 983044
  12.2 7.0 %collective-permute-start.3 = (f32[1,32]{1,0:T(1,128)S(1)}, f32[1,32]{1,0:T(1,128)S(1)}, u32[]{:S(2)}, u32[]{:S(2)}) collective-permute-start(f32[1,32]{1,0:T(1,128)S(1)} %bitcast.10), channel_id=1, source_target_pairs={{0,8},{8,0},{16,24},{24,16},{1,9},{9,1},{17,25},{25,17},{2,10},{10... | collective-permute-start | bytes 392 | tf_op jit(solution)/shard_map/ppermute | solution.py:370
  14.1 8.9 %collective-permute-start = (f32[1,128]{1,0:T(1,128)S(1)}, f32[1,128]{1,0:T(1,128)S(1)}, u32[]{:S(2)}, u32[]{:S(2)}) collective-permute-start(f32[1,128]{1,0:T(1,128)S(1)} %bitcast.12), channel_id=1, source_target_pairs={{0,1},{1,0},{2,3},{3,2},{4,5},{5,4},{6,7},{7,6},{8,9},{9,8},{10,11... | collective-permute-start | bytes 1544 | tf_op jit(solution)/shard_map/ppermute | solution.py:370
  19.3 3.7 %collective-permute-start.4 = (f32[2,32]{1,0:T(2,128)S(1)}, f32[2,32]{1,0:T(2,128)S(1)}, u32[]{:S(2)}, u32[]{:S(2)}) collective-permute-start(f32[2,32]{1,0:T(2,128)S(1)} %pad_maximum_fusion.4), channel_id=1, source_target_pairs={{0,16},{8,24},{16,0},{24,8},{1,17},{9,25},{17,1},{25,9},{2,18},{10... | collective-permute-start | bytes 776 | tf_op jit(solution)/shard_map/ppermute | solution.py:370
  23.1 6.9 %collective-permute-start.1 = (f32[2,128]{1,0:T(2,128)S(1)}, f32[2,128]{1,0:T(2,128)S(1)}, u32[]{:S(2)}, u32[]{:S(2)}) collective-permute-start(f32[2,128]{1,0:T(2,128)S(1)} %pad_maximum_fusion.3), channel_id=1, source_target_pairs={{0,2},{1,3},{2,0},{3,1},{4,6},{5,7},{6,4},{7,5},{8,10},{9,11},{10,... | collective-permute-start | bytes 3080 | tf_op jit(solution)/shard_map/ppermute | solution.py:370
  30.0 8.6 %collective-permute-start.2 = (f32[4,128]{1,0:T(4,128)S(1)}, f32[4,128]{1,0:T(4,128)S(1)}, u32[]{:S(2)}, u32[]{:S(2)}) collective-permute-start(f32[4,128]{1,0:T(4,128)S(1)} %pad_maximum_fusion.1), channel_id=1, source_target_pairs={{0,4},{1,5},{2,6},{3,7},{4,0},{5,1},{6,2},{7,3},{8,12},{9,13},{10,... | collective-permute-start | bytes 6152 | tf_op jit(solution)/shard_map/ppermute | solution.py:370
  41.7 30.1 %copy-start.1 = (bf16[7,128,256]{2,1,0:T(8,128)(2,1)S(1)}, bf16[7,128,256]{2,1,0:T(8,128)(2,1)}, u32[]{:S(2)}) copy-start(bf16[7,128,256]{2,1,0:T(8,128)(2,1)} %constant.31.clone.m_ref) | copy-start | bytes 1376260

commit v18 on v17

--- a/solution.py
+++ b/solution.py
@@ -119,6 +119,13 @@
     return jnp.concatenate([half[rows] for rows in children for half in (upper, below)], axis=0)
 
 
+def whole_matrices(uppers):
+    upper = np.stack(uppers).astype(np.float32).reshape(-1, 2, HALF, 2, 2, HALF)
+    below = np.stack([-upper[:, :, :, :, 1], upper[:, :, :, :, 0]], axis=4)
+    both = np.concatenate([upper, below], axis=2)
+    return jnp.asarray(both.reshape(-1, 2 * WIDE, 2 * WIDE).astype(ml_dtypes.bfloat16))
+
+
 def butterfly(load, store, count, apart, matrix, phase_of, group):
     lows = [i for i in range(count) if not i & apart]
     for start in range(0, len(lows), group):
@@ -198,6 +205,7 @@
             8,
         )
 
+    shuffle = shuffle_matrix()
     m_copies[0].wait()
     each = rows // SPAN
     for piece in range(cols // PIECE):
@@ -225,7 +233,7 @@
         store_block,
         rows // 16,
         cols // 16,
-        shuffle_matrix(),
+        shuffle,
     )
 
 
@@ -258,7 +266,7 @@
     tgt_count = cs_ref.shape[0] // run
     for step, (apart, by_source) in enumerate(levels):
         source = x_ref if step == 0 else o_ref
-        matrix = whole_matrix(m_ref[step])
+        matrix = m_ref[step]
         for col in range(run):
             own = slice(col * rows, (col + 1) * rows)
 
@@ -301,7 +309,7 @@
 
     for level in range(levels):
         source = x_ref if level == 0 else state_ref
-        matrix = whole_matrix(m_ref[level])
+        matrix = m_ref[level]
         for start in range(0, rows, 16):
             own = slice(start, start + 16)
             cosine, sine = halved((c_ref[own, :], s_ref[own, :]))
@@ -387,16 +395,13 @@
     total = first_target + tgt_bits + col_bits
     matrices = [level_matrix(number) for number in range(total)]
 
-    def matrices_of(low, high):
-        return jnp.asarray(np.stack(matrices[low:high]))
-
     run = cols // devices
     place = lax.axis_index("src") * tgt_count + lax.axis_index("tgt")
 
     def traded(state):
         return lax.all_to_all(state, ("src", "tgt"), 0, 0, tiled=True)
 
-    state = source_levels(box_weights, matrices_of(0, row_bits), slowness)
+    state = source_levels(box_weights, jnp.asarray(np.stack(matrices[:row_bits])), slowness)
 
     state, slowness, dip_field = lax.optimization_barrier((state, slowness, dip_field))
     all_dip = gathered(dip_field, "src")
@@ -409,7 +414,7 @@
     levels += [(1 << bit, False) for bit in reversed(range(tgt_bits))]
     state = middle_levels(
         state,
-        matrices_of(row_bits, first_target + tgt_bits),
+        whole_matrices(matrices[row_bits : first_target + tgt_bits]),
         tables(run_slowness.reshape(-1)),
         tables(all_dip),
         levels,
@@ -418,7 +423,7 @@
 
     return target_levels(
         state.reshape(cols, rows, WIDE),
-        matrices_of(first_target + tgt_bits, total),
+        whole_matrices(matrices[first_target + tgt_bits :]),
         tables(dip_field),
     )
 

time: 75.5 us -> 75.2 us (level)
  no operation moved by 1% of the time
where the time goes in v18:
time: 75.2 us; the launch traced here: 74.9 us
  blocking collectives  30.1 us (40%)
  starting transfers between devices  17.3 us (23%)
  waiting for transfers between devices  16.1 us (21%)
  Pallas kernels  9.82 us (13%)
  local copies, waits for them, and re-layouts  0.84 us (1%)
    all_to_all x1, blocking collectives, traded(): return lax.all_to_all(state, ('src', 'tgt'), 0, 0, tiled=True)  30.1 us
    ppermute x5, waiting for transfers between devices, gathered(): other = lax.ppermute(values, axis, [(i, i ^ apart) for i in range(count)])  15.2 us
    ppermute x5, starting transfers between devices, gathered(): other = lax.ppermute(values, axis, [(i, i ^ apart) for i in range(count)])  10 us
    all_to_all x1, starting transfers between devices, traded(): return lax.all_to_all(state, ('src', 'tgt'), 0, 0, tiled=True)  7.3 us
    pallas_call x1, Pallas kernels, source_levels(): pl.pallas_call(source_kernel, out_shape=jax.ShapeDtypeStruct((cols, rows,...  4.83 us
    pallas_call x1, Pallas kernels, target_levels(): pl.pallas_call(target_kernel, out_shape=jax.ShapeDtypeStruct(shape, x.dty...  3.31 us
    pallas_call x1, Pallas kernels, middle_levels(): pl.pallas_call(functools.partial(middle_kernel, levels, rows), out_shape=...  1.69 us
  transfers between devices with their start and end apart: 6, of which 5 were waited for; matrix products, arithmetic and copies ran while one was open for 1% of the time, Pallas kernels for 0%

profile of v18, /device:TPU:0, one launch (start us, length us, event | category | flops | bytes accessed | tf_op | source)
XLA Modules:
  0.0 74.9 jit_solution(6412120479573735911)
XLA Ops:
  0.0 4.8 %shard_map.118 = bf16[128,32,128]{2,1,0:T(8,128)(2,1)} custom-call(f32[1,128]{1,0:T(1,128)} %bitcast.11, bf16[32,128,128]{2,1,0:T(8,128)(2,1)} %x_hbm.1, bf16[5,128,256]{2,1,0:T(8,128)(2,1)} %constant.30.clone.m_hbm), custom_call_target="tpu_custom_call" | custom-call | tf_op jit(solution)/shard_map/pallas_call | solution.py:245
  4.8 0.0 copy-start.1
  4.9 7.3 %all-to-all-start = ((bf16[32,128,128]{2,1,0:T(8,128)(2,1)}), bf16[32,128,128]{2,1,0:T(8,128)(2,1)S(1)}, u32[]{:S(2)}, u32[]{:S(2)}) async-start(bf16[32,128,128]{2,1,0:T(8,128)(2,1)} %bitcast.1), calls=%async_computation | async-start | bytes 2097152 | tf_op jit(solution)/shard_map/all_to_all | solution.py:402
  12.2 0.0 copy-start.4
  12.2 0.6 copy-done.4
  12.8 0.0 copy-start.5
  12.8 1.8 %collective-permute-start.3 = (f32[1,32]{1,0:T(1,128)S(1)}, f32[1,32]{1,0:T(1,128)S(1)}, u32[]{:S(2)}, u32[]{:S(2)}) collective-permute-start(f32[1,32]{1,0:T(1,128)S(1)} %bitcast.10), channel_id=1, source_target_pairs={{0,8},{8,0},{16,24},{24,16},{1,9},{9,1},{17,25},{25,17},{2,10},{10... | collective-permute-start | bytes 392 | tf_op jit(solution)/shard_map/ppermute | solution.py:378
  14.6 0.0 copy-done.5
  14.6 0.0 collective-permute-start
  14.6 4.6 %collective-permute-done.3 = f32[1,32]{1,0:T(1,128)S(1)} collective-permute-done((f32[1,32]{1,0:T(1,128)S(1)}, f32[1,32]{1,0:T(1,128)S(1)}, u32[]{:S(2)}, u32[]{:S(2)}) %collective-permute-start.3) | collective-permute-done | bytes 160 | tf_op jit(solution)/shard_map/ppermute | solution.py:378
  19.2 1.5 %collective-permute-start.4 = (f32[2,32]{1,0:T(2,128)S(1)}, f32[2,32]{1,0:T(2,128)S(1)}, u32[]{:S(2)}, u32[]{:S(2)}) collective-permute-start(f32[2,32]{1,0:T(2,128)S(1)} %pad_maximum_fusion.4), channel_id=1, source_target_pairs={{0,16},{8,24},{16,0},{24,8},{1,17},{9,25},{17,1},{25,9},{2,18},{10... | collective-permute-start | bytes 776 | tf_op jit(solution)/shard_map/ppermute | solution.py:378
  20.7 2.2 %collective-permute-done.4 = f32[2,32]{1,0:T(2,128)S(1)} collective-permute-done((f32[2,32]{1,0:T(2,128)S(1)}, f32[2,32]{1,0:T(2,128)S(1)}, u32[]{:S(2)}, u32[]{:S(2)}) %collective-permute-start.4) | collective-permute-done | bytes 288 | tf_op jit(solution)/shard_map/ppermute | solution.py:378
  23.0 0.0 collective-permute-done
  23.0 2.1 %collective-permute-start.1 = (f32[2,128]{1,0:T(2,128)S(1)}, f32[2,128]{1,0:T(2,128)S(1)}, u32[]{:S(2)}, u32[]{:S(2)}) collective-permute-start(f32[2,128]{1,0:T(2,128)S(1)} %pad_maximum_fusion.3), channel_id=1, source_target_pairs={{0,2},{1,3},{2,0},{3,1},{4,6},{5,7},{6,4},{7,5},{8,10},{9,11},{10,... | collective-permute-start | bytes 3080 | tf_op jit(solution)/shard_map/ppermute | solution.py:378
  25.1 4.7 %collective-permute-done.1 = f32[2,128]{1,0:T(2,128)S(1)} collective-permute-done((f32[2,128]{1,0:T(2,128)S(1)}, f32[2,128]{1,0:T(2,128)S(1)}, u32[]{:S(2)}, u32[]{:S(2)}) %collective-permute-start.1) | collective-permute-done | bytes 1056 | tf_op jit(solution)/shard_map/ppermute | solution.py:378
  29.9 0.0 copy-start.2
  29.9 0.0 copy-start.3
  29.9 4.6 %collective-permute-start.2 = (f32[4,128]{1,0:T(4,128)S(1)}, f32[4,128]{1,0:T(4,128)S(1)}, u32[]{:S(2)}, u32[]{:S(2)}) collective-permute-start(f32[4,128]{1,0:T(4,128)S(1)} %pad_maximum_fusion.1), channel_id=1, source_target_pairs={{0,4},{1,5},{2,6},{3,7},{4,0},{5,1},{6,2},{7,3},{8,12},{9,13},{10,... | collective-permute-start | bytes 6152 | tf_op jit(solution)/shard_map/ppermute | solution.py:378
  34.5 0.0 copy-done.2
  34.5 0.0 copy-done.3
  34.5 0.3 fusion
  34.8 3.7 %collective-permute-done.2 = f32[4,128]{1,0:T(4,128)S(1)} collective-permute-done((f32[4,128]{1,0:T(4,128)S(1)}, f32[4,128]{1,0:T(4,128)S(1)}, u32[]{:S(2)}, u32[]{:S(2)}) %collective-permute-start.2) | collective-permute-done | bytes 2080 | tf_op jit(solution)/shard_map/ppermute | solution.py:378
  38.5 0.1 constant_dynamic-slice_fusion
  38.6 0.1 mul.78
  38.7 0.2 fusion.2
  38.9 0.9 %all-to-all-done.x_ref = bf16[32,128,128]{2,1,0:T(8,128)(2,1)S(1)} async-done(((bf16[32,128,128]{2,1,0:T(8,128)(2,1)}), bf16[32,128,128]{2,1,0:T(8,128)(2,1)S(1)}, u32[]{:S(2)}, u32[]{:S(2)}) %all-to-all-start) | async-done | bytes 1048608 | tf_op jit(solution)/shard_map/all_to_all | solution.py:402
  39.8 0.0 copy-done.1
  39.8 1.7 %shard_map.119 = bf16[32,128,128]{2,1,0:T(8,128)(2,1)S(1)} custom-call(bf16[32,128,128]{2,1,0:T(8,128)(2,1)S(1)} %all-to-all-done.x_ref, bf16[5,256,256]{2,1,0:T(8,128)(2,1)S(1)} %copy-done.1, f32[32,128]{1,0:T(8,128)S(1)} %get-tuple-element.24.cs_ref, f32[32,128]{1,0:T(8,128)S(1)} %get-tuple-element.21.ss_ref, f32[4,32,128]{2,1,0:T(8,128)S(1)} %get-tuple-element.14.ct_ref, ...), custom_call_target="tpu_custom_call" | custom-call | tf_op jit(solution)/shard_map/pallas_call | solution.py:297
  41.5 0.0 copy-start
  41.5 30.1 %all_to_all.10 = bf16[32,128,128]{2,1,0:T(8,128)(2,1)S(1)} all-to-all(bf16[32,128,128]{2,1,0:T(8,128)(2,1)S(1)} %shard_map.119), channel_id=1, replica_groups=mesh['src'=4,'tgt'=8] {'src','tgt'}, dimensions={0} | all-to-all | bytes 2097152 | tf_op jit(solution)/shard_map/all_to_all | solution.py:402
  71.6 0.0 copy-done
  71.6 3.3 %shard_map.120 = bf16[32,128,128]{2,1,0:T(8,128)(2,1)} custom-call(bf16[7,256,256]{2,1,0:T(8,128)(2,1)S(1)} %copy-done, f32[32,128]{1,0:T(8,128)S(1)} %get-tuple-element.23.c_ref, f32[32,128]{1,0:T(8,128)S(1)} %get-tuple-element.22.s_ref, bf16[128,32,128]{2,1,0:T(8,128)(2,1)S(1)} %bitcast.9), custom_call_target="tpu_custom_call" | custom-call | tf_op jit(solution)/shard_map/pallas_call | solution.py:358
  (10 shorter events, 0.1 us)
Async XLA Ops:
  4.8 35.0 %copy-start.1 = (bf16[5,256,256]{2,1,0:T(8,128)(2,1)S(1)}, bf16[5,256,256]{2,1,0:T(8,128)(2,1)}, u32[]{:S(2)}) copy-start(bf16[5,256,256]{2,1,0:T(8,128)(2,1)} %constant.31.clone.m_ref) | copy-start | bytes 1966084
  4.9 34.9 %all-to-all-start = ((bf16[32,128,128]{2,1,0:T(8,128)(2,1)}), bf16[32,128,128]{2,1,0:T(8,128)(2,1)S(1)}, u32[]{:S(2)}, u32[]{:S(2)}) async-start(bf16[32,128,128]{2,1,0:T(8,128)(2,1)} %bitcast.1), calls=%async_computation | async-start | bytes 2097152 | tf_op jit(solution)/shard_map/all_to_all | solution.py:402
  12.2 0.7 copy-start.4
  12.8 1.8 %copy-start.5 = (f32[128]{0:T(128)S(1)}, f32[128]{0:T(128)}, u32[]{:S(2)}) copy-start(f32[128]{0:T(128)} %param.13) | copy-start | bytes 1540
  12.8 6.4 %collective-permute-start.3 = (f32[1,32]{1,0:T(1,128)S(1)}, f32[1,32]{1,0:T(1,128)S(1)}, u32[]{:S(2)}, u32[]{:S(2)}) collective-permute-start(f32[1,32]{1,0:T(1,128)S(1)} %bitcast.10), channel_id=1, source_target_pairs={{0,8},{8,0},{16,24},{24,16},{1,9},{9,1},{17,25},{25,17},{2,10},{10... | collective-permute-start | bytes 392 | tf_op jit(solution)/shard_map/ppermute | solution.py:378
  14.6 8.4 %collective-permute-start = (f32[1,128]{1,0:T(1,128)S(1)}, f32[1,128]{1,0:T(1,128)S(1)}, u32[]{:S(2)}, u32[]{:S(2)}) collective-permute-start(f32[1,128]{1,0:T(1,128)S(1)} %bitcast.12), channel_id=1, source_target_pairs={{0,1},{1,0},{2,3},{3,2},{4,5},{5,4},{6,7},{7,6},{8,9},{9,8},{10,11... | collective-permute-start | bytes 1544 | tf_op jit(solution)/shard_map/ppermute | solution.py:378
  19.2 3.7 %collective-permute-start.4 = (f32[2,32]{1,0:T(2,128)S(1)}, f32[2,32]{1,0:T(2,128)S(1)}, u32[]{:S(2)}, u32[]{:S(2)}) collective-permute-start(f32[2,32]{1,0:T(2,128)S(1)} %pad_maximum_fusion.4), channel_id=1, source_target_pairs={{0,16},{8,24},{16,0},{24,8},{1,17},{9,25},{17,1},{25,9},{2,18},{10... | collective-permute-start | bytes 776 | tf_op jit(solution)/shard_map/ppermute | solution.py:378
  23.0 6.9 %collective-permute-start.1 = (f32[2,128]{1,0:T(2,128)S(1)}, f32[2,128]{1,0:T(2,128)S(1)}, u32[]{:S(2)}, u32[]{:S(2)}) collective-permute-start(f32[2,128]{1,0:T(2,128)S(1)} %pad_maximum_fusion.3), channel_id=1, source_target_pairs={{0,2},{1,3},{2,0},{3,1},{4,6},{5,7},{6,4},{7,5},{8,10},{9,11},{10,... | collective-permute-start | bytes 3080 | tf_op jit(solution)/shard_map/ppermute | solution.py:378
  29.9 4.6 %copy-start.2 = (f32[128]{0:T(128)S(1)}, f32[128]{0:T(128)}, u32[]{:S(2)}) copy-start(f32[128]{0:T(128)} %constant.33.clone) | copy-start | bytes 1540
  29.9 4.6 %copy-start.3 = (f32[128]{0:T(128)S(1)}, f32[128]{0:T(128)}, u32[]{:S(2)}) copy-start(f32[128]{0:T(128)} %constant.32.clone) | copy-start | bytes 1540
  29.9 8.6 %collective-permute-start.2 = (f32[4,128]{1,0:T(4,128)S(1)}, f32[4,128]{1,0:T(4,128)S(1)}, u32[]{:S(2)}, u32[]{:S(2)}) collective-permute-start(f32[4,128]{1,0:T(4,128)S(1)} %pad_maximum_fusion.1), channel_id=1, source_target_pairs={{0,4},{1,5},{2,6},{3,7},{4,0},{5,1},{6,2},{7,3},{8,12},{9,13},{10,... | collective-permute-start | bytes 6152 | tf_op jit(solution)/shard_map/ppermute | solution.py:378
  41.5 30.1 %copy-start = (bf16[7,256,256]{2,1,0:T(8,128)(2,1)S(1)}, bf16[7,256,256]{2,1,0:T(8,128)(2,1)}, u32[]{:S(2)}) copy-start(bf16[7,256,256]{2,1,0:T(8,128)(2,1)} %constant.34.clone.m_ref) | copy-start | bytes 2752516

commit v19 on v18

--- a/solution.py
+++ b/solution.py
@@ -162,8 +162,8 @@
     return (slice(first * 16, first * 16 + 16), slice(second * 16, second * 16 + 16))
 
 
-PIECE = 64
-SPAN = 8
+PIECE = 32
+SPAN = 16
 BLOCK = 32
 VMEM = pl.BlockSpec(memory_space=pltpu.VMEM)
 FAR = pl.BlockSpec(memory_space=pltpu.HBM)
@@ -206,15 +206,14 @@
         )
 
     shuffle = shuffle_matrix()
+    a_copy.wait()
+    cosines, sines = halved(rotation(column_of(a_ref[...], cols)))
     m_copies[0].wait()
+    expand(0)
     each = rows // SPAN
     for piece in range(cols // PIECE):
         for copy in x_copies[piece * each : (piece + 1) * each]:
             copy.wait()
-        if piece == 0:
-            a_copy.wait()
-            expand(0)
-            cosines, sines = halved(rotation(column_of(a_ref[...], cols)))
         for begin in range(piece * PIECE, (piece + 1) * PIECE, BLOCK):
             level_on(0, begin)
     for copy in m_copies[1:]:

time: 75.2 us -> 75.8 us (level)
  no operation moved by 1% of the time
where the time goes in v19:
time: 75.8 us; the launch traced here: 75.6 us
  blocking collectives  30.1 us (40%)
  starting transfers between devices  17.3 us (23%)
  waiting for transfers between devices  16.1 us (21%)
  Pallas kernels  10.5 us (14%)
  local copies, waits for them, and re-layouts  0.84 us (1%)
    all_to_all x1, blocking collectives, traded(): return lax.all_to_all(state, ('src', 'tgt'), 0, 0, tiled=True)  30.1 us
    ppermute x5, waiting for transfers between devices, gathered(): other = lax.ppermute(values, axis, [(i, i ^ apart) for i in range(count)])  15.2 us
    ppermute x5, starting transfers between devices, gathered(): other = lax.ppermute(values, axis, [(i, i ^ apart) for i in range(count)])  10 us
    all_to_all x1, starting transfers between devices, traded(): return lax.all_to_all(state, ('src', 'tgt'), 0, 0, tiled=True)  7.3 us
    pallas_call x1, Pallas kernels, source_levels(): pl.pallas_call(source_kernel, out_shape=jax.ShapeDtypeStruct((cols, rows,...  5.5 us
    pallas_call x1, Pallas kernels, target_levels(): pl.pallas_call(target_kernel, out_shape=jax.ShapeDtypeStruct(shape, x.dty...  3.31 us
    pallas_call x1, Pallas kernels, middle_levels(): pl.pallas_call(functools.partial(middle_kernel, levels, rows), out_shape=...  1.69 us
  transfers between devices with their start and end apart: 6, of which 5 were waited for; matrix products, arithmetic and copies ran while one was open for 1% of the time, Pallas kernels for 0%

profile of v19, /device:TPU:0, one launch (start us, length us, event | category | flops | bytes accessed | tf_op | source)
XLA Modules:
  0.0 75.6 jit_solution(5457559771055835569)
XLA Ops:
  0.0 5.5 %shard_map.118 = bf16[128,32,128]{2,1,0:T(8,128)(2,1)} custom-call(f32[1,128]{1,0:T(1,128)} %bitcast.11, bf16[32,128,128]{2,1,0:T(8,128)(2,1)} %x_hbm.1, bf16[5,128,256]{2,1,0:T(8,128)(2,1)} %constant.30.clone.m_hbm), custom_call_target="tpu_custom_call" | custom-call | tf_op jit(solution)/shard_map/pallas_call | solution.py:244
  5.5 0.0 copy-start.1
  5.5 7.3 %all-to-all-start = ((bf16[32,128,128]{2,1,0:T(8,128)(2,1)}), bf16[32,128,128]{2,1,0:T(8,128)(2,1)S(1)}, u32[]{:S(2)}, u32[]{:S(2)}) async-start(bf16[32,128,128]{2,1,0:T(8,128)(2,1)} %bitcast.1), calls=%async_computation | async-start | bytes 2097152 | tf_op jit(solution)/shard_map/all_to_all | solution.py:401
  12.8 0.0 copy-start.4
  12.8 0.6 copy-done.4
  13.5 0.0 copy-start.5
  13.5 1.8 %collective-permute-start.3 = (f32[1,32]{1,0:T(1,128)S(1)}, f32[1,32]{1,0:T(1,128)S(1)}, u32[]{:S(2)}, u32[]{:S(2)}) collective-permute-start(f32[1,32]{1,0:T(1,128)S(1)} %bitcast.10), channel_id=1, source_target_pairs={{0,8},{8,0},{16,24},{24,16},{1,9},{9,1},{17,25},{25,17},{2,10},{10... | collective-permute-start | bytes 392 | tf_op jit(solution)/shard_map/ppermute | solution.py:377
  15.3 0.0 copy-done.5
  15.3 0.0 collective-permute-start
  15.3 4.6 %collective-permute-done.3 = f32[1,32]{1,0:T(1,128)S(1)} collective-permute-done((f32[1,32]{1,0:T(1,128)S(1)}, f32[1,32]{1,0:T(1,128)S(1)}, u32[]{:S(2)}, u32[]{:S(2)}) %collective-permute-start.3) | collective-permute-done | bytes 160 | tf_op jit(solution)/shard_map/ppermute | solution.py:377
  19.9 1.5 %collective-permute-start.4 = (f32[2,32]{1,0:T(2,128)S(1)}, f32[2,32]{1,0:T(2,128)S(1)}, u32[]{:S(2)}, u32[]{:S(2)}) collective-permute-start(f32[2,32]{1,0:T(2,128)S(1)} %pad_maximum_fusion.4), channel_id=1, source_target_pairs={{0,16},{8,24},{16,0},{24,8},{1,17},{9,25},{17,1},{25,9},{2,18},{10... | collective-permute-start | bytes 776 | tf_op jit(solution)/shard_map/ppermute | solution.py:377
  21.4 2.2 %collective-permute-done.4 = f32[2,32]{1,0:T(2,128)S(1)} collective-permute-done((f32[2,32]{1,0:T(2,128)S(1)}, f32[2,32]{1,0:T(2,128)S(1)}, u32[]{:S(2)}, u32[]{:S(2)}) %collective-permute-start.4) | collective-permute-done | bytes 288 | tf_op jit(solution)/shard_map/ppermute | solution.py:377
  23.6 0.0 collective-permute-done
  23.7 2.1 %collective-permute-start.1 = (f32[2,128]{1,0:T(2,128)S(1)}, f32[2,128]{1,0:T(2,128)S(1)}, u32[]{:S(2)}, u32[]{:S(2)}) collective-permute-start(f32[2,128]{1,0:T(2,128)S(1)} %pad_maximum_fusion.3), channel_id=1, source_target_pairs={{0,2},{1,3},{2,0},{3,1},{4,6},{5,7},{6,4},{7,5},{8,10},{9,11},{10,... | collective-permute-start | bytes 3080 | tf_op jit(solution)/shard_map/ppermute | solution.py:377
  25.8 4.7 %collective-permute-done.1 = f32[2,128]{1,0:T(2,128)S(1)} collective-permute-done((f32[2,128]{1,0:T(2,128)S(1)}, f32[2,128]{1,0:T(2,128)S(1)}, u32[]{:S(2)}, u32[]{:S(2)}) %collective-permute-start.1) | collective-permute-done | bytes 1056 | tf_op jit(solution)/shard_map/ppermute | solution.py:377
  30.6 0.0 copy-start.2
  30.6 0.0 copy-start.3
  30.6 4.6 %collective-permute-start.2 = (f32[4,128]{1,0:T(4,128)S(1)}, f32[4,128]{1,0:T(4,128)S(1)}, u32[]{:S(2)}, u32[]{:S(2)}) collective-permute-start(f32[4,128]{1,0:T(4,128)S(1)} %pad_maximum_fusion.1), channel_id=1, source_target_pairs={{0,4},{1,5},{2,6},{3,7},{4,0},{5,1},{6,2},{7,3},{8,12},{9,13},{10,... | collective-permute-start | bytes 6152 | tf_op jit(solution)/shard_map/ppermute | solution.py:377
  35.1 0.0 copy-done.2
  35.1 0.0 copy-done.3
  35.1 0.3 fusion
  35.5 3.7 %collective-permute-done.2 = f32[4,128]{1,0:T(4,128)S(1)} collective-permute-done((f32[4,128]{1,0:T(4,128)S(1)}, f32[4,128]{1,0:T(4,128)S(1)}, u32[]{:S(2)}, u32[]{:S(2)}) %collective-permute-start.2) | collective-permute-done | bytes 2080 | tf_op jit(solution)/shard_map/ppermute | solution.py:377
  39.2 0.1 constant_dynamic-slice_fusion
  39.3 0.1 mul.78
  39.3 0.2 fusion.2
  39.6 0.9 %all-to-all-done.x_ref = bf16[32,128,128]{2,1,0:T(8,128)(2,1)S(1)} async-done(((bf16[32,128,128]{2,1,0:T(8,128)(2,1)}), bf16[32,128,128]{2,1,0:T(8,128)(2,1)S(1)}, u32[]{:S(2)}, u32[]{:S(2)}) %all-to-all-start) | async-done | bytes 1048608 | tf_op jit(solution)/shard_map/all_to_all | solution.py:401
  40.5 0.0 copy-done.1
  40.5 1.7 %shard_map.119 = bf16[32,128,128]{2,1,0:T(8,128)(2,1)S(1)} custom-call(bf16[32,128,128]{2,1,0:T(8,128)(2,1)S(1)} %all-to-all-done.x_ref, bf16[5,256,256]{2,1,0:T(8,128)(2,1)S(1)} %copy-done.1, f32[32,128]{1,0:T(8,128)S(1)} %get-tuple-element.24.cs_ref, f32[32,128]{1,0:T(8,128)S(1)} %get-tuple-element.21.ss_ref, f32[4,32,128]{2,1,0:T(8,128)S(1)} %get-tuple-element.14.ct_ref, ...), custom_call_target="tpu_custom_call" | custom-call | tf_op jit(solution)/shard_map/pallas_call | solution.py:296
  42.2 0.0 copy-start
  42.2 30.1 %all_to_all.10 = bf16[32,128,128]{2,1,0:T(8,128)(2,1)S(1)} all-to-all(bf16[32,128,128]{2,1,0:T(8,128)(2,1)S(1)} %shard_map.119), channel_id=1, replica_groups=mesh['src'=4,'tgt'=8] {'src','tgt'}, dimensions={0} | all-to-all | bytes 2097152 | tf_op jit(solution)/shard_map/all_to_all | solution.py:401
  72.3 0.0 copy-done
  72.3 3.3 %shard_map.120 = bf16[32,128,128]{2,1,0:T(8,128)(2,1)} custom-call(bf16[7,256,256]{2,1,0:T(8,128)(2,1)S(1)} %copy-done, f32[32,128]{1,0:T(8,128)S(1)} %get-tuple-element.23.c_ref, f32[32,128]{1,0:T(8,128)S(1)} %get-tuple-element.22.s_ref, bf16[128,32,128]{2,1,0:T(8,128)(2,1)S(1)} %bitcast.9), custom_call_target="tpu_custom_call" | custom-call | tf_op jit(solution)/shard_map/pallas_call | solution.py:357
  (10 shorter events, 0.1 us)
Async XLA Ops:
  5.5 35.0 %copy-start.1 = (bf16[5,256,256]{2,1,0:T(8,128)(2,1)S(1)}, bf16[5,256,256]{2,1,0:T(8,128)(2,1)}, u32[]{:S(2)}) copy-start(bf16[5,256,256]{2,1,0:T(8,128)(2,1)} %constant.31.clone.m_ref) | copy-start | bytes 1966084
  5.5 34.9 %all-to-all-start = ((bf16[32,128,128]{2,1,0:T(8,128)(2,1)}), bf16[32,128,128]{2,1,0:T(8,128)(2,1)S(1)}, u32[]{:S(2)}, u32[]{:S(2)}) async-start(bf16[32,128,128]{2,1,0:T(8,128)(2,1)} %bitcast.1), calls=%async_computation | async-start | bytes 2097152 | tf_op jit(solution)/shard_map/all_to_all | solution.py:401
  12.8 0.7 copy-start.4
  13.5 1.8 %copy-start.5 = (f32[128]{0:T(128)S(1)}, f32[128]{0:T(128)}, u32[]{:S(2)}) copy-start(f32[128]{0:T(128)} %param.13) | copy-start | bytes 1540
  13.5 6.4 %collective-permute-start.3 = (f32[1,32]{1,0:T(1,128)S(1)}, f32[1,32]{1,0:T(1,128)S(1)}, u32[]{:S(2)}, u32[]{:S(2)}) collective-permute-start(f32[1,32]{1,0:T(1,128)S(1)} %bitcast.10), channel_id=1, source_target_pairs={{0,8},{8,0},{16,24},{24,16},{1,9},{9,1},{17,25},{25,17},{2,10},{10... | collective-permute-start | bytes 392 | tf_op jit(solution)/shard_map/ppermute | solution.py:377
  15.3 8.4 %collective-permute-start = (f32[1,128]{1,0:T(1,128)S(1)}, f32[1,128]{1,0:T(1,128)S(1)}, u32[]{:S(2)}, u32[]{:S(2)}) collective-permute-start(f32[1,128]{1,0:T(1,128)S(1)} %bitcast.12), channel_id=1, source_target_pairs={{0,1},{1,0},{2,3},{3,2},{4,5},{5,4},{6,7},{7,6},{8,9},{9,8},{10,11... | collective-permute-start | bytes 1544 | tf_op jit(solution)/shard_map/ppermute | solution.py:377
  19.9 3.7 %collective-permute-start.4 = (f32[2,32]{1,0:T(2,128)S(1)}, f32[2,32]{1,0:T(2,128)S(1)}, u32[]{:S(2)}, u32[]{:S(2)}) collective-permute-start(f32[2,32]{1,0:T(2,128)S(1)} %pad_maximum_fusion.4), channel_id=1, source_target_pairs={{0,16},{8,24},{16,0},{24,8},{1,17},{9,25},{17,1},{25,9},{2,18},{10... | collective-permute-start | bytes 776 | tf_op jit(solution)/shard_map/ppermute | solution.py:377
  23.7 6.9 %collective-permute-start.1 = (f32[2,128]{1,0:T(2,128)S(1)}, f32[2,128]{1,0:T(2,128)S(1)}, u32[]{:S(2)}, u32[]{:S(2)}) collective-permute-start(f32[2,128]{1,0:T(2,128)S(1)} %pad_maximum_fusion.3), channel_id=1, source_target_pairs={{0,2},{1,3},{2,0},{3,1},{4,6},{5,7},{6,4},{7,5},{8,10},{9,11},{10,... | collective-permute-start | bytes 3080 | tf_op jit(solution)/shard_map/ppermute | solution.py:377
  30.6 4.6 %copy-start.2 = (f32[128]{0:T(128)S(1)}, f32[128]{0:T(128)}, u32[]{:S(2)}) copy-start(f32[128]{0:T(128)} %constant.33.clone) | copy-start | bytes 1540
  30.6 4.6 %copy-start.3 = (f32[128]{0:T(128)S(1)}, f32[128]{0:T(128)}, u32[]{:S(2)}) copy-start(f32[128]{0:T(128)} %constant.32.clone) | copy-start | bytes 1540
  30.6 8.6 %collective-permute-start.2 = (f32[4,128]{1,0:T(4,128)S(1)}, f32[4,128]{1,0:T(4,128)S(1)}, u32[]{:S(2)}, u32[]{:S(2)}) collective-permute-start(f32[4,128]{1,0:T(4,128)S(1)} %pad_maximum_fusion.1), channel_id=1, source_target_pairs={{0,4},{1,5},{2,6},{3,7},{4,0},{5,1},{6,2},{7,3},{8,12},{9,13},{10,... | collective-permute-start | bytes 6152 | tf_op jit(solution)/shard_map/ppermute | solution.py:377
  42.2 30.1 %copy-start = (bf16[7,256,256]{2,1,0:T(8,128)(2,1)S(1)}, bf16[7,256,256]{2,1,0:T(8,128)(2,1)}, u32[]{:S(2)}) copy-start(bf16[7,256,256]{2,1,0:T(8,128)(2,1)} %constant.34.clone.m_ref) | copy-start | bytes 2752516

commit v20 on v18

--- a/solution.py
+++ b/solution.py
@@ -162,7 +162,6 @@
     return (slice(first * 16, first * 16 + 16), slice(second * 16, second * 16 + 16))
 
 
-PIECE = 64
 SPAN = 8
 BLOCK = 32
 VMEM = pl.BlockSpec(memory_space=pltpu.VMEM)
@@ -175,15 +174,14 @@
     levels = m_ref.shape[0]
     a_copy = pltpu.make_async_copy(a_hbm, a_ref, a_sem)
     x_copies = []
-    for piece in range(cols // PIECE):
-        for at in range(0, rows, SPAN):
-            own = (pl.ds(at, SPAN), pl.ds(piece * PIECE, PIECE))
-            sem = x_sems.at[len(x_copies)]
-            x_copies.append(pltpu.make_async_copy(x_hbm.at[own], x_ref.at[own], sem))
+    for piece in range(rows // SPAN):
+        own = pl.ds(piece * SPAN, SPAN)
+        x_copies.append(pltpu.make_async_copy(x_hbm.at[own], x_ref.at[own], x_sems.at[piece]))
     m_copies = [
         pltpu.make_async_copy(m_hbm.at[i], m_ref.at[i], m_sems.at[i]) for i in range(levels)
     ]
-    for copy in (a_copy, m_copies[0], *x_copies, *m_copies[1:]):
+    loads = (a_copy, *m_copies, *x_copies)
+    for copy in loads:
         copy.start()
 
     def expand(level):
@@ -206,22 +204,11 @@
         )
 
     shuffle = shuffle_matrix()
-    m_copies[0].wait()
-    each = rows // SPAN
-    for piece in range(cols // PIECE):
-        for copy in x_copies[piece * each : (piece + 1) * each]:
-            copy.wait()
-        if piece == 0:
-            a_copy.wait()
-            expand(0)
-            cosines, sines = halved(rotation(column_of(a_ref[...], cols)))
-        for begin in range(piece * PIECE, (piece + 1) * PIECE, BLOCK):
-            level_on(0, begin)
-    for copy in m_copies[1:]:
+    for copy in loads:
         copy.wait()
-    for level in range(1, levels):
+    cosines, sines = halved(rotation(column_of(a_ref[...], cols)))
+    for level in range(levels):
         expand(level)
-    for level in range(1, levels):
         for begin in range(0, cols, BLOCK):
             level_on(level, begin)
 
@@ -253,7 +240,7 @@
             pltpu.VMEM(matrices.shape, x.dtype),
             pltpu.VMEM((levels, 2 * WIDE, 2 * WIDE), x.dtype),
             pltpu.SemaphoreType.DMA,
-            pltpu.SemaphoreType.DMA((cols // PIECE * (rows // SPAN),)),
+            pltpu.SemaphoreType.DMA((rows // SPAN,)),
             pltpu.SemaphoreType.DMA((levels,)),
         ],
         compiler_params=PARAMS,

time: 75.2 us -> 74.9 us (level)
  no operation moved by 1% of the time
where the time goes in v20:
time: 74.9 us; the launch traced here: 74.7 us
  blocking collectives  30.1 us (40%)
  starting transfers between devices  17.3 us (23%)
  waiting for transfers between devices  16.1 us (21%)
  Pallas kernels  9.59 us (13%)
  local copies, waits for them, and re-layouts  0.84 us (1%)
    all_to_all x1, blocking collectives, traded(): return lax.all_to_all(state, ('src', 'tgt'), 0, 0, tiled=True)  30.1 us
    ppermute x5, waiting for transfers between devices, gathered(): other = lax.ppermute(values, axis, [(i, i ^ apart) for i in range(count)])  15.2 us
    ppermute x5, starting transfers between devices, gathered(): other = lax.ppermute(values, axis, [(i, i ^ apart) for i in range(count)])  10 us
    all_to_all x1, starting transfers between devices, traded(): return lax.all_to_all(state, ('src', 'tgt'), 0, 0, tiled=True)  7.3 us
    pallas_call x1, Pallas kernels, source_levels(): pl.pallas_call(source_kernel, out_shape=jax.ShapeDtypeStruct((cols, rows,...  4.59 us
    pallas_call x1, Pallas kernels, target_levels(): pl.pallas_call(target_kernel, out_shape=jax.ShapeDtypeStruct(shape, x.dty...  3.31 us
    pallas_call x1, Pallas kernels, middle_levels(): pl.pallas_call(functools.partial(middle_kernel, levels, rows), out_shape=...  1.69 us
  transfers between devices with their start and end apart: 6, of which 5 were waited for; matrix products, arithmetic and copies ran while one was open for 1% of the time, Pallas kernels for 0%

profile of v20, /device:TPU:0, one launch (start us, length us, event | category | flops | bytes accessed | tf_op | source)
XLA Modules:
  0.0 74.7 jit_solution(2370200179794809004)
XLA Ops:
  0.0 4.6 %shard_map.118 = bf16[128,32,128]{2,1,0:T(8,128)(2,1)} custom-call(f32[1,128]{1,0:T(1,128)} %bitcast.11, bf16[32,128,128]{2,1,0:T(8,128)(2,1)} %x_hbm.1, bf16[5,128,256]{2,1,0:T(8,128)(2,1)} %constant.30.clone.m_hbm), custom_call_target="tpu_custom_call" | custom-call | tf_op jit(solution)/shard_map/pallas_call | solution.py:232
  4.6 0.0 copy-start.1
  4.6 7.3 %all-to-all-start = ((bf16[32,128,128]{2,1,0:T(8,128)(2,1)}), bf16[32,128,128]{2,1,0:T(8,128)(2,1)S(1)}, u32[]{:S(2)}, u32[]{:S(2)}) async-start(bf16[32,128,128]{2,1,0:T(8,128)(2,1)} %bitcast.1), calls=%async_computation | async-start | bytes 2097152 | tf_op jit(solution)/shard_map/all_to_all | solution.py:389
  11.9 0.0 copy-start.4
  11.9 0.6 copy-done.4
  12.6 0.0 copy-start.5
  12.6 1.8 %collective-permute-start.3 = (f32[1,32]{1,0:T(1,128)S(1)}, f32[1,32]{1,0:T(1,128)S(1)}, u32[]{:S(2)}, u32[]{:S(2)}) collective-permute-start(f32[1,32]{1,0:T(1,128)S(1)} %bitcast.10), channel_id=1, source_target_pairs={{0,8},{8,0},{16,24},{24,16},{1,9},{9,1},{17,25},{25,17},{2,10},{10... | collective-permute-start | bytes 392 | tf_op jit(solution)/shard_map/ppermute | solution.py:365
  14.4 0.0 copy-done.5
  14.4 0.0 collective-permute-start
  14.4 4.6 %collective-permute-done.3 = f32[1,32]{1,0:T(1,128)S(1)} collective-permute-done((f32[1,32]{1,0:T(1,128)S(1)}, f32[1,32]{1,0:T(1,128)S(1)}, u32[]{:S(2)}, u32[]{:S(2)}) %collective-permute-start.3) | collective-permute-done | bytes 160 | tf_op jit(solution)/shard_map/ppermute | solution.py:365
  19.0 1.5 %collective-permute-start.4 = (f32[2,32]{1,0:T(2,128)S(1)}, f32[2,32]{1,0:T(2,128)S(1)}, u32[]{:S(2)}, u32[]{:S(2)}) collective-permute-start(f32[2,32]{1,0:T(2,128)S(1)} %pad_maximum_fusion.4), channel_id=1, source_target_pairs={{0,16},{8,24},{16,0},{24,8},{1,17},{9,25},{17,1},{25,9},{2,18},{10... | collective-permute-start | bytes 776 | tf_op jit(solution)/shard_map/ppermute | solution.py:365
  20.5 2.2 %collective-permute-done.4 = f32[2,32]{1,0:T(2,128)S(1)} collective-permute-done((f32[2,32]{1,0:T(2,128)S(1)}, f32[2,32]{1,0:T(2,128)S(1)}, u32[]{:S(2)}, u32[]{:S(2)}) %collective-permute-start.4) | collective-permute-done | bytes 288 | tf_op jit(solution)/shard_map/ppermute | solution.py:365
  22.7 0.0 collective-permute-done
  22.8 2.1 %collective-permute-start.1 = (f32[2,128]{1,0:T(2,128)S(1)}, f32[2,128]{1,0:T(2,128)S(1)}, u32[]{:S(2)}, u32[]{:S(2)}) collective-permute-start(f32[2,128]{1,0:T(2,128)S(1)} %pad_maximum_fusion.3), channel_id=1, source_target_pairs={{0,2},{1,3},{2,0},{3,1},{4,6},{5,7},{6,4},{7,5},{8,10},{9,11},{10,... | collective-permute-start | bytes 3080 | tf_op jit(solution)/shard_map/ppermute | solution.py:365
  24.9 4.7 %collective-permute-done.1 = f32[2,128]{1,0:T(2,128)S(1)} collective-permute-done((f32[2,128]{1,0:T(2,128)S(1)}, f32[2,128]{1,0:T(2,128)S(1)}, u32[]{:S(2)}, u32[]{:S(2)}) %collective-permute-start.1) | collective-permute-done | bytes 1056 | tf_op jit(solution)/shard_map/ppermute | solution.py:365
  29.6 0.0 copy-start.2
  29.6 0.0 copy-start.3
  29.7 4.6 %collective-permute-start.2 = (f32[4,128]{1,0:T(4,128)S(1)}, f32[4,128]{1,0:T(4,128)S(1)}, u32[]{:S(2)}, u32[]{:S(2)}) collective-permute-start(f32[4,128]{1,0:T(4,128)S(1)} %pad_maximum_fusion.1), channel_id=1, source_target_pairs={{0,4},{1,5},{2,6},{3,7},{4,0},{5,1},{6,2},{7,3},{8,12},{9,13},{10,... | collective-permute-start | bytes 6152 | tf_op jit(solution)/shard_map/ppermute | solution.py:365
  34.2 0.0 copy-done.2
  34.2 0.0 copy-done.3
  34.2 0.3 fusion
  34.6 3.7 %collective-permute-done.2 = f32[4,128]{1,0:T(4,128)S(1)} collective-permute-done((f32[4,128]{1,0:T(4,128)S(1)}, f32[4,128]{1,0:T(4,128)S(1)}, u32[]{:S(2)}, u32[]{:S(2)}) %collective-permute-start.2) | collective-permute-done | bytes 2080 | tf_op jit(solution)/shard_map/ppermute | solution.py:365
  38.3 0.1 constant_dynamic-slice_fusion
  38.4 0.1 mul.78
  38.4 0.2 fusion.2
  38.6 0.9 %all-to-all-done.x_ref = bf16[32,128,128]{2,1,0:T(8,128)(2,1)S(1)} async-done(((bf16[32,128,128]{2,1,0:T(8,128)(2,1)}), bf16[32,128,128]{2,1,0:T(8,128)(2,1)S(1)}, u32[]{:S(2)}, u32[]{:S(2)}) %all-to-all-start) | async-done | bytes 1048608 | tf_op jit(solution)/shard_map/all_to_all | solution.py:389
  39.6 0.0 copy-done.1
  39.6 1.7 %shard_map.119 = bf16[32,128,128]{2,1,0:T(8,128)(2,1)S(1)} custom-call(bf16[32,128,128]{2,1,0:T(8,128)(2,1)S(1)} %all-to-all-done.x_ref, bf16[5,256,256]{2,1,0:T(8,128)(2,1)S(1)} %copy-done.1, f32[32,128]{1,0:T(8,128)S(1)} %get-tuple-element.24.cs_ref, f32[32,128]{1,0:T(8,128)S(1)} %get-tuple-element.21.ss_ref, f32[4,32,128]{2,1,0:T(8,128)S(1)} %get-tuple-element.14.ct_ref, ...), custom_call_target="tpu_custom_call" | custom-call | tf_op jit(solution)/shard_map/pallas_call | solution.py:284
  41.3 0.0 copy-start
  41.3 30.1 %all_to_all.10 = bf16[32,128,128]{2,1,0:T(8,128)(2,1)S(1)} all-to-all(bf16[32,128,128]{2,1,0:T(8,128)(2,1)S(1)} %shard_map.119), channel_id=1, replica_groups=mesh['src'=4,'tgt'=8] {'src','tgt'}, dimensions={0} | all-to-all | bytes 2097152 | tf_op jit(solution)/shard_map/all_to_all | solution.py:389
  71.4 0.0 copy-done
  71.4 3.3 %shard_map.120 = bf16[32,128,128]{2,1,0:T(8,128)(2,1)} custom-call(bf16[7,256,256]{2,1,0:T(8,128)(2,1)S(1)} %copy-done, f32[32,128]{1,0:T(8,128)S(1)} %get-tuple-element.23.c_ref, f32[32,128]{1,0:T(8,128)S(1)} %get-tuple-element.22.s_ref, bf16[128,32,128]{2,1,0:T(8,128)(2,1)S(1)} %bitcast.9), custom_call_target="tpu_custom_call" | custom-call | tf_op jit(solution)/shard_map/pallas_call | solution.py:345
  (10 shorter events, 0.1 us)
Async XLA Ops:
  4.6 35.0 %copy-start.1 = (bf16[5,256,256]{2,1,0:T(8,128)(2,1)S(1)}, bf16[5,256,256]{2,1,0:T(8,128)(2,1)}, u32[]{:S(2)}) copy-start(bf16[5,256,256]{2,1,0:T(8,128)(2,1)} %constant.31.clone.m_ref) | copy-start | bytes 1966084
  4.6 34.9 %all-to-all-start = ((bf16[32,128,128]{2,1,0:T(8,128)(2,1)}), bf16[32,128,128]{2,1,0:T(8,128)(2,1)S(1)}, u32[]{:S(2)}, u32[]{:S(2)}) async-start(bf16[32,128,128]{2,1,0:T(8,128)(2,1)} %bitcast.1), calls=%async_computation | async-start | bytes 2097152 | tf_op jit(solution)/shard_map/all_to_all | solution.py:389
  11.9 0.7 copy-start.4
  12.6 1.8 %copy-start.5 = (f32[128]{0:T(128)S(1)}, f32[128]{0:T(128)}, u32[]{:S(2)}) copy-start(f32[128]{0:T(128)} %param.13) | copy-start | bytes 1540
  12.6 6.4 %collective-permute-start.3 = (f32[1,32]{1,0:T(1,128)S(1)}, f32[1,32]{1,0:T(1,128)S(1)}, u32[]{:S(2)}, u32[]{:S(2)}) collective-permute-start(f32[1,32]{1,0:T(1,128)S(1)} %bitcast.10), channel_id=1, source_target_pairs={{0,8},{8,0},{16,24},{24,16},{1,9},{9,1},{17,25},{25,17},{2,10},{10... | collective-permute-start | bytes 392 | tf_op jit(solution)/shard_map/ppermute | solution.py:365
  14.4 8.4 %collective-permute-start = (f32[1,128]{1,0:T(1,128)S(1)}, f32[1,128]{1,0:T(1,128)S(1)}, u32[]{:S(2)}, u32[]{:S(2)}) collective-permute-start(f32[1,128]{1,0:T(1,128)S(1)} %bitcast.12), channel_id=1, source_target_pairs={{0,1},{1,0},{2,3},{3,2},{4,5},{5,4},{6,7},{7,6},{8,9},{9,8},{10,11... | collective-permute-start | bytes 1544 | tf_op jit(solution)/shard_map/ppermute | solution.py:365
  19.0 3.7 %collective-permute-start.4 = (f32[2,32]{1,0:T(2,128)S(1)}, f32[2,32]{1,0:T(2,128)S(1)}, u32[]{:S(2)}, u32[]{:S(2)}) collective-permute-start(f32[2,32]{1,0:T(2,128)S(1)} %pad_maximum_fusion.4), channel_id=1, source_target_pairs={{0,16},{8,24},{16,0},{24,8},{1,17},{9,25},{17,1},{25,9},{2,18},{10... | collective-permute-start | bytes 776 | tf_op jit(solution)/shard_map/ppermute | solution.py:365
  22.8 6.9 %collective-permute-start.1 = (f32[2,128]{1,0:T(2,128)S(1)}, f32[2,128]{1,0:T(2,128)S(1)}, u32[]{:S(2)}, u32[]{:S(2)}) collective-permute-start(f32[2,128]{1,0:T(2,128)S(1)} %pad_maximum_fusion.3), channel_id=1, source_target_pairs={{0,2},{1,3},{2,0},{3,1},{4,6},{5,7},{6,4},{7,5},{8,10},{9,11},{10,... | collective-permute-start | bytes 3080 | tf_op jit(solution)/shard_map/ppermute | solution.py:365
  29.6 4.6 %copy-start.2 = (f32[128]{0:T(128)S(1)}, f32[128]{0:T(128)}, u32[]{:S(2)}) copy-start(f32[128]{0:T(128)} %constant.33.clone) | copy-start | bytes 1540
  29.6 4.6 %copy-start.3 = (f32[128]{0:T(128)S(1)}, f32[128]{0:T(128)}, u32[]{:S(2)}) copy-start(f32[128]{0:T(128)} %constant.32.clone) | copy-start | bytes 1540
  29.7 8.6 %collective-permute-start.2 = (f32[4,128]{1,0:T(4,128)S(1)}, f32[4,128]{1,0:T(4,128)S(1)}, u32[]{:S(2)}, u32[]{:S(2)}) collective-permute-start(f32[4,128]{1,0:T(4,128)S(1)} %pad_maximum_fusion.1), channel_id=1, source_target_pairs={{0,4},{1,5},{2,6},{3,7},{4,0},{5,1},{6,2},{7,3},{8,12},{9,13},{10,... | collective-permute-start | bytes 6152 | tf_op jit(solution)/shard_map/ppermute | solution.py:365
  41.3 30.1 %copy-start = (bf16[7,256,256]{2,1,0:T(8,128)(2,1)S(1)}, bf16[7,256,256]{2,1,0:T(8,128)(2,1)}, u32[]{:S(2)}) copy-start(bf16[7,256,256]{2,1,0:T(8,128)(2,1)} %constant.34.clone.m_ref) | copy-start | bytes 2752516

commit v21 on v20

--- a/solution.py
+++ b/solution.py
@@ -180,8 +180,7 @@
     m_copies = [
         pltpu.make_async_copy(m_hbm.at[i], m_ref.at[i], m_sems.at[i]) for i in range(levels)
     ]
-    loads = (a_copy, *m_copies, *x_copies)
-    for copy in loads:
+    for copy in (a_copy, *m_copies, *x_copies):
         copy.start()
 
     def expand(level):
@@ -204,11 +203,14 @@
         )
 
     shuffle = shuffle_matrix()
-    for copy in loads:
+    for copy in (a_copy, *m_copies):
         copy.wait()
     cosines, sines = halved(rotation(column_of(a_ref[...], cols)))
     for level in range(levels):
         expand(level)
+    for copy in x_copies:
+        copy.wait()
+    for level in range(levels):
         for begin in range(0, cols, BLOCK):
             level_on(level, begin)
 

time: 74.9 us -> 74.8 us (level)
  no operation moved by 1% of the time
where the time goes in v21:
time: 74.8 us; the launch traced here: 74.5 us
  blocking collectives  30.1 us (40%)
  starting transfers between devices  17.3 us (23%)
  waiting for transfers between devices  16.1 us (22%)
  Pallas kernels  9.44 us (13%)
  local copies, waits for them, and re-layouts  0.84 us (1%)
    all_to_all x1, blocking collectives, traded(): return lax.all_to_all(state, ('src', 'tgt'), 0, 0, tiled=True)  30.1 us
    ppermute x5, waiting for transfers between devices, gathered(): other = lax.ppermute(values, axis, [(i, i ^ apart) for i in range(count)])  15.2 us
    ppermute x5, starting transfers between devices, gathered(): other = lax.ppermute(values, axis, [(i, i ^ apart) for i in range(count)])  10 us
    all_to_all x1, starting transfers between devices, traded(): return lax.all_to_all(state, ('src', 'tgt'), 0, 0, tiled=True)  7.3 us
    pallas_call x1, Pallas kernels, source_levels(): pl.pallas_call(source_kernel, out_shape=jax.ShapeDtypeStruct((cols, rows,...  4.44 us
    pallas_call x1, Pallas kernels, target_levels(): pl.pallas_call(target_kernel, out_shape=jax.ShapeDtypeStruct(shape, x.dty...  3.31 us
    pallas_call x1, Pallas kernels, middle_levels(): pl.pallas_call(functools.partial(middle_kernel, levels, rows), out_shape=...  1.69 us
  transfers between devices with their start and end apart: 6, of which 5 were waited for; matrix products, arithmetic and copies ran while one was open for 1% of the time, Pallas kernels for 0%

profile of v21, /device:TPU:0, one launch (start us, length us, event | category | flops | bytes accessed | tf_op | source)
XLA Modules:
  0.0 74.5 jit_solution(2380366557025258680)
XLA Ops:
  0.0 4.4 %shard_map.118 = bf16[128,32,128]{2,1,0:T(8,128)(2,1)} custom-call(f32[1,128]{1,0:T(1,128)} %bitcast.11, bf16[32,128,128]{2,1,0:T(8,128)(2,1)} %x_hbm.1, bf16[5,128,256]{2,1,0:T(8,128)(2,1)} %constant.30.clone.m_hbm), custom_call_target="tpu_custom_call" | custom-call | tf_op jit(solution)/shard_map/pallas_call | solution.py:234
  4.4 0.0 copy-start.1
  4.5 7.3 %all-to-all-start = ((bf16[32,128,128]{2,1,0:T(8,128)(2,1)}), bf16[32,128,128]{2,1,0:T(8,128)(2,1)S(1)}, u32[]{:S(2)}, u32[]{:S(2)}) async-start(bf16[32,128,128]{2,1,0:T(8,128)(2,1)} %bitcast.1), calls=%async_computation | async-start | bytes 2097152 | tf_op jit(solution)/shard_map/all_to_all | solution.py:391
  11.8 0.0 copy-start.4
  11.8 0.6 copy-done.4
  12.4 0.0 copy-start.5
  12.4 1.8 %collective-permute-start.3 = (f32[1,32]{1,0:T(1,128)S(1)}, f32[1,32]{1,0:T(1,128)S(1)}, u32[]{:S(2)}, u32[]{:S(2)}) collective-permute-start(f32[1,32]{1,0:T(1,128)S(1)} %bitcast.10), channel_id=1, source_target_pairs={{0,8},{8,0},{16,24},{24,16},{1,9},{9,1},{17,25},{25,17},{2,10},{10... | collective-permute-start | bytes 392 | tf_op jit(solution)/shard_map/ppermute | solution.py:367
  14.2 0.0 copy-done.5
  14.2 0.0 collective-permute-start
  14.2 4.6 %collective-permute-done.3 = f32[1,32]{1,0:T(1,128)S(1)} collective-permute-done((f32[1,32]{1,0:T(1,128)S(1)}, f32[1,32]{1,0:T(1,128)S(1)}, u32[]{:S(2)}, u32[]{:S(2)}) %collective-permute-start.3) | collective-permute-done | bytes 160 | tf_op jit(solution)/shard_map/ppermute | solution.py:367
  18.8 1.5 %collective-permute-start.4 = (f32[2,32]{1,0:T(2,128)S(1)}, f32[2,32]{1,0:T(2,128)S(1)}, u32[]{:S(2)}, u32[]{:S(2)}) collective-permute-start(f32[2,32]{1,0:T(2,128)S(1)} %pad_maximum_fusion.4), channel_id=1, source_target_pairs={{0,16},{8,24},{16,0},{24,8},{1,17},{9,25},{17,1},{25,9},{2,18},{10... | collective-permute-start | bytes 776 | tf_op jit(solution)/shard_map/ppermute | solution.py:367
  20.4 2.2 %collective-permute-done.4 = f32[2,32]{1,0:T(2,128)S(1)} collective-permute-done((f32[2,32]{1,0:T(2,128)S(1)}, f32[2,32]{1,0:T(2,128)S(1)}, u32[]{:S(2)}, u32[]{:S(2)}) %collective-permute-start.4) | collective-permute-done | bytes 288 | tf_op jit(solution)/shard_map/ppermute | solution.py:367
  22.6 0.0 collective-permute-done
  22.6 2.1 %collective-permute-start.1 = (f32[2,128]{1,0:T(2,128)S(1)}, f32[2,128]{1,0:T(2,128)S(1)}, u32[]{:S(2)}, u32[]{:S(2)}) collective-permute-start(f32[2,128]{1,0:T(2,128)S(1)} %pad_maximum_fusion.3), channel_id=1, source_target_pairs={{0,2},{1,3},{2,0},{3,1},{4,6},{5,7},{6,4},{7,5},{8,10},{9,11},{10,... | collective-permute-start | bytes 3080 | tf_op jit(solution)/shard_map/ppermute | solution.py:367
  24.8 4.7 %collective-permute-done.1 = f32[2,128]{1,0:T(2,128)S(1)} collective-permute-done((f32[2,128]{1,0:T(2,128)S(1)}, f32[2,128]{1,0:T(2,128)S(1)}, u32[]{:S(2)}, u32[]{:S(2)}) %collective-permute-start.1) | collective-permute-done | bytes 1056 | tf_op jit(solution)/shard_map/ppermute | solution.py:367
  29.5 0.0 copy-start.2
  29.5 0.0 copy-start.3
  29.5 4.6 %collective-permute-start.2 = (f32[4,128]{1,0:T(4,128)S(1)}, f32[4,128]{1,0:T(4,128)S(1)}, u32[]{:S(2)}, u32[]{:S(2)}) collective-permute-start(f32[4,128]{1,0:T(4,128)S(1)} %pad_maximum_fusion.1), channel_id=1, source_target_pairs={{0,4},{1,5},{2,6},{3,7},{4,0},{5,1},{6,2},{7,3},{8,12},{9,13},{10,... | collective-permute-start | bytes 6152 | tf_op jit(solution)/shard_map/ppermute | solution.py:367
  34.1 0.0 copy-done.2
  34.1 0.0 copy-done.3
  34.1 0.3 fusion
  34.4 3.7 %collective-permute-done.2 = f32[4,128]{1,0:T(4,128)S(1)} collective-permute-done((f32[4,128]{1,0:T(4,128)S(1)}, f32[4,128]{1,0:T(4,128)S(1)}, u32[]{:S(2)}, u32[]{:S(2)}) %collective-permute-start.2) | collective-permute-done | bytes 2080 | tf_op jit(solution)/shard_map/ppermute | solution.py:367
  38.1 0.1 constant_dynamic-slice_fusion
  38.2 0.1 mul.78
  38.3 0.2 fusion.2
  38.5 0.9 %all-to-all-done.x_ref = bf16[32,128,128]{2,1,0:T(8,128)(2,1)S(1)} async-done(((bf16[32,128,128]{2,1,0:T(8,128)(2,1)}), bf16[32,128,128]{2,1,0:T(8,128)(2,1)S(1)}, u32[]{:S(2)}, u32[]{:S(2)}) %all-to-all-start) | async-done | bytes 1048608 | tf_op jit(solution)/shard_map/all_to_all | solution.py:391
  39.4 0.0 copy-done.1
  39.4 1.7 %shard_map.119 = bf16[32,128,128]{2,1,0:T(8,128)(2,1)S(1)} custom-call(bf16[32,128,128]{2,1,0:T(8,128)(2,1)S(1)} %all-to-all-done.x_ref, bf16[5,256,256]{2,1,0:T(8,128)(2,1)S(1)} %copy-done.1, f32[32,128]{1,0:T(8,128)S(1)} %get-tuple-element.24.cs_ref, f32[32,128]{1,0:T(8,128)S(1)} %get-tuple-element.21.ss_ref, f32[4,32,128]{2,1,0:T(8,128)S(1)} %get-tuple-element.14.ct_ref, ...), custom_call_target="tpu_custom_call" | custom-call | tf_op jit(solution)/shard_map/pallas_call | solution.py:286
  41.1 0.0 copy-start
  41.1 30.1 %all_to_all.10 = bf16[32,128,128]{2,1,0:T(8,128)(2,1)S(1)} all-to-all(bf16[32,128,128]{2,1,0:T(8,128)(2,1)S(1)} %shard_map.119), channel_id=1, replica_groups=mesh['src'=4,'tgt'=8] {'src','tgt'}, dimensions={0} | all-to-all | bytes 2097152 | tf_op jit(solution)/shard_map/all_to_all | solution.py:391
  71.2 0.0 copy-done
  71.2 3.3 %shard_map.120 = bf16[32,128,128]{2,1,0:T(8,128)(2,1)} custom-call(bf16[7,256,256]{2,1,0:T(8,128)(2,1)S(1)} %copy-done, f32[32,128]{1,0:T(8,128)S(1)} %get-tuple-element.23.c_ref, f32[32,128]{1,0:T(8,128)S(1)} %get-tuple-element.22.s_ref, bf16[128,32,128]{2,1,0:T(8,128)(2,1)S(1)} %bitcast.9), custom_call_target="tpu_custom_call" | custom-call | tf_op jit(solution)/shard_map/pallas_call | solution.py:347
  (10 shorter events, 0.1 us)
Async XLA Ops:
  4.4 35.0 %copy-start.1 = (bf16[5,256,256]{2,1,0:T(8,128)(2,1)S(1)}, bf16[5,256,256]{2,1,0:T(8,128)(2,1)}, u32[]{:S(2)}) copy-start(bf16[5,256,256]{2,1,0:T(8,128)(2,1)} %constant.31.clone.m_ref) | copy-start | bytes 1966084
  4.5 34.9 %all-to-all-start = ((bf16[32,128,128]{2,1,0:T(8,128)(2,1)}), bf16[32,128,128]{2,1,0:T(8,128)(2,1)S(1)}, u32[]{:S(2)}, u32[]{:S(2)}) async-start(bf16[32,128,128]{2,1,0:T(8,128)(2,1)} %bitcast.1), calls=%async_computation | async-start | bytes 2097152 | tf_op jit(solution)/shard_map/all_to_all | solution.py:391
  11.8 0.7 copy-start.4
  12.4 1.8 %copy-start.5 = (f32[128]{0:T(128)S(1)}, f32[128]{0:T(128)}, u32[]{:S(2)}) copy-start(f32[128]{0:T(128)} %param.13) | copy-start | bytes 1540
  12.4 6.4 %collective-permute-start.3 = (f32[1,32]{1,0:T(1,128)S(1)}, f32[1,32]{1,0:T(1,128)S(1)}, u32[]{:S(2)}, u32[]{:S(2)}) collective-permute-start(f32[1,32]{1,0:T(1,128)S(1)} %bitcast.10), channel_id=1, source_target_pairs={{0,8},{8,0},{16,24},{24,16},{1,9},{9,1},{17,25},{25,17},{2,10},{10... | collective-permute-start | bytes 392 | tf_op jit(solution)/shard_map/ppermute | solution.py:367
  14.2 8.4 %collective-permute-start = (f32[1,128]{1,0:T(1,128)S(1)}, f32[1,128]{1,0:T(1,128)S(1)}, u32[]{:S(2)}, u32[]{:S(2)}) collective-permute-start(f32[1,128]{1,0:T(1,128)S(1)} %bitcast.12), channel_id=1, source_target_pairs={{0,1},{1,0},{2,3},{3,2},{4,5},{5,4},{6,7},{7,6},{8,9},{9,8},{10,11... | collective-permute-start | bytes 1544 | tf_op jit(solution)/shard_map/ppermute | solution.py:367
  18.8 3.7 %collective-permute-start.4 = (f32[2,32]{1,0:T(2,128)S(1)}, f32[2,32]{1,0:T(2,128)S(1)}, u32[]{:S(2)}, u32[]{:S(2)}) collective-permute-start(f32[2,32]{1,0:T(2,128)S(1)} %pad_maximum_fusion.4), channel_id=1, source_target_pairs={{0,16},{8,24},{16,0},{24,8},{1,17},{9,25},{17,1},{25,9},{2,18},{10... | collective-permute-start | bytes 776 | tf_op jit(solution)/shard_map/ppermute | solution.py:367
  22.6 6.9 %collective-permute-start.1 = (f32[2,128]{1,0:T(2,128)S(1)}, f32[2,128]{1,0:T(2,128)S(1)}, u32[]{:S(2)}, u32[]{:S(2)}) collective-permute-start(f32[2,128]{1,0:T(2,128)S(1)} %pad_maximum_fusion.3), channel_id=1, source_target_pairs={{0,2},{1,3},{2,0},{3,1},{4,6},{5,7},{6,4},{7,5},{8,10},{9,11},{10,... | collective-permute-start | bytes 3080 | tf_op jit(solution)/shard_map/ppermute | solution.py:367
  29.5 4.6 %copy-start.2 = (f32[128]{0:T(128)S(1)}, f32[128]{0:T(128)}, u32[]{:S(2)}) copy-start(f32[128]{0:T(128)} %constant.33.clone) | copy-start | bytes 1540
  29.5 4.6 %copy-start.3 = (f32[128]{0:T(128)S(1)}, f32[128]{0:T(128)}, u32[]{:S(2)}) copy-start(f32[128]{0:T(128)} %constant.32.clone) | copy-start | bytes 1540
  29.5 8.6 %collective-permute-start.2 = (f32[4,128]{1,0:T(4,128)S(1)}, f32[4,128]{1,0:T(4,128)S(1)}, u32[]{:S(2)}, u32[]{:S(2)}) collective-permute-start(f32[4,128]{1,0:T(4,128)S(1)} %pad_maximum_fusion.1), channel_id=1, source_target_pairs={{0,4},{1,5},{2,6},{3,7},{4,0},{5,1},{6,2},{7,3},{8,12},{9,13},{10,... | collective-permute-start | bytes 6152 | tf_op jit(solution)/shard_map/ppermute | solution.py:367
  41.1 30.1 %copy-start = (bf16[7,256,256]{2,1,0:T(8,128)(2,1)S(1)}, bf16[7,256,256]{2,1,0:T(8,128)(2,1)}, u32[]{:S(2)}) copy-start(bf16[7,256,256]{2,1,0:T(8,128)(2,1)} %constant.34.clone.m_ref) | copy-start | bytes 2752516

commit v22 on v21

--- a/solution.py
+++ b/solution.py
@@ -169,7 +169,7 @@
 PARAMS = pltpu.CompilerParams(vmem_limit_bytes=32 << 20)
 
 
-def source_kernel(a_hbm, x_hbm, m_hbm, o_ref, a_ref, x_ref, m_ref, w_ref, a_sem, x_sems, m_sems):
+def source_kernel(a_hbm, x_hbm, m_hbm, o_ref, a_ref, x_ref, m_ref, w_ref, a_sem, x_sems, m_sem):
     rows, cols, _ = x_ref.shape
     levels = m_ref.shape[0]
     a_copy = pltpu.make_async_copy(a_hbm, a_ref, a_sem)
@@ -177,10 +177,8 @@
     for piece in range(rows // SPAN):
         own = pl.ds(piece * SPAN, SPAN)
         x_copies.append(pltpu.make_async_copy(x_hbm.at[own], x_ref.at[own], x_sems.at[piece]))
-    m_copies = [
-        pltpu.make_async_copy(m_hbm.at[i], m_ref.at[i], m_sems.at[i]) for i in range(levels)
-    ]
-    for copy in (a_copy, *m_copies, *x_copies):
+    m_copy = pltpu.make_async_copy(m_hbm, m_ref, m_sem)
+    for copy in (a_copy, m_copy, *x_copies):
         copy.start()
 
     def expand(level):
@@ -203,7 +201,7 @@
         )
 
     shuffle = shuffle_matrix()
-    for copy in (a_copy, *m_copies):
+    for copy in (a_copy, m_copy):
         copy.wait()
     cosines, sines = halved(rotation(column_of(a_ref[...], cols)))
     for level in range(levels):
@@ -243,7 +241,7 @@
             pltpu.VMEM((levels, 2 * WIDE, 2 * WIDE), x.dtype),
             pltpu.SemaphoreType.DMA,
             pltpu.SemaphoreType.DMA((rows // SPAN,)),
-            pltpu.SemaphoreType.DMA((levels,)),
+            pltpu.SemaphoreType.DMA,
         ],
         compiler_params=PARAMS,
     )(*far)

time: 74.8 us -> 74.8 us (level)
  no operation moved by 1% of the time
where the time goes in v22:
time: 74.8 us; the launch traced here: 74.5 us
  blocking collectives  30.1 us (40%)
  starting transfers between devices  17.3 us (23%)
  waiting for transfers between devices  16.1 us (22%)
  Pallas kernels  9.42 us (13%)
  local copies, waits for them, and re-layouts  0.84 us (1%)
    all_to_all x1, blocking collectives, traded(): return lax.all_to_all(state, ('src', 'tgt'), 0, 0, tiled=True)  30.1 us
    ppermute x5, waiting for transfers between devices, gathered(): other = lax.ppermute(values, axis, [(i, i ^ apart) for i in range(count)])  15.2 us
    ppermute x5, starting transfers between devices, gathered(): other = lax.ppermute(values, axis, [(i, i ^ apart) for i in range(count)])  10 us
    all_to_all x1, starting transfers between devices, traded(): return lax.all_to_all(state, ('src', 'tgt'), 0, 0, tiled=True)  7.3 us
    pallas_call x1, Pallas kernels, source_levels(): pl.pallas_call(source_kernel, out_shape=jax.ShapeDtypeStruct((cols, rows,...  4.42 us
    pallas_call x1, Pallas kernels, target_levels(): pl.pallas_call(target_kernel, out_shape=jax.ShapeDtypeStruct(shape, x.dty...  3.31 us
    pallas_call x1, Pallas kernels, middle_levels(): pl.pallas_call(functools.partial(middle_kernel, levels, rows), out_shape=...  1.69 us
  transfers between devices with their start and end apart: 6, of which 5 were waited for; matrix products, arithmetic and copies ran while one was open for 1% of the time, Pallas kernels for 0%

profile of v22, /device:TPU:0, one launch (start us, length us, event | category | flops | bytes accessed | tf_op | source)
XLA Modules:
  0.0 74.5 jit_solution(11326178227010609403)
XLA Ops:
  0.0 4.4 %shard_map.118 = bf16[128,32,128]{2,1,0:T(8,128)(2,1)} custom-call(f32[1,128]{1,0:T(1,128)} %bitcast.11, bf16[32,128,128]{2,1,0:T(8,128)(2,1)} %x_hbm.1, bf16[5,128,256]{2,1,0:T(8,128)(2,1)} %constant.30.clone.m_hbm), custom_call_target="tpu_custom_call" | custom-call | tf_op jit(solution)/shard_map/pallas_call | solution.py:232
  4.4 0.0 copy-start.1
  4.4 7.3 %all-to-all-start = ((bf16[32,128,128]{2,1,0:T(8,128)(2,1)}), bf16[32,128,128]{2,1,0:T(8,128)(2,1)S(1)}, u32[]{:S(2)}, u32[]{:S(2)}) async-start(bf16[32,128,128]{2,1,0:T(8,128)(2,1)} %bitcast.1), calls=%async_computation | async-start | bytes 2097152 | tf_op jit(solution)/shard_map/all_to_all | solution.py:389
  11.8 0.0 copy-start.4
  11.8 0.6 copy-done.4
  12.4 0.0 copy-start.5
  12.4 1.8 %collective-permute-start.3 = (f32[1,32]{1,0:T(1,128)S(1)}, f32[1,32]{1,0:T(1,128)S(1)}, u32[]{:S(2)}, u32[]{:S(2)}) collective-permute-start(f32[1,32]{1,0:T(1,128)S(1)} %bitcast.10), channel_id=1, source_target_pairs={{0,8},{8,0},{16,24},{24,16},{1,9},{9,1},{17,25},{25,17},{2,10},{10... | collective-permute-start | bytes 392 | tf_op jit(solution)/shard_map/ppermute | solution.py:365
  14.2 0.0 copy-done.5
  14.2 0.0 collective-permute-start
  14.2 4.6 %collective-permute-done.3 = f32[1,32]{1,0:T(1,128)S(1)} collective-permute-done((f32[1,32]{1,0:T(1,128)S(1)}, f32[1,32]{1,0:T(1,128)S(1)}, u32[]{:S(2)}, u32[]{:S(2)}) %collective-permute-start.3) | collective-permute-done | bytes 160 | tf_op jit(solution)/shard_map/ppermute | solution.py:365
  18.8 1.5 %collective-permute-start.4 = (f32[2,32]{1,0:T(2,128)S(1)}, f32[2,32]{1,0:T(2,128)S(1)}, u32[]{:S(2)}, u32[]{:S(2)}) collective-permute-start(f32[2,32]{1,0:T(2,128)S(1)} %pad_maximum_fusion.4), channel_id=1, source_target_pairs={{0,16},{8,24},{16,0},{24,8},{1,17},{9,25},{17,1},{25,9},{2,18},{10... | collective-permute-start | bytes 776 | tf_op jit(solution)/shard_map/ppermute | solution.py:365
  20.3 2.2 %collective-permute-done.4 = f32[2,32]{1,0:T(2,128)S(1)} collective-permute-done((f32[2,32]{1,0:T(2,128)S(1)}, f32[2,32]{1,0:T(2,128)S(1)}, u32[]{:S(2)}, u32[]{:S(2)}) %collective-permute-start.4) | collective-permute-done | bytes 288 | tf_op jit(solution)/shard_map/ppermute | solution.py:365
  22.5 0.0 collective-permute-done
  22.6 2.1 %collective-permute-start.1 = (f32[2,128]{1,0:T(2,128)S(1)}, f32[2,128]{1,0:T(2,128)S(1)}, u32[]{:S(2)}, u32[]{:S(2)}) collective-permute-start(f32[2,128]{1,0:T(2,128)S(1)} %pad_maximum_fusion.3), channel_id=1, source_target_pairs={{0,2},{1,3},{2,0},{3,1},{4,6},{5,7},{6,4},{7,5},{8,10},{9,11},{10,... | collective-permute-start | bytes 3080 | tf_op jit(solution)/shard_map/ppermute | solution.py:365
  24.7 4.7 %collective-permute-done.1 = f32[2,128]{1,0:T(2,128)S(1)} collective-permute-done((f32[2,128]{1,0:T(2,128)S(1)}, f32[2,128]{1,0:T(2,128)S(1)}, u32[]{:S(2)}, u32[]{:S(2)}) %collective-permute-start.1) | collective-permute-done | bytes 1056 | tf_op jit(solution)/shard_map/ppermute | solution.py:365
  29.5 0.0 copy-start.2
  29.5 0.0 copy-start.3
  29.5 4.6 %collective-permute-start.2 = (f32[4,128]{1,0:T(4,128)S(1)}, f32[4,128]{1,0:T(4,128)S(1)}, u32[]{:S(2)}, u32[]{:S(2)}) collective-permute-start(f32[4,128]{1,0:T(4,128)S(1)} %pad_maximum_fusion.1), channel_id=1, source_target_pairs={{0,4},{1,5},{2,6},{3,7},{4,0},{5,1},{6,2},{7,3},{8,12},{9,13},{10,... | collective-permute-start | bytes 6152 | tf_op jit(solution)/shard_map/ppermute | solution.py:365
  34.1 0.0 copy-done.2
  34.1 0.0 copy-done.3
  34.1 0.3 fusion
  34.4 3.7 %collective-permute-done.2 = f32[4,128]{1,0:T(4,128)S(1)} collective-permute-done((f32[4,128]{1,0:T(4,128)S(1)}, f32[4,128]{1,0:T(4,128)S(1)}, u32[]{:S(2)}, u32[]{:S(2)}) %collective-permute-start.2) | collective-permute-done | bytes 2080 | tf_op jit(solution)/shard_map/ppermute | solution.py:365
  38.1 0.1 constant_dynamic-slice_fusion
  38.2 0.1 mul.78
  38.3 0.2 fusion.2
  38.5 0.9 %all-to-all-done.x_ref = bf16[32,128,128]{2,1,0:T(8,128)(2,1)S(1)} async-done(((bf16[32,128,128]{2,1,0:T(8,128)(2,1)}), bf16[32,128,128]{2,1,0:T(8,128)(2,1)S(1)}, u32[]{:S(2)}, u32[]{:S(2)}) %all-to-all-start) | async-done | bytes 1048608 | tf_op jit(solution)/shard_map/all_to_all | solution.py:389
  39.4 0.0 copy-done.1
  39.4 1.7 %shard_map.119 = bf16[32,128,128]{2,1,0:T(8,128)(2,1)S(1)} custom-call(bf16[32,128,128]{2,1,0:T(8,128)(2,1)S(1)} %all-to-all-done.x_ref, bf16[5,256,256]{2,1,0:T(8,128)(2,1)S(1)} %copy-done.1, f32[32,128]{1,0:T(8,128)S(1)} %get-tuple-element.24.cs_ref, f32[32,128]{1,0:T(8,128)S(1)} %get-tuple-element.21.ss_ref, f32[4,32,128]{2,1,0:T(8,128)S(1)} %get-tuple-element.14.ct_ref, ...), custom_call_target="tpu_custom_call" | custom-call | tf_op jit(solution)/shard_map/pallas_call | solution.py:284
  41.1 0.0 copy-start
  41.1 30.1 %all_to_all.10 = bf16[32,128,128]{2,1,0:T(8,128)(2,1)S(1)} all-to-all(bf16[32,128,128]{2,1,0:T(8,128)(2,1)S(1)} %shard_map.119), channel_id=1, replica_groups=mesh['src'=4,'tgt'=8] {'src','tgt'}, dimensions={0} | all-to-all | bytes 2097152 | tf_op jit(solution)/shard_map/all_to_all | solution.py:389
  71.2 0.0 copy-done
  71.2 3.3 %shard_map.120 = bf16[32,128,128]{2,1,0:T(8,128)(2,1)} custom-call(bf16[7,256,256]{2,1,0:T(8,128)(2,1)S(1)} %copy-done, f32[32,128]{1,0:T(8,128)S(1)} %get-tuple-element.23.c_ref, f32[32,128]{1,0:T(8,128)S(1)} %get-tuple-element.22.s_ref, bf16[128,32,128]{2,1,0:T(8,128)(2,1)S(1)} %bitcast.9), custom_call_target="tpu_custom_call" | custom-call | tf_op jit(solution)/shard_map/pallas_call | solution.py:345
  (10 shorter events, 0.1 us)
Async XLA Ops:
  4.4 35.0 %copy-start.1 = (bf16[5,256,256]{2,1,0:T(8,128)(2,1)S(1)}, bf16[5,256,256]{2,1,0:T(8,128)(2,1)}, u32[]{:S(2)}) copy-start(bf16[5,256,256]{2,1,0:T(8,128)(2,1)} %constant.31.clone.m_ref) | copy-start | bytes 1966084
  4.4 34.9 %all-to-all-start = ((bf16[32,128,128]{2,1,0:T(8,128)(2,1)}), bf16[32,128,128]{2,1,0:T(8,128)(2,1)S(1)}, u32[]{:S(2)}, u32[]{:S(2)}) async-start(bf16[32,128,128]{2,1,0:T(8,128)(2,1)} %bitcast.1), calls=%async_computation | async-start | bytes 2097152 | tf_op jit(solution)/shard_map/all_to_all | solution.py:389
  11.8 0.7 copy-start.4
  12.4 1.8 %copy-start.5 = (f32[128]{0:T(128)S(1)}, f32[128]{0:T(128)}, u32[]{:S(2)}) copy-start(f32[128]{0:T(128)} %param.13) | copy-start | bytes 1540
  12.4 6.4 %collective-permute-start.3 = (f32[1,32]{1,0:T(1,128)S(1)}, f32[1,32]{1,0:T(1,128)S(1)}, u32[]{:S(2)}, u32[]{:S(2)}) collective-permute-start(f32[1,32]{1,0:T(1,128)S(1)} %bitcast.10), channel_id=1, source_target_pairs={{0,8},{8,0},{16,24},{24,16},{1,9},{9,1},{17,25},{25,17},{2,10},{10... | collective-permute-start | bytes 392 | tf_op jit(solution)/shard_map/ppermute | solution.py:365
  14.2 8.4 %collective-permute-start = (f32[1,128]{1,0:T(1,128)S(1)}, f32[1,128]{1,0:T(1,128)S(1)}, u32[]{:S(2)}, u32[]{:S(2)}) collective-permute-start(f32[1,128]{1,0:T(1,128)S(1)} %bitcast.12), channel_id=1, source_target_pairs={{0,1},{1,0},{2,3},{3,2},{4,5},{5,4},{6,7},{7,6},{8,9},{9,8},{10,11... | collective-permute-start | bytes 1544 | tf_op jit(solution)/shard_map/ppermute | solution.py:365
  18.8 3.7 %collective-permute-start.4 = (f32[2,32]{1,0:T(2,128)S(1)}, f32[2,32]{1,0:T(2,128)S(1)}, u32[]{:S(2)}, u32[]{:S(2)}) collective-permute-start(f32[2,32]{1,0:T(2,128)S(1)} %pad_maximum_fusion.4), channel_id=1, source_target_pairs={{0,16},{8,24},{16,0},{24,8},{1,17},{9,25},{17,1},{25,9},{2,18},{10... | collective-permute-start | bytes 776 | tf_op jit(solution)/shard_map/ppermute | solution.py:365
  22.6 6.9 %collective-permute-start.1 = (f32[2,128]{1,0:T(2,128)S(1)}, f32[2,128]{1,0:T(2,128)S(1)}, u32[]{:S(2)}, u32[]{:S(2)}) collective-permute-start(f32[2,128]{1,0:T(2,128)S(1)} %pad_maximum_fusion.3), channel_id=1, source_target_pairs={{0,2},{1,3},{2,0},{3,1},{4,6},{5,7},{6,4},{7,5},{8,10},{9,11},{10,... | collective-permute-start | bytes 3080 | tf_op jit(solution)/shard_map/ppermute | solution.py:365
  29.5 4.6 %copy-start.2 = (f32[128]{0:T(128)S(1)}, f32[128]{0:T(128)}, u32[]{:S(2)}) copy-start(f32[128]{0:T(128)} %constant.33.clone) | copy-start | bytes 1540
  29.5 4.6 %copy-start.3 = (f32[128]{0:T(128)S(1)}, f32[128]{0:T(128)}, u32[]{:S(2)}) copy-start(f32[128]{0:T(128)} %constant.32.clone) | copy-start | bytes 1540
  29.5 8.6 %collective-permute-start.2 = (f32[4,128]{1,0:T(4,128)S(1)}, f32[4,128]{1,0:T(4,128)S(1)}, u32[]{:S(2)}, u32[]{:S(2)}) collective-permute-start(f32[4,128]{1,0:T(4,128)S(1)} %pad_maximum_fusion.1), channel_id=1, source_target_pairs={{0,4},{1,5},{2,6},{3,7},{4,0},{5,1},{6,2},{7,3},{8,12},{9,13},{10,... | collective-permute-start | bytes 6152 | tf_op jit(solution)/shard_map/ppermute | solution.py:365
  41.1 30.1 %copy-start = (bf16[7,256,256]{2,1,0:T(8,128)(2,1)S(1)}, bf16[7,256,256]{2,1,0:T(8,128)(2,1)}, u32[]{:S(2)}) copy-start(bf16[7,256,256]{2,1,0:T(8,128)(2,1)} %constant.34.clone.m_ref) | copy-start | bytes 2752516
